TPU v7x, 32 devices: a whole 2x2x4 slice. The times are simulated.
32 devices in a mesh: seq: 8 (over z, x), grp: 4 (over y, core).
Axes of the slice: x: 2, y: 2, z: 4, core: 2. Of those that a mesh axis runs over, the one named last changes fastest.
Arguments:
- query: bfloat16 [128, 24576], P(('grp', 'seq')), parts along dimension 0
- dec_query: bfloat16 [32, 24576], P(('grp', 'seq')), parts along dimension 0
- cache_kv: bfloat16 [32768, 576], P(('grp', 'seq')), parts along dimension 0
- span_kv: bfloat16 [128, 576], P(('grp', 'seq')), parts along dimension 0, may hold values from -4 to 4
- dec_kv: bfloat16 [32, 576], P(('grp', 'seq')), parts along dimension 0
- cache_fill: int32 [32], P('grp'), parts along dimension 0, may hold values from 128 to 992, as said below
- owner: int32 [128], P('grp'), parts along dimension 0, may hold values from 0 to 7, as said below
- slot: int32 [128], P('grp'), parts along dimension 0, may hold values from 128 to 1023, as said below
- dec_len: int32 [32], P('grp'), parts along dimension 0, may hold values from 1 to 32
- w_uk: bfloat16 [128, 128, 512], P('seq'), may hold values from -0.5 to 0.5
- w_uv: bfloat16 [128, 512, 128], P('seq'), may hold values from -0.25 to 0.25
Outputs:
- span_out: bfloat16 [128, 16384], P('grp', 'seq'), parts along dimension 0
- dec_out: bfloat16 [32, 16384], P('grp', 'seq'), parts along dimension 0
- new_cache: bfloat16 [32768, 576], P(('grp', 'seq')), parts along dimension 0
There are 4 independent parts, one for each index of `grp`. A program takes and returns all parts, laid end to end along the dimension named above; an argument that names none is the same for every part. Nothing has to cross between parts.
Inputs may be any that keep to these rules, and one draw needn't show every extreme that they name: `cache_fill`: every block keeps at least 128 filled slots and room for all 32 new rows. `owner`: a block index for each prefill token; blocks receive unequal numbers of rows. slot[t] = cache_fill[owner[t]] plus the number of earlier prefill tokens with the same owner.
All inputs are finite; a program needn't handle non-finite values.
Results may differ from a plain program's by a relative error of at most 0.014.
Values may be sent and summed in bfloat16 or wider, within the bound.
No kernel may reach another device: no remote copies, remote signals or barrier semaphores. Data moves between devices by JAX's collectives and lax.ppermute only.
A program may use at most 192 MiB of HBM per device.

v0:
```python
import jax
import jax.numpy as jnp
from jax import lax
from jax.sharding import PartitionSpec as P

DN = 128
DC = 512


score_scale = 0.1353


def tag_rows(rows, cache_fill, owner, slot, pos_dev, span):
    block = rows // pos_dev
    local = rows % pos_dev
    count = cache_fill.shape[0]
    fills = jnp.sum(
        jnp.where(
            block[:, None] == jnp.arange(count, dtype=jnp.int32)[None, :], cache_fill[None, :], 0
        ),
        axis=1,
    )
    base = jnp.where(local < fills, -1, span + 1)
    target = owner * pos_dev + slot
    token = jnp.arange(span, dtype=jnp.int32)
    placed = jnp.sum(jnp.where(rows[:, None] == target[None, :], token[None, :] + 1, 0), axis=1)
    return jnp.where(placed > 0, placed - 1, base)


def combine(state, peak, total, output):
    old_peak, old_total, old_acc = state
    top = jnp.maximum(old_peak, peak)
    keep = jnp.exp(old_peak - top)
    fresh = jnp.exp(peak - top)
    return (
        top,
        old_total * keep + total * fresh,
        old_acc * keep[..., None] + output * fresh[..., None],
    )


def block_partial(absorbed, keys, tags, limits):
    scores = (
        jnp.einsum("qhc,pc->qhp", absorbed, keys, preferred_element_type=jnp.float32) * score_scale
    )
    visible = tags[None, None, :] < limits[:, None, None]
    peak = jnp.max(jnp.where(visible, scores, -1e30), axis=2)
    weights = jnp.where(visible, jnp.exp(scores - peak[..., None]), 0.0)
    total = jnp.sum(weights, axis=2)
    output = jnp.einsum(
        "qhp,pc->qhc",
        weights.astype(jnp.bfloat16),
        keys[:, :DC],
        preferred_element_type=jnp.float32,
    )
    return (peak, total, output)


def grouped(absorbed, keys, tags, limits):
    heads = absorbed.shape[1]
    group = 32
    count = heads // group
    rows = absorbed.shape[0]

    def one_group(index):
        return block_partial(
            lax.dynamic_slice_in_dim(absorbed, index * group, group, 1), keys, tags, limits
        )

    peak, total, output = lax.map(one_group, jnp.arange(count, dtype=jnp.int32))
    peak = jnp.moveaxis(peak, 0, 1).reshape(rows, heads)
    total = jnp.moveaxis(total, 0, 1).reshape(rows, heads)
    output = jnp.moveaxis(output, 0, 1).reshape(rows, heads, DC)
    return (peak, total, output)


def body(query, dec_query, cache_kv, span_kv, dec_kv, cache_fill, owner, slot, dec_len, w_uk, w_uv):
    me = lax.axis_index("seq")
    pos_dev = cache_kv.shape[0]
    span = owner.shape[0]
    new_rows, dec_keys = (
        lax.all_gather(span_kv, "seq", axis=0, tiled=True),
        lax.all_gather(dec_kv, "seq", axis=0, tiled=True),
    )
    local = jnp.arange(pos_dev, dtype=jnp.int32)
    target = jnp.where(owner == me, slot, -1)
    onehot = local[:, None] == target[None, :]
    placed = jnp.dot(
        onehot.astype(jnp.bfloat16), new_rows, preferred_element_type=jnp.float32
    ).astype(jnp.bfloat16)
    new_cache = jnp.where(jnp.any(onehot, axis=1)[:, None], placed, cache_kv)
    heads_all = w_uk.shape[0] * lax.axis_size("seq")
    width = query.shape[1] // heads_all
    q_span, q_dec = (
        lax.all_to_all(
            query.reshape(query.shape[0], heads_all, width),
            "seq",
            split_axis=1,
            concat_axis=0,
            tiled=True,
        ),
        lax.all_to_all(
            dec_query.reshape(dec_query.shape[0], heads_all, width),
            "seq",
            split_axis=1,
            concat_axis=0,
            tiled=True,
        ),
    )
    both = jnp.concatenate([q_span, q_dec], axis=0)
    latent = jnp.einsum(
        "thn,hnc->thc", both[:, :, :DN], w_uk, preferred_element_type=jnp.float32
    ).astype(jnp.bfloat16)
    absorbed = jnp.concatenate([latent, both[:, :, DN:]], axis=2)
    limits = jnp.concatenate([jnp.arange(1, span + 1, dtype=jnp.int32), dec_len])
    count = absorbed.shape[0]
    heads = absorbed.shape[1]
    everyone = lax.all_gather(absorbed, "seq", axis=1, tiled=True)
    rows = me * pos_dev + local
    peak, total, output = grouped(
        everyone, new_cache, tag_rows(rows, cache_fill, owner, slot, pos_dev, span), limits
    )
    peaks, totals, outputs = (
        lax.all_to_all(peak[None], "seq", split_axis=2, concat_axis=0, tiled=True),
        lax.all_to_all(total[None], "seq", split_axis=2, concat_axis=0, tiled=True),
        lax.all_to_all(output[None], "seq", split_axis=2, concat_axis=0, tiled=True),
    )
    peak = jnp.max(peaks, axis=0)
    factor = jnp.exp(peaks - peak[None])
    total = jnp.sum(factor * totals, axis=0)
    acc = jnp.sum(factor[..., None] * outputs, axis=0)
    dec_abs = absorbed[span:]
    own = (
        jnp.einsum("rhc,rc->rh", dec_abs, dec_keys, preferred_element_type=jnp.float32)
        * score_scale
    )
    rows_dec = dec_abs.shape[0]
    own_out = jnp.broadcast_to(dec_keys[:, None, :DC].astype(jnp.float32), (rows_dec, heads, DC))
    dec_state = combine(
        (peak[span:], total[span:], acc[span:]),
        own,
        jnp.ones((rows_dec, heads), jnp.float32),
        own_out,
    )
    total = jnp.concatenate([total[:span], dec_state[1]], axis=0)
    acc = jnp.concatenate([acc[:span], dec_state[2]], axis=0)
    latent_out = (acc / total[..., None]).astype(jnp.bfloat16)
    result = jnp.einsum(
        "qhc,hcv->qhv", latent_out, w_uv, preferred_element_type=jnp.float32
    ).astype(jnp.bfloat16)
    result = result.reshape(count, heads * w_uv.shape[2])
    return (result[:span], result[span:], new_cache)


def solution(mesh):
    in_specs = (
        P(("grp", "seq"), None),
        P(("grp", "seq"), None),
        P(("grp", "seq"), None),
        P(("grp", "seq"), None),
        P(("grp", "seq"), None),
        P("grp"),
        P("grp"),
        P("grp"),
        P("grp"),
        P("seq", None, None),
        P("seq", None, None),
    )
    out_specs = (P("grp", "seq"), P("grp", "seq"), P(("grp", "seq"), None))
    return jax.shard_map(body, mesh=mesh, in_specs=in_specs, out_specs=out_specs, check_vma=False)
```

profile of v0, /device:TPU:0, one launch (start us, length us, event | category | flops | bytes accessed | tf_op | source)
XLA Modules:
  0.0 486.4 jit_solution(3941874224271232000)
XLA Ops:
  10.9 7.3 %all-to-all-start.1 = ((bf16[8,2,1536]{2,1,0:T(2,128)(2,1)}), bf16[8,2,1536]{2,1,0:T(2,128)(2,1)S(1)}, u32[]{:S(2)}, u32[]{:S(2)}) async-start(bf16[8,2,1536]{2,1,0:T(2,128)(2,1)} %reshape.104), calls=%async_computation.1 | async-start | bytes 98304 | tf_op jit(solution)/shard_map/all_to_all | solution.py:102
  20.3 4.7 all-to-all-done.1
  25.0 3.4 all-to-all-start
  28.6 8.0 %all-to-all-done = bf16[4,128,192]{2,0,1:T(4,128)(2,1)S(1)} async-done(((bf16[4,128,192]{2,0,1:T(4,128)(2,1)}), bf16[4,128,192]{2,0,1:T(4,128)(2,1)S(1)}, u32[]{:S(2)}, u32[]{:S(2)}) %all-to-all-start) | async-done | bytes 196640 | tf_op jit(solution)/shard_map/all_to_all | solution.py:95
  38.6 30.9 %all-gather = bf16[8,4,576]{2,1,0:T(4,128)(2,1)S(1)} all-gather(bf16[1,4,576]{2,1,0:T(4,128)(2,1)S(1)} %bitcast.107), channel_id=1, replica_groups=mesh['seq'=8,'grp'=4] {'seq'}, dimensions={0}, use_global_device_ids=true | all-gather | bytes 41472 | tf_op jit(solution)/shard_map/all_gather | solution.py:82
  69.7 1.8 fusion.17
  71.5 1.5 copy.97
  73.3 66.5 %all-gather.4.cloned.1.call-done = bf16[40,128,576]{2,0,1:T(8,128)(2,1)} async-done(((bf16[40,16,576]{2,0,1:T(8,128)(2,1)}), bf16[40,128,576]{2,0,1:T(8,128)(2,1)}) %all-gather.4.cloned.1.call-update) | async-done | bytes 5898256 | tf_op jit(solution)/shard_map/all_gather | solution.py:118
  139.8 40.8 %while.14 = (s32[]{:T(128)}, f32[4,40,32]{2,1,0:T(8,128)S(1)}, f32[4,40,32]{2,1,0:T(8,128)S(1)}, f32[4,40,32,512]{3,2,0,1:T(8,128)}, s32[1024]{0:T(1024)S(1)}, /...) while((s32[]{:T(128)}, f32[4,40,32]{2,1,0:T(8,128)S(1)}, ...), condition=%wide.region_6.7_spmd, body=%wide.region_3.6_spmd.sunk | while | flops 2866583040 | bytes 30006664 | solution.py:70
  141.1 1.7 constant_dynamic-slice_fusion.2
  142.8 2.5 select_reduce_fusion.4
  145.4 1.5 fusion.49
  146.9 3.1 bitcast_dynamic-update-slice_fusion.6
  151.4 1.7 constant_dynamic-slice_fusion.2
  153.1 2.6 select_reduce_fusion.4
  155.6 1.5 fusion.49
  157.1 3.1 bitcast_dynamic-update-slice_fusion.6
  161.5 1.7 constant_dynamic-slice_fusion.2
  163.2 2.6 select_reduce_fusion.4
  165.8 1.5 fusion.49
  167.3 3.1 bitcast_dynamic-update-slice_fusion.6
  171.7 1.7 constant_dynamic-slice_fusion.2
  173.4 2.6 select_reduce_fusion.4
  176.0 1.5 fusion.49
  177.5 3.1 bitcast_dynamic-update-slice_fusion.6
  182.8 3.3 all-to-all-start.2
  187.7 5.0 %all-to-all-done.2 = f32[8,1,640]{2,1,0:T(1,128)S(1)} async-done(((f32[8,1,640]{2,1,0:T(1,128)}), f32[8,1,640]{2,1,0:T(1,128)S(1)}, u32[]{:S(2)}, u32[]{:S(2)}) %all-to-all-start.2) | async-done | bytes 20512 | tf_op jit(solution)/shard_map/all_to_all | solution.py:124
  192.6 3.5 all-to-all-start.4
  196.2 13.9 %copy.102 = f32[1,40,128,512]{3,1,0,2:T(8,128)} copy(f32[1,40,128,512]{3,2,1,0:T(8,128)} %bitcast.93) | data formatting | bytes 20971520 | tf_op jit(solution)/shard_map/broadcast_in_dim;reshape | solution.py:126
  210.1 5.9 %all-to-all-start.3 = ((f32[1,40,128,512]{3,1,0,2:T(8,128)}), f32[1,40,128,512]{3,1,0,2:T(8,128)}, u32[]{:S(2)}, u32[]{:S(2)}) async-start(f32[1,40,128,512]{3,1,0,2:T(8,128)} %copy.102), calls=%async_computation.3 | async-start | bytes 20971520 | tf_op jit(solution)/shard_map/all_to_all | solution.py:126
  215.9 245.9 %all-gather.1 = bf16[8,1,576]{2,1,0:T(2,128)(2,1)S(1)} all-gather(bf16[1,1,576]{2,1,0:T(2,128)(2,1)S(1)} %bitcast.108), channel_id=1, replica_groups=mesh['seq'=8,'grp'=4] {'seq'}, dimensions={0}, use_global_device_ids=true | all-gather | bytes 10368 | tf_op jit(solution)/shard_map/all_gather | solution.py:83
  464.4 10.0 %copy.103 = f32[1,40,128,512]{3,2,1,0:T(8,128)S(1)} copy(f32[1,40,128,512]{3,1,0,2:T(8,128)} %all-to-all-done.3) | data formatting | bytes 20971520 | tf_op jit(solution)/shard_map/all_to_all | solution.py:126
  (105 shorter events, 22.4 us)
Async XLA Ops:
  7.2 29.9 %copy-start = (bf16[16,128,512]{2,1,0:T(8,128)(2,1)S(1)}, bf16[16,128,512]{2,1,0:T(8,128)(2,1)}, u32[]{:S(2)}) copy-start(bf16[16,128,512]{2,1,0:T(8,128)(2,1)} %param.22) | copy-start | bytes 6291460
  10.9 14.0 %all-to-all-start.1 = ((bf16[8,2,1536]{2,1,0:T(2,128)(2,1)}), bf16[8,2,1536]{2,1,0:T(2,128)(2,1)S(1)}, u32[]{:S(2)}, u32[]{:S(2)}) async-start(bf16[8,2,1536]{2,1,0:T(2,128)(2,1)} %reshape.104), calls=%async_computation.1 | async-start | bytes 98304 | tf_op jit(solution)/shard_map/all_to_all | solution.py:102
  25.0 11.6 %all-to-all-start = ((bf16[4,128,192]{2,0,1:T(4,128)(2,1)}), bf16[4,128,192]{2,0,1:T(4,128)(2,1)S(1)}, u32[]{:S(2)}, u32[]{:S(2)}) async-start(bf16[4,128,192]{2,0,1:T(4,128)(2,1)} %copy.91), calls=%async_computation | async-start | bytes 524288 | tf_op jit(solution)/shard_map/all_to_all | solution.py:95
  28.4 111.4 %all-gather.4.cloned.1.call-start = ((), (), s32[]{:S(2)}) async-start(), calls=%async_computation.5 | async-start | bytes 7372800 | tf_op jit(solution)/shard_map/all_gather | solution.py:118
  37.1 1.5 copy-start.5
  37.1 32.5 %copy-start.7 = (s32[32]{0:T(128)S(1)}, s32[32]{0:T(128)}, u32[]{:S(2)}) copy-start(s32[32]{0:T(128)} %param.20) | copy-start | bytes 388
  37.1 32.5 %copy-start.8 = (s32[32]{0:T(128)S(1)}, s32[32]{0:T(128)}, u32[]{:S(2)}) copy-start(s32[32]{0:T(128)} %param.19) | copy-start | bytes 388
  38.5 34.5 %copy-start.10 = (s32[8]{0:T(128)S(1)}, s32[8]{0:T(128)}, u32[]{:S(2)}) copy-start(s32[8]{0:T(128)} %param.21) | copy-start | bytes 100
  38.5 34.5 %copy-start.9 = (s32[8]{0:T(128)S(1)}, s32[8]{0:T(128)}, u32[]{:S(2)}) copy-start(s32[8]{0:T(128)} %param.18) | copy-start | bytes 100
  71.5 68.3 %copy-start.2 = (bf16[1024,576]{0,1:T(8,128)(2,1)}, bf16[1024,576]{0,1:T(8,128)(2,1)S(1)}, u32[]{:S(2)}) copy-start(bf16[1024,576]{0,1:T(8,128)(2,1)S(1)} %fusion.17) | copy-start | bytes 3538948
  141.0 1.8 copy-start.4
  151.2 1.8 copy-start.4
  161.4 1.8 copy-start.4
  171.6 1.8 copy-start.4
  182.8 9.9 %all-to-all-start.2 = ((f32[8,1,640]{2,1,0:T(1,128)}), f32[8,1,640]{2,1,0:T(1,128)S(1)}, u32[]{:S(2)}, u32[]{:S(2)}) async-start(f32[8,1,640]{2,1,0:T(1,128)} %reshape.106), calls=%async_computation.2 | async-start | bytes 40960 | tf_op jit(solution)/shard_map/all_to_all | solution.py:124
  192.6 17.4 %all-to-all-start.4 = ((f32[8,1,640]{2,1,0:T(1,128)}), f32[8,1,640]{2,1,0:T(1,128)S(1)}, u32[]{:S(2)}, u32[]{:S(2)}) async-start(f32[8,1,640]{2,1,0:T(1,128)} %reshape.108), calls=%async_computation.4 | async-start | bytes 40960 | tf_op jit(solution)/shard_map/all_to_all | solution.py:125
  210.0 5.9 %copy-start.6 = (bf16[1,576]{1,0:T(2,128)(2,1)S(1)}, bf16[1,576]{1,0:T(2,128)(2,1)}, u32[]{:S(2)}) copy-start(bf16[1,576]{1,0:T(2,128)(2,1)} %param.17) | copy-start | bytes 3460
  210.1 254.3 %all-to-all-start.3 = ((f32[1,40,128,512]{3,1,0,2:T(8,128)}), f32[1,40,128,512]{3,1,0,2:T(8,128)}, u32[]{:S(2)}, u32[]{:S(2)}) async-start(f32[1,40,128,512]{3,1,0,2:T(8,128)} %copy.102), calls=%async_computation.3 | async-start | bytes 20971520 | tf_op jit(solution)/shard_map/all_to_all | solution.py:126
  475.8 1.6 copy-start.3
  475.9 3.6 copy-start.1
Sparse Core Ops, SparseCore 0:
  38.6 101.0 all-gather.3
where the time goes:
time: 487 us; the launch traced here: 486 us
  blocking collectives  277 us (57%)
  waiting for transfers between devices  84.1 us (17%)
  local copies, waits for them, and re-layouts  44.2 us (9%)
  matrix products  25.9 us (5%)
  starting transfers between devices  23.4 us (5%)
  other arithmetic  14.7 us (3%)
  between operations  14.4 us (3%)
    all_gather x1, blocking collectives, body(): lax.all_gather(dec_kv, 'seq', axis=0, tiled=True)  246 us
    all_gather x1, waiting for transfers between devices, body(): everyone = lax.all_gather(absorbed, 'seq', axis=1, tiled=True)  66.5 us
    all_gather x1, blocking collectives, body(): lax.all_gather(span_kv, 'seq', axis=0, tiled=True)  30.9 us
    another operation x1, local copies, waits for them, and re-layouts, body(): output[None]  13.9 us
    dot_general x4, matrix products, block_partial(): jnp.einsum('qhp,pc->qhc', weights.astype(jnp.bfloat16), keys[:, :DC], pre...  12.5 us
    dot_general x4, matrix products, block_partial(): jnp.einsum('qhc,pc->qhp', absorbed, keys, preferred_element_type=jnp.floa...  10.2 us
    all_to_all x1, local copies, waits for them, and re-layouts, body(): lax.all_to_all(output[None], 'seq', split_axis=2, concat_axis=0, tiled=True)  10 us
  transfers between devices with their start and end apart: 6, of which 4 were waited for; matrix products, arithmetic and copies ran while one was open for 5% of the time, Pallas kernels for 0%

commit v1 on v0

v1 whole, which is shorter than its diff:
```python
import functools

import jax
import jax.numpy as jnp
from jax import lax
from jax.experimental import pallas as pl
from jax.experimental.pallas import tpu as pltpu
from jax.sharding import PartitionSpec as P

DN = 128
DC = 512
LANES = 128
CHUNKS = 4

score_scale = 0.1353
LOG2E = 1.4426950408889634
HIDDEN = -1e30
FLOOR = -1e25


def lanes(x, width):
    return jnp.concatenate([x] * (width // LANES), axis=1) if width > LANES else x


def attend_kernel(pieces, extra, first, last, *refs):
    refs = list(refs)
    fills = refs.pop(0)
    q_ref = refs.pop(0)
    keys = [refs.pop(0) for _ in pieces]
    if extra:
        new_ref = refs.pop(0)
        bias_ref = refs.pop(0)
    if not first:
        m_in, l_in, acc_in = refs.pop(0), refs.pop(0), refs.pop(0)
    q = q_ref[...]
    rows = q.shape[0]
    scores = []
    for (start, width, which), ref in zip(pieces, keys):
        s = jnp.dot(q, ref[...], preferred_element_type=jnp.float32)
        slot = start + lax.broadcasted_iota(jnp.int32, (1, width), 1)
        scores.append(jnp.where(slot < fills[which], s, HIDDEN))
    if extra:
        s = lax.dot_general(
            q, new_ref[...], (((1,), (1,)), ((), ())), preferred_element_type=jnp.float32
        )
        bias = bias_ref[...]
        scores.append(s + jnp.concatenate([bias] * (rows // bias.shape[0]), axis=0))
    peak = functools.reduce(jnp.maximum, [jnp.max(s, axis=1, keepdims=True) for s in scores])
    peak = jnp.maximum(peak, FLOOR)
    if not first:
        old = m_in[...]
        peak = jnp.maximum(peak, old[:, :1])
    scale = score_scale * LOG2E
    total = 0.0
    acc = 0.0
    for i, s in enumerate(scores):
        e = jnp.exp2((s - peak) * scale)
        total = total + jnp.sum(e, axis=1, keepdims=True)
        w = e.astype(jnp.bfloat16)
        if i < len(pieces):
            acc = acc + lax.dot_general(
                w, keys[i][:DC, :], (((1,), (1,)), ((), ())), preferred_element_type=jnp.float32
            )
        else:
            acc = acc + jnp.dot(w, new_ref[:, :DC], preferred_element_type=jnp.float32)
    if not first:
        keep = jnp.exp2((old[:, :1] - peak) * scale)
        total = total + l_in[:, :1] * keep
        acc = acc + acc_in[...] * keep
    if not last:
        m_out, l_out, acc_out = refs
        m_out[...] = jnp.broadcast_to(peak, (rows, LANES))
        l_out[...] = jnp.broadcast_to(total, (rows, LANES))
        acc_out[...] = acc
        return
    (out,) = refs
    out[:rows, :] = (acc * (1.0 / total)).astype(jnp.bfloat16)
    weight = jnp.broadcast_to(peak * scale + jnp.log2(total), (rows, LANES))
    tail = out.shape[0] - rows
    place = lax.broadcasted_iota(jnp.int32, (tail, LANES), 0)
    packed = jnp.zeros((tail, LANES), jnp.float32)
    for g in range(rows // LANES):
        turned = jnp.transpose(weight[g * LANES : (g + 1) * LANES, :])
        packed = jnp.where(place == g, turned[:tail, :], packed)
    high = packed.astype(jnp.bfloat16)
    rest = packed - high.astype(jnp.float32)
    mid = rest.astype(jnp.bfloat16)
    low = (rest - mid.astype(jnp.float32)).astype(jnp.bfloat16)
    out[rows:, :] = jnp.concatenate([high, mid, low, jnp.zeros_like(low)], axis=1)


def attend(fills, q, pieces, new=None, state=None, last=False, tile=None):
    rows, width = q.shape
    tile = rows if tile is None else tile
    spec = tuple((start, keys.shape[1], which) for start, which, keys in pieces)
    operands = [fills, q]
    in_specs = [
        pl.BlockSpec(memory_space=pltpu.SMEM),
        pl.BlockSpec((tile, width), lambda i: (i, 0)),
    ]
    for _, _, keys in pieces:
        operands.append(keys)
        in_specs.append(pl.BlockSpec(keys.shape, lambda i: (0, 0)))
    if new is not None:
        for x in new:
            operands.append(x)
            in_specs.append(pl.BlockSpec(x.shape, lambda i: (0, 0)))
    state_specs = [
        pl.BlockSpec((tile, LANES), lambda i: (i, 0)),
        pl.BlockSpec((tile, LANES), lambda i: (i, 0)),
        pl.BlockSpec((tile, DC), lambda i: (i, 0)),
    ]
    if state is not None:
        operands += list(state)
        in_specs += state_specs
    if last:
        tail = -(-rows // (LANES * 16)) * 16
        out_shape = jax.ShapeDtypeStruct((rows + tail, DC), jnp.bfloat16)
        out_specs = pl.BlockSpec((rows + tail, DC), lambda i: (0, 0))
    else:
        out_shape = (
            jax.ShapeDtypeStruct((rows, LANES), jnp.float32),
            jax.ShapeDtypeStruct((rows, LANES), jnp.float32),
            jax.ShapeDtypeStruct((rows, DC), jnp.float32),
        )
        out_specs = tuple(state_specs)
    count = sum(piece[1] for piece in spec)
    return pl.pallas_call(
        functools.partial(attend_kernel, spec, new is not None, state is None, last),
        grid=(rows // tile,),
        in_specs=in_specs,
        out_specs=out_specs,
        out_shape=out_shape,
        compiler_params=pltpu.CompilerParams(vmem_limit_bytes=40 * 1024 * 1024),
        cost_estimate=pl.CostEstimate(
            flops=2 * rows * count * (width + DC),
            bytes_accessed=2 * count * width + 4 * rows * DC * 2,
            transcendentals=rows * count,
        ),
        name="attend",
    )(*operands)


def finish_kernel(count, m_ref, l_ref, acc_ref, far_ref, w_ref, out_ref):
    rows = m_ref.shape[0]
    heads = w_ref.shape[0]
    scale = score_scale * LOG2E
    parts = far_ref[rows:, :].astype(jnp.float32)
    packed = parts[:, :LANES] + parts[:, LANES : 2 * LANES] + parts[:, 2 * LANES : 3 * LANES]
    columns = []
    for g in range(rows // LANES):
        row = jnp.broadcast_to(packed[g : g + 1, :], (LANES, LANES))
        columns.append(jnp.transpose(row))
    far = jnp.concatenate(columns, axis=0)
    near = m_ref[...] * scale
    top = jnp.maximum(near, far)
    w_near = jnp.exp2(near - top)
    w_far = jnp.exp2(far - top)
    total = l_ref[...] * w_near + w_far
    inverse = 1.0 / total
    w_near = lanes(w_near * inverse, DC)
    w_far = lanes(w_far * inverse, DC)
    for h in range(heads):
        a, b = h * count, (h + 1) * count
        near_part = acc_ref[a:b, :] * w_near[a:b, :]
        far_part = far_ref[:rows, :].astype(jnp.float32)[a:b, :] * w_far[a:b, :]
        latent = (near_part + far_part).astype(jnp.bfloat16)
        out_ref[:, h * LANES : (h + 1) * LANES] = jnp.dot(
            latent, w_ref[h], preferred_element_type=jnp.float32
        ).astype(jnp.bfloat16)


def finish(count, state, far, w_uv):
    heads = w_uv.shape[0]
    return pl.pallas_call(
        functools.partial(finish_kernel, count),
        out_shape=jax.ShapeDtypeStruct((count, heads * w_uv.shape[2]), jnp.bfloat16),
        compiler_params=pltpu.CompilerParams(vmem_limit_bytes=40 * 1024 * 1024),
        cost_estimate=pl.CostEstimate(
            flops=2 * count * heads * DC * w_uv.shape[2],
            bytes_accessed=2 * w_uv.size + 6 * state[2].size,
            transcendentals=0,
        ),
        name="finish",
    )(*state, far, w_uv)


def body(query, dec_query, cache_kv, span_kv, dec_kv, cache_fill, owner, slot, dec_len, w_uk, w_uv):
    me = lax.axis_index("seq")
    n = lax.axis_size("seq")
    pos_dev = cache_kv.shape[0]
    span = owner.shape[0]
    rows_dec = dec_len.shape[0]
    count = span + rows_dec
    heads = w_uk.shape[0]
    row = cache_kv.shape[1]
    width = query.shape[1] // (heads * n)

    def swap(x, stride):
        return lax.ppermute(x, "seq", [(i, i ^ stride) for i in range(n)])

    far, pair = n // 2, n // 4
    near = [1 << b for b in range(pair.bit_length() - 1)]
    keys = cache_kv.T
    size = pos_dev // CHUNKS

    mine = jnp.concatenate([query, dec_query], axis=0)
    local = mine.shape[0]
    mine = jnp.swapaxes(mine.reshape(local, n, heads * width), 0, 1)
    fresh = jnp.concatenate([span_kv, dec_kv], axis=0)
    mine = jnp.concatenate([mine, jnp.broadcast_to(fresh[None], (n, local, row))], axis=2)
    got = lax.all_to_all(mine, "seq", split_axis=0, concat_axis=0, tiled=True)

    blocks = [(jnp.int32(0), [keys])]
    for stride in near:
        blocks += [(offset ^ stride, [swap(x, stride) for x in held]) for offset, held in blocks]
    pieces = []
    for c in range(CHUNKS):
        part = [(jnp.int32(far), swap(keys[:, c * size : (c + 1) * size], far))]
        for stride in near:
            part += [(offset ^ stride, swap(x, stride)) for offset, x in part]
        pieces.append(part)

    per = span // n
    got_span = got[:, :per].reshape(span, -1)
    got_dec = got[:, per:].reshape(rows_dec, -1)
    both = jnp.concatenate([got_span, got_dec], axis=0)
    new_rows = both[:, heads * width :]
    q = both[:, : heads * width].reshape(count, heads, width)
    latent = jnp.einsum(
        "thn,hnc->htc", q[:, :, :DN], w_uk, preferred_element_type=jnp.float32
    ).astype(jnp.bfloat16)
    absorbed = jnp.concatenate([latent, jnp.swapaxes(q[:, :, DN:], 0, 1)], axis=2)
    absorbed = absorbed.reshape(heads * count, row)
    other = swap(absorbed, pair)

    target = jnp.where(owner == me, slot, -1)
    onehot = jnp.arange(pos_dev, dtype=jnp.int32)[None, :] == target[:, None]
    placed = lax.dot_general(
        new_rows[:span],
        onehot.astype(jnp.bfloat16),
        (((0,), (0,)), ((), ())),
        preferred_element_type=jnp.float32,
    ).astype(jnp.bfloat16)
    new_cache = jnp.where(jnp.any(onehot, axis=0)[None, :], placed, keys).T

    limits = jnp.concatenate([jnp.arange(1, span + 1, dtype=jnp.int32), dec_len])
    index = jnp.arange(LANES, dtype=jnp.int32)
    queries = jnp.arange(count, dtype=jnp.int32)
    seen = (index[None, :] < span) & (index[None, :] < limits[:, None])
    seen |= (index[None, :] >= span) & (index[None, :] == queries[:, None])
    bias = jnp.where(seen, 0.0, HIDDEN).astype(jnp.float32)
    extra = jnp.zeros((LANES, row), jnp.bfloat16).at[:count].set(new_rows)

    held = [offset for offset, _ in blocks]
    offsets = held + [offset ^ far for offset in held]
    which = jnp.stack([me ^ offset for offset in offsets])
    fills = jnp.sum(
        jnp.where(which[:, None] == jnp.arange(n, dtype=jnp.int32)[None, :], cache_fill[None, :], 0),
        axis=1,
    )
    base = len(blocks)
    tile = heads // 2 * count
    stages = [[(0, i, xs[0]) for i, (_, xs) in enumerate(blocks)]]
    flat = [[(c * size, base + i, x) for i, (_, x) in enumerate(part)] for c, part in enumerate(pieces)]
    half = CHUNKS // 2
    stages.append([p for part in flat[:half] for p in part])
    stages.append([p for part in flat[half:-1] for p in part] + flat[-1][:1])
    final = flat[-1][1:]

    state = attend(fills, absorbed, stages[0], new=(extra, bias), tile=tile)
    guest = attend(fills, other, stages[0], tile=tile)
    for stage in stages[1:]:
        guest = attend(fills, other, stage, state=guest, tile=tile)
        state = attend(fills, absorbed, stage, state=state, tile=tile)
    sent = attend(fills, other, final, state=guest, last=True)
    back = swap(sent, pair)
    state = attend(fills, absorbed, final, state=state, tile=tile)
    result = finish(count, state, back, w_uv)
    return (result[:span], result[span:], new_cache)


def solution(mesh):
    in_specs = (
        P(("grp", "seq"), None),
        P(("grp", "seq"), None),
        P(("grp", "seq"), None),
        P(("grp", "seq"), None),
        P(("grp", "seq"), None),
        P("grp"),
        P("grp"),
        P("grp"),
        P("grp"),
        P("seq", None, None),
        P("seq", None, None),
    )
    out_specs = (P("grp", "seq"), P("grp", "seq"), P(("grp", "seq"), None))
    return jax.shard_map(body, mesh=mesh, in_specs=in_specs, out_specs=out_specs, check_vma=False)
```

time: 487 us -> 130 us (0.27)
  blocking collectives: 277 us -> 0 us
  Pallas kernels: 0 us -> 35.7 us
  local copies, waits for them, and re-layouts: 44.2 us -> 9.07 us
  waiting for transfers between devices: 84.1 us -> 58.2 us
  matrix products: 25.9 us -> 3.23 us
  between operations: 14.4 us -> 0.98 us
  other arithmetic: 14.7 us -> 3.52 us
    all_gather x2 -> x0, blocking collectives: 277 us -> none  [the longest x1 246 us: body(): lax.all_gather(dec_kv, 'seq', axis=0, tiled=True)]
    all_gather x1 -> x0, waiting for transfers between devices: 66.5 us -> none  [body(): everyone = lax.all_gather(absorbed, 'seq', axis=1, tiled=True)]
    pallas_call x0 -> x9, Pallas kernels: none -> 35.7 us  [the longest x8 35.1 us: attend(): pl.pallas_call(functools.partial(attend_kernel, spec, new is not None, st...]
    ppermute x0 -> x11, waiting for transfers between devices: none -> 34 us  [swap(): return lax.ppermute(x, 'seq', [(i, i ^ stride) for i in range(n)])]
    dot_general x12 -> x2, matrix products: 25.9 us -> 3.23 us  [the longest x1 2.82 us: body(): lax.dot_general(new_rows[:span], onehot.astype(jnp.bfloat16), (((0,), (0,...]
    all_to_all x5 -> x1, starting transfers between devices: 23.4 us -> 7.25 us  [body(): got = lax.all_to_all(mine, 'seq', split_axis=0, concat_axis=0, tiled=True)]
    another operation x3 -> x0, local copies, waits for them, and re-layouts: 14 us -> none  [the longest x1 13.9 us: body(): output[None]]
    ppermute x0 -> x11, starting transfers between devices: none -> 11.4 us  [swap(): return lax.ppermute(x, 'seq', [(i, i ^ stride) for i in range(n)])]
  transfers between devices with their start and end apart: 6 -> 12, of which waited for: 4 -> 6; matrix products, arithmetic and copies ran while one was open for 5% -> 8% of each run, Pallas kernels for 0% -> 25%
where the time goes in v1:
time: 130 us; the launch traced here: 129 us
  waiting for transfers between devices  58.2 us (45%)
  Pallas kernels  35.7 us (27%)
  starting transfers between devices  18.6 us (14%)
  local copies, waits for them, and re-layouts  9.07 us (7%)
  other arithmetic  3.52 us (3%)
  matrix products  3.23 us (2%)
    pallas_call x8, Pallas kernels, attend(): pl.pallas_call(functools.partial(attend_kernel, spec, new is not None, st...  35.1 us
    ppermute x11, waiting for transfers between devices, swap(): return lax.ppermute(x, 'seq', [(i, i ^ stride) for i in range(n)])  34 us
    all_to_all x1, waiting for transfers between devices, body(): got = lax.all_to_all(mine, 'seq', split_axis=0, concat_axis=0, tiled=True)  24.2 us
    ppermute x11, starting transfers between devices, swap(): return lax.ppermute(x, 'seq', [(i, i ^ stride) for i in range(n)])  11.4 us
    all_to_all x1, starting transfers between devices, body(): got = lax.all_to_all(mine, 'seq', split_axis=0, concat_axis=0, tiled=True)  7.25 us
    dot_general x1, matrix products, body(): lax.dot_general(new_rows[:span], onehot.astype(jnp.bfloat16), (((0,), (0,...  2.82 us
  transfers between devices with their start and end apart: 12, of which 6 were waited for; matrix products, arithmetic and copies ran while one was open for 8% of the time, Pallas kernels for 25%

profile of v1, /device:TPU:0, one launch (start us, length us, event | category | flops | bytes accessed | tf_op | source)
XLA Modules:
  0.0 129.4 jit_solution(17380558127993961464)
XLA Ops:
  0.6 1.3 %pad_maximum_fusion.2 = bf16[5,24576]{1,0:T(8,128)(2,1)S(1)} fusion(bf16[1,24576]{1,0:T(2,128)(2,1)} %param.14, bf16[4,24576]{1,0:T(4,128)(2,1)} %param.13), kind=kLoop, calls=%fused_computation.5 | loop fusion | flops 491520 | bytes 491520 | tf_op jit(solution)/shard_map/concatenate | solution.py:207
  2.0 0.7 pad_maximum_fusion.3
  2.7 0.9 pad_maximum_fusion.1
  3.6 7.3 %all-to-all-start = ((bf16[8,5,3648]{2,1,0:T(8,128)(2,1)}), bf16[8,5,3648]{2,1,0:T(8,128)(2,1)S(1)}, u32[]{:S(2)}, u32[]{:S(2)}) async-start(bf16[8,5,3648]{2,1,0:T(8,128)(2,1)} %pad_maximum_fusion.1), calls=%async_computation | async-start | bytes 950272 | tf_op jit(solution)/shard_map/all_to_all | solution.py:212
  10.8 2.0 %collective-permute-start.8 = (bf16[576,1024]{1,0:T(8,128)(2,1)}, bf16[576,1024]{1,0:T(8,128)(2,1)}, u32[]{:S(2)}, u32[]{:S(2)}) collective-permute-start(bf16[576,1024]{1,0:T(8,128)(2,1)} %bitcast.9.refs_2_), channel_id=1, source_target_pairs={{0,4},{4,0},{8,12},{12,8},{16,20},{20,16},{24,28},{28,24},{1,5},{5... | collective-permute-start | bytes 3538952 | tf_op jit(solution)/shard_map/ppermute | solution.py:200
  12.8 2.3 %fusion.13 = (bf16[576,256]{1,0:T(8,128)(2,1)}, bf16[576,256]{1,0:T(8,128)(2,1)}, bf16[576,256]{1,0:T(8,128)(2,1)}, bf16[576,256]{1,0:T(8,128)(2,1)}) fusion(bf16[576,1024]{1,0:T(8,128)(2,1)} %bitcast.9.refs_2_), kind=kLoop, calls=%fused_computation.35 | loop fusion | bytes 2359296 | tf_op jit(solution)/shard_map/slice | solution.py:219
  15.1 2.4 %collective-permute-start.4 = (bf16[576,256]{1,0:T(8,128)(2,1)}, bf16[576,256]{1,0:T(8,128)(2,1)}, u32[]{:S(2)}, u32[]{:S(2)}) collective-permute-start(bf16[576,256]{1,0:T(8,128)(2,1)} %get-tuple-element.58), channel_id=1, source_target_pairs={{0,16},{4,20},{8,24},{12,28},{16,0},{20,4},{24,8},{28,12},{1,17},{... | collective-permute-start | bytes 884744 | tf_op jit(solution)/shard_map/ppermute | solution.py:200
  17.5 0.6 collective-permute-start.6
  18.0 2.4 %collective-permute-start.2 = (bf16[576,256]{1,0:T(8,128)(2,1)}, bf16[576,256]{1,0:T(8,128)(2,1)S(1)}, u32[]{:S(2)}, u32[]{:S(2)}) collective-permute-start(bf16[576,256]{1,0:T(8,128)(2,1)} %get-tuple-element.59), channel_id=1, source_target_pairs={{0,16},{4,20},{8,24},{12,28},{16,0},{20,4},{24,8},{28,12},{1,17},{... | collective-permute-start | bytes 884744 | tf_op jit(solution)/shard_map/ppermute | solution.py:200
  20.4 24.2 %all-to-all-done = bf16[8,5,3648]{2,1,0:T(8,128)(2,1)S(1)} async-done(((bf16[8,5,3648]{2,1,0:T(8,128)(2,1)}), bf16[8,5,3648]{2,1,0:T(8,128)(2,1)S(1)}, u32[]{:S(2)}, u32[]{:S(2)}) %all-to-all-start) | async-done | bytes 291872 | tf_op jit(solution)/shard_map/all_to_all | solution.py:212
  46.1 1.2 copy.30
  47.6 3.6 %collective-permute-done.4.refs_2_ = bf16[576,256]{1,0:T(8,128)(2,1)} collective-permute-done((bf16[576,256]{1,0:T(8,128)(2,1)}, bf16[576,256]{1,0:T(8,128)(2,1)}, u32[]{:S(2)}, u32[]{:S(2)}) %collective-permute-start.4) | collective-permute-done | bytes 294944 | tf_op jit(solution)/shard_map/ppermute | solution.py:200
  51.3 6.2 %collective-permute-done.6.refs_4_ = bf16[576,256]{1,0:T(8,128)(2,1)} collective-permute-done((bf16[576,256]{1,0:T(8,128)(2,1)}, bf16[576,256]{1,0:T(8,128)(2,1)}, u32[]{:S(2)}, u32[]{:S(2)}) %collective-permute-start.6) | collective-permute-done | bytes 294944 | tf_op jit(solution)/shard_map/ppermute | solution.py:200
  57.5 1.1 collective-permute-start.5
  58.6 6.6 %collective-permute-done.2.refs_2_ = bf16[576,256]{1,0:T(8,128)(2,1)S(1)} collective-permute-done((bf16[576,256]{1,0:T(8,128)(2,1)}, bf16[576,256]{1,0:T(8,128)(2,1)S(1)}, u32[]{:S(2)}, u32[]{:S(2)}) %collective-permute-start.2) | collective-permute-done | bytes 294944 | tf_op jit(solution)/shard_map/ppermute | solution.py:200
  65.4 9.6 %collective-permute-done.refs_4_ = bf16[576,256]{1,0:T(8,128)(2,1)} collective-permute-done((bf16[576,256]{1,0:T(8,128)(2,1)S(1)}, bf16[576,256]{1,0:T(8,128)(2,1)}, u32[]{:S(2)}, u32[]{:S(2)}) %collective-permute-start) | collective-permute-done | bytes 294944 | tf_op jit(solution)/shard_map/ppermute | solution.py:200
  75.1 1.5 %collective-permute-start.3 = (bf16[576,256]{1,0:T(8,128)(2,1)S(1)}, bf16[576,256]{1,0:T(8,128)(2,1)}, u32[]{:S(2)}, u32[]{:S(2)}) collective-permute-start(bf16[576,256]{1,0:T(8,128)(2,1)S(1)} %collective-permute-done.2.refs_2_), channel_id=1, source_target_pairs={{0,4},{4,0},{8,12},{12,8},{16,20},{20,16},{24,28},{28,24},{1,5},{5... | collective-permute-start | bytes 884744 | tf_op jit(solution)/shard_map/ppermute | solution.py:200
  76.5 7.9 %collective-permute-done.9 = bf16[640,576]{0,1:T(8,128)(2,1)} collective-permute-done((bf16[640,576]{0,1:T(8,128)(2,1)}, bf16[640,576]{0,1:T(8,128)(2,1)}, u32[]{:S(2)}, u32[]{:S(2)}) %collective-permute-start.9) | collective-permute-done | bytes 737312 | tf_op jit(solution)/shard_map/ppermute | solution.py:200
  84.4 1.5 %collective-permute-start.1 = (bf16[576,256]{1,0:T(8,128)(2,1)}, bf16[576,256]{1,0:T(8,128)(2,1)S(1)}, u32[]{:S(2)}, u32[]{:S(2)}) collective-permute-start(bf16[576,256]{1,0:T(8,128)(2,1)} %collective-permute-done.refs_4_), channel_id=1, source_target_pairs={{0,4},{4,0},{8,12},{12,8},{16,20},{20,16},{24,28},{28,24},{1,5},{5... | collective-permute-start | bytes 884744 | tf_op jit(solution)/shard_map/ppermute | solution.py:200
  85.9 2.3 %copy.34.refs_1_ = bf16[640,576]{1,0:T(8,128)(2,1)} copy(bf16[640,576]{0,1:T(8,128)(2,1)} %collective-permute-done.9) | data formatting | bytes 1474560 | tf_op jit(solution)/shard_map/ppermute | solution.py:200
  88.2 1.1 copy-done.1
  89.3 6.4 %attend.12 = (f32[640,128]{1,0:T(8,128)S(1)}, f32[640,128]{1,0:T(8,128)S(1)}, f32[640,512]{1,0:T(8,128)S(1)}) custom-call(s32[4]{0:T(128)S(1)} %select_reduce_fusion.refs_0_, bf16[640,576]{1,0:T(8,128)(2,1)S(1)} %copy-done.1, bf16[576,1024]{1,0:T(8,128)(2,1)} %bitcast.9.refs_2_, bf16[576,1024]{1,0:T(8,128)(2,1)} %collective-permute-done.8.refs_3_), custom_call_target="tpu_custom_call" | custom-call | flops 2852126720 | bytes 4980736 | tf_op jit(solution)/shard_map/attend/pallas_call | solution.py:128
  95.8 4.0 %attend.13 = (f32[640,128]{1,0:T(8,128)S(1)}, f32[640,128]{1,0:T(8,128)S(1)}, f32[640,512]{1,0:T(8,128)S(1)}) custom-call(s32[4]{0:T(128)S(1)} %select_reduce_fusion.refs_0_, bf16[640,576]{1,0:T(8,128)(2,1)S(1)} %copy-done.2, bf16[576,256]{1,0:T(8,128)(2,1)} %collective-permute-done.4.refs_2_, bf16[576,256]{1,0:T(8,128)(2,1)} %collective-permute-done.5.refs_3_, ...), custom_call_target="tpu_custom_call" | custom-call | flops 1426063360 | bytes 3801088 | tf_op jit(solution)/shard_map/attend/pallas_call | solution.py:128
  99.8 4.2 %attend.14 = (f32[640,128]{1,0:T(8,128)S(1)}, f32[640,128]{1,0:T(8,128)S(1)}, f32[640,512]{1,0:T(8,128)S(1)}) custom-call(s32[4]{0:T(128)S(1)} %select_reduce_fusion.refs_0_, bf16[640,576]{1,0:T(8,128)(2,1)S(1)} %copy-done.2, bf16[576,256]{1,0:T(8,128)(2,1)S(1)} %collective-permute-done.2.refs_2_, bf16[576,256]{1,0:T(8,128)(2,1)} %collective-permute-done.3.refs_3_, ...), custom_call_target="tpu_custom_call" | custom-call | flops 1069547520 | bytes 3506176 | tf_op jit(solution)/shard_map/attend/pallas_call | solution.py:128
  104.0 3.0 %attend.15 = bf16[656,512]{1,0:T(8,128)(2,1)S(1)} custom-call(s32[4]{0:T(128)S(1)} %select_reduce_fusion.refs_0_, bf16[640,576]{1,0:T(8,128)(2,1)S(1)} %copy-done.2, bf16[576,256]{1,0:T(8,128)(2,1)S(1)} %collective-permute-done.1.refs_2_, f32[640,128]{1,0:T(8,128)S(1)} %get-tuple-element.54.refs_3_, f32[640,128]{1,0:T(8,128)S(1)} %get-tuple-element.55.refs_4_, ...), custom_call_target="tpu_custom_call" | custom-call | flops 356515840 | bytes 2916352 | tf_op jit(solution)/shard_map/attend/pallas_call | solution.py:128
  107.1 2.8 %fusion = bf16[1024,576]{0,1:T(8,128)(2,1)} fusion(bf16[1024,576]{0,1:T(8,128)(2,1)} %param.15, pred[1024]{0:T(1024)(128)(4,1)S(1)} %fusion.6, s32[32]{0:T(128)S(1)} %compare_select_fusion, bf16[32,3648]{1,0:T(8,128)(2,1)S(1)} %copy-done.5), kind=kOutput, calls=%fused_computation.1 | convolution fusion | flops 38961152 | bytes 2401792 | tf_op jit(solution)/shard_map/dot_general | solution.py:239
  110.0 6.8 %attend.8 = (f32[640,128]{1,0:T(8,128)S(1)}, f32[640,128]{1,0:T(8,128)S(1)}, f32[640,512]{1,0:T(8,128)S(1)}) custom-call(s32[4]{0:T(128)S(1)} %select_reduce_fusion.refs_0_, bf16[640,576]{1,0:T(8,128)(2,1)S(1)} %bitcast.17, bf16[576,1024]{1,0:T(8,128)(2,1)} %bitcast.9.refs_2_, bf16[576,1024]{1,0:T(8,128)(2,1)} %collective-permute-done.8.refs_3_, ...), custom_call_target="tpu_custom_call" | custom-call | flops 2852126720 | bytes 4980736 | tf_op jit(solution)/shard_map/attend/pallas_call | solution.py:128
  116.8 4.2 %attend.9 = (f32[640,128]{1,0:T(8,128)S(1)}, f32[640,128]{1,0:T(8,128)S(1)}, f32[640,512]{1,0:T(8,128)S(1)}) custom-call(s32[4]{0:T(128)S(1)} %select_reduce_fusion.refs_0_, bf16[640,576]{1,0:T(8,128)(2,1)S(1)} %bitcast.18, bf16[576,256]{1,0:T(8,128)(2,1)} %collective-permute-done.4.refs_2_, bf16[576,256]{1,0:T(8,128)(2,1)} %collective-permute-done.5.refs_3_, ...), custom_call_target="tpu_custom_call" | custom-call | flops 1426063360 | bytes 3801088 | tf_op jit(solution)/shard_map/attend/pallas_call | solution.py:128
  121.0 4.2 %attend.10 = (f32[640,128]{1,0:T(8,128)S(1)}, f32[640,128]{1,0:T(8,128)S(1)}, f32[640,512]{1,0:T(8,128)S(1)}) custom-call(s32[4]{0:T(128)S(1)} %select_reduce_fusion.refs_0_, bf16[640,576]{1,0:T(8,128)(2,1)S(1)} %bitcast.19, bf16[576,256]{1,0:T(8,128)(2,1)S(1)} %collective-permute-done.2.refs_2_, bf16[576,256]{1,0:T(8,128)(2,1)} %collective-permute-done.3.refs_3_, ...), custom_call_target="tpu_custom_call" | custom-call | flops 1069547520 | bytes 3506176 | tf_op jit(solution)/shard_map/attend/pallas_call | solution.py:128
  125.2 2.3 %attend.11 = (f32[640,128]{1,0:T(8,128)S(1)}, f32[640,128]{1,0:T(8,128)S(1)}, f32[640,512]{1,0:T(8,128)S(1)}) custom-call(s32[4]{0:T(128)S(1)} %select_reduce_fusion.refs_0_, bf16[640,576]{1,0:T(8,128)(2,1)S(1)} %bitcast.20, bf16[576,256]{1,0:T(8,128)(2,1)S(1)} %collective-permute-done.1.refs_2_, f32[640,128]{1,0:T(8,128)S(1)} %get-tuple-element.42.refs_3_, ...), custom_call_target="tpu_custom_call" | custom-call | flops 356515840 | bytes 2916352 | tf_op jit(solution)/shard_map/attend/pallas_call | solution.py:128
  128.1 0.7 slice.80
  128.8 0.6 slice.81
  (57 shorter events, 2.6 us)
Async XLA Ops:
  0.6 45.0 %copy-start = (bf16[16,128,512]{2,1,0:T(8,128)(2,1)S(1)}, bf16[16,128,512]{2,1,0:T(8,128)(2,1)}, u32[]{:S(2)}) copy-start(bf16[16,128,512]{2,1,0:T(8,128)(2,1)} %param.22) | copy-start | bytes 6291460
  3.6 41.1 %all-to-all-start = ((bf16[8,5,3648]{2,1,0:T(8,128)(2,1)}), bf16[8,5,3648]{2,1,0:T(8,128)(2,1)S(1)}, u32[]{:S(2)}, u32[]{:S(2)}) async-start(bf16[8,5,3648]{2,1,0:T(8,128)(2,1)} %pad_maximum_fusion.1), calls=%async_computation | async-start | bytes 950272 | tf_op jit(solution)/shard_map/all_to_all | solution.py:212
  10.8 9.6 %copy-start.9 = (s32[32]{0:T(128)S(1)}, s32[32]{0:T(128)}, u32[]{:S(2)}) copy-start(s32[32]{0:T(128)} %param.20) | copy-start | bytes 388
  10.8 9.6 %copy-start.10 = (s32[32]{0:T(128)S(1)}, s32[32]{0:T(128)}, u32[]{:S(2)}) copy-start(s32[32]{0:T(128)} %param.19) | copy-start | bytes 388
  10.8 77.3 %collective-permute-start.8 = (bf16[576,1024]{1,0:T(8,128)(2,1)}, bf16[576,1024]{1,0:T(8,128)(2,1)}, u32[]{:S(2)}, u32[]{:S(2)}) collective-permute-start(bf16[576,1024]{1,0:T(8,128)(2,1)} %bitcast.9.refs_2_), channel_id=1, source_target_pairs={{0,4},{4,0},{8,12},{12,8},{16,20},{20,16},{24,28},{28,24},{1,5},{5... | collective-permute-start | bytes 3538952 | tf_op jit(solution)/shard_map/ppermute | solution.py:200
  15.1 36.1 %collective-permute-start.4 = (bf16[576,256]{1,0:T(8,128)(2,1)}, bf16[576,256]{1,0:T(8,128)(2,1)}, u32[]{:S(2)}, u32[]{:S(2)}) collective-permute-start(bf16[576,256]{1,0:T(8,128)(2,1)} %get-tuple-element.58), channel_id=1, source_target_pairs={{0,16},{4,20},{8,24},{12,28},{16,0},{20,4},{24,8},{28,12},{1,17},{... | collective-permute-start | bytes 884744 | tf_op jit(solution)/shard_map/ppermute | solution.py:200
  17.5 40.0 %collective-permute-start.6 = (bf16[576,256]{1,0:T(8,128)(2,1)}, bf16[576,256]{1,0:T(8,128)(2,1)}, u32[]{:S(2)}, u32[]{:S(2)}) collective-permute-start(bf16[576,256]{1,0:T(8,128)(2,1)} %get-tuple-element.57), channel_id=1, source_target_pairs={{0,16},{4,20},{8,24},{12,28},{16,0},{20,4},{24,8},{28,12},{1,17},{... | collective-permute-start | bytes 884744 | tf_op jit(solution)/shard_map/ppermute | solution.py:200
  18.0 47.1 %collective-permute-start.2 = (bf16[576,256]{1,0:T(8,128)(2,1)}, bf16[576,256]{1,0:T(8,128)(2,1)S(1)}, u32[]{:S(2)}, u32[]{:S(2)}) collective-permute-start(bf16[576,256]{1,0:T(8,128)(2,1)} %get-tuple-element.59), channel_id=1, source_target_pairs={{0,16},{4,20},{8,24},{12,28},{16,0},{20,4},{24,8},{28,12},{1,17},{... | collective-permute-start | bytes 884744 | tf_op jit(solution)/shard_map/ppermute | solution.py:200
  44.9 1.1 copy-start.4
  45.0 1.0 copy-start.6
  46.0 1.3 %copy-start.11 = (s32[8]{0:T(128)S(1)}, s32[8]{0:T(128)}, u32[]{:S(2)}) copy-start(s32[8]{0:T(128)} %param.21) | copy-start | bytes 100
  46.0 5.2 %copy-start.8 = (bf16[576,256]{1,0:T(8,128)(2,1)S(1)}, bf16[576,256]{1,0:T(8,128)(2,1)}, u32[]{:S(2)}) copy-start(bf16[576,256]{1,0:T(8,128)(2,1)} %get-tuple-element.60) | copy-start | bytes 884740
  46.1 19.2 %copy-start.12 = (s32[8]{0:T(128)S(1)}, s32[8]{0:T(128)}, u32[]{:S(2)}) copy-start(s32[8]{0:T(128)} %param.18) | copy-start | bytes 100
  47.3 37.1 %collective-permute-start.9 = (bf16[640,576]{0,1:T(8,128)(2,1)}, bf16[640,576]{0,1:T(8,128)(2,1)}, u32[]{:S(2)}, u32[]{:S(2)}) collective-permute-start(bf16[640,576]{0,1:T(8,128)(2,1)} %copy.30), channel_id=1, source_target_pairs={{0,8},{4,12},{8,0},{12,4},{16,24},{20,28},{24,16},{28,20},{1,9},{5... | collective-permute-start | bytes 2211848 | tf_op jit(solution)/shard_map/ppermute | solution.py:200
  51.2 23.9 %collective-permute-start = (bf16[576,256]{1,0:T(8,128)(2,1)S(1)}, bf16[576,256]{1,0:T(8,128)(2,1)}, u32[]{:S(2)}, u32[]{:S(2)}) collective-permute-start(bf16[576,256]{1,0:T(8,128)(2,1)S(1)} %copy-done.8), channel_id=1, source_target_pairs={{0,16},{4,20},{8,24},{12,28},{16,0},{20,4},{24,8},{28,12},{1,17},{... | collective-permute-start | bytes 884744 | tf_op jit(solution)/shard_map/ppermute | solution.py:200
  57.5 38.2 %collective-permute-start.5 = (bf16[576,256]{1,0:T(8,128)(2,1)}, bf16[576,256]{1,0:T(8,128)(2,1)}, u32[]{:S(2)}, u32[]{:S(2)}) collective-permute-start(bf16[576,256]{1,0:T(8,128)(2,1)} %collective-permute-done.4.refs_2_), channel_id=1, source_target_pairs={{0,4},{4,0},{8,12},{12,8},{16,20},{20,16},{24,28},{28,24},{1,5},{5... | collective-permute-start | bytes 884744 | tf_op jit(solution)/shard_map/ppermute | solution.py:200
  65.2 30.6 %collective-permute-start.7 = (bf16[576,256]{1,0:T(8,128)(2,1)}, bf16[576,256]{1,0:T(8,128)(2,1)}, u32[]{:S(2)}, u32[]{:S(2)}) collective-permute-start(bf16[576,256]{1,0:T(8,128)(2,1)} %collective-permute-done.6.refs_4_), channel_id=1, source_target_pairs={{0,4},{4,0},{8,12},{12,8},{16,20},{20,16},{24,28},{28,24},{1,5},{5... | collective-permute-start | bytes 884744 | tf_op jit(solution)/shard_map/ppermute | solution.py:200
  75.1 24.7 %collective-permute-start.3 = (bf16[576,256]{1,0:T(8,128)(2,1)S(1)}, bf16[576,256]{1,0:T(8,128)(2,1)}, u32[]{:S(2)}, u32[]{:S(2)}) collective-permute-start(bf16[576,256]{1,0:T(8,128)(2,1)S(1)} %collective-permute-done.2.refs_2_), channel_id=1, source_target_pairs={{0,4},{4,0},{8,12},{12,8},{16,20},{20,16},{24,28},{28,24},{1,5},{5... | collective-permute-start | bytes 884744 | tf_op jit(solution)/shard_map/ppermute | solution.py:200
  84.4 19.6 %collective-permute-start.1 = (bf16[576,256]{1,0:T(8,128)(2,1)}, bf16[576,256]{1,0:T(8,128)(2,1)S(1)}, u32[]{:S(2)}, u32[]{:S(2)}) collective-permute-start(bf16[576,256]{1,0:T(8,128)(2,1)} %collective-permute-done.refs_4_), channel_id=1, source_target_pairs={{0,4},{4,0},{8,12},{12,8},{16,20},{20,16},{24,28},{28,24},{1,5},{5... | collective-permute-start | bytes 884744 | tf_op jit(solution)/shard_map/ppermute | solution.py:200
  88.2 1.1 copy-start.1
  89.3 6.5 %copy-start.2 = (bf16[640,576]{1,0:T(8,128)(2,1)S(1)}, bf16[640,576]{1,0:T(8,128)(2,1)}, u32[]{:S(2)}) copy-start(bf16[640,576]{1,0:T(8,128)(2,1)} %copy.34.refs_1_) | copy-start | bytes 2211844
  104.0 3.1 %copy-start.5 = (bf16[32,3648]{1,0:T(8,128)(2,1)S(1)}, bf16[32,3648]{1,0:T(8,128)(2,1)}, u32[]{:S(2)}) copy-start(bf16[32,3648]{1,0:T(8,128)(2,1)} %copy-done.4) | copy-start | bytes 700420
  107.0 2.9 %copy-start.7 = (bf16[8,1,3648]{2,0,1:T(8,128)(2,1)S(1)}, bf16[8,1,3648]{2,0,1:T(8,128)(2,1)}, u32[]{:S(2)}) copy-start(bf16[8,1,3648]{2,0,1:T(8,128)(2,1)} %copy-done.6) | copy-start | bytes 175108
  107.0 20.5 %collective-permute-start.10 = (bf16[656,512]{1,0:T(8,128)(2,1)S(1)}, bf16[656,512]{1,0:T(8,128)(2,1)S(1)}, u32[]{:S(2)}, u32[]{:S(2)}) collective-permute-start(bf16[656,512]{1,0:T(8,128)(2,1)S(1)} %attend.15), channel_id=1, source_target_pairs={{0,8},{4,12},{8,0},{12,4},{16,24},{20,28},{24,16},{28,20},{1,9},{5... | collective-permute-start | bytes 2015240 | tf_op jit(solution)/shard_map/ppermute | solution.py:200
  125.2 2.3 %copy-start.3 = (bf16[16,512,128]{2,1,0:T(8,128)(2,1)S(1)}, bf16[16,512,128]{2,1,0:T(8,128)(2,1)}, u32[]{:S(2)}) copy-start(bf16[16,512,128]{2,1,0:T(8,128)(2,1)} %w_ref.1) | copy-start | bytes 6291460

commit v2 on v1

--- a/solution.py
+++ b/solution.py
@@ -22,7 +22,7 @@
     return jnp.concatenate([x] * (width // LANES), axis=1) if width > LANES else x
 
 
-def attend_kernel(pieces, extra, first, last, *refs):
+def attend_kernel(pieces, extra, first, last, through, *refs):
     refs = list(refs)
     fills = refs.pop(0)
     q_ref = refs.pop(0)
@@ -32,8 +32,9 @@
         bias_ref = refs.pop(0)
     if not first:
         m_in, l_in, acc_in = refs.pop(0), refs.pop(0), refs.pop(0)
-    q = q_ref[...]
-    rows = q.shape[0]
+    refs = refs[through : len(refs) - through]
+    rows = q_ref.shape[0]
+    q = q_ref[:, : keys[0].shape[0]]
     scores = []
     for (start, width, which), ref in zip(pieces, keys):
         s = jnp.dot(q, ref[...], preferred_element_type=jnp.float32)
@@ -89,7 +90,7 @@
     out[rows:, :] = jnp.concatenate([high, mid, low, jnp.zeros_like(low)], axis=1)
 
 
-def attend(fills, q, pieces, new=None, state=None, last=False, tile=None):
+def attend(fills, q, pieces, new=None, state=None, last=False, tile=None, through=()):
     rows, width = q.shape
     tile = rows if tile is None else tile
     spec = tuple((start, keys.shape[1], which) for start, which, keys in pieces)
@@ -115,18 +116,24 @@
         in_specs += state_specs
     if last:
         tail = -(-rows // (LANES * 16)) * 16
-        out_shape = jax.ShapeDtypeStruct((rows + tail, DC), jnp.bfloat16)
-        out_specs = pl.BlockSpec((rows + tail, DC), lambda i: (0, 0))
+        out_shape = [jax.ShapeDtypeStruct((rows + tail, DC), jnp.bfloat16)]
+        out_specs = [pl.BlockSpec((rows + tail, DC), lambda i: (0, 0))]
     else:
-        out_shape = (
+        out_shape = [
             jax.ShapeDtypeStruct((rows, LANES), jnp.float32),
             jax.ShapeDtypeStruct((rows, LANES), jnp.float32),
             jax.ShapeDtypeStruct((rows, DC), jnp.float32),
-        )
-        out_specs = tuple(state_specs)
+        ]
+        out_specs = list(state_specs)
+    aliases = {len(operands) + i: len(out_shape) + i for i in range(len(through))}
+    operands += list(through)
+    in_specs += [pl.BlockSpec(memory_space=pl.ANY)] * len(through)
+    made = len(out_shape)
+    out_shape += [jax.ShapeDtypeStruct(x.shape, x.dtype) for x in through]
+    out_specs += [pl.BlockSpec(memory_space=pl.ANY)] * len(through)
     count = sum(piece[1] for piece in spec)
-    return pl.pallas_call(
-        functools.partial(attend_kernel, spec, new is not None, state is None, last),
+    out = pl.pallas_call(
+        functools.partial(attend_kernel, spec, new is not None, state is None, last, len(through)),
         grid=(rows // tile,),
         in_specs=in_specs,
         out_specs=out_specs,
@@ -137,11 +144,76 @@
             bytes_accessed=2 * count * width + 4 * rows * DC * 2,
             transcendentals=rows * count,
         ),
+        input_output_aliases=aliases,
         name="attend",
     )(*operands)
-
-
-def finish_kernel(count, m_ref, l_ref, acc_ref, far_ref, w_ref, out_ref):
+    result = out[0] if last else tuple(out[:made])
+    return (result, *out[made:]) if through else result
+
+
+def absorb_kernel(span_ref, dec_ref, w_ref, absorbed_ref, extra_ref):
+    heads = w_ref.shape[0]
+    row = extra_ref.shape[1]
+    width = (span_ref.shape[1] - row) // heads
+    count = span_ref.shape[0] + dec_ref.shape[0]
+    rows = jnp.concatenate(
+        [span_ref[...].astype(jnp.float32), dec_ref[...].astype(jnp.float32)], axis=0
+    )
+    q = rows.astype(jnp.bfloat16)
+    blank = jnp.zeros((count, absorbed_ref.shape[1] - row), jnp.float32)
+    for h in range(0, heads, 2):
+        parts = []
+        for g in (h, h + 1):
+            mine = q[:, g * width : (g + 1) * width]
+            latent = jnp.dot(mine[:, :DN], w_ref[g], preferred_element_type=jnp.float32)
+            rope = mine[:, DN:].astype(jnp.float32)
+            parts.append(jnp.concatenate([latent, rope, blank], axis=1))
+        pair = jnp.concatenate(parts, axis=0).astype(jnp.bfloat16)
+        absorbed_ref[h * count : (h + 2) * count, :] = pair
+    blank = jnp.zeros((extra_ref.shape[0] - count, row), jnp.float32)
+    new = jnp.concatenate([rows[:, heads * width :], blank], axis=0)
+    extra_ref[...] = new.astype(jnp.bfloat16)
+
+
+def absorb(got_span, got_dec, w_uk, row):
+    heads = w_uk.shape[0]
+    count = got_span.shape[0] + got_dec.shape[0]
+    return pl.pallas_call(
+        absorb_kernel,
+        out_shape=(
+            jax.ShapeDtypeStruct((heads * count, -(-row // LANES) * LANES), jnp.bfloat16),
+            jax.ShapeDtypeStruct((LANES, row), jnp.bfloat16),
+        ),
+        compiler_params=pltpu.CompilerParams(vmem_limit_bytes=40 * 1024 * 1024),
+        cost_estimate=pl.CostEstimate(
+            flops=2 * count * heads * DN * DC,
+            bytes_accessed=2 * w_uk.size + 4 * got_span.size,
+            transcendentals=0,
+        ),
+        name="absorb",
+    )(got_span, got_dec, w_uk)
+
+
+def split_kernel(size, skip, x_ref, after_ref, *out_refs):
+    for i, ref in enumerate(out_refs):
+        ref[...] = x_ref[:, (skip + i) * size : (skip + i + 1) * size]
+
+
+def split(x, size, skip, after):
+    pieces = x.shape[1] // size - skip
+    return pl.pallas_call(
+        functools.partial(split_kernel, size, skip),
+        in_specs=[
+            pl.BlockSpec(memory_space=pltpu.VMEM),
+            pl.BlockSpec(memory_space=pl.ANY),
+        ],
+        out_shape=[jax.ShapeDtypeStruct((x.shape[0], size), x.dtype)] * pieces,
+        compiler_params=pltpu.CompilerParams(vmem_limit_bytes=16 * 1024 * 1024),
+        name="split",
+    )(x, after)
+
+
+def finish_kernel(count, m_ref, l_ref, acc_ref, far_ref, w_ref, span_ref, dec_ref):
     rows = m_ref.shape[0]
     heads = w_ref.shape[0]
     scale = score_scale * LOG2E
@@ -165,16 +237,21 @@
         near_part = acc_ref[a:b, :] * w_near[a:b, :]
         far_part = far_ref[:rows, :].astype(jnp.float32)[a:b, :] * w_far[a:b, :]
         latent = (near_part + far_part).astype(jnp.bfloat16)
-        out_ref[:, h * LANES : (h + 1) * LANES] = jnp.dot(
-            latent, w_ref[h], preferred_element_type=jnp.float32
-        ).astype(jnp.bfloat16)
-
-
-def finish(count, state, far, w_uv):
+        done = jnp.dot(latent, w_ref[h], preferred_element_type=jnp.float32)
+        span = span_ref.shape[0]
+        span_ref[:, h * LANES : (h + 1) * LANES] = done[:span].astype(jnp.bfloat16)
+        dec_ref[:, h * LANES : (h + 1) * LANES] = done[span:].astype(jnp.bfloat16)
+
+
+def finish(count, span, state, far, w_uv):
     heads = w_uv.shape[0]
+    wide = heads * w_uv.shape[2]
     return pl.pallas_call(
         functools.partial(finish_kernel, count),
-        out_shape=jax.ShapeDtypeStruct((count, heads * w_uv.shape[2]), jnp.bfloat16),
+        out_shape=(
+            jax.ShapeDtypeStruct((span, wide), jnp.bfloat16),
+            jax.ShapeDtypeStruct((count - span, wide), jnp.bfloat16),
+        ),
         compiler_params=pltpu.CompilerParams(vmem_limit_bytes=40 * 1024 * 1024),
         cost_estimate=pl.CostEstimate(
             flops=2 * count * heads * DC * w_uv.shape[2],
@@ -204,40 +281,38 @@
     keys = cache_kv.T
     size = pos_dev // CHUNKS
 
-    mine = jnp.concatenate([query, dec_query], axis=0)
-    local = mine.shape[0]
-    mine = jnp.swapaxes(mine.reshape(local, n, heads * width), 0, 1)
-    fresh = jnp.concatenate([span_kv, dec_kv], axis=0)
-    mine = jnp.concatenate([mine, jnp.broadcast_to(fresh[None], (n, local, row))], axis=2)
+    per, per_dec = span // n, rows_dec // n
+    mine = jnp.swapaxes(query.reshape(per, n, heads * width), 0, 1)
+    fresh = jnp.broadcast_to(span_kv[None], (n, per, row))
+    mine_dec = jnp.swapaxes(dec_query.reshape(per_dec, n, heads * width), 0, 1)
+    fresh_dec = jnp.broadcast_to(dec_kv[None], (n, per_dec, row))
+    mine_dec = jnp.concatenate([mine_dec, fresh_dec], axis=2).reshape(n, per, -1)
+    mine = jnp.concatenate([mine, fresh, mine_dec], axis=2)
     got = lax.all_to_all(mine, "seq", split_axis=0, concat_axis=0, tiled=True)
+    full = heads * width + row
+    got_span = got[:, :, :full].reshape(span, full)
+    got_dec = got[:, :, full:].reshape(rows_dec, full)
+    absorbed, extra = absorb(got_span, got_dec, w_uk, row)
+    new_rows = extra[:span]
+    other = swap(absorbed, pair)
 
     blocks = [(jnp.int32(0), [keys])]
     for stride in near:
         blocks += [(offset ^ stride, [swap(x, stride) for x in held]) for offset, held in blocks]
-    pieces = []
-    for c in range(CHUNKS):
-        part = [(jnp.int32(far), swap(keys[:, c * size : (c + 1) * size], far))]
+    cuts = [keys[:, :size]] + list(split(keys, size, 1, extra))
+
+    def spread(x):
+        part = [(far, x)]
         for stride in near:
-            part += [(offset ^ stride, swap(x, stride)) for offset, x in part]
-        pieces.append(part)
-
-    per = span // n
-    got_span = got[:, :per].reshape(span, -1)
-    got_dec = got[:, per:].reshape(rows_dec, -1)
-    both = jnp.concatenate([got_span, got_dec], axis=0)
-    new_rows = both[:, heads * width :]
-    q = both[:, : heads * width].reshape(count, heads, width)
-    latent = jnp.einsum(
-        "thn,hnc->htc", q[:, :, :DN], w_uk, preferred_element_type=jnp.float32
-    ).astype(jnp.bfloat16)
-    absorbed = jnp.concatenate([latent, jnp.swapaxes(q[:, :, DN:], 0, 1)], axis=2)
-    absorbed = absorbed.reshape(heads * count, row)
-    other = swap(absorbed, pair)
+            part += [(offset ^ stride, swap(y, stride)) for offset, y in part]
+        return part
+
+    pieces = [swap(x, far) for x in cuts]
 
     target = jnp.where(owner == me, slot, -1)
     onehot = jnp.arange(pos_dev, dtype=jnp.int32)[None, :] == target[:, None]
     placed = lax.dot_general(
-        new_rows[:span],
+        new_rows,
         onehot.astype(jnp.bfloat16),
         (((0,), (0,)), ((), ())),
         preferred_element_type=jnp.float32,
@@ -250,8 +325,6 @@
     seen = (index[None, :] < span) & (index[None, :] < limits[:, None])
     seen |= (index[None, :] >= span) & (index[None, :] == queries[:, None])
     bias = jnp.where(seen, 0.0, HIDDEN).astype(jnp.float32)
-    extra = jnp.zeros((LANES, row), jnp.bfloat16).at[:count].set(new_rows)
-
     held = [offset for offset, _ in blocks]
     offsets = held + [offset ^ far for offset in held]
     which = jnp.stack([me ^ offset for offset in offsets])
@@ -261,23 +334,29 @@
     )
     base = len(blocks)
     tile = heads // 2 * count
-    stages = [[(0, i, xs[0]) for i, (_, xs) in enumerate(blocks)]]
-    flat = [[(c * size, base + i, x) for i, (_, x) in enumerate(part)] for c, part in enumerate(pieces)]
-    half = CHUNKS // 2
-    stages.append([p for part in flat[:half] for p in part])
-    stages.append([p for part in flat[half:-1] for p in part] + flat[-1][:1])
-    final = flat[-1][1:]
-
-    state = attend(fills, absorbed, stages[0], new=(extra, bias), tile=tile)
-    guest = attend(fills, other, stages[0], tile=tile)
-    for stage in stages[1:]:
-        guest = attend(fills, other, stage, state=guest, tile=tile)
-        state = attend(fills, absorbed, stage, state=state, tile=tile)
-    sent = attend(fills, other, final, state=guest, last=True)
+
+    def stage_of(c, part):
+        return [(c * size, base + i, x) for i, (_, x) in enumerate(part)]
+
+    home = [(0, i, xs[0]) for i, (_, xs) in enumerate(blocks)]
+    first = stage_of(0, spread(pieces[0]))
+    state, pieces[1] = attend(
+        fills, absorbed, home, new=(extra, bias), tile=tile, through=(pieces[1],)
+    )
+    first += stage_of(1, spread(pieces[1]))
+    guest, pieces[2] = attend(fills, other, home, tile=tile, through=(pieces[2],))
+    second = stage_of(2, spread(pieces[2]))
+    guest, pieces[3] = attend(fills, other, first, state=guest, tile=tile, through=(pieces[3],))
+    third = stage_of(3, spread(pieces[3]))
+    second, third = second + third[:1], third[1:]
+    state = attend(fills, absorbed, first, state=state, tile=tile)
+    guest = attend(fills, other, second, state=guest, tile=tile)
+    sent = attend(fills, other, third, state=guest, last=True)
     back = swap(sent, pair)
-    state = attend(fills, absorbed, final, state=state, tile=tile)
-    result = finish(count, state, back, w_uv)
-    return (result[:span], result[span:], new_cache)
+    state = attend(fills, absorbed, second, state=state, tile=tile)
+    state = attend(fills, absorbed, third, state=state, tile=tile)
+    span_out, dec_out = finish(count, span, state, back, w_uv)
+    return (span_out, dec_out, new_cache)
 
 
 def solution(mesh):

time: 130 us -> 121 us (0.931)
  waiting for transfers between devices: 58.2 us -> 46.1 us
  starting transfers between devices: 18.6 us -> 24.6 us
  matrix products: 3.23 us -> 1.54 us
    ppermute x11, starting transfers between devices: 11.4 us -> 19.6 us  [swap(): return lax.ppermute(x, 'seq', [(i, i ^ stride) for i in range(n)])]
    all_to_all x1, waiting for transfers between devices: 24.2 us -> 16.1 us  [body(): got = lax.all_to_all(mine, 'seq', split_axis=0, concat_axis=0, tiled=True)]
    ppermute x11, waiting for transfers between devices: 34 us -> 30 us  [swap(): return lax.ppermute(x, 'seq', [(i, i ^ stride) for i in range(n)])]
    concatenate x6 -> x1, other arithmetic: 3 us -> 0.02 us  [body(): jnp.concatenate([mine_dec, fresh_dec], axis=2).reshape(n, per, -1)]
    pallas_call x8, Pallas kernels: 35.1 us -> 32.8 us  [attend(): pl.pallas_call(functools.partial(attend_kernel, spec, new is not None, st...]
    ppermute x1 -> x0, local copies, waits for them, and re-layouts: 2.31 us -> none  [swap(): return lax.ppermute(x, 'seq', [(i, i ^ stride) for i in range(n)])]
    all_to_all x1, starting transfers between devices: 7.25 us -> 5.01 us  [body(): got = lax.all_to_all(mine, 'seq', split_axis=0, concat_axis=0, tiled=True)]
    concatenate x0 -> x2, local copies, waits for them, and re-layouts: none -> 1.89 us  [the longest x1 1.88 us: body(): mine = jnp.concatenate([mine, fresh, mine_dec], axis=2)]
  transfers between devices with their start and end apart: 12 -> 12, of which waited for: 6 -> 5; matrix products, arithmetic and copies ran while one was open for 8% -> 11% of each run, Pallas kernels for 25% -> 25%
where the time goes in v2:
time: 121 us; the launch traced here: 120 us
  waiting for transfers between devices  46.1 us (38%)
  Pallas kernels  34.6 us (29%)
  starting transfers between devices  24.6 us (20%)
  local copies, waits for them, and re-layouts  10.3 us (9%)
  other arithmetic  2.41 us (2%)
  matrix products  1.54 us (1%)
    pallas_call x8, Pallas kernels, attend(): pl.pallas_call(functools.partial(attend_kernel, spec, new is not None, st...  32.8 us
    ppermute x11, waiting for transfers between devices, swap(): return lax.ppermute(x, 'seq', [(i, i ^ stride) for i in range(n)])  30 us
    ppermute x11, starting transfers between devices, swap(): return lax.ppermute(x, 'seq', [(i, i ^ stride) for i in range(n)])  19.6 us
    all_to_all x1, waiting for transfers between devices, body(): got = lax.all_to_all(mine, 'seq', split_axis=0, concat_axis=0, tiled=True)  16.1 us
    all_to_all x1, starting transfers between devices, body(): got = lax.all_to_all(mine, 'seq', split_axis=0, concat_axis=0, tiled=True)  5.01 us
  transfers between devices with their start and end apart: 12, of which 5 were waited for; matrix products, arithmetic and copies ran while one was open for 11% of the time, Pallas kernels for 25%

profile of v2, /device:TPU:0, one launch (start us, length us, event | category | flops | bytes accessed | tf_op | source)
XLA Modules:
  0.0 120.3 jit_solution(2594028913099656910)
XLA Ops:
  0.6 3.0 %collective-permute-start.3 = (bf16[576,1024]{1,0:T(8,128)(2,1)}, bf16[576,1024]{1,0:T(8,128)(2,1)}, u32[]{:S(2)}, u32[]{:S(2)}) collective-permute-start(bf16[576,1024]{1,0:T(8,128)(2,1)} %bitcast.10), channel_id=1, source_target_pairs={{0,4},{4,0},{8,12},{12,8},{16,20},{20,16},{24,28},{28,24},{1,5},{5... | collective-permute-start | bytes 3538952 | tf_op jit(solution)/shard_map/ppermute | solution.py:277
  3.6 1.2 reduce
  6.4 1.9 %concatenate.10 = bf16[8,4,4560]{2,1,0:T(4,128)(2,1)} concatenate(bf16[8,4,3072]{2,1,0:T(4,128)(2,1)} %bitcast.15, bf16[8,4,576]{2,1,0:T(4,128)(2,1)S(1)} %broadcast_in_dim.60, bf16[8,4,912]{2,1,0:T(4,128)(2,1)S(1)} %reshape.38), dimensions={2} | concatenate | bytes 583680 | tf_op jit(solution)/shard_map/concatenate | solution.py:290
  8.3 5.0 %all-to-all-start = ((bf16[8,4,4560]{2,1,0:T(4,128)(2,1)}), bf16[8,4,4560]{2,1,0:T(4,128)(2,1)}, u32[]{:S(2)}, u32[]{:S(2)}) async-start(bf16[8,4,4560]{2,1,0:T(4,128)(2,1)} %concatenate.10), calls=%async_computation | async-start | bytes 589824 | tf_op jit(solution)/shard_map/all_to_all | solution.py:291
  13.3 0.8 slice.18
  14.1 2.9 %collective-permute-start.1 = (bf16[576,256]{1,0:T(8,128)(2,1)}, bf16[576,256]{1,0:T(8,128)(2,1)}, u32[]{:S(2)}, u32[]{:S(2)}) collective-permute-start(bf16[576,256]{1,0:T(8,128)(2,1)} %slice.18), channel_id=1, source_target_pairs={{0,16},{4,20},{8,24},{12,28},{16,0},{20,4},{24,8},{28,12},{1,17},{... | collective-permute-start | bytes 884744 | tf_op jit(solution)/shard_map/ppermute | solution.py:277
  17.0 16.1 %all-to-all-done = bf16[8,4,4560]{2,1,0:T(4,128)(2,1)} async-done(((bf16[8,4,4560]{2,1,0:T(4,128)(2,1)}), bf16[8,4,4560]{2,1,0:T(4,128)(2,1)}, u32[]{:S(2)}, u32[]{:S(2)}) %all-to-all-start) | async-done | bytes 291872 | tf_op jit(solution)/shard_map/all_to_all | solution.py:291
  33.1 1.7 %slice.16 = bf16[8,4,3648]{2,1,0:T(4,128)(2,1)} slice(bf16[8,4,4560]{2,1,0:T(4,128)(2,1)} %all-to-all-done), slice={[0:8], [0:4], [0:3648]} | slice | bytes 466944 | tf_op jit(solution)/shard_map/slice | solution.py:293
  34.8 1.0 reshape.39.span_ref
  35.9 1.6 %slice.17 = bf16[8,4,912]{2,1,0:T(4,128)(2,1)} slice(bf16[8,4,4560]{2,1,0:T(4,128)(2,1)} %all-to-all-done), slice={[0:8], [0:4], [3648:4560]} | slice | bytes 116736 | tf_op jit(solution)/shard_map/slice | solution.py:294
  37.4 1.6 %reshape.40.dec_ref = bf16[8,3648]{1,0:T(8,128)(2,1)} reshape(bf16[8,4,912]{2,1,0:T(4,128)(2,1)} %slice.17) | data formatting | bytes 116736 | tf_op jit(solution)/shard_map/reshape | solution.py:294
  39.1 0.8 copy-done.3
  40.3 1.9 %collective-permute-start = (bf16[640,640]{1,0:T(8,128)(2,1)S(1)}, bf16[640,640]{1,0:T(8,128)(2,1)S(1)}, u32[]{:S(2)}, u32[]{:S(2)}) collective-permute-start(bf16[640,640]{1,0:T(8,128)(2,1)S(1)} %get-tuple-element.34.refs_1_), channel_id=1, source_target_pairs={{0,8},{4,12},{8,0},{12,4},{16,24},{20,28},{24,16},{28,20},{1,9},{5... | collective-permute-start | bytes 2457608 | tf_op jit(solution)/shard_map/ppermute | solution.py:277
  42.6 2.7 %collective-permute-start.4 = (bf16[576,256]{1,0:T(8,128)(2,1)S(1)}, bf16[576,256]{1,0:T(8,128)(2,1)S(1)}, u32[]{:S(2)}, u32[]{:S(2)}) collective-permute-start(bf16[576,256]{1,0:T(8,128)(2,1)S(1)} %get-tuple-element.36), channel_id=1, source_target_pairs={{0,16},{4,20},{8,24},{12,28},{16,0},{20,4},{24,8},{28,12},{1,17},{... | collective-permute-start | bytes 884744 | tf_op jit(solution)/shard_map/ppermute | solution.py:277
  45.4 1.6 %collective-permute-start.2 = (bf16[576,256]{1,0:T(8,128)(2,1)}, bf16[576,256]{1,0:T(8,128)(2,1)S(1)}, u32[]{:S(2)}, u32[]{:S(2)}) collective-permute-start(bf16[576,256]{1,0:T(8,128)(2,1)} %collective-permute-done.1.refs_2_), channel_id=1, source_target_pairs={{0,4},{4,0},{8,12},{12,8},{16,20},{20,16},{24,28},{28,24},{1,5},{5... | collective-permute-start | bytes 884744 | tf_op jit(solution)/shard_map/ppermute | solution.py:277
  47.3 20.0 %collective-permute-done.4.refs_6_ = bf16[576,256]{1,0:T(8,128)(2,1)S(1)} collective-permute-done((bf16[576,256]{1,0:T(8,128)(2,1)S(1)}, bf16[576,256]{1,0:T(8,128)(2,1)S(1)}, u32[]{:S(2)}, u32[]{:S(2)}) %collective-permute-start.4) | collective-permute-done | bytes 294944 | tf_op jit(solution)/shard_map/ppermute | solution.py:277
  67.3 3.5 %collective-permute-start.7 = (bf16[576,256]{1,0:T(8,128)(2,1)S(1)}, bf16[576,256]{1,0:T(8,128)(2,1)S(1)}, u32[]{:S(2)}, u32[]{:S(2)}) collective-permute-start(bf16[576,256]{1,0:T(8,128)(2,1)S(1)} %get-tuple-element.42), channel_id=1, source_target_pairs={{0,16},{4,20},{8,24},{12,28},{16,0},{20,4},{24,8},{28,12},{1,17},{... | collective-permute-start | bytes 884744 | tf_op jit(solution)/shard_map/ppermute | solution.py:277
  70.7 6.5 %attend.8 = (f32[640,128]{1,0:T(8,128)S(1)}, f32[640,128]{1,0:T(8,128)S(1)}, f32[640,512]{1,0:T(8,128)S(1)}, bf16[576,256]{1,0:T(8,128)(2,1)S(1)}) custom-call(s32[4]{0:T(128)S(1)} %select_reduce_fusion.refs_0_, bf16[640,640]{1,0:T(8,128)(2,1)S(1)} %get-tuple-element.34.refs_1_, bf16[576,1024]{1,0:T(8,128)(2,1)S(1)} %bitcast.13, ...), custom_call_target="tpu_custom_call", output_to_operand_aliasing={{3}: (6, {})} | custom-call | flops 3019898880 | bytes 5242880 | tf_op jit(solution)/shard_map/attend/pallas_call | solution.py:135
  77.2 1.6 %collective-permute-start.5 = (bf16[576,256]{1,0:T(8,128)(2,1)S(1)}, bf16[576,256]{1,0:T(8,128)(2,1)S(1)}, u32[]{:S(2)}, u32[]{:S(2)}) collective-permute-start(bf16[576,256]{1,0:T(8,128)(2,1)S(1)} %get-tuple-element.37.refs_4_), channel_id=1, source_target_pairs={{0,4},{4,0},{8,12},{12,8},{16,20},{20,16},{24,28},{28,24},{1,5},{5... | collective-permute-start | bytes 884744 | tf_op jit(solution)/shard_map/ppermute | solution.py:277
  78.8 6.0 %attend.9 = (f32[640,128]{1,0:T(8,128)S(1)}, f32[640,128]{1,0:T(8,128)S(1)}, f32[640,512]{1,0:T(8,128)S(1)}, bf16[576,256]{1,0:T(8,128)(2,1)S(1)}) custom-call(s32[4]{0:T(128)S(1)} %select_reduce_fusion.refs_0_, bf16[640,640]{1,0:T(8,128)(2,1)S(1)} %collective-permute-done.refs_1_, bf16[576,1024]{1,0:T(8,128)(2,1)S(1)} %bitcast.14, ...), custom_call_target="tpu_custom_call", output_to_operand_aliasing={{3}: (4, {})} | custom-call | flops 3019898880 | bytes 5242880 | tf_op jit(solution)/shard_map/attend/pallas_call | solution.py:135
  85.4 1.7 %collective-permute-done.7.refs_9_ = bf16[576,256]{1,0:T(8,128)(2,1)S(1)} collective-permute-done((bf16[576,256]{1,0:T(8,128)(2,1)S(1)}, bf16[576,256]{1,0:T(8,128)(2,1)S(1)}, u32[]{:S(2)}, u32[]{:S(2)}) %collective-permute-start.7) | collective-permute-done | bytes 294944 | tf_op jit(solution)/shard_map/ppermute | solution.py:277
  87.1 3.8 %attend.10 = (f32[640,128]{1,0:T(8,128)S(1)}, f32[640,128]{1,0:T(8,128)S(1)}, f32[640,512]{1,0:T(8,128)S(1)}, bf16[576,256]{1,0:T(8,128)(2,1)S(1)}) custom-call(s32[4]{0:T(128)S(1)} %select_reduce_fusion.refs_0_, bf16[640,640]{1,0:T(8,128)(2,1)S(1)} %collective-permute-done.refs_1_, ...), custom_call_target="tpu_custom_call", output_to_operand_aliasing={{3}: (9, {})} | custom-call | flops 1509949440 | bytes 3932160 | tf_op jit(solution)/shard_map/attend/pallas_call | solution.py:135
  90.9 1.6 %collective-permute-start.8 = (bf16[576,256]{1,0:T(8,128)(2,1)S(1)}, bf16[576,256]{1,0:T(8,128)(2,1)S(1)}, u32[]{:S(2)}, u32[]{:S(2)}) collective-permute-start(bf16[576,256]{1,0:T(8,128)(2,1)S(1)} %get-tuple-element.43.refs_4_), channel_id=1, source_target_pairs={{0,4},{4,0},{8,12},{12,8},{16,20},{20,16},{24,28},{28,24},{1,5},{5... | collective-permute-start | bytes 884744 | tf_op jit(solution)/shard_map/ppermute | solution.py:277
  92.4 3.7 %attend.14 = (f32[640,128]{1,0:T(8,128)S(1)}, f32[640,128]{1,0:T(8,128)S(1)}, f32[640,512]{1,0:T(8,128)S(1)}) custom-call(s32[4]{0:T(128)S(1)} %select_reduce_fusion.refs_0_, bf16[640,640]{1,0:T(8,128)(2,1)S(1)} %collective-permute-done.refs_1_, bf16[576,256]{1,0:T(8,128)(2,1)S(1)} %get-tuple-element.44.refs_2_, ...), custom_call_target="tpu_custom_call" | custom-call | flops 1132462080 | bytes 3604480 | tf_op jit(solution)/shard_map/attend/pallas_call | solution.py:135
  96.2 3.7 %collective-permute-done.8.refs_2_ = bf16[576,256]{1,0:T(8,128)(2,1)S(1)} collective-permute-done((bf16[576,256]{1,0:T(8,128)(2,1)S(1)}, bf16[576,256]{1,0:T(8,128)(2,1)S(1)}, u32[]{:S(2)}, u32[]{:S(2)}) %collective-permute-start.8) | collective-permute-done | bytes 294944 | tf_op jit(solution)/shard_map/ppermute | solution.py:277
  99.9 3.0 %attend.15 = bf16[656,512]{1,0:T(8,128)(2,1)S(1)} custom-call(s32[4]{0:T(128)S(1)} %select_reduce_fusion.refs_0_, bf16[640,640]{1,0:T(8,128)(2,1)S(1)} %collective-permute-done.refs_1_, bf16[576,256]{1,0:T(8,128)(2,1)S(1)} %collective-permute-done.8.refs_2_, f32[640,128]{1,0:T(8,128)S(1)} %get-tuple-element.60.refs_3_, ...), custom_call_target="tpu_custom_call" | custom-call | flops 377487360 | bytes 2949120 | tf_op jit(solution)/shard_map/attend/pallas_call | solution.py:135
  103.1 1.5 %fusion = bf16[1024,576]{0,1:T(8,128)(2,1)} fusion(bf16[1024,576]{0,1:T(8,128)(2,1)S(1)} %copy-done, pred[1024]{0:T(1024)(128)(4,1)S(1)} %fusion.1, s32[32]{0:T(128)S(1)} %compare_select_fusion, bf16[128,576]{1,0:T(8,128)(2,1)S(1)} %get-tuple-element.35.after_ref.refs_4_), kind=kOutput, calls=%fused_computation.1 | convolution fusion | flops 38961152 | bytes 2401792 | tf_op jit(solution)/shard_map/dot_general | solution.py:314
  104.6 3.8 %attend.11 = (f32[640,128]{1,0:T(8,128)S(1)}, f32[640,128]{1,0:T(8,128)S(1)}, f32[640,512]{1,0:T(8,128)S(1)}) custom-call(s32[4]{0:T(128)S(1)} %select_reduce_fusion.refs_0_, bf16[640,640]{1,0:T(8,128)(2,1)S(1)} %get-tuple-element.34.refs_1_, bf16[576,256]{1,0:T(8,128)(2,1)} %collective-permute-done.1.refs_2_, ...), custom_call_target="tpu_custom_call" | custom-call | flops 1509949440 | bytes 3932160 | tf_op jit(solution)/shard_map/attend/pallas_call | solution.py:135
  108.4 3.7 %attend.12 = (f32[640,128]{1,0:T(8,128)S(1)}, f32[640,128]{1,0:T(8,128)S(1)}, f32[640,512]{1,0:T(8,128)S(1)}) custom-call(s32[4]{0:T(128)S(1)} %select_reduce_fusion.refs_0_, bf16[640,640]{1,0:T(8,128)(2,1)S(1)} %get-tuple-element.34.refs_1_, bf16[576,256]{1,0:T(8,128)(2,1)S(1)} %get-tuple-element.44.refs_2_, ...), custom_call_target="tpu_custom_call" | custom-call | flops 1132462080 | bytes 3604480 | tf_op jit(solution)/shard_map/attend/pallas_call | solution.py:135
  112.1 2.3 %attend.13 = (f32[640,128]{1,0:T(8,128)S(1)}, f32[640,128]{1,0:T(8,128)S(1)}, f32[640,512]{1,0:T(8,128)S(1)}) custom-call(s32[4]{0:T(128)S(1)} %select_reduce_fusion.refs_0_, bf16[640,640]{1,0:T(8,128)(2,1)S(1)} %get-tuple-element.34.refs_1_, bf16[576,256]{1,0:T(8,128)(2,1)S(1)} %collective-permute-done.8.refs_2_, f32[640,128]{1,0:T(8,128)S(1)} %get-tuple-element.51.refs_3_, ...), custom_call_target="tpu_custom_call" | custom-call | flops 377487360 | bytes 2949120 | tf_op jit(solution)/shard_map/attend/pallas_call | solution.py:135
  114.4 4.7 %collective-permute-done.10.far_ref = bf16[656,512]{1,0:T(8,128)(2,1)S(1)} collective-permute-done((bf16[656,512]{1,0:T(8,128)(2,1)S(1)}, bf16[656,512]{1,0:T(8,128)(2,1)S(1)}, u32[]{:S(2)}, u32[]{:S(2)}) %collective-permute-start.10) | collective-permute-done | bytes 671776 | tf_op jit(solution)/shard_map/ppermute | solution.py:277
  119.1 1.2 %finish.1 = (bf16[32,2048]{1,0:T(8,128)(2,1)}, bf16[8,2048]{1,0:T(8,128)(2,1)}) custom-call(f32[640,128]{1,0:T(8,128)S(1)} %get-tuple-element.54.m_ref, f32[640,128]{1,0:T(8,128)S(1)} %get-tuple-element.55.l_ref, f32[640,512]{1,0:T(8,128)S(1)} %get-tuple-element.56.acc_ref, bf16[656,512]{1,0:T(8,128)(2,1)S(1)} %collective-permute-done.10.far_ref, ...), custom_call_target="tpu_custom_call" | custom-call | flops 83886080 | bytes 4063232 | tf_op jit(solution)/shard_map/finish/pallas_call | solution.py:249
  (41 shorter events, 3.7 us)
Async XLA Ops:
  0.6 12.7 %copy-start = (bf16[1024,576]{0,1:T(8,128)(2,1)S(1)}, bf16[1024,576]{0,1:T(8,128)(2,1)}, u32[]{:S(2)}) copy-start(bf16[1024,576]{0,1:T(8,128)(2,1)} %param.13) | copy-start | bytes 3538948
  0.6 70.1 %collective-permute-start.3 = (bf16[576,1024]{1,0:T(8,128)(2,1)}, bf16[576,1024]{1,0:T(8,128)(2,1)}, u32[]{:S(2)}, u32[]{:S(2)}) collective-permute-start(bf16[576,1024]{1,0:T(8,128)(2,1)} %bitcast.10), channel_id=1, source_target_pairs={{0,4},{4,0},{8,12},{12,8},{16,20},{20,16},{24,28},{28,24},{1,5},{5... | collective-permute-start | bytes 3538952 | tf_op jit(solution)/shard_map/ppermute | solution.py:277
  8.3 30.7 %copy-start.1 = (bf16[16,128,512]{2,1,0:T(8,128)(2,1)S(1)}, bf16[16,128,512]{2,1,0:T(8,128)(2,1)}, u32[]{:S(2)}) copy-start(bf16[16,128,512]{2,1,0:T(8,128)(2,1)} %w_ref.2) | copy-start | bytes 6291460
  8.3 24.8 %all-to-all-start = ((bf16[8,4,4560]{2,1,0:T(4,128)(2,1)}), bf16[8,4,4560]{2,1,0:T(4,128)(2,1)}, u32[]{:S(2)}, u32[]{:S(2)}) async-start(bf16[8,4,4560]{2,1,0:T(4,128)(2,1)} %concatenate.10), calls=%async_computation | async-start | bytes 589824 | tf_op jit(solution)/shard_map/all_to_all | solution.py:291
  14.1 31.3 %collective-permute-start.1 = (bf16[576,256]{1,0:T(8,128)(2,1)}, bf16[576,256]{1,0:T(8,128)(2,1)}, u32[]{:S(2)}, u32[]{:S(2)}) collective-permute-start(bf16[576,256]{1,0:T(8,128)(2,1)} %slice.18), channel_id=1, source_target_pairs={{0,16},{4,20},{8,24},{12,28},{16,0},{20,4},{24,8},{28,12},{1,17},{... | collective-permute-start | bytes 884744 | tf_op jit(solution)/shard_map/ppermute | solution.py:277
  35.9 6.5 %copy-start.6 = (s32[8]{0:T(128)S(1)}, s32[8]{0:T(128)}, u32[]{:S(2)}) copy-start(s32[8]{0:T(128)} %param.16) | copy-start | bytes 100
  39.1 0.8 copy-start.3
  39.9 5.3 %copy-start.7 = (s32[8]{0:T(128)S(1)}, s32[8]{0:T(128)}, u32[]{:S(2)}) copy-start(s32[8]{0:T(128)} %param.19) | copy-start | bytes 100
  40.3 38.4 %collective-permute-start = (bf16[640,640]{1,0:T(8,128)(2,1)S(1)}, bf16[640,640]{1,0:T(8,128)(2,1)S(1)}, u32[]{:S(2)}, u32[]{:S(2)}) collective-permute-start(bf16[640,640]{1,0:T(8,128)(2,1)S(1)} %get-tuple-element.34.refs_1_), channel_id=1, source_target_pairs={{0,8},{4,12},{8,0},{12,4},{16,24},{20,28},{24,16},{28,20},{1,9},{5... | collective-permute-start | bytes 2457608 | tf_op jit(solution)/shard_map/ppermute | solution.py:277
  42.6 24.7 %collective-permute-start.4 = (bf16[576,256]{1,0:T(8,128)(2,1)S(1)}, bf16[576,256]{1,0:T(8,128)(2,1)S(1)}, u32[]{:S(2)}, u32[]{:S(2)}) collective-permute-start(bf16[576,256]{1,0:T(8,128)(2,1)S(1)} %get-tuple-element.36), channel_id=1, source_target_pairs={{0,16},{4,20},{8,24},{12,28},{16,0},{20,4},{24,8},{28,12},{1,17},{... | collective-permute-start | bytes 884744 | tf_op jit(solution)/shard_map/ppermute | solution.py:277
  45.4 40.0 %collective-permute-start.2 = (bf16[576,256]{1,0:T(8,128)(2,1)}, bf16[576,256]{1,0:T(8,128)(2,1)S(1)}, u32[]{:S(2)}, u32[]{:S(2)}) collective-permute-start(bf16[576,256]{1,0:T(8,128)(2,1)} %collective-permute-done.1.refs_2_), channel_id=1, source_target_pairs={{0,4},{4,0},{8,12},{12,8},{16,20},{20,16},{24,28},{28,24},{1,5},{5... | collective-permute-start | bytes 884744 | tf_op jit(solution)/shard_map/ppermute | solution.py:277
  47.0 31.8 %collective-permute-start.6 = (bf16[576,256]{1,0:T(8,128)(2,1)S(1)}, bf16[576,256]{1,0:T(8,128)(2,1)S(1)}, u32[]{:S(2)}, u32[]{:S(2)}) collective-permute-start(bf16[576,256]{1,0:T(8,128)(2,1)S(1)} %get-tuple-element.38), channel_id=1, source_target_pairs={{0,16},{4,20},{8,24},{12,28},{16,0},{20,4},{24,8},{28,12},{1,17},{... | collective-permute-start | bytes 884744 | tf_op jit(solution)/shard_map/ppermute | solution.py:277
  67.3 19.8 %collective-permute-start.7 = (bf16[576,256]{1,0:T(8,128)(2,1)S(1)}, bf16[576,256]{1,0:T(8,128)(2,1)S(1)}, u32[]{:S(2)}, u32[]{:S(2)}) collective-permute-start(bf16[576,256]{1,0:T(8,128)(2,1)S(1)} %get-tuple-element.42), channel_id=1, source_target_pairs={{0,16},{4,20},{8,24},{12,28},{16,0},{20,4},{24,8},{28,12},{1,17},{... | collective-permute-start | bytes 884744 | tf_op jit(solution)/shard_map/ppermute | solution.py:277
  77.2 9.9 %collective-permute-start.5 = (bf16[576,256]{1,0:T(8,128)(2,1)S(1)}, bf16[576,256]{1,0:T(8,128)(2,1)S(1)}, u32[]{:S(2)}, u32[]{:S(2)}) collective-permute-start(bf16[576,256]{1,0:T(8,128)(2,1)S(1)} %get-tuple-element.37.refs_4_), channel_id=1, source_target_pairs={{0,4},{4,0},{8,12},{12,8},{16,20},{20,16},{24,28},{28,24},{1,5},{5... | collective-permute-start | bytes 884744 | tf_op jit(solution)/shard_map/ppermute | solution.py:277
  84.8 7.6 %collective-permute-start.9 = (bf16[576,256]{1,0:T(8,128)(2,1)S(1)}, bf16[576,256]{1,0:T(8,128)(2,1)S(1)}, u32[]{:S(2)}, u32[]{:S(2)}) collective-permute-start(bf16[576,256]{1,0:T(8,128)(2,1)S(1)} %get-tuple-element.44.refs_2_), channel_id=1, source_target_pairs={{0,4},{4,0},{8,12},{12,8},{16,20},{20,16},{24,28},{28,24},{1,5},{5... | collective-permute-start | bytes 884744 | tf_op jit(solution)/shard_map/ppermute | solution.py:277
  87.1 5.3 %copy-start.4 = (s32[32]{0:T(128)S(1)}, s32[32]{0:T(128)}, u32[]{:S(2)}) copy-start(s32[32]{0:T(128)} %param.18) | copy-start | bytes 388
  87.1 5.3 %copy-start.5 = (s32[32]{0:T(128)S(1)}, s32[32]{0:T(128)}, u32[]{:S(2)}) copy-start(s32[32]{0:T(128)} %param.17) | copy-start | bytes 388
  90.9 9.0 %collective-permute-start.8 = (bf16[576,256]{1,0:T(8,128)(2,1)S(1)}, bf16[576,256]{1,0:T(8,128)(2,1)S(1)}, u32[]{:S(2)}, u32[]{:S(2)}) collective-permute-start(bf16[576,256]{1,0:T(8,128)(2,1)S(1)} %get-tuple-element.43.refs_4_), channel_id=1, source_target_pairs={{0,4},{4,0},{8,12},{12,8},{16,20},{20,16},{24,28},{28,24},{1,5},{5... | collective-permute-start | bytes 884744 | tf_op jit(solution)/shard_map/ppermute | solution.py:277
  102.9 16.2 %collective-permute-start.10 = (bf16[656,512]{1,0:T(8,128)(2,1)S(1)}, bf16[656,512]{1,0:T(8,128)(2,1)S(1)}, u32[]{:S(2)}, u32[]{:S(2)}) collective-permute-start(bf16[656,512]{1,0:T(8,128)(2,1)S(1)} %attend.15), channel_id=1, source_target_pairs={{0,8},{4,12},{8,0},{12,4},{16,24},{20,28},{24,16},{28,20},{1,9},{5... | collective-permute-start | bytes 2015240 | tf_op jit(solution)/shard_map/ppermute | solution.py:277
  112.1 7.0 %copy-start.2 = (bf16[16,512,128]{2,1,0:T(8,128)(2,1)S(1)}, bf16[16,512,128]{2,1,0:T(8,128)(2,1)}, u32[]{:S(2)}) copy-start(bf16[16,512,128]{2,1,0:T(8,128)(2,1)} %w_ref.3) | copy-start | bytes 6291460

commit v3 on v2

--- a/solution.py
+++ b/solution.py
@@ -10,7 +10,7 @@
 DN = 128
 DC = 512
 LANES = 128
-CHUNKS = 4
+VMEM = 60 * 1024 * 1024
 
 score_scale = 0.1353
 LOG2E = 1.4426950408889634
@@ -22,7 +22,7 @@
     return jnp.concatenate([x] * (width // LANES), axis=1) if width > LANES else x
 
 
-def attend_kernel(pieces, extra, first, last, through, *refs):
+def attend_kernel(pieces, extra, first, last, *refs):
     refs = list(refs)
     fills = refs.pop(0)
     q_ref = refs.pop(0)
@@ -32,7 +32,6 @@
         bias_ref = refs.pop(0)
     if not first:
         m_in, l_in, acc_in = refs.pop(0), refs.pop(0), refs.pop(0)
-    refs = refs[through : len(refs) - through]
     rows = q_ref.shape[0]
     q = q_ref[:, : keys[0].shape[0]]
     scores = []
@@ -90,7 +89,7 @@
     out[rows:, :] = jnp.concatenate([high, mid, low, jnp.zeros_like(low)], axis=1)
 
 
-def attend(fills, q, pieces, new=None, state=None, last=False, tile=None, through=()):
+def attend(fills, q, pieces, new=None, state=None, last=False, tile=None):
     rows, width = q.shape
     tile = rows if tile is None else tile
     spec = tuple((start, keys.shape[1], which) for start, which, keys in pieces)
@@ -125,41 +124,115 @@
             jax.ShapeDtypeStruct((rows, DC), jnp.float32),
         ]
         out_specs = list(state_specs)
-    aliases = {len(operands) + i: len(out_shape) + i for i in range(len(through))}
-    operands += list(through)
-    in_specs += [pl.BlockSpec(memory_space=pl.ANY)] * len(through)
-    made = len(out_shape)
-    out_shape += [jax.ShapeDtypeStruct(x.shape, x.dtype) for x in through]
-    out_specs += [pl.BlockSpec(memory_space=pl.ANY)] * len(through)
-    count = sum(piece[1] for piece in spec)
     out = pl.pallas_call(
-        functools.partial(attend_kernel, spec, new is not None, state is None, last, len(through)),
+        functools.partial(attend_kernel, spec, new is not None, state is None, last),
         grid=(rows // tile,),
         in_specs=in_specs,
         out_specs=out_specs,
         out_shape=out_shape,
         compiler_params=pltpu.CompilerParams(vmem_limit_bytes=40 * 1024 * 1024),
         cost_estimate=pl.CostEstimate(
-            flops=2 * rows * count * (width + DC),
-            bytes_accessed=2 * count * width + 4 * rows * DC * 2,
-            transcendentals=rows * count,
+            flops=0, bytes_accessed=0, transcendentals=0
         ),
-        input_output_aliases=aliases,
         name="attend",
     )(*operands)
-    result = out[0] if last else tuple(out[:made])
-    return (result, *out[made:]) if through else result
-
-
-def absorb_kernel(span_ref, dec_ref, w_ref, absorbed_ref, extra_ref):
+    return out[0] if last else out
+
+
+def after_kernel(x_ref, token_ref, out_ref):
+    pass
+
+
+def after(x, token):
+    return pl.pallas_call(
+        after_kernel,
+        in_specs=[pl.BlockSpec(memory_space=pl.ANY)] * 2,
+        out_specs=pl.BlockSpec(memory_space=pl.ANY),
+        out_shape=jax.ShapeDtypeStruct(x.shape, x.dtype),
+        input_output_aliases={0: 0},
+        compiler_params=pltpu.CompilerParams(vmem_limit_bytes=VMEM),
+        name="after",
+    )(x, token)
+
+
+def pack_kernel(query_ref, dec_ref, span_kv_ref, dec_kv_ref, out_ref):
+    n, per, _ = out_ref.shape
+    row = span_kv_ref.shape[1]
+    per_dec = dec_ref.shape[0]
+    part = query_ref.shape[1] // n
+    cut = part // per
+    pad = -(-row // LANES) * LANES - row
+
+    def padded(ref):
+        x = ref[...].astype(jnp.float32)
+        return jnp.concatenate([x, jnp.zeros((x.shape[0], pad), jnp.float32)], axis=1)
+
+    fresh = padded(span_kv_ref)
+    dec_kv = padded(dec_kv_ref)
+    tail = [fresh]
+    for e in range(per_dec):
+        for j in range(0, row + pad, per * LANES):
+            strips = [dec_kv[e : e + 1, k : k + LANES] for k in range(j, min(j + per * LANES, row + pad), LANES)]
+            strips += [jnp.zeros((1, LANES), jnp.float32)] * (per - len(strips))
+            tail.append(jnp.concatenate(strips, axis=0))
+    tail = jnp.concatenate(tail, axis=1).astype(jnp.bfloat16)
+    for d in range(n):
+        out_ref[d, :, :part] = query_ref[:, d * part : (d + 1) * part]
+        for e in range(per_dec):
+            strips = dec_ref[e : e + 1, d * part : (d + 1) * part].astype(jnp.float32)
+            strips = [strips[:, i * cut : (i + 1) * cut] for i in range(per)]
+            at = part + e * cut
+            out_ref[d, :, at : at + cut] = jnp.concatenate(strips, axis=0).astype(jnp.bfloat16)
+        out_ref[d, :, part + per_dec * cut :] = tail
+
+
+def pack(n, query, dec_query, span_kv, dec_kv):
+    per, row = span_kv.shape
+    per_dec = dec_kv.shape[0]
+    part = query.shape[1] // n
+    wide = -(-row // LANES) * LANES
+    fold = -(-wide // (per * LANES)) * LANES
+    total = part + per_dec * (part // per) + wide + per_dec * fold
+    operands = (query, dec_query, span_kv, dec_kv)
+    return pl.pallas_call(
+        pack_kernel,
+        grid=(1,),
+        in_specs=[pl.BlockSpec(x.shape, lambda i: (0, 0)) for x in operands],
+        out_specs=pl.BlockSpec((n, per, total), lambda i: (0, 0, 0)),
+        out_shape=jax.ShapeDtypeStruct((n, per, total), jnp.bfloat16),
+        compiler_params=pltpu.CompilerParams(vmem_limit_bytes=VMEM),
+        name="pack",
+    )(*operands)
+
+
+def absorb_kernel(per_dec, got_ref, w_ref, absorbed_ref, extra_ref):
     heads = w_ref.shape[0]
+    n, per, _ = got_ref.shape
     row = extra_ref.shape[1]
-    width = (span_ref.shape[1] - row) // heads
-    count = span_ref.shape[0] + dec_ref.shape[0]
-    rows = jnp.concatenate(
-        [span_ref[...].astype(jnp.float32), dec_ref[...].astype(jnp.float32)], axis=0
-    )
-    q = rows.astype(jnp.bfloat16)
+    count = absorbed_ref.shape[0] // heads
+    wide = -(-row // LANES) * LANES
+    fold = -(-wide // (per * LANES)) * LANES
+    part = (got_ref.shape[2] - wide - per_dec * fold) * per // (per + per_dec)
+    width = part // heads
+    cut = part // per
+    at = part + per_dec * cut
+
+    def unfold(x, length):
+        strips = []
+        for j in range(0, x.shape[1], length):
+            strips += [x[i : i + 1, j : j + length] for i in range(per)]
+        return jnp.concatenate(strips, axis=1)
+
+    blocks = [got_ref[d].astype(jnp.float32) for d in range(n)]
+    queries = [x[:, :part] for x in blocks]
+    fresh = [x[:, at : at + wide] for x in blocks]
+    for x in blocks:
+        for e in range(per_dec):
+            queries.append(unfold(x[:, part + e * cut : part + (e + 1) * cut], cut))
+            begin = at + wide + e * fold
+            fresh.append(unfold(x[:, begin : begin + fold], LANES)[:, :wide])
+    q = jnp.concatenate(queries, axis=0).astype(jnp.bfloat16)
+    new = jnp.concatenate(fresh, axis=0)
     blank = jnp.zeros((count, absorbed_ref.shape[1] - row), jnp.float32)
     for h in range(0, heads, 2):
         parts = []
@@ -171,15 +244,13 @@
         pair = jnp.concatenate(parts, axis=0).astype(jnp.bfloat16)
         absorbed_ref[h * count : (h + 2) * count, :] = pair
     blank = jnp.zeros((extra_ref.shape[0] - count, row), jnp.float32)
-    new = jnp.concatenate([rows[:, heads * width :], blank], axis=0)
-    extra_ref[...] = new.astype(jnp.bfloat16)
-
-
-def absorb(got_span, got_dec, w_uk, row):
+    extra_ref[...] = jnp.concatenate([new[:, :row], blank], axis=0).astype(jnp.bfloat16)
+
+
+def absorb(count, per_dec, got, w_uk, row):
     heads = w_uk.shape[0]
-    count = got_span.shape[0] + got_dec.shape[0]
     return pl.pallas_call(
-        absorb_kernel,
+        functools.partial(absorb_kernel, per_dec),
         out_shape=(
             jax.ShapeDtypeStruct((heads * count, -(-row // LANES) * LANES), jnp.bfloat16),
             jax.ShapeDtypeStruct((LANES, row), jnp.bfloat16),
@@ -187,28 +258,29 @@
         compiler_params=pltpu.CompilerParams(vmem_limit_bytes=40 * 1024 * 1024),
         cost_estimate=pl.CostEstimate(
             flops=2 * count * heads * DN * DC,
-            bytes_accessed=2 * w_uk.size + 4 * got_span.size,
+            bytes_accessed=2 * w_uk.size + 2 * got.size,
             transcendentals=0,
         ),
         name="absorb",
-    )(got_span, got_dec, w_uk)
-
-
-def split_kernel(size, skip, x_ref, after_ref, *out_refs):
-    for i, ref in enumerate(out_refs):
-        ref[...] = x_ref[:, (skip + i) * size : (skip + i + 1) * size]
-
-
-def split(x, size, skip, after):
-    pieces = x.shape[1] // size - skip
+    )(got, w_uk)
+
+
+def split_kernel(spans, x_ref, after_ref, *out_refs):
+    for (a, b), ref in zip(spans, out_refs):
+        ref[...] = x_ref[:, a:b]
+
+
+def split(x, spans, after):
     return pl.pallas_call(
-        functools.partial(split_kernel, size, skip),
+        functools.partial(split_kernel, spans),
+        grid=(1,),
         in_specs=[
-            pl.BlockSpec(memory_space=pltpu.VMEM),
+            pl.BlockSpec(x.shape, lambda i: (0, 0)),
             pl.BlockSpec(memory_space=pl.ANY),
         ],
-        out_shape=[jax.ShapeDtypeStruct((x.shape[0], size), x.dtype)] * pieces,
-        compiler_params=pltpu.CompilerParams(vmem_limit_bytes=16 * 1024 * 1024),
+        out_specs=[pl.BlockSpec((x.shape[0], b - a), lambda i: (0, 0)) for a, b in spans],
+        out_shape=[jax.ShapeDtypeStruct((x.shape[0], b - a), x.dtype) for a, b in spans],
+        compiler_params=pltpu.CompilerParams(vmem_limit_bytes=VMEM),
         name="split",
     )(x, after)
 
@@ -271,7 +343,6 @@
     count = span + rows_dec
     heads = w_uk.shape[0]
     row = cache_kv.shape[1]
-    width = query.shape[1] // (heads * n)
 
     def swap(x, stride):
         return lax.ppermute(x, "seq", [(i, i ^ stride) for i in range(n)])
@@ -279,35 +350,29 @@
     far, pair = n // 2, n // 4
     near = [1 << b for b in range(pair.bit_length() - 1)]
     keys = cache_kv.T
-    size = pos_dev // CHUNKS
-
-    per, per_dec = span // n, rows_dec // n
-    mine = jnp.swapaxes(query.reshape(per, n, heads * width), 0, 1)
-    fresh = jnp.broadcast_to(span_kv[None], (n, per, row))
-    mine_dec = jnp.swapaxes(dec_query.reshape(per_dec, n, heads * width), 0, 1)
-    fresh_dec = jnp.broadcast_to(dec_kv[None], (n, per_dec, row))
-    mine_dec = jnp.concatenate([mine_dec, fresh_dec], axis=2).reshape(n, per, -1)
-    mine = jnp.concatenate([mine, fresh, mine_dec], axis=2)
+    eighth = pos_dev // 8
+    edges = [0, 2 * eighth, 5 * eighth, 7 * eighth, pos_dev]
+
+    mine = pack(n, query, dec_query, span_kv, dec_kv)
     got = lax.all_to_all(mine, "seq", split_axis=0, concat_axis=0, tiled=True)
-    full = heads * width + row
-    got_span = got[:, :, :full].reshape(span, full)
-    got_dec = got[:, :, full:].reshape(rows_dec, full)
-    absorbed, extra = absorb(got_span, got_dec, w_uk, row)
+    absorbed, extra = absorb(count, rows_dec // n, got, w_uk, row)
     new_rows = extra[:span]
     other = swap(absorbed, pair)
 
-    blocks = [(jnp.int32(0), [keys])]
+    lead = keys[:, : edges[1]]
+    *pieces, rest = split(
+        keys, [*zip(edges[1:], edges[2:]), (edges[1], pos_dev)], extra
+    )
+    blocks = [(0, [lead, rest])]
     for stride in near:
         blocks += [(offset ^ stride, [swap(x, stride) for x in held]) for offset, held in blocks]
-    cuts = [keys[:, :size]] + list(split(keys, size, 1, extra))
+    pieces = [swap(x, far) for x in [lead, *pieces]]
 
     def spread(x):
         part = [(far, x)]
         for stride in near:
             part += [(offset ^ stride, swap(y, stride)) for offset, y in part]
         return part
-
-    pieces = [swap(x, far) for x in cuts]
 
     target = jnp.where(owner == me, slot, -1)
     onehot = jnp.arange(pos_dev, dtype=jnp.int32)[None, :] == target[:, None]
@@ -336,20 +401,20 @@
     tile = heads // 2 * count
 
     def stage_of(c, part):
-        return [(c * size, base + i, x) for i, (_, x) in enumerate(part)]
-
-    home = [(0, i, xs[0]) for i, (_, xs) in enumerate(blocks)]
+        return [(edges[c], base + i, x) for i, (_, x) in enumerate(part)]
+
+    home = [(0, 0, keys)]
+    for i, (_, (x, y)) in enumerate(blocks[1:], 1):
+        home += [(0, i, x), (edges[1], i, y)]
+    state = attend(fills, absorbed, home, new=(extra, bias), tile=tile)
     first = stage_of(0, spread(pieces[0]))
-    state, pieces[1] = attend(
-        fills, absorbed, home, new=(extra, bias), tile=tile, through=(pieces[1],)
-    )
-    first += stage_of(1, spread(pieces[1]))
-    guest, pieces[2] = attend(fills, other, home, tile=tile, through=(pieces[2],))
-    second = stage_of(2, spread(pieces[2]))
-    guest, pieces[3] = attend(fills, other, first, state=guest, tile=tile, through=(pieces[3],))
-    third = stage_of(3, spread(pieces[3]))
+    first += stage_of(1, spread(after(pieces[1], state[0])))
+    guest = attend(fills, other, home, tile=tile)
+    second = stage_of(2, spread(after(pieces[2], guest[0])))
+    guest = attend(fills, other, first, state=guest, tile=tile)
+    state = attend(fills, absorbed, first, state=state, tile=tile)
+    third = stage_of(3, spread(after(after(pieces[3], guest[0]), state[0])))
     second, third = second + third[:1], third[1:]
-    state = attend(fills, absorbed, first, state=state, tile=tile)
     guest = attend(fills, other, second, state=guest, tile=tile)
     sent = attend(fills, other, third, state=guest, last=True)
     back = swap(sent, pair)

time: 121 us -> 131 us (1.083)
  waiting for transfers between devices: 46.1 us -> 28.4 us
  blocking collectives: 0 us -> 17.7 us
  starting transfers between devices: 24.6 us -> 12.7 us
  local copies, waits for them, and re-layouts: 10.3 us -> 21.8 us
  Pallas kernels: 34.6 us -> 44 us
    unnamed x16 -> x84, local copies, waits for them, and re-layouts: 0.86 us -> 21 us
    all_to_all x0 -> x1, blocking collectives: none -> 17.7 us  [body(): got = lax.all_to_all(mine, 'seq', split_axis=0, concat_axis=0, tiled=True)]
    all_to_all x1 -> x0, waiting for transfers between devices: 16.1 us -> none  [body(): got = lax.all_to_all(mine, 'seq', split_axis=0, concat_axis=0, tiled=True)]
    ppermute x11 -> x12, starting transfers between devices: 19.6 us -> 12.7 us  [swap(): return lax.ppermute(x, 'seq', [(i, i ^ stride) for i in range(n)])]
    pallas_call x8, Pallas kernels: 32.8 us -> 38 us  [attend(): pl.pallas_call(functools.partial(attend_kernel, spec, new is not None, st...]
    all_to_all x1 -> x0, starting transfers between devices: 5.01 us -> none  [body(): got = lax.all_to_all(mine, 'seq', split_axis=0, concat_axis=0, tiled=True)]
    pallas_call x2 -> x7, Pallas kernels: 0.52 us -> 4.79 us  [the longest x1 2.52 us: split(): pl.pallas_call(functools.partial(split_kernel, spans), grid=(1,), in_spec...]
    slice x3 -> x1, local copies, waits for them, and re-layouts: 4.05 us -> 0.75 us  [body(): lead = keys[:, :edges[1]]]
  transfers between devices with their start and end apart: 12 -> 12, of which waited for: 5 -> 3; matrix products, arithmetic and copies ran while one was open for 11% -> 4% of each run, Pallas kernels for 25% -> 27%
where the time goes in v3:
time: 131 us; the launch traced here: 130 us
  Pallas kernels  44 us (34%)
  waiting for transfers between devices  28.4 us (22%)
  local copies, waits for them, and re-layouts  21.8 us (17%)
  blocking collectives  17.7 us (14%)
  starting transfers between devices  12.7 us (10%)
  matrix products  2.43 us (2%)
  other arithmetic  1.79 us (1%)
    pallas_call x8, Pallas kernels, attend(): pl.pallas_call(functools.partial(attend_kernel, spec, new is not None, st...  38 us
    ppermute x12, waiting for transfers between devices, swap(): return lax.ppermute(x, 'seq', [(i, i ^ stride) for i in range(n)])  28.4 us
    unnamed x84, local copies, waits for them, and re-layouts  21 us
    all_to_all x1, blocking collectives, body(): got = lax.all_to_all(mine, 'seq', split_axis=0, concat_axis=0, tiled=True)  17.7 us
    ppermute x12, starting transfers between devices, swap(): return lax.ppermute(x, 'seq', [(i, i ^ stride) for i in range(n)])  12.7 us
  transfers between devices with their start and end apart: 12, of which 3 were waited for; matrix products, arithmetic and copies ran while one was open for 4% of the time, Pallas kernels for 27%

profile of v3, /device:TPU:0, one launch (start us, length us, event | category | flops | bytes accessed | tf_op | source)
XLA Modules:
  0.0 129.7 jit_solution(17662099778144999345)
XLA Ops:
  0.6 1.8 %pack.1 = bf16[8,4,4736]{2,1,0:T(4,128)(2,1)} custom-call(bf16[4,24576]{1,0:T(4,128)(2,1)} %query_ref.1, bf16[1,24576]{1,0:T(2,128)(2,1)} %dec_ref.1, bf16[4,576]{1,0:T(4,128)(2,1)} %span_kv_ref.1, bf16[1,576]{1,0:T(2,128)(2,1)} %dec_kv_ref.1), custom_call_target="tpu_custom_call" | custom-call | tf_op jit(solution)/shard_map/pack/pallas_call | solution.py:197
  2.4 17.7 %all_to_all.5.got_ref = bf16[8,4,4736]{2,1,0:T(4,128)(2,1)S(1)} all-to-all(bf16[8,4,4736]{2,1,0:T(4,128)(2,1)} %pack.1), channel_id=1, replica_groups=mesh['seq'=8,'grp'=4] {'seq'}, dimensions={0} | all-to-all | bytes 606208 | tf_op jit(solution)/shard_map/all_to_all | solution.py:357
  20.1 1.6 %copy-done.7 = bf16[16,128,512]{2,1,0:T(8,128)(2,1)S(1)} copy-done((bf16[16,128,512]{2,1,0:T(8,128)(2,1)S(1)}, bf16[16,128,512]{2,1,0:T(8,128)(2,1)}, u32[]{:S(2)}) %copy-start.7) | copy-done | bytes 2097176
  22.9 2.5 %split.1 = (bf16[576,384]{1,0:T(8,128)(2,1)}, bf16[576,256]{1,0:T(8,128)(2,1)}, bf16[576,128]{1,0:T(8,128)(2,1)}, bf16[576,768]{1,0:T(8,128)(2,1)}) custom-call(bf16[576,1024]{1,0:T(8,128)(2,1)} %bitcast.5, bf16[128,576]{1,0:T(8,128)(2,1)} %copy-done.27), custom_call_target="tpu_custom_call" | custom-call | tf_op jit(solution)/shard_map/split/pallas_call | solution.py:274
  26.9 1.3 %collective-permute-start.5 = (bf16[576,256]{1,0:T(8,128)(2,1)}, bf16[576,256]{1,0:T(8,128)(2,1)S(1)}, u32[]{:S(2)}, u32[]{:S(2)}) collective-permute-start(bf16[576,256]{1,0:T(8,128)(2,1)} %slice.8), channel_id=1, source_target_pairs={{0,4},{4,0},{8,12},{12,8},{16,20},{20,16},{24,28},{28,24},{1,5},{5... | collective-permute-start | bytes 884744 | tf_op jit(solution)/shard_map/ppermute | solution.py:348
  28.9 1.4 %collective-permute-start.1 = (bf16[640,640]{1,0:T(8,128)(2,1)S(1)}, bf16[640,640]{1,0:T(8,128)(2,1)S(1)}, u32[]{:S(2)}, u32[]{:S(2)}) collective-permute-start(bf16[640,640]{1,0:T(8,128)(2,1)S(1)} %get-tuple-element.32.refs_1_), channel_id=1, source_target_pairs={{0,8},{4,12},{8,0},{12,4},{16,24},{20,28},{24,16},{28,20},{1,9},{5... | collective-permute-start | bytes 2457608 | tf_op jit(solution)/shard_map/ppermute | solution.py:348
  30.3 1.6 %collective-permute-start.4 = (bf16[576,384]{1,0:T(8,128)(2,1)}, bf16[576,384]{1,0:T(8,128)(2,1)S(1)}, u32[]{:S(2)}, u32[]{:S(2)}) collective-permute-start(bf16[576,384]{1,0:T(8,128)(2,1)} %get-tuple-element.35), channel_id=1, source_target_pairs={{0,16},{4,20},{8,24},{12,28},{16,0},{20,4},{24,8},{28,12},{1,17},{... | collective-permute-start | bytes 1327112 | tf_op jit(solution)/shard_map/ppermute | solution.py:348
  33.5 17.7 %collective-permute-done.5.refs_3_ = bf16[576,256]{1,0:T(8,128)(2,1)S(1)} collective-permute-done((bf16[576,256]{1,0:T(8,128)(2,1)}, bf16[576,256]{1,0:T(8,128)(2,1)S(1)}, u32[]{:S(2)}, u32[]{:S(2)}) %collective-permute-start.5) | collective-permute-done | bytes 294944 | tf_op jit(solution)/shard_map/ppermute | solution.py:348
  51.2 1.0 copy-done.28
  52.9 9.0 %attend.8 = (f32[640,128]{1,0:T(8,128)S(1)}, f32[640,128]{1,0:T(8,128)S(1)}, f32[640,512]{1,0:T(8,128)S(1)}) custom-call(s32[4]{0:T(128)S(1)} %select_reduce_fusion.refs_0_, bf16[640,640]{1,0:T(8,128)(2,1)S(1)} %get-tuple-element.32.refs_1_, bf16[576,1024]{1,0:T(8,128)(2,1)S(1)} %bitcast.7, bf16[576,256]{1,0:T(8,128)(2,1)S(1)} %collective-permute-done.5.refs_3_, ...), custom_call_target="tpu_custom_call" | custom-call | tf_op jit(solution)/shard_map/attend/pallas_call | solution.py:127
  62.7 1.1 copy-done.13
  65.3 1.1 collective-permute-start.7
  66.4 1.9 %collective-permute-start.9 = (bf16[576,256]{1,0:T(8,128)(2,1)}, bf16[576,256]{1,0:T(8,128)(2,1)S(1)}, u32[]{:S(2)}, u32[]{:S(2)}) collective-permute-start(bf16[576,256]{1,0:T(8,128)(2,1)} %get-tuple-element.45), channel_id=1, source_target_pairs={{0,16},{4,20},{8,24},{12,28},{16,0},{20,4},{24,8},{28,12},{1,17},{... | collective-permute-start | bytes 884744 | tf_op jit(solution)/shard_map/ppermute | solution.py:348
  68.3 1.4 %collective-permute-start.3 = (bf16[576,256]{1,0:T(8,128)(2,1)}, bf16[576,256]{1,0:T(8,128)(2,1)}, u32[]{:S(2)}, u32[]{:S(2)}) collective-permute-start(bf16[576,256]{1,0:T(8,128)(2,1)} %collective-permute-done.2.refs_2_), channel_id=1, source_target_pairs={{0,4},{4,0},{8,12},{12,8},{16,20},{20,16},{24,28},{28,24},{1,5},{5... | collective-permute-start | bytes 884744 | tf_op jit(solution)/shard_map/ppermute | solution.py:348
  71.9 5.8 %attend.9 = (f32[640,128]{1,0:T(8,128)S(1)}, f32[640,128]{1,0:T(8,128)S(1)}, f32[640,512]{1,0:T(8,128)S(1)}) custom-call(s32[4]{0:T(128)S(1)} %copy-done.37, bf16[640,640]{1,0:T(8,128)(2,1)S(1)} %collective-permute-done.1.refs_1_, bf16[576,1024]{1,0:T(8,128)(2,1)S(1)} %bitcast.8, bf16[576,256]{1,0:T(8,128)(2,1)S(1)} %copy-done.26, ...), custom_call_target="tpu_custom_call" | custom-call | tf_op jit(solution)/shard_map/attend/pallas_call | solution.py:127
  78.4 1.1 copy-done.15
  80.2 4.7 %collective-permute-done.9.x_ref = bf16[576,256]{1,0:T(8,128)(2,1)S(1)} collective-permute-done((bf16[576,256]{1,0:T(8,128)(2,1)}, bf16[576,256]{1,0:T(8,128)(2,1)S(1)}, u32[]{:S(2)}, u32[]{:S(2)}) %collective-permute-start.9) | collective-permute-done | bytes 294944 | tf_op jit(solution)/shard_map/ppermute | solution.py:348
  86.0 1.3 %copy-done.14 = f32[640,512]{1,0:T(8,128)S(1)} copy-done((f32[640,512]{1,0:T(8,128)S(1)}, f32[640,512]{1,0:T(8,128)}, u32[]{:S(2)}) %copy-start.14) | copy-done | bytes 1310744
  87.3 1.0 copy-done.30
  88.3 4.9 %attend.11 = (f32[640,128]{1,0:T(8,128)S(1)}, f32[640,128]{1,0:T(8,128)S(1)}, f32[640,512]{1,0:T(8,128)S(1)}) custom-call(s32[4]{0:T(128)S(1)} %copy-done.38, bf16[640,640]{1,0:T(8,128)(2,1)S(1)} %get-tuple-element.32.refs_1_, bf16[576,256]{1,0:T(8,128)(2,1)} %collective-permute-done.2.refs_2_, bf16[576,256]{1,0:T(8,128)(2,1)} %collective-permute-done.3.refs_3_, ...), custom_call_target="tpu_custom_call" | custom-call | tf_op jit(solution)/shard_map/attend/pallas_call | solution.py:127
  93.2 1.1 copy-done.17
  95.1 4.9 %attend.10 = (f32[640,128]{1,0:T(8,128)S(1)}, f32[640,128]{1,0:T(8,128)S(1)}, f32[640,512]{1,0:T(8,128)S(1)}) custom-call(s32[4]{0:T(128)S(1)} %copy-done.38, bf16[640,640]{1,0:T(8,128)(2,1)S(1)} %collective-permute-done.1.refs_1_, bf16[576,256]{1,0:T(8,128)(2,1)} %collective-permute-done.2.refs_2_, bf16[576,256]{1,0:T(8,128)(2,1)} %collective-permute-done.3.refs_3_, ...), custom_call_target="tpu_custom_call" | custom-call | tf_op jit(solution)/shard_map/attend/pallas_call | solution.py:127
  100.0 1.1 copy-done.19
  102.5 1.7 %collective-permute-start.8 = (bf16[576,128]{1,0:T(8,128)(2,1)}, bf16[576,128]{1,0:T(8,128)(2,1)S(1)}, u32[]{:S(2)}, u32[]{:S(2)}) collective-permute-start(bf16[576,128]{1,0:T(8,128)(2,1)} %after.6.refs_4_), channel_id=1, source_target_pairs={{0,4},{4,0},{8,12},{12,8},{16,20},{20,16},{24,28},{28,24},{1,5},{5... | collective-permute-start | bytes 442376 | tf_op jit(solution)/shard_map/ppermute | solution.py:348
  105.1 1.3 %copy-done.20 = f32[640,512]{1,0:T(8,128)S(1)} copy-done((f32[640,512]{1,0:T(8,128)S(1)}, f32[640,512]{1,0:T(8,128)}, u32[]{:S(2)}) %copy-start.20) | copy-done | bytes 1310744
  106.5 4.2 %attend.14 = (f32[640,128]{1,0:T(8,128)S(1)}, f32[640,128]{1,0:T(8,128)S(1)}, f32[640,512]{1,0:T(8,128)S(1)}) custom-call(s32[4]{0:T(128)S(1)} %copy-done.38, bf16[640,640]{1,0:T(8,128)(2,1)S(1)} %collective-permute-done.1.refs_1_, bf16[576,256]{1,0:T(8,128)(2,1)S(1)} %copy-done.4, bf16[576,256]{1,0:T(8,128)(2,1)} %collective-permute-done.10.refs_3_, ...), custom_call_target="tpu_custom_call" | custom-call | tf_op jit(solution)/shard_map/attend/pallas_call | solution.py:127
  110.7 2.9 %attend.15 = bf16[656,512]{1,0:T(8,128)(2,1)S(1)} custom-call(s32[4]{0:T(128)S(1)} %copy-done.38, bf16[640,640]{1,0:T(8,128)(2,1)S(1)} %collective-permute-done.1.refs_1_, bf16[576,128]{1,0:T(8,128)(2,1)S(1)} %collective-permute-done.8.refs_2_, f32[640,128]{1,0:T(8,128)S(1)} %get-tuple-element.56.refs_3_, f32[640,128]{1,0:T(8,128)S(1)} %get-tuple-element.57.refs_4_, ...), custom_call_target="tpu_custom_call" | custom-call | tf_op jit(solution)/shard_map/attend/pallas_call | solution.py:127
  113.8 2.4 %fusion = bf16[1024,576]{0,1:T(8,128)(2,1)} fusion(bf16[1024,576]{0,1:T(8,128)(2,1)S(1)} %copy-done, pred[1024]{0:T(1024)(128)(4,1)S(1)} %fusion.1, s32[32]{0:T(128)S(1)} %compare_select_fusion, bf16[128,576]{1,0:T(8,128)(2,1)} %copy-done.27), kind=kOutput, calls=%fused_computation.1 | convolution fusion | flops 38961152 | bytes 2401408 | tf_op jit(solution)/shard_map/dot_general | solution.py:379
  116.3 4.0 %attend.12 = (f32[640,128]{1,0:T(8,128)S(1)}, f32[640,128]{1,0:T(8,128)S(1)}, f32[640,512]{1,0:T(8,128)S(1)}) custom-call(s32[4]{0:T(128)S(1)} %copy-done.38, bf16[640,640]{1,0:T(8,128)(2,1)S(1)} %get-tuple-element.32.refs_1_, bf16[576,256]{1,0:T(8,128)(2,1)S(1)} %copy-done.4, bf16[576,256]{1,0:T(8,128)(2,1)} %collective-permute-done.10.refs_3_, ...), custom_call_target="tpu_custom_call" | custom-call | tf_op jit(solution)/shard_map/attend/pallas_call | solution.py:127
  120.3 2.2 %attend.13 = (f32[640,128]{1,0:T(8,128)S(1)}, f32[640,128]{1,0:T(8,128)S(1)}, f32[640,512]{1,0:T(8,128)S(1)}) custom-call(s32[4]{0:T(128)S(1)} %copy-done.38, bf16[640,640]{1,0:T(8,128)(2,1)S(1)} %get-tuple-element.32.refs_1_, bf16[576,128]{1,0:T(8,128)(2,1)S(1)} %collective-permute-done.8.refs_2_, f32[640,128]{1,0:T(8,128)S(1)} %get-tuple-element.48.refs_3_, ...), custom_call_target="tpu_custom_call" | custom-call | tf_op jit(solution)/shard_map/attend/pallas_call | solution.py:127
  122.5 6.0 %collective-permute-done.11.far_ref = bf16[656,512]{1,0:T(8,128)(2,1)S(1)} collective-permute-done((bf16[656,512]{1,0:T(8,128)(2,1)S(1)}, bf16[656,512]{1,0:T(8,128)(2,1)S(1)}, u32[]{:S(2)}, u32[]{:S(2)}) %collective-permute-start.11) | collective-permute-done | bytes 671776 | tf_op jit(solution)/shard_map/ppermute | solution.py:348
  128.5 1.2 finish.1
  (103 shorter events, 15.8 us)
Async XLA Ops:
  20.1 1.6 %copy-start.7 = (bf16[16,128,512]{2,1,0:T(8,128)(2,1)S(1)}, bf16[16,128,512]{2,1,0:T(8,128)(2,1)}, u32[]{:S(2)}) copy-start(bf16[16,128,512]{2,1,0:T(8,128)(2,1)} %w_ref.2) | copy-start | bytes 6291460
  21.7 4.4 %copy-start = (bf16[1024,576]{0,1:T(8,128)(2,1)S(1)}, bf16[1024,576]{0,1:T(8,128)(2,1)}, u32[]{:S(2)}) copy-start(bf16[1024,576]{0,1:T(8,128)(2,1)} %param.13) | copy-start | bytes 3538948
  22.9 7.3 %copy-start.41 = (s32[8]{0:T(128)S(1)}, s32[8]{0:T(128)}, u32[]{:S(2)}) copy-start(s32[8]{0:T(128)} %param.19) | copy-start | bytes 100
  25.4 25.8 %collective-permute-start.6 = (bf16[576,768]{1,0:T(8,128)(2,1)}, bf16[576,768]{1,0:T(8,128)(2,1)}, u32[]{:S(2)}, u32[]{:S(2)}) collective-permute-start(bf16[576,768]{1,0:T(8,128)(2,1)} %get-tuple-element.36), channel_id=1, source_target_pairs={{0,4},{4,0},{8,12},{12,8},{16,20},{20,16},{24,28},{28,24},{1,5},{5... | collective-permute-start | bytes 2654216 | tf_op jit(solution)/shard_map/ppermute | solution.py:348
  26.9 24.3 %collective-permute-start.5 = (bf16[576,256]{1,0:T(8,128)(2,1)}, bf16[576,256]{1,0:T(8,128)(2,1)S(1)}, u32[]{:S(2)}, u32[]{:S(2)}) collective-permute-start(bf16[576,256]{1,0:T(8,128)(2,1)} %slice.8), channel_id=1, source_target_pairs={{0,4},{4,0},{8,12},{12,8},{16,20},{20,16},{24,28},{28,24},{1,5},{5... | collective-permute-start | bytes 884744 | tf_op jit(solution)/shard_map/ppermute | solution.py:348
  28.2 40.1 %collective-permute-start.2 = (bf16[576,256]{1,0:T(8,128)(2,1)}, bf16[576,256]{1,0:T(8,128)(2,1)}, u32[]{:S(2)}, u32[]{:S(2)}) collective-permute-start(bf16[576,256]{1,0:T(8,128)(2,1)} %slice.8), channel_id=1, source_target_pairs={{0,16},{4,20},{8,24},{12,28},{16,0},{20,4},{24,8},{28,12},{1,17},{... | collective-permute-start | bytes 884744 | tf_op jit(solution)/shard_map/ppermute | solution.py:348
  28.9 41.4 %collective-permute-start.1 = (bf16[640,640]{1,0:T(8,128)(2,1)S(1)}, bf16[640,640]{1,0:T(8,128)(2,1)S(1)}, u32[]{:S(2)}, u32[]{:S(2)}) collective-permute-start(bf16[640,640]{1,0:T(8,128)(2,1)S(1)} %get-tuple-element.32.refs_1_), channel_id=1, source_target_pairs={{0,8},{4,12},{8,0},{12,4},{16,24},{20,28},{24,16},{28,20},{1,9},{5... | collective-permute-start | bytes 2457608 | tf_op jit(solution)/shard_map/ppermute | solution.py:348
  30.3 34.2 %collective-permute-start.4 = (bf16[576,384]{1,0:T(8,128)(2,1)}, bf16[576,384]{1,0:T(8,128)(2,1)S(1)}, u32[]{:S(2)}, u32[]{:S(2)}) collective-permute-start(bf16[576,384]{1,0:T(8,128)(2,1)} %get-tuple-element.35), channel_id=1, source_target_pairs={{0,16},{4,20},{8,24},{12,28},{16,0},{20,4},{24,8},{28,12},{1,17},{... | collective-permute-start | bytes 1327112 | tf_op jit(solution)/shard_map/ppermute | solution.py:348
  33.5 28.5 %copy-start.36 = (s32[4]{0:T(128)}, s32[4]{0:T(128)S(1)}, u32[]{:S(2)}) copy-start(s32[4]{0:T(128)S(1)} %select_reduce_fusion.refs_0_) | copy-start | bytes 52
  51.2 10.8 %copy-start.25 = (bf16[576,256]{1,0:T(8,128)(2,1)}, bf16[576,256]{1,0:T(8,128)(2,1)S(1)}, u32[]{:S(2)}) copy-start(bf16[576,256]{1,0:T(8,128)(2,1)S(1)} %collective-permute-done.5.refs_3_) | copy-start | bytes 884740
  65.3 20.7 %collective-permute-start.7 = (bf16[576,384]{1,0:T(8,128)(2,1)}, bf16[576,384]{1,0:T(8,128)(2,1)}, u32[]{:S(2)}, u32[]{:S(2)}) collective-permute-start(bf16[576,384]{1,0:T(8,128)(2,1)} %after.4.refs_4_), channel_id=1, source_target_pairs={{0,4},{4,0},{8,12},{12,8},{16,20},{20,16},{24,28},{28,24},{1,5},{5... | collective-permute-start | bytes 1327112 | tf_op jit(solution)/shard_map/ppermute | solution.py:348
  66.4 18.6 %collective-permute-start.9 = (bf16[576,256]{1,0:T(8,128)(2,1)}, bf16[576,256]{1,0:T(8,128)(2,1)S(1)}, u32[]{:S(2)}, u32[]{:S(2)}) collective-permute-start(bf16[576,256]{1,0:T(8,128)(2,1)} %get-tuple-element.45), channel_id=1, source_target_pairs={{0,16},{4,20},{8,24},{12,28},{16,0},{20,4},{24,8},{28,12},{1,17},{... | collective-permute-start | bytes 884744 | tf_op jit(solution)/shard_map/ppermute | solution.py:348
  68.3 17.6 %collective-permute-start.3 = (bf16[576,256]{1,0:T(8,128)(2,1)}, bf16[576,256]{1,0:T(8,128)(2,1)}, u32[]{:S(2)}, u32[]{:S(2)}) collective-permute-start(bf16[576,256]{1,0:T(8,128)(2,1)} %collective-permute-done.2.refs_2_), channel_id=1, source_target_pairs={{0,4},{4,0},{8,12},{12,8},{16,20},{20,16},{24,28},{28,24},{1,5},{5... | collective-permute-start | bytes 884744 | tf_op jit(solution)/shard_map/ppermute | solution.py:348
  69.8 16.2 %copy-start.38 = (s32[4]{0:T(128)S(1)}, s32[4]{0:T(128)}, u32[]{:S(2)}) copy-start(s32[4]{0:T(128)} %copy-done.36) | copy-start | bytes 52
  69.8 16.2 %copy-start.2 = (bf16[576,384]{1,0:T(8,128)(2,1)S(1)}, bf16[576,384]{1,0:T(8,128)(2,1)}, u32[]{:S(2)}) copy-start(bf16[576,384]{1,0:T(8,128)(2,1)} %after.4.refs_4_) | copy-start | bytes 1327108
  69.8 16.2 %copy-start.12 = (f32[640,128]{1,0:T(8,128)S(1)}, f32[640,128]{1,0:T(8,128)}, u32[]{:S(2)}) copy-start(f32[640,128]{1,0:T(8,128)} %copy-done.11) | copy-start | bytes 983044
  69.8 32.0 %collective-permute-start = (bf16[576,128]{1,0:T(8,128)(2,1)}, bf16[576,128]{1,0:T(8,128)(2,1)S(1)}, u32[]{:S(2)}, u32[]{:S(2)}) collective-permute-start(bf16[576,128]{1,0:T(8,128)(2,1)} %get-tuple-element.34), channel_id=1, source_target_pairs={{0,16},{4,20},{8,24},{12,28},{16,0},{20,4},{24,8},{28,12},{1,17},{... | collective-permute-start | bytes 442376 | tf_op jit(solution)/shard_map/ppermute | solution.py:348
  85.7 18.5 %collective-permute-start.10 = (bf16[576,256]{1,0:T(8,128)(2,1)}, bf16[576,256]{1,0:T(8,128)(2,1)}, u32[]{:S(2)}, u32[]{:S(2)}) collective-permute-start(bf16[576,256]{1,0:T(8,128)(2,1)} %after.7.refs_2_), channel_id=1, source_target_pairs={{0,4},{4,0},{8,12},{12,8},{16,20},{20,16},{24,28},{28,24},{1,5},{5... | collective-permute-start | bytes 884744 | tf_op jit(solution)/shard_map/ppermute | solution.py:348
  88.3 6.8 %copy-start.10 = (f32[640,128]{1,0:T(8,128)S(1)}, f32[640,128]{1,0:T(8,128)}, u32[]{:S(2)}) copy-start(f32[640,128]{1,0:T(8,128)} %copy-done.9) | copy-start | bytes 983044
  88.3 6.8 %copy-start.16 = (f32[640,512]{1,0:T(8,128)S(1)}, f32[640,512]{1,0:T(8,128)}, u32[]{:S(2)}) copy-start(f32[640,512]{1,0:T(8,128)} %copy-done.15) | copy-start | bytes 3932164
  88.3 6.8 %copy-start.32 = (f32[640,128]{1,0:T(8,128)S(1)}, f32[640,128]{1,0:T(8,128)}, u32[]{:S(2)}) copy-start(f32[640,128]{1,0:T(8,128)} %copy-done.31) | copy-start | bytes 983044
  95.0 4.9 %copy-start.21 = (f32[640,128]{1,0:T(8,128)}, f32[640,128]{1,0:T(8,128)S(1)}, u32[]{:S(2)}) copy-start(f32[640,128]{1,0:T(8,128)S(1)} %get-tuple-element.44.token_ref.refs_5_) | copy-start | bytes 983044
  101.8 2.4 %copy-start.4 = (bf16[576,256]{1,0:T(8,128)(2,1)S(1)}, bf16[576,256]{1,0:T(8,128)(2,1)}, u32[]{:S(2)}) copy-start(bf16[576,256]{1,0:T(8,128)(2,1)} %after.7.refs_2_) | copy-start | bytes 884740
  101.8 2.4 %copy-start.24 = (f32[640,128]{1,0:T(8,128)S(1)}, f32[640,128]{1,0:T(8,128)}, u32[]{:S(2)}) copy-start(f32[640,128]{1,0:T(8,128)} %copy-done.23) | copy-start | bytes 983044
  102.5 8.2 %collective-permute-start.8 = (bf16[576,128]{1,0:T(8,128)(2,1)}, bf16[576,128]{1,0:T(8,128)(2,1)S(1)}, u32[]{:S(2)}, u32[]{:S(2)}) collective-permute-start(bf16[576,128]{1,0:T(8,128)(2,1)} %after.6.refs_4_), channel_id=1, source_target_pairs={{0,4},{4,0},{8,12},{12,8},{16,20},{20,16},{24,28},{28,24},{1,5},{5... | collective-permute-start | bytes 442376 | tf_op jit(solution)/shard_map/ppermute | solution.py:348
  110.7 3.0 %copy-start.39 = (s32[32]{0:T(128)S(1)}, s32[32]{0:T(128)}, u32[]{:S(2)}) copy-start(s32[32]{0:T(128)} %param.18) | copy-start | bytes 388
  110.7 3.0 %copy-start.40 = (s32[32]{0:T(128)S(1)}, s32[32]{0:T(128)}, u32[]{:S(2)}) copy-start(s32[32]{0:T(128)} %param.17) | copy-start | bytes 388
  113.6 2.7 %copy-start.18 = (f32[640,512]{1,0:T(8,128)S(1)}, f32[640,512]{1,0:T(8,128)}, u32[]{:S(2)}) copy-start(f32[640,512]{1,0:T(8,128)} %copy-done.17) | copy-start | bytes 3932164
  113.6 2.7 %copy-start.22 = (f32[640,128]{1,0:T(8,128)S(1)}, f32[640,128]{1,0:T(8,128)}, u32[]{:S(2)}) copy-start(f32[640,128]{1,0:T(8,128)} %copy-done.21) | copy-start | bytes 983044
  113.6 2.7 %copy-start.34 = (f32[640,128]{1,0:T(8,128)S(1)}, f32[640,128]{1,0:T(8,128)}, u32[]{:S(2)}) copy-start(f32[640,128]{1,0:T(8,128)} %copy-done.33) | copy-start | bytes 983044
  113.6 14.9 %collective-permute-start.11 = (bf16[656,512]{1,0:T(8,128)(2,1)S(1)}, bf16[656,512]{1,0:T(8,128)(2,1)S(1)}, u32[]{:S(2)}, u32[]{:S(2)}) collective-permute-start(bf16[656,512]{1,0:T(8,128)(2,1)S(1)} %attend.15), channel_id=1, source_target_pairs={{0,8},{4,12},{8,0},{12,4},{16,24},{20,28},{24,16},{28,20},{1,9},{5... | collective-permute-start | bytes 2015240 | tf_op jit(solution)/shard_map/ppermute | solution.py:348
  120.3 8.2 %copy-start.8 = (bf16[16,512,128]{2,1,0:T(8,128)(2,1)S(1)}, bf16[16,512,128]{2,1,0:T(8,128)(2,1)}, u32[]{:S(2)}) copy-start(bf16[16,512,128]{2,1,0:T(8,128)(2,1)} %w_ref.3) | copy-start | bytes 6291460
  (22 other events, 19.4 us)

commit v4 on v3

v4 whole, which is shorter than its diff:
```python
import functools

import jax
import jax.numpy as jnp
from jax import lax
from jax.experimental import pallas as pl
from jax.experimental.pallas import tpu as pltpu
from jax.sharding import PartitionSpec as P

DN = 128
DC = 512
LANES = 128
ANY = pl.BlockSpec(memory_space=pl.ANY)
WHOLE = pl.BlockSpec(memory_space=pltpu.VMEM)


def room(mebibytes):
    return pltpu.CompilerParams(vmem_limit_bytes=mebibytes * 1024 * 1024)

score_scale = 0.1353
LOG2E = 1.4426950408889634
HIDDEN = -1e30
FLOOR = -1e25


def lanes(x, width):
    return jnp.concatenate([x] * (width // LANES), axis=1) if width > LANES else x


def attend_kernel(pieces, extra, first, last, tile, *refs):
    refs = list(refs)
    fills = refs.pop(0)
    q_ref = refs.pop(0)
    keys = [refs.pop(0) for _ in pieces]
    if extra:
        new_ref = refs.pop(0)
        bias_ref = refs.pop(0)
    if not first:
        m_in, l_in, acc_in = refs.pop(0), refs.pop(0), refs.pop(0)
    scale = score_scale * LOG2E
    weights = []
    for at in range(0, q_ref.shape[0], tile):
        rows = slice(at, at + tile)
        q = q_ref[rows, : keys[0].shape[0]]
        scores = []
        for (start, width, which), ref in zip(pieces, keys):
            s = jnp.dot(q, ref[...], preferred_element_type=jnp.float32)
            slot = start + lax.broadcasted_iota(jnp.int32, (1, width), 1)
            scores.append(jnp.where(slot < fills[which], s, HIDDEN))
        if extra:
            s = lax.dot_general(
                q, new_ref[...], (((1,), (1,)), ((), ())), preferred_element_type=jnp.float32
            )
            bias = bias_ref[...]
            scores.append(s + jnp.concatenate([bias] * (tile // bias.shape[0]), axis=0))
        peak = functools.reduce(jnp.maximum, [jnp.max(s, axis=1, keepdims=True) for s in scores])
        peak = jnp.maximum(peak, FLOOR)
        if not first:
            old = m_in[rows, :1]
            peak = jnp.maximum(peak, old)
        total = 0.0
        acc = 0.0
        for i, s in enumerate(scores):
            e = jnp.exp2((s - peak) * scale)
            total = total + jnp.sum(e, axis=1, keepdims=True)
            w = e.astype(jnp.bfloat16)
            if i < len(pieces):
                acc = acc + lax.dot_general(
                    w, keys[i][:DC, :], (((1,), (1,)), ((), ())), preferred_element_type=jnp.float32
                )
            else:
                acc = acc + jnp.dot(w, new_ref[:, :DC], preferred_element_type=jnp.float32)
        if not first:
            keep = jnp.exp2((old - peak) * scale)
            total = total + l_in[rows, :1] * keep
            acc = acc + acc_in[rows, :] * keep
        if last:
            refs[0][rows, :] = (acc * (1.0 / total)).astype(jnp.bfloat16)
            weights.append(jnp.broadcast_to(peak * scale + jnp.log2(total), (tile, LANES)))
        else:
            m_out, l_out, acc_out = refs
            m_out[rows, :] = jnp.broadcast_to(peak, (tile, LANES))
            l_out[rows, :] = jnp.broadcast_to(total, (tile, LANES))
            acc_out[rows, :] = acc
    if not last:
        return
    out = refs[0]
    count = q_ref.shape[0]
    weight = jnp.concatenate(weights, axis=0)
    tail = out.shape[0] - count
    place = lax.broadcasted_iota(jnp.int32, (tail, LANES), 0)
    packed = jnp.zeros((tail, LANES), jnp.float32)
    for g in range(count // LANES):
        turned = jnp.transpose(weight[g * LANES : (g + 1) * LANES, :])
        packed = jnp.where(place == g, turned[:tail, :], packed)
    high = packed.astype(jnp.bfloat16)
    rest = packed - high.astype(jnp.float32)
    mid = rest.astype(jnp.bfloat16)
    low = (rest - mid.astype(jnp.float32)).astype(jnp.bfloat16)
    out[count:, :] = jnp.concatenate([high, mid, low, jnp.zeros_like(low)], axis=1)


def attend(fills, q, pieces, tile, new=None, state=None, last=False):
    rows = q.shape[0]
    spec = tuple((start, keys.shape[1], which) for start, which, keys in pieces)
    operands = [fills, q] + [keys for _, _, keys in pieces]
    if new is not None:
        operands += list(new)
    aliases = {}
    if state is not None:
        if not last:
            aliases = {len(operands) + i: i for i in range(3)}
        operands += list(state)
    if last:
        tail = -(-rows // (LANES * 16)) * 16
        out_shape = [jax.ShapeDtypeStruct((rows + tail, DC), jnp.bfloat16)]
    else:
        out_shape = [
            jax.ShapeDtypeStruct((rows, LANES), jnp.float32),
            jax.ShapeDtypeStruct((rows, LANES), jnp.float32),
            jax.ShapeDtypeStruct((rows, DC), jnp.float32),
        ]
    out = pl.pallas_call(
        functools.partial(attend_kernel, spec, new is not None, state is None, last, tile),
        in_specs=[pl.BlockSpec(memory_space=pltpu.SMEM)] + [WHOLE] * (len(operands) - 1),
        out_specs=[WHOLE] * len(out_shape),
        out_shape=out_shape,
        input_output_aliases=aliases,
        compiler_params=room(24),
        cost_estimate=pl.CostEstimate(flops=0, bytes_accessed=0, transcendentals=0),
        name="attend",
    )(*operands)
    return out[0] if last else out


def after_kernel(x_ref, *refs):
    pass


def after(x, *tokens):
    return pl.pallas_call(
        after_kernel,
        in_specs=[ANY] * (1 + len(tokens)),
        out_specs=ANY,
        out_shape=jax.ShapeDtypeStruct(x.shape, x.dtype),
        input_output_aliases={0: 0},
        compiler_params=room(1),
        name="after",
    )(x, *tokens)


def pack_kernel(n, me_ref, query_ref, dec_ref, span_kv_ref, dec_kv_ref, *out_refs):
    per, row = span_kv_ref.shape
    per_dec = dec_ref.shape[0]
    part = query_ref.shape[1] // n
    cut = part // per
    pad = -(-row // LANES) * LANES - row

    def padded(ref):
        x = ref[...].astype(jnp.float32)
        return jnp.concatenate([x, jnp.zeros((x.shape[0], pad), jnp.float32)], axis=1)

    dec_kv = padded(dec_kv_ref)
    tail = [padded(span_kv_ref)]
    for e in range(per_dec):
        for j in range(0, row + pad, per * LANES):
            ends = range(j, min(j + per * LANES, row + pad), LANES)
            strips = [dec_kv[e : e + 1, k : k + LANES] for k in ends]
            strips += [jnp.zeros((1, LANES), jnp.float32)] * (per - len(strips))
            tail.append(jnp.concatenate(strips, axis=0))
    tail = jnp.concatenate(tail, axis=1).astype(jnp.bfloat16)
    for r, out_ref in enumerate(out_refs):
        begin = (me_ref[0] ^ r) * part
        out_ref[:, :part] = query_ref[:, pl.ds(pl.multiple_of(begin, LANES), part)]
        for e in range(per_dec):
            strips = []
            for i in range(per):
                at = pl.multiple_of(begin + i * cut, LANES)
                strips.append(dec_ref[e : e + 1, pl.ds(at, cut)].astype(jnp.float32))
            at = part + e * cut
            out_ref[:, at : at + cut] = jnp.concatenate(strips, axis=0).astype(jnp.bfloat16)
        out_ref[:, part + per_dec * cut :] = tail


def pack(n, me, query, dec_query, span_kv, dec_kv):
    per, row = span_kv.shape
    per_dec = dec_kv.shape[0]
    part = query.shape[1] // n
    wide = -(-row // LANES) * LANES
    fold = -(-wide // (per * LANES)) * LANES
    total = part + per_dec * (part // per) + wide + per_dec * fold
    operands = (query, dec_query, span_kv, dec_kv)
    return pl.pallas_call(
        functools.partial(pack_kernel, n),
        grid=(1,),
        in_specs=[pl.BlockSpec(memory_space=pltpu.SMEM)]
        + [pl.BlockSpec(x.shape, lambda i: (0, 0)) for x in operands],
        out_specs=[pl.BlockSpec((per, total), lambda i: (0, 0))] * n,
        out_shape=[jax.ShapeDtypeStruct((per, total), jnp.bfloat16)] * n,
        compiler_params=room(60),
        name="pack",
    )(me, *operands)


def absorb_kernel(per_dec, n, me_ref, w_ref, *refs):
    got_refs, absorbed_ref, extra_ref, placed = refs[:n], refs[n], refs[n + 1], refs[n + 2]
    heads = w_ref.shape[0]
    per = got_refs[0].shape[0]
    row = extra_ref.shape[1]
    count = absorbed_ref.shape[0] // heads
    wide = -(-row // LANES) * LANES
    fold = -(-wide // (per * LANES)) * LANES
    part = (got_refs[0].shape[1] - wide - per_dec * fold) * per // (per + per_dec)
    width = part // heads
    cut = part // per
    at = part + per_dec * cut
    for r, ref in enumerate(got_refs):
        placed[me_ref[0] ^ r] = ref[...].astype(jnp.float32)

    def unfold(x, length):
        strips = []
        for j in range(0, x.shape[1], length):
            strips += [x[i : i + 1, j : j + length] for i in range(per)]
        return jnp.concatenate(strips, axis=1)

    blocks = [placed[d] for d in range(n)]
    queries = [x[:, :part] for x in blocks]
    fresh = [x[:, at : at + wide] for x in blocks]
    for x in blocks:
        for e in range(per_dec):
            queries.append(unfold(x[:, part + e * cut : part + (e + 1) * cut], cut))
            begin = at + wide + e * fold
            fresh.append(unfold(x[:, begin : begin + fold], LANES)[:, :wide])
    q = jnp.concatenate(queries, axis=0).astype(jnp.bfloat16)
    new = jnp.concatenate(fresh, axis=0)
    blank = jnp.zeros((count, absorbed_ref.shape[1] - row), jnp.float32)
    for h in range(0, heads, 2):
        parts = []
        for g in (h, h + 1):
            mine = q[:, g * width : (g + 1) * width]
            latent = jnp.dot(mine[:, :DN], w_ref[g], preferred_element_type=jnp.float32)
            rope = mine[:, DN:].astype(jnp.float32)
            parts.append(jnp.concatenate([latent, rope, blank], axis=1))
        pair = jnp.concatenate(parts, axis=0).astype(jnp.bfloat16)
        absorbed_ref[h * count : (h + 2) * count, :] = pair
    blank = jnp.zeros((extra_ref.shape[0] - count, row), jnp.float32)
    extra_ref[...] = jnp.concatenate([new[:, :row], blank], axis=0).astype(jnp.bfloat16)


def absorb(count, per_dec, me, got, w_uk, row):
    heads = w_uk.shape[0]
    return pl.pallas_call(
        functools.partial(absorb_kernel, per_dec, len(got)),
        in_specs=[pl.BlockSpec(memory_space=pltpu.SMEM)] + [WHOLE] * (1 + len(got)),
        out_shape=(
            jax.ShapeDtypeStruct((heads * count, -(-row // LANES) * LANES), jnp.bfloat16),
            jax.ShapeDtypeStruct((LANES, row), jnp.bfloat16),
        ),
        scratch_shapes=[pltpu.VMEM((len(got), *got[0].shape), jnp.float32)],
        compiler_params=room(24),
        cost_estimate=pl.CostEstimate(
            flops=2 * count * heads * DN * DC,
            bytes_accessed=2 * w_uk.size,
            transcendentals=0,
        ),
        name="absorb",
    )(me, w_uk, *got)


def split_kernel(spans, x_ref, *refs):
    for (a, b), ref in zip(spans, refs[-len(spans) :]):
        ref[...] = x_ref[:, a:b]


def split(x, spans, tokens):
    return pl.pallas_call(
        functools.partial(split_kernel, spans),
        grid=(1,),
        in_specs=[pl.BlockSpec(x.shape, lambda i: (0, 0))] + [ANY] * len(tokens),
        out_specs=[pl.BlockSpec((x.shape[0], b - a), lambda i: (0, 0)) for a, b in spans],
        out_shape=[jax.ShapeDtypeStruct((x.shape[0], b - a), x.dtype) for a, b in spans],
        compiler_params=room(16),
        name="split",
    )(x, *tokens)


def finish_kernel(count, m_ref, l_ref, acc_ref, far_ref, w_ref, span_ref, dec_ref):
    rows = m_ref.shape[0]
    heads = w_ref.shape[0]
    scale = score_scale * LOG2E
    parts = far_ref[rows:, :].astype(jnp.float32)
    packed = parts[:, :LANES] + parts[:, LANES : 2 * LANES] + parts[:, 2 * LANES : 3 * LANES]
    columns = []
    for g in range(rows // LANES):
        row = jnp.broadcast_to(packed[g : g + 1, :], (LANES, LANES))
        columns.append(jnp.transpose(row))
    far = jnp.concatenate(columns, axis=0)
    near = m_ref[...] * scale
    top = jnp.maximum(near, far)
    w_near = jnp.exp2(near - top)
    w_far = jnp.exp2(far - top)
    total = l_ref[...] * w_near + w_far
    inverse = 1.0 / total
    w_near = lanes(w_near * inverse, DC)
    w_far = lanes(w_far * inverse, DC)
    for h in range(heads):
        a, b = h * count, (h + 1) * count
        near_part = acc_ref[a:b, :] * w_near[a:b, :]
        far_part = far_ref[:rows, :].astype(jnp.float32)[a:b, :] * w_far[a:b, :]
        latent = (near_part + far_part).astype(jnp.bfloat16)
        done = jnp.dot(latent, w_ref[h], preferred_element_type=jnp.float32)
        span = span_ref.shape[0]
        span_ref[:, h * LANES : (h + 1) * LANES] = done[:span].astype(jnp.bfloat16)
        dec_ref[:, h * LANES : (h + 1) * LANES] = done[span:].astype(jnp.bfloat16)


def finish(count, span, state, far, w_uv):
    heads = w_uv.shape[0]
    wide = heads * w_uv.shape[2]
    return pl.pallas_call(
        functools.partial(finish_kernel, count),
        out_shape=(
            jax.ShapeDtypeStruct((span, wide), jnp.bfloat16),
            jax.ShapeDtypeStruct((count - span, wide), jnp.bfloat16),
        ),
        compiler_params=room(24),
        cost_estimate=pl.CostEstimate(
            flops=2 * count * heads * DC * w_uv.shape[2],
            bytes_accessed=2 * w_uv.size + 6 * state[2].size,
            transcendentals=0,
        ),
        name="finish",
    )(*state, far, w_uv)


def body(query, dec_query, cache_kv, span_kv, dec_kv, cache_fill, owner, slot, dec_len, w_uk, w_uv):
    me = lax.axis_index("seq")
    n = lax.axis_size("seq")
    pos_dev = cache_kv.shape[0]
    span = owner.shape[0]
    rows_dec = dec_len.shape[0]
    count = span + rows_dec
    heads = w_uk.shape[0]
    row = cache_kv.shape[1]

    def swap(x, stride):
        return lax.ppermute(x, "seq", [(i, i ^ stride) for i in range(n)])

    far, pair = n // 2, n // 4
    near = [1 << b for b in range(pair.bit_length() - 1)]
    keys = cache_kv.T
    edges = [0, pos_dev // 2, pos_dev // 8 * 7, pos_dev]

    place = me[None].astype(jnp.int32)
    mine = pack(n, place, query, dec_query, span_kv, dec_kv)
    got = [mine[0]] + [swap(x, r) for r, x in enumerate(mine) if r]
    absorbed, extra = absorb(count, rows_dec // n, place, got, w_uk, row)
    new_rows = extra[:span]
    other = swap(absorbed, pair)

    *cuts, copy = split(keys, [*zip(edges, edges[1:]), (0, pos_dev)], got[1:])
    blocks = [(0, copy)]
    for stride in near:
        blocks += [(offset ^ stride, swap(x, stride)) for offset, x in blocks]
    pieces = [swap(cuts[0], far)]

    def spread(x):
        part = [(far, x)]
        for stride in near:
            part += [(offset ^ stride, swap(y, stride)) for offset, y in part]
        return part

    target = jnp.where(owner == me, slot, -1)
    onehot = jnp.arange(pos_dev, dtype=jnp.int32)[None, :] == target[:, None]
    placed = lax.dot_general(
        new_rows,
        onehot.astype(jnp.bfloat16),
        (((0,), (0,)), ((), ())),
        preferred_element_type=jnp.float32,
    ).astype(jnp.bfloat16)
    new_cache = jnp.where(jnp.any(onehot, axis=0)[None, :], placed, keys).T

    limits = jnp.concatenate([jnp.arange(1, span + 1, dtype=jnp.int32), dec_len])
    index = jnp.arange(LANES, dtype=jnp.int32)
    queries = jnp.arange(count, dtype=jnp.int32)
    seen = (index[None, :] < span) & (index[None, :] < limits[:, None])
    seen |= (index[None, :] >= span) & (index[None, :] == queries[:, None])
    bias = jnp.where(seen, 0.0, HIDDEN).astype(jnp.float32)
    held = [offset for offset, _ in blocks]
    offsets = held + [offset ^ far for offset in held]
    which = jnp.stack([me ^ offset for offset in offsets])
    fills = jnp.sum(
        jnp.where(which[:, None] == jnp.arange(n, dtype=jnp.int32)[None, :], cache_fill[None, :], 0),
        axis=1,
    )
    base = len(blocks)
    tile = heads // 2 * count

    def stage_of(c, part):
        return [(edges[c], base + i, x) for i, (_, x) in enumerate(part)]

    home = [(0, 0, keys)]
    side = [(0, i, x) for i, (_, x) in enumerate(blocks) if i]
    state = attend(fills, absorbed, home, tile, new=(extra, bias))
    pieces.append(swap(after(cuts[1], state[0], pieces[0]), far))
    first = stage_of(0, spread(after(pieces[0], state[0])))
    state = attend(fills, absorbed, side, tile, state=state)
    other = after(other, state[0])
    guest = attend(fills, other, home + side, tile)
    pieces.append(swap(after(cuts[2], guest[0], pieces[1]), far))
    second = stage_of(1, spread(after(pieces[1], guest[0])))
    guest = attend(fills, other, first, tile, state=guest)
    state = attend(fills, absorbed, first, tile, state=state)
    third = stage_of(2, spread(after(pieces[2], guest[0], state[0])))
    second, third = second + third[:1], third[1:]
    guest = attend(fills, other, second, tile, state=guest)
    sent = attend(fills, other, third, tile, state=guest, last=True)
    back = swap(sent, pair)
    state = attend(fills, absorbed, second + third, tile, state=state)
    span_out, dec_out = finish(count, span, state, back, w_uv)
    return (span_out, dec_out, new_cache)


def solution(mesh):
    in_specs = (
        P(("grp", "seq"), None),
        P(("grp", "seq"), None),
        P(("grp", "seq"), None),
        P(("grp", "seq"), None),
        P(("grp", "seq"), None),
        P("grp"),
        P("grp"),
        P("grp"),
        P("grp"),
        P("seq", None, None),
        P("seq", None, None),
    )
    out_specs = (P("grp", "seq"), P("grp", "seq"), P(("grp", "seq"), None))
    return jax.shard_map(body, mesh=mesh, in_specs=in_specs, out_specs=out_specs, check_vma=False)
```

time: 131 us -> 107 us (0.82)
  blocking collectives: 17.7 us -> 0 us
  waiting for transfers between devices: 28.4 us -> 44.5 us
  local copies, waits for them, and re-layouts: 21.8 us -> 6.65 us
  Pallas kernels: 44 us -> 33.6 us
  starting transfers between devices: 12.7 us -> 17.5 us
    all_to_all x1 -> x0, blocking collectives: 17.7 us -> none  [body(): got = lax.all_to_all(mine, 'seq', split_axis=0, concat_axis=0, tiled=True)]
    ppermute x12 -> x16, waiting for transfers between devices: 28.4 us -> 44.5 us  [swap(): return lax.ppermute(x, 'seq', [(i, i ^ stride) for i in range(n)])]
    unnamed x84 -> x34, local copies, waits for them, and re-layouts: 21 us -> 6.65 us
    pallas_call x8, Pallas kernels: 38 us -> 28.7 us  [attend(): pl.pallas_call(functools.partial(attend_kernel, spec, new is not None, st...]
    ppermute x12 -> x16, starting transfers between devices: 12.7 us -> 17.5 us  [swap(): return lax.ppermute(x, 'seq', [(i, i ^ stride) for i in range(n)])]
  transfers between devices with their start and end apart: 12 -> 16, of which waited for: 3 -> 9; matrix products, arithmetic and copies ran while one was open for 4% -> 3% of each run, Pallas kernels for 27% -> 26%
where the time goes in v4:
time: 107 us; the launch traced here: 106 us
  waiting for transfers between devices  44.5 us (42%)
  Pallas kernels  33.6 us (31%)
  starting transfers between devices  17.5 us (16%)
  local copies, waits for them, and re-layouts  6.65 us (6%)
  other arithmetic  1.69 us (2%)
  matrix products  1.55 us (1%)
    ppermute x16, waiting for transfers between devices, swap(): return lax.ppermute(x, 'seq', [(i, i ^ stride) for i in range(n)])  44.5 us
    pallas_call x8, Pallas kernels, attend(): pl.pallas_call(functools.partial(attend_kernel, spec, new is not None, st...  28.7 us
    ppermute x16, starting transfers between devices, swap(): return lax.ppermute(x, 'seq', [(i, i ^ stride) for i in range(n)])  17.5 us
    unnamed x34, local copies, waits for them, and re-layouts  6.65 us
  transfers between devices with their start and end apart: 16, of which 9 were waited for; matrix products, arithmetic and copies ran while one was open for 3% of the time, Pallas kernels for 26%

profile of v4, /device:TPU:0, one launch (start us, length us, event | category | flops | bytes accessed | tf_op | source)
XLA Modules:
  0.0 106.3 jit_solution(9904687203685327046)
XLA Ops:
  0.6 1.8 %pack.1 = (bf16[4,4736]{1,0:T(4,128)(2,1)}, bf16[4,4736]{1,0:T(4,128)(2,1)}, bf16[4,4736]{1,0:T(4,128)(2,1)}, bf16[4,4736]{1,0:T(4,128)(2,1)}, bf16[4,4736]{1,0:...) custom-call(s32[1]{0:T(128)} %bitcast.me_ref, ...), custom_call_target="tpu_custom_call" | custom-call | tf_op jit(solution)/shard_map/pack/pallas_call | solution.py:193
  2.4 3.0 %collective-permute-start = (bf16[4,4736]{1,0:T(4,128)(2,1)}, bf16[4,4736]{1,0:T(4,128)(2,1)S(1)}, u32[]{:S(2)}, u32[]{:S(2)}) collective-permute-start(bf16[4,4736]{1,0:T(4,128)(2,1)} %get-tuple-element.41), channel_id=1, source_target_pairs={{0,4},{4,0},{8,12},{12,8},{16,20},{20,16},{24,28},{28,24},{1,5},{5... | collective-permute-start | bytes 113672 | tf_op jit(solution)/shard_map/ppermute | solution.py:347
  5.4 1.6 %collective-permute-start.1 = (bf16[4,4736]{1,0:T(4,128)(2,1)}, bf16[4,4736]{1,0:T(4,128)(2,1)S(1)}, u32[]{:S(2)}, u32[]{:S(2)}) collective-permute-start(bf16[4,4736]{1,0:T(4,128)(2,1)} %get-tuple-element.42), channel_id=1, source_target_pairs={{0,8},{4,12},{8,0},{12,4},{16,24},{20,28},{24,16},{28,20},{1,9},{5... | collective-permute-start | bytes 113672 | tf_op jit(solution)/shard_map/ppermute | solution.py:347
  6.9 3.0 %collective-permute-start.3 = (bf16[4,4736]{1,0:T(4,128)(2,1)}, bf16[4,4736]{1,0:T(4,128)(2,1)S(1)}, u32[]{:S(2)}, u32[]{:S(2)}) collective-permute-start(bf16[4,4736]{1,0:T(4,128)(2,1)} %get-tuple-element.44), channel_id=1, source_target_pairs={{0,16},{4,20},{8,24},{12,28},{16,0},{20,4},{24,8},{28,12},{1,17},{... | collective-permute-start | bytes 113672 | tf_op jit(solution)/shard_map/ppermute | solution.py:347
  9.9 1.3 %collective-permute-start.4 = (bf16[4,4736]{1,0:T(4,128)(2,1)}, bf16[4,4736]{1,0:T(4,128)(2,1)S(1)}, u32[]{:S(2)}, u32[]{:S(2)}) collective-permute-start(bf16[4,4736]{1,0:T(4,128)(2,1)} %get-tuple-element.45), channel_id=1, source_target_pairs={{0,20},{4,16},{8,28},{12,24},{16,4},{20,0},{24,12},{28,8},{1,21},{... | collective-permute-start | bytes 113672 | tf_op jit(solution)/shard_map/ppermute | solution.py:347
  11.2 3.6 %collective-permute-start.5 = (bf16[4,4736]{1,0:T(4,128)(2,1)}, bf16[4,4736]{1,0:T(4,128)(2,1)S(1)}, u32[]{:S(2)}, u32[]{:S(2)}) collective-permute-start(bf16[4,4736]{1,0:T(4,128)(2,1)} %get-tuple-element.46), channel_id=1, source_target_pairs={{0,24},{4,28},{8,16},{12,20},{16,8},{20,12},{24,0},{28,4},{1,25},{... | collective-permute-start | bytes 113672 | tf_op jit(solution)/shard_map/ppermute | solution.py:347
  14.9 1.3 %collective-permute-done.4.refs_5_.refs_4_ = bf16[4,4736]{1,0:T(4,128)(2,1)S(1)} collective-permute-done((bf16[4,4736]{1,0:T(4,128)(2,1)}, bf16[4,4736]{1,0:T(4,128)(2,1)S(1)}, u32[]{:S(2)}, u32[]{:S(2)}) %collective-permute-start.4) | collective-permute-done | bytes 37920 | tf_op jit(solution)/shard_map/ppermute | solution.py:347
  16.2 1.2 %collective-permute-done.5.refs_6_.refs_5_ = bf16[4,4736]{1,0:T(4,128)(2,1)S(1)} collective-permute-done((bf16[4,4736]{1,0:T(4,128)(2,1)}, bf16[4,4736]{1,0:T(4,128)(2,1)S(1)}, u32[]{:S(2)}, u32[]{:S(2)}) %collective-permute-start.5) | collective-permute-done | bytes 37920 | tf_op jit(solution)/shard_map/ppermute | solution.py:347
  17.4 4.3 %collective-permute-done.6.refs_7_.refs_6_ = bf16[4,4736]{1,0:T(4,128)(2,1)S(1)} collective-permute-done((bf16[4,4736]{1,0:T(4,128)(2,1)}, bf16[4,4736]{1,0:T(4,128)(2,1)S(1)}, u32[]{:S(2)}, u32[]{:S(2)}) %collective-permute-start.6) | collective-permute-done | bytes 37920 | tf_op jit(solution)/shard_map/ppermute | solution.py:347
  21.7 1.3 %copy-done = bf16[1024,576]{0,1:T(8,128)(2,1)S(1)} copy-done((bf16[1024,576]{0,1:T(8,128)(2,1)S(1)}, bf16[1024,576]{0,1:T(8,128)(2,1)}, u32[]{:S(2)}) %copy-start) | copy-done | bytes 1179672
  23.0 1.4 %split.1 = (bf16[576,512]{1,0:T(8,128)(2,1)}, bf16[576,384]{1,0:T(8,128)(2,1)S(1)}, bf16[576,128]{1,0:T(8,128)(2,1)S(1)}, bf16[576,1024]{1,0:T(8,128)(2,1)}) custom-call(bf16[576,1024]{1,0:T(8,128)(2,1)S(1)} %bitcast.5, bf16[4,4736]{1,0:T(4,128)(2,1)S(1)} %collective-permute-done.refs_1_.refs_0_, bf16[4,4736]{1,0:T(4,128)(2,1)S(1)} %collective-permute-done.1.refs_2_.refs_1_, ...), custom_call_target="tpu_custom_call" | custom-call | tf_op jit(solution)/shard_map/split/pallas_call | solution.py:276
  26.3 1.6 %copy-done.2 = bf16[16,128,512]{2,1,0:T(8,128)(2,1)S(1)} copy-done((bf16[16,128,512]{2,1,0:T(8,128)(2,1)S(1)}, bf16[16,128,512]{2,1,0:T(8,128)(2,1)}, u32[]{:S(2)}) %copy-start.2) | copy-done | bytes 2097176
  31.5 1.0 collective-permute-start.9
  33.5 3.5 %attend.8 = (f32[640,128]{1,0:T(8,128)S(1)}, f32[640,128]{1,0:T(8,128)S(1)}, f32[640,512]{1,0:T(8,128)S(1)}) custom-call(s32[4]{0:T(128)S(1)} %select_reduce_fusion.refs_0_, bf16[640,640]{1,0:T(8,128)(2,1)S(1)} %get-tuple-element.48.refs_1_, bf16[576,1024]{1,0:T(8,128)(2,1)S(1)} %bitcast.6, bf16[128,576]{1,0:T(8,128)(2,1)S(1)} %get-tuple-element.50.refs_3_, ...), custom_call_target="tpu_custom_call" | custom-call | tf_op jit(solution)/shard_map/attend/pallas_call | solution.py:123
  37.0 12.6 %collective-permute-done.7.refs_1_.x_ref = bf16[576,512]{1,0:T(8,128)(2,1)S(1)} collective-permute-done((bf16[576,512]{1,0:T(8,128)(2,1)}, bf16[576,512]{1,0:T(8,128)(2,1)S(1)}, u32[]{:S(2)}, u32[]{:S(2)}) %collective-permute-start.7) | collective-permute-done | bytes 589856 | tf_op jit(solution)/shard_map/ppermute | solution.py:347
  49.6 1.1 %collective-permute-start.13 = (bf16[576,512]{1,0:T(8,128)(2,1)S(1)}, bf16[576,512]{1,0:T(8,128)(2,1)S(1)}, u32[]{:S(2)}, u32[]{:S(2)}) collective-permute-start(bf16[576,512]{1,0:T(8,128)(2,1)S(1)} %after.10.refs_2_), channel_id=1, source_target_pairs={{0,4},{4,0},{8,12},{12,8},{16,20},{20,16},{24,28},{28,24},{1,5},{5... | collective-permute-start | bytes 1769480 | tf_op jit(solution)/shard_map/ppermute | solution.py:347
  50.8 3.5 %attend.9 = (f32[640,128]{1,0:T(8,128)S(1)}, f32[640,128]{1,0:T(8,128)S(1)}, f32[640,512]{1,0:T(8,128)S(1)}) custom-call(s32[4]{0:T(128)S(1)} %select_reduce_fusion.refs_0_, bf16[640,640]{1,0:T(8,128)(2,1)S(1)} %get-tuple-element.48.refs_1_, ...), custom_call_target="tpu_custom_call", output_to_operand_aliasing={{0}: (3, {}), {1}: (4, {}), {2}: (5, {})} | custom-call | tf_op jit(solution)/shard_map/attend/pallas_call | solution.py:123
  54.3 8.4 %collective-permute-done.9.x_ref = bf16[640,640]{1,0:T(8,128)(2,1)S(1)} collective-permute-done((bf16[640,640]{1,0:T(8,128)(2,1)S(1)}, bf16[640,640]{1,0:T(8,128)(2,1)S(1)}, u32[]{:S(2)}, u32[]{:S(2)}) %collective-permute-start.9) | collective-permute-done | bytes 819232 | tf_op jit(solution)/shard_map/ppermute | solution.py:347
  62.7 4.9 %attend.10 = (f32[640,128]{1,0:T(8,128)S(1)}, f32[640,128]{1,0:T(8,128)S(1)}, f32[640,512]{1,0:T(8,128)S(1)}) custom-call(s32[4]{0:T(128)S(1)} %select_reduce_fusion.refs_0_, bf16[640,640]{1,0:T(8,128)(2,1)S(1)} %after.7.refs_1_, bf16[576,1024]{1,0:T(8,128)(2,1)S(1)} %bitcast.7, bf16[576,1024]{1,0:T(8,128)(2,1)S(1)} %collective-permute-done.10.refs_2_.refs_3_), custom_call_target="tpu_custom_call" | custom-call | tf_op jit(solution)/shard_map/attend/pallas_call | solution.py:123
  67.6 4.2 %collective-permute-done.8.x_ref.refs_1_ = bf16[576,384]{1,0:T(8,128)(2,1)S(1)} collective-permute-done((bf16[576,384]{1,0:T(8,128)(2,1)S(1)}, bf16[576,384]{1,0:T(8,128)(2,1)S(1)}, u32[]{:S(2)}, u32[]{:S(2)}) %collective-permute-start.8) | collective-permute-done | bytes 442400 | tf_op jit(solution)/shard_map/ppermute | solution.py:347
  71.8 0.9 collective-permute-start.11
  72.8 3.5 %attend.12 = (f32[640,128]{1,0:T(8,128)S(1)}, f32[640,128]{1,0:T(8,128)S(1)}, f32[640,512]{1,0:T(8,128)S(1)}) custom-call(s32[4]{0:T(128)S(1)} %select_reduce_fusion.refs_0_, bf16[640,640]{1,0:T(8,128)(2,1)S(1)} %get-tuple-element.48.refs_1_, bf16[576,512]{1,0:T(8,128)(2,1)S(1)} %after.10.refs_2_, ...), custom_call_target="tpu_custom_call", output_to_operand_aliasing={{0}: (4, {}), {1}: (5, {}), {2}: (6, {})} | custom-call | tf_op jit(solution)/shard_map/attend/pallas_call | solution.py:123
  76.3 3.4 %attend.11 = (f32[640,128]{1,0:T(8,128)S(1)}, f32[640,128]{1,0:T(8,128)S(1)}, f32[640,512]{1,0:T(8,128)S(1)}) custom-call(s32[4]{0:T(128)S(1)} %select_reduce_fusion.refs_0_, bf16[640,640]{1,0:T(8,128)(2,1)S(1)} %after.7.refs_1_, bf16[576,512]{1,0:T(8,128)(2,1)S(1)} %after.10.refs_2_, ...), custom_call_target="tpu_custom_call", output_to_operand_aliasing={{0}: (4, {}), {1}: (5, {}), {2}: (6, {})} | custom-call | tf_op jit(solution)/shard_map/attend/pallas_call | solution.py:123
  79.7 1.0 collective-permute-done.12.x_ref
  80.7 1.3 %collective-permute-start.14 = (bf16[576,128]{1,0:T(8,128)(2,1)S(1)}, bf16[576,128]{1,0:T(8,128)(2,1)S(1)}, u32[]{:S(2)}, u32[]{:S(2)}) collective-permute-start(bf16[576,128]{1,0:T(8,128)(2,1)S(1)} %after.11.refs_4_), channel_id=1, source_target_pairs={{0,4},{4,0},{8,12},{12,8},{16,20},{20,16},{24,28},{28,24},{1,5},{5... | collective-permute-start | bytes 442376 | tf_op jit(solution)/shard_map/ppermute | solution.py:347
  82.0 1.8 %collective-permute-done.11.refs_3_ = bf16[576,384]{1,0:T(8,128)(2,1)S(1)} collective-permute-done((bf16[576,384]{1,0:T(8,128)(2,1)S(1)}, bf16[576,384]{1,0:T(8,128)(2,1)S(1)}, u32[]{:S(2)}, u32[]{:S(2)}) %collective-permute-start.11) | collective-permute-done | bytes 442400 | tf_op jit(solution)/shard_map/ppermute | solution.py:347
  83.8 3.9 %attend.14 = (f32[640,128]{1,0:T(8,128)S(1)}, f32[640,128]{1,0:T(8,128)S(1)}, f32[640,512]{1,0:T(8,128)S(1)}) custom-call(s32[4]{0:T(128)S(1)} %select_reduce_fusion.refs_0_, bf16[640,640]{1,0:T(8,128)(2,1)S(1)} %after.7.refs_1_, bf16[576,384]{1,0:T(8,128)(2,1)S(1)} %after.8.refs_2_, ...), custom_call_target="tpu_custom_call", output_to_operand_aliasing={{0}: (5, {}), {1}: (6, {}), {2}: (7, {})} | custom-call | tf_op jit(solution)/shard_map/attend/pallas_call | solution.py:123
  87.8 1.8 %attend.15 = bf16[656,512]{1,0:T(8,128)(2,1)S(1)} custom-call(s32[4]{0:T(128)S(1)} %select_reduce_fusion.refs_0_, bf16[640,640]{1,0:T(8,128)(2,1)S(1)} %after.7.refs_1_, bf16[576,128]{1,0:T(8,128)(2,1)S(1)} %collective-permute-done.14.refs_5_.refs_2_, f32[640,128]{1,0:T(8,128)S(1)} %get-tuple-element.72.refs_3_, f32[640,128]{1,0:T(8,128)S(1)} %get-tuple-element.73.refs_4_, ...), custom_call_target="tpu_custom_call" | custom-call | tf_op jit(solution)/shard_map/attend/pallas_call | solution.py:123
  89.8 1.5 %fusion = bf16[1024,576]{0,1:T(8,128)(2,1)} fusion(bf16[1024,576]{0,1:T(8,128)(2,1)S(1)} %copy-done.1, pred[1024]{0:T(1024)(128)(4,1)S(1)} %fusion.1, s32[32]{0:T(128)S(1)} %compare_select_fusion, bf16[128,576]{1,0:T(8,128)(2,1)S(1)} %get-tuple-element.50.refs_3_), kind=kOutput, calls=%fused_computation.1 | convolution fusion | flops 38961152 | bytes 2401792 | tf_op jit(solution)/shard_map/dot_general | solution.py:375
  91.4 4.1 %attend.13 = (f32[640,128]{1,0:T(8,128)S(1)}, f32[640,128]{1,0:T(8,128)S(1)}, f32[640,512]{1,0:T(8,128)S(1)}) custom-call(s32[4]{0:T(128)S(1)} %select_reduce_fusion.refs_0_, bf16[640,640]{1,0:T(8,128)(2,1)S(1)} %get-tuple-element.48.refs_1_, bf16[576,384]{1,0:T(8,128)(2,1)S(1)} %after.8.refs_2_, ...), custom_call_target="tpu_custom_call", output_to_operand_aliasing={{0}: (6, {}), {1}: (7, {}), {2}: (8, {})} | custom-call | tf_op jit(solution)/shard_map/attend/pallas_call | solution.py:123
  95.5 9.6 %collective-permute-done.15.far_ref = bf16[656,512]{1,0:T(8,128)(2,1)S(1)} collective-permute-done((bf16[656,512]{1,0:T(8,128)(2,1)S(1)}, bf16[656,512]{1,0:T(8,128)(2,1)S(1)}, u32[]{:S(2)}, u32[]{:S(2)}) %collective-permute-start.15) | collective-permute-done | bytes 671776 | tf_op jit(solution)/shard_map/ppermute | solution.py:347
  105.1 1.2 %finish.1 = (bf16[32,2048]{1,0:T(8,128)(2,1)}, bf16[8,2048]{1,0:T(8,128)(2,1)}) custom-call(f32[640,128]{1,0:T(8,128)S(1)} %get-tuple-element.67.m_ref, f32[640,128]{1,0:T(8,128)S(1)} %get-tuple-element.68.l_ref, f32[640,512]{1,0:T(8,128)S(1)} %get-tuple-element.69.acc_ref, bf16[656,512]{1,0:T(8,128)(2,1)S(1)} %collective-permute-done.15.far_ref, ...), custom_call_target="tpu_custom_call" | custom-call | flops 83886080 | bytes 4063232 | tf_op jit(solution)/shard_map/finish/pallas_call | solution.py:320
  (61 shorter events, 6.7 us)
Async XLA Ops:
  0.6 25.0 %copy-start.16 = (s32[8]{0:T(128)S(1)}, s32[8]{0:T(128)}, u32[]{:S(2)}) copy-start(s32[8]{0:T(128)} %param.19) | copy-start | bytes 100
  2.4 8.8 %collective-permute-start = (bf16[4,4736]{1,0:T(4,128)(2,1)}, bf16[4,4736]{1,0:T(4,128)(2,1)S(1)}, u32[]{:S(2)}, u32[]{:S(2)}) collective-permute-start(bf16[4,4736]{1,0:T(4,128)(2,1)} %get-tuple-element.41), channel_id=1, source_target_pairs={{0,4},{4,0},{8,12},{12,8},{16,20},{20,16},{24,28},{28,24},{1,5},{5... | collective-permute-start | bytes 113672 | tf_op jit(solution)/shard_map/ppermute | solution.py:347
  5.4 9.5 %collective-permute-start.1 = (bf16[4,4736]{1,0:T(4,128)(2,1)}, bf16[4,4736]{1,0:T(4,128)(2,1)S(1)}, u32[]{:S(2)}, u32[]{:S(2)}) collective-permute-start(bf16[4,4736]{1,0:T(4,128)(2,1)} %get-tuple-element.42), channel_id=1, source_target_pairs={{0,8},{4,12},{8,0},{12,4},{16,24},{20,28},{24,16},{28,20},{1,9},{5... | collective-permute-start | bytes 113672 | tf_op jit(solution)/shard_map/ppermute | solution.py:347
  6.9 7.9 %collective-permute-start.2 = (bf16[4,4736]{1,0:T(4,128)(2,1)}, bf16[4,4736]{1,0:T(4,128)(2,1)S(1)}, u32[]{:S(2)}, u32[]{:S(2)}) collective-permute-start(bf16[4,4736]{1,0:T(4,128)(2,1)} %get-tuple-element.43), channel_id=1, source_target_pairs={{0,12},{4,8},{8,4},{12,0},{16,28},{20,24},{24,20},{28,16},{1,13},{... | collective-permute-start | bytes 113672 | tf_op jit(solution)/shard_map/ppermute | solution.py:347
  6.9 7.9 %collective-permute-start.3 = (bf16[4,4736]{1,0:T(4,128)(2,1)}, bf16[4,4736]{1,0:T(4,128)(2,1)S(1)}, u32[]{:S(2)}, u32[]{:S(2)}) collective-permute-start(bf16[4,4736]{1,0:T(4,128)(2,1)} %get-tuple-element.44), channel_id=1, source_target_pairs={{0,16},{4,20},{8,24},{12,28},{16,0},{20,4},{24,8},{28,12},{1,17},{... | collective-permute-start | bytes 113672 | tf_op jit(solution)/shard_map/ppermute | solution.py:347
  9.9 6.2 %collective-permute-start.4 = (bf16[4,4736]{1,0:T(4,128)(2,1)}, bf16[4,4736]{1,0:T(4,128)(2,1)S(1)}, u32[]{:S(2)}, u32[]{:S(2)}) collective-permute-start(bf16[4,4736]{1,0:T(4,128)(2,1)} %get-tuple-element.45), channel_id=1, source_target_pairs={{0,20},{4,16},{8,28},{12,24},{16,4},{20,0},{24,12},{28,8},{1,21},{... | collective-permute-start | bytes 113672 | tf_op jit(solution)/shard_map/ppermute | solution.py:347
  11.2 6.2 %collective-permute-start.5 = (bf16[4,4736]{1,0:T(4,128)(2,1)}, bf16[4,4736]{1,0:T(4,128)(2,1)S(1)}, u32[]{:S(2)}, u32[]{:S(2)}) collective-permute-start(bf16[4,4736]{1,0:T(4,128)(2,1)} %get-tuple-element.46), channel_id=1, source_target_pairs={{0,24},{4,28},{8,16},{12,20},{16,8},{20,12},{24,0},{28,4},{1,25},{... | collective-permute-start | bytes 113672 | tf_op jit(solution)/shard_map/ppermute | solution.py:347
  14.8 6.9 %collective-permute-start.6 = (bf16[4,4736]{1,0:T(4,128)(2,1)}, bf16[4,4736]{1,0:T(4,128)(2,1)S(1)}, u32[]{:S(2)}, u32[]{:S(2)}) collective-permute-start(bf16[4,4736]{1,0:T(4,128)(2,1)} %get-tuple-element.47), channel_id=1, source_target_pairs={{0,28},{4,24},{8,20},{12,16},{16,12},{20,8},{24,4},{28,0},{1,29},{... | collective-permute-start | bytes 113672 | tf_op jit(solution)/shard_map/ppermute | solution.py:347
  16.2 9.4 %copy-start.4 = (bf16[4,4736]{1,0:T(4,128)(2,1)}, bf16[4,4736]{1,0:T(4,128)(2,1)S(1)}, u32[]{:S(2)}) copy-start(bf16[4,4736]{1,0:T(4,128)(2,1)S(1)} %collective-permute-done.4.refs_5_.refs_4_) | copy-start | bytes 113668
  17.4 8.2 %copy-start.6 = (bf16[4,4736]{1,0:T(4,128)(2,1)}, bf16[4,4736]{1,0:T(4,128)(2,1)S(1)}, u32[]{:S(2)}) copy-start(bf16[4,4736]{1,0:T(4,128)(2,1)S(1)} %collective-permute-done.5.refs_6_.refs_5_) | copy-start | bytes 113668
  21.7 4.0 %copy-start.8 = (bf16[4,4736]{1,0:T(4,128)(2,1)}, bf16[4,4736]{1,0:T(4,128)(2,1)S(1)}, u32[]{:S(2)}) copy-start(bf16[4,4736]{1,0:T(4,128)(2,1)S(1)} %collective-permute-done.6.refs_7_.refs_6_) | copy-start | bytes 113668
  21.7 1.3 %copy-start = (bf16[1024,576]{0,1:T(8,128)(2,1)S(1)}, bf16[1024,576]{0,1:T(8,128)(2,1)}, u32[]{:S(2)}) copy-start(bf16[1024,576]{0,1:T(8,128)(2,1)} %param.13) | copy-start | bytes 3538948
  25.0 8.5 %copy-start.1 = (bf16[1024,576]{0,1:T(8,128)(2,1)S(1)}, bf16[1024,576]{0,1:T(8,128)(2,1)}, u32[]{:S(2)}) copy-start(bf16[1024,576]{0,1:T(8,128)(2,1)} %param.13) | copy-start | bytes 3538948
  25.0 25.7 %collective-permute-start.10 = (bf16[576,1024]{1,0:T(8,128)(2,1)}, bf16[576,1024]{1,0:T(8,128)(2,1)S(1)}, u32[]{:S(2)}, u32[]{:S(2)}) collective-permute-start(bf16[576,1024]{1,0:T(8,128)(2,1)} %get-tuple-element.53), channel_id=1, source_target_pairs={{0,4},{4,0},{8,12},{12,8},{16,20},{20,16},{24,28},{28,24},{1,5},{5... | collective-permute-start | bytes 3538952 | tf_op jit(solution)/shard_map/ppermute | solution.py:347
  25.6 24.1 %collective-permute-start.7 = (bf16[576,512]{1,0:T(8,128)(2,1)}, bf16[576,512]{1,0:T(8,128)(2,1)S(1)}, u32[]{:S(2)}, u32[]{:S(2)}) collective-permute-start(bf16[576,512]{1,0:T(8,128)(2,1)} %get-tuple-element.52), channel_id=1, source_target_pairs={{0,16},{4,20},{8,24},{12,28},{16,0},{20,4},{24,8},{28,12},{1,17},{... | collective-permute-start | bytes 1769480 | tf_op jit(solution)/shard_map/ppermute | solution.py:347
  26.3 1.6 %copy-start.2 = (bf16[16,128,512]{2,1,0:T(8,128)(2,1)S(1)}, bf16[16,128,512]{2,1,0:T(8,128)(2,1)}, u32[]{:S(2)}) copy-start(bf16[16,128,512]{2,1,0:T(8,128)(2,1)} %w_ref.2) | copy-start | bytes 6291460
  27.9 0.8 copy-start.5
  28.6 0.8 copy-start.7
  29.4 0.8 copy-start.9
  30.2 0.8 copy-start.12
  30.9 2.5 %copy-start.13 = (s32[40]{0:T(128)S(1)}, s32[40]{0:T(128)}, u32[]{:S(2)}) copy-start(s32[40]{0:T(128)} %pad_add_fusion.1) | copy-start | bytes 484
  31.5 31.2 %collective-permute-start.9 = (bf16[640,640]{1,0:T(8,128)(2,1)S(1)}, bf16[640,640]{1,0:T(8,128)(2,1)S(1)}, u32[]{:S(2)}, u32[]{:S(2)}) collective-permute-start(bf16[640,640]{1,0:T(8,128)(2,1)S(1)} %get-tuple-element.48.refs_1_), channel_id=1, source_target_pairs={{0,8},{4,12},{8,0},{12,4},{16,24},{20,28},{24,16},{28,20},{1,9},{5... | collective-permute-start | bytes 2457608 | tf_op jit(solution)/shard_map/ppermute | solution.py:347
  49.6 22.2 %collective-permute-start.8 = (bf16[576,384]{1,0:T(8,128)(2,1)S(1)}, bf16[576,384]{1,0:T(8,128)(2,1)S(1)}, u32[]{:S(2)}, u32[]{:S(2)}) collective-permute-start(bf16[576,384]{1,0:T(8,128)(2,1)S(1)} %after.6), channel_id=1, source_target_pairs={{0,16},{4,20},{8,24},{12,28},{16,0},{20,4},{24,8},{28,12},{1,17},{... | collective-permute-start | bytes 1327112 | tf_op jit(solution)/shard_map/ppermute | solution.py:347
  49.6 23.2 %collective-permute-start.13 = (bf16[576,512]{1,0:T(8,128)(2,1)S(1)}, bf16[576,512]{1,0:T(8,128)(2,1)S(1)}, u32[]{:S(2)}, u32[]{:S(2)}) collective-permute-start(bf16[576,512]{1,0:T(8,128)(2,1)S(1)} %after.10.refs_2_), channel_id=1, source_target_pairs={{0,4},{4,0},{8,12},{12,8},{16,20},{20,16},{24,28},{28,24},{1,5},{5... | collective-permute-start | bytes 1769480 | tf_op jit(solution)/shard_map/ppermute | solution.py:347
  62.7 9.1 %copy-start.11 = (bf16[576,128]{1,0:T(8,128)(2,1)S(1)}, bf16[576,128]{1,0:T(8,128)(2,1)}, u32[]{:S(2)}) copy-start(bf16[576,128]{1,0:T(8,128)(2,1)} %copy-done.10) | copy-start | bytes 442372
  71.8 12.0 %collective-permute-start.11 = (bf16[576,384]{1,0:T(8,128)(2,1)S(1)}, bf16[576,384]{1,0:T(8,128)(2,1)S(1)}, u32[]{:S(2)}, u32[]{:S(2)}) collective-permute-start(bf16[576,384]{1,0:T(8,128)(2,1)S(1)} %after.8.refs_2_), channel_id=1, source_target_pairs={{0,4},{4,0},{8,12},{12,8},{16,20},{20,16},{24,28},{28,24},{1,5},{5... | collective-permute-start | bytes 1327112 | tf_op jit(solution)/shard_map/ppermute | solution.py:347
  72.8 7.9 %collective-permute-start.12 = (bf16[576,128]{1,0:T(8,128)(2,1)S(1)}, bf16[576,128]{1,0:T(8,128)(2,1)S(1)}, u32[]{:S(2)}, u32[]{:S(2)}) collective-permute-start(bf16[576,128]{1,0:T(8,128)(2,1)S(1)} %after.9), channel_id=1, source_target_pairs={{0,16},{4,20},{8,24},{12,28},{16,0},{20,4},{24,8},{28,12},{1,17},{... | collective-permute-start | bytes 442376 | tf_op jit(solution)/shard_map/ppermute | solution.py:347
  80.7 7.0 %collective-permute-start.14 = (bf16[576,128]{1,0:T(8,128)(2,1)S(1)}, bf16[576,128]{1,0:T(8,128)(2,1)S(1)}, u32[]{:S(2)}, u32[]{:S(2)}) collective-permute-start(bf16[576,128]{1,0:T(8,128)(2,1)S(1)} %after.11.refs_4_), channel_id=1, source_target_pairs={{0,4},{4,0},{8,12},{12,8},{16,20},{20,16},{24,28},{28,24},{1,5},{5... | collective-permute-start | bytes 442376 | tf_op jit(solution)/shard_map/ppermute | solution.py:347
  87.8 1.9 %copy-start.14 = (s32[32]{0:T(128)S(1)}, s32[32]{0:T(128)}, u32[]{:S(2)}) copy-start(s32[32]{0:T(128)} %param.18) | copy-start | bytes 388
  87.8 1.9 %copy-start.15 = (s32[32]{0:T(128)S(1)}, s32[32]{0:T(128)}, u32[]{:S(2)}) copy-start(s32[32]{0:T(128)} %param.17) | copy-start | bytes 388
  89.6 15.4 %collective-permute-start.15 = (bf16[656,512]{1,0:T(8,128)(2,1)S(1)}, bf16[656,512]{1,0:T(8,128)(2,1)S(1)}, u32[]{:S(2)}, u32[]{:S(2)}) collective-permute-start(bf16[656,512]{1,0:T(8,128)(2,1)S(1)} %attend.15), channel_id=1, source_target_pairs={{0,8},{4,12},{8,0},{12,4},{16,24},{20,28},{24,16},{28,20},{1,9},{5... | collective-permute-start | bytes 2015240 | tf_op jit(solution)/shard_map/ppermute | solution.py:347
  91.4 13.7 %copy-start.3 = (bf16[16,512,128]{2,1,0:T(8,128)(2,1)S(1)}, bf16[16,512,128]{2,1,0:T(8,128)(2,1)}, u32[]{:S(2)}) copy-start(bf16[16,512,128]{2,1,0:T(8,128)(2,1)} %w_ref.3) | copy-start | bytes 6291460
  (1 other events, 0.7 us)

commit v5 on v4

--- a/solution.py
+++ b/solution.py
@@ -202,20 +202,29 @@
     )(me, *operands)
 
 
-def absorb_kernel(per_dec, n, me_ref, w_ref, *refs):
-    got_refs, absorbed_ref, extra_ref, placed = refs[:n], refs[n], refs[n + 1], refs[n + 2]
+def absorb_kernel(per_dec, n, me_ref, w_hbm, *refs):
+    got_refs, refs = refs[:n], refs[-6:]
+    absorbed_ref, extra_ref, w_ref, placed, w_sem, sems = refs
     heads = w_ref.shape[0]
-    per = got_refs[0].shape[0]
+    _, per, total = placed.shape
     row = extra_ref.shape[1]
     count = absorbed_ref.shape[0] // heads
     wide = -(-row // LANES) * LANES
     fold = -(-wide // (per * LANES)) * LANES
-    part = (got_refs[0].shape[1] - wide - per_dec * fold) * per // (per + per_dec)
+    part = (total - wide - per_dec * fold) * per // (per + per_dec)
     width = part // heads
     cut = part // per
     at = part + per_dec * cut
-    for r, ref in enumerate(got_refs):
-        placed[me_ref[0] ^ r] = ref[...].astype(jnp.float32)
+    weights = pltpu.make_async_copy(w_hbm, w_ref, w_sem)
+    weights.start()
+    copies = [
+        pltpu.make_async_copy(ref, placed.at[me_ref[0] ^ r], sems.at[r])
+        for r, ref in enumerate(got_refs)
+    ]
+    for copy in copies:
+        copy.start()
+    for copy in copies:
+        copy.wait()
 
     def unfold(x, length):
         strips = []
@@ -223,7 +232,7 @@
             strips += [x[i : i + 1, j : j + length] for i in range(per)]
         return jnp.concatenate(strips, axis=1)
 
-    blocks = [placed[d] for d in range(n)]
+    blocks = [placed[d].astype(jnp.float32) for d in range(n)]
     queries = [x[:, :part] for x in blocks]
     fresh = [x[:, at : at + wide] for x in blocks]
     for x in blocks:
@@ -234,6 +243,7 @@
     q = jnp.concatenate(queries, axis=0).astype(jnp.bfloat16)
     new = jnp.concatenate(fresh, axis=0)
     blank = jnp.zeros((count, absorbed_ref.shape[1] - row), jnp.float32)
+    weights.wait()
     for h in range(0, heads, 2):
         parts = []
         for g in (h, h + 1):
@@ -247,24 +257,25 @@
     extra_ref[...] = jnp.concatenate([new[:, :row], blank], axis=0).astype(jnp.bfloat16)
 
 
-def absorb(count, per_dec, me, got, w_uk, row):
+def absorb(count, per_dec, me, got, w_uk, row, tokens):
     heads = w_uk.shape[0]
+    n = len(got)
     return pl.pallas_call(
-        functools.partial(absorb_kernel, per_dec, len(got)),
-        in_specs=[pl.BlockSpec(memory_space=pltpu.SMEM)] + [WHOLE] * (1 + len(got)),
-        out_shape=(
+        functools.partial(absorb_kernel, per_dec, n),
+        in_specs=[pl.BlockSpec(memory_space=pltpu.SMEM)] + [ANY] * (1 + n + len(tokens)),
+        out_shape=[
             jax.ShapeDtypeStruct((heads * count, -(-row // LANES) * LANES), jnp.bfloat16),
             jax.ShapeDtypeStruct((LANES, row), jnp.bfloat16),
-        ),
-        scratch_shapes=[pltpu.VMEM((len(got), *got[0].shape), jnp.float32)],
-        compiler_params=room(24),
-        cost_estimate=pl.CostEstimate(
-            flops=2 * count * heads * DN * DC,
-            bytes_accessed=2 * w_uk.size,
-            transcendentals=0,
-        ),
+        ],
+        scratch_shapes=[
+            pltpu.VMEM(w_uk.shape, w_uk.dtype),
+            pltpu.VMEM((n, *got[0].shape), got[0].dtype),
+            pltpu.SemaphoreType.DMA(()),
+            pltpu.SemaphoreType.DMA((n,)),
+        ],
+        compiler_params=room(16),
         name="absorb",
-    )(me, w_uk, *got)
+    )(me, w_uk, *got, *tokens)
 
 
 def split_kernel(spans, x_ref, *refs):
@@ -349,20 +360,21 @@
     far, pair = n // 2, n // 4
     near = [1 << b for b in range(pair.bit_length() - 1)]
     keys = cache_kv.T
-    edges = [0, pos_dev // 2, pos_dev // 8 * 7, pos_dev]
+    edges = [0, pos_dev // 4, pos_dev // 4 * 3, pos_dev]
 
     place = me[None].astype(jnp.int32)
     mine = pack(n, place, query, dec_query, span_kv, dec_kv)
     got = [mine[0]] + [swap(x, r) for r, x in enumerate(mine) if r]
-    absorbed, extra = absorb(count, rows_dec // n, place, got, w_uk, row)
+
+    pieces = [swap(keys[:, : edges[1]], far)]
+    absorbed, extra = absorb(count, rows_dec // n, place, got, w_uk, row, pieces)
     new_rows = extra[:span]
     other = swap(absorbed, pair)
-
-    *cuts, copy = split(keys, [*zip(edges, edges[1:]), (0, pos_dev)], got[1:])
+    *cuts, copy = split(keys, [*zip(edges[1:], edges[2:]), (0, pos_dev)], got[1:] + pieces)
     blocks = [(0, copy)]
     for stride in near:
         blocks += [(offset ^ stride, swap(x, stride)) for offset, x in blocks]
-    pieces = [swap(cuts[0], far)]
+    pieces.append(swap(cuts[0], far))
 
     def spread(x):
         part = [(far, x)]
@@ -402,21 +414,17 @@
     home = [(0, 0, keys)]
     side = [(0, i, x) for i, (_, x) in enumerate(blocks) if i]
     state = attend(fills, absorbed, home, tile, new=(extra, bias))
-    pieces.append(swap(after(cuts[1], state[0], pieces[0]), far))
-    first = stage_of(0, spread(after(pieces[0], state[0])))
+    first = stage_of(0, spread(pieces[0]))
+    pieces.append(swap(after(cuts[1], state[0], pieces[1]), far))
+    first += stage_of(1, spread(after(pieces[1], state[0])))
     state = attend(fills, absorbed, side, tile, state=state)
     other = after(other, state[0])
     guest = attend(fills, other, home + side, tile)
-    pieces.append(swap(after(cuts[2], guest[0], pieces[1]), far))
-    second = stage_of(1, spread(after(pieces[1], guest[0])))
+    second = stage_of(2, spread(after(pieces[2], guest[0])))
     guest = attend(fills, other, first, tile, state=guest)
-    state = attend(fills, absorbed, first, tile, state=state)
-    third = stage_of(2, spread(after(pieces[2], guest[0], state[0])))
-    second, third = second + third[:1], third[1:]
-    guest = attend(fills, other, second, tile, state=guest)
-    sent = attend(fills, other, third, tile, state=guest, last=True)
+    sent = attend(fills, other, second, tile, state=guest, last=True)
     back = swap(sent, pair)
-    state = attend(fills, absorbed, second + third, tile, state=state)
+    state = attend(fills, absorbed, first + second, tile, state=state)
     span_out, dec_out = finish(count, span, state, back, w_uv)
     return (span_out, dec_out, new_cache)
 

time: 107 us -> 105 us (0.981)
  Pallas kernels: 33.6 us -> 29.4 us
  starting transfers between devices: 17.5 us -> 21.5 us
  waiting for transfers between devices: 44.5 us -> 47.5 us
  local copies, waits for them, and re-layouts: 6.65 us -> 3.87 us
  other arithmetic: 1.69 us -> 0.53 us
    pallas_call x8 -> x6, Pallas kernels: 28.7 us -> 24 us  [attend(): pl.pallas_call(functools.partial(attend_kernel, spec, new is not None, st...]
    ppermute x16, starting transfers between devices: 17.5 us -> 21.5 us  [swap(): return lax.ppermute(x, 'seq', [(i, i ^ stride) for i in range(n)])]
    unnamed x34 -> x18, local copies, waits for them, and re-layouts: 6.65 us -> 2.88 us
    ppermute x16, waiting for transfers between devices: 44.5 us -> 47.5 us  [swap(): return lax.ppermute(x, 'seq', [(i, i ^ stride) for i in range(n)])]
  transfers between devices with their start and end apart: 16 -> 16, of which waited for: 9 -> 9; matrix products, arithmetic and copies ran while one was open for 3% -> 2% of each run, Pallas kernels for 26% -> 23%
where the time goes in v5:
time: 105 us
  waiting for transfers between devices  47.5 us (45%)
  Pallas kernels  29.4 us (28%)
  starting transfers between devices  21.5 us (20%)
  local copies, waits for them, and re-layouts  3.87 us (4%)
  matrix products  1.55 us (1%)
    ppermute x16, waiting for transfers between devices, swap(): return lax.ppermute(x, 'seq', [(i, i ^ stride) for i in range(n)])  47.5 us
    pallas_call x6, Pallas kernels, attend(): pl.pallas_call(functools.partial(attend_kernel, spec, new is not None, st...  24 us
    ppermute x16, starting transfers between devices, swap(): return lax.ppermute(x, 'seq', [(i, i ^ stride) for i in range(n)])  21.5 us
    unnamed x18, local copies, waits for them, and re-layouts  2.88 us
  transfers between devices with their start and end apart: 16, of which 9 were waited for; matrix products, arithmetic and copies ran while one was open for 2% of the time, Pallas kernels for 23%

profile of v5, /device:TPU:0, one launch (start us, length us, event | category | flops | bytes accessed | tf_op | source)
XLA Modules:
  0.0 105.2 jit_solution(8359703145090441547)
XLA Ops:
  0.6 1.0 slice.8
  1.6 4.1 %collective-permute-start.7 = (bf16[576,256]{1,0:T(8,128)(2,1)S(1)}, bf16[576,256]{1,0:T(8,128)(2,1)S(1)}, u32[]{:S(2)}, u32[]{:S(2)}) collective-permute-start(bf16[576,256]{1,0:T(8,128)(2,1)S(1)} %slice.8), channel_id=1, source_target_pairs={{0,16},{4,20},{8,24},{12,28},{16,0},{20,4},{24,8},{28,12},{1,17},{... | collective-permute-start | bytes 884744 | tf_op jit(solution)/shard_map/ppermute | solution.py:358
  5.7 1.8 %pack.1 = (bf16[4,4736]{1,0:T(4,128)(2,1)}, bf16[4,4736]{1,0:T(4,128)(2,1)}, bf16[4,4736]{1,0:T(4,128)(2,1)}, bf16[4,4736]{1,0:T(4,128)(2,1)}, bf16[4,4736]{1,0:...) custom-call(s32[1]{0:T(128)} %bitcast.me_ref, ...), custom_call_target="tpu_custom_call" | custom-call | tf_op jit(solution)/shard_map/pack/pallas_call | solution.py:193
  7.5 1.5 %collective-permute-start = (bf16[4,4736]{1,0:T(4,128)(2,1)}, bf16[4,4736]{1,0:T(4,128)(2,1)S(1)}, u32[]{:S(2)}, u32[]{:S(2)}) collective-permute-start(bf16[4,4736]{1,0:T(4,128)(2,1)} %get-tuple-element.34), channel_id=1, source_target_pairs={{0,4},{4,0},{8,12},{12,8},{16,20},{20,16},{24,28},{28,24},{1,5},{5... | collective-permute-start | bytes 113672 | tf_op jit(solution)/shard_map/ppermute | solution.py:358
  9.0 1.6 %collective-permute-start.1 = (bf16[4,4736]{1,0:T(4,128)(2,1)}, bf16[4,4736]{1,0:T(4,128)(2,1)S(1)}, u32[]{:S(2)}, u32[]{:S(2)}) collective-permute-start(bf16[4,4736]{1,0:T(4,128)(2,1)} %get-tuple-element.35), channel_id=1, source_target_pairs={{0,8},{4,12},{8,0},{12,4},{16,24},{20,28},{24,16},{28,20},{1,9},{5... | collective-permute-start | bytes 113672 | tf_op jit(solution)/shard_map/ppermute | solution.py:358
  11.0 0.7 collective-permute-done.refs_1_.refs_0_
  11.7 3.2 %collective-permute-start.4 = (bf16[4,4736]{1,0:T(4,128)(2,1)}, bf16[4,4736]{1,0:T(4,128)(2,1)S(1)}, u32[]{:S(2)}, u32[]{:S(2)}) collective-permute-start(bf16[4,4736]{1,0:T(4,128)(2,1)} %get-tuple-element.38), channel_id=1, source_target_pairs={{0,20},{4,16},{8,28},{12,24},{16,4},{20,0},{24,12},{28,8},{1,21},{... | collective-permute-start | bytes 113672 | tf_op jit(solution)/shard_map/ppermute | solution.py:358
  14.9 1.7 %collective-permute-start.5 = (bf16[4,4736]{1,0:T(4,128)(2,1)}, bf16[4,4736]{1,0:T(4,128)(2,1)S(1)}, u32[]{:S(2)}, u32[]{:S(2)}) collective-permute-start(bf16[4,4736]{1,0:T(4,128)(2,1)} %get-tuple-element.39), channel_id=1, source_target_pairs={{0,24},{4,28},{8,16},{12,20},{16,8},{20,12},{24,0},{28,4},{1,25},{... | collective-permute-start | bytes 113672 | tf_op jit(solution)/shard_map/ppermute | solution.py:358
  16.6 2.3 %collective-permute-start.6 = (bf16[4,4736]{1,0:T(4,128)(2,1)}, bf16[4,4736]{1,0:T(4,128)(2,1)S(1)}, u32[]{:S(2)}, u32[]{:S(2)}) collective-permute-start(bf16[4,4736]{1,0:T(4,128)(2,1)} %get-tuple-element.40), channel_id=1, source_target_pairs={{0,28},{4,24},{8,20},{12,16},{16,12},{20,8},{24,4},{28,0},{1,29},{... | collective-permute-start | bytes 113672 | tf_op jit(solution)/shard_map/ppermute | solution.py:358
  18.9 5.1 %collective-permute-done.3.refs_4_.refs_3_ = bf16[4,4736]{1,0:T(4,128)(2,1)S(1)} collective-permute-done((bf16[4,4736]{1,0:T(4,128)(2,1)}, bf16[4,4736]{1,0:T(4,128)(2,1)S(1)}, u32[]{:S(2)}, u32[]{:S(2)}) %collective-permute-start.3) | collective-permute-done | bytes 37920 | tf_op jit(solution)/shard_map/ppermute | solution.py:358
  23.9 1.8 %collective-permute-done.4.refs_5_.refs_4_ = bf16[4,4736]{1,0:T(4,128)(2,1)S(1)} collective-permute-done((bf16[4,4736]{1,0:T(4,128)(2,1)}, bf16[4,4736]{1,0:T(4,128)(2,1)S(1)}, u32[]{:S(2)}, u32[]{:S(2)}) %collective-permute-start.4) | collective-permute-done | bytes 37920 | tf_op jit(solution)/shard_map/ppermute | solution.py:358
  25.7 1.3 %copy-done = bf16[1024,576]{0,1:T(8,128)(2,1)S(1)} copy-done((bf16[1024,576]{0,1:T(8,128)(2,1)S(1)}, bf16[1024,576]{0,1:T(8,128)(2,1)}, u32[]{:S(2)}) %copy-start) | copy-done | bytes 1179672
  27.0 1.1 %split.1 = (bf16[576,512]{1,0:T(8,128)(2,1)S(1)}, bf16[576,256]{1,0:T(8,128)(2,1)S(1)}, bf16[576,1024]{1,0:T(8,128)(2,1)}) custom-call(bf16[576,1024]{1,0:T(8,128)(2,1)S(1)} %bitcast.6, bf16[4,4736]{1,0:T(4,128)(2,1)S(1)} %collective-permute-done.refs_1_.refs_0_, bf16[4,4736]{1,0:T(4,128)(2,1)S(1)} %collective-permute-done.1.refs_2_.refs_1_, ...), custom_call_target="tpu_custom_call" | custom-call | tf_op jit(solution)/shard_map/split/pallas_call | solution.py:287
  28.6 3.4 %collective-permute-start.9 = (bf16[576,512]{1,0:T(8,128)(2,1)S(1)}, bf16[576,512]{1,0:T(8,128)(2,1)S(1)}, u32[]{:S(2)}, u32[]{:S(2)}) collective-permute-start(bf16[576,512]{1,0:T(8,128)(2,1)S(1)} %get-tuple-element.42), channel_id=1, source_target_pairs={{0,16},{4,20},{8,24},{12,28},{16,0},{20,4},{24,8},{28,12},{1,17},{... | collective-permute-start | bytes 1769480 | tf_op jit(solution)/shard_map/ppermute | solution.py:358
  32.2 1.6 %copy-done.2 = bf16[16,128,512]{2,1,0:T(8,128)(2,1)S(1)} copy-done((bf16[16,128,512]{2,1,0:T(8,128)(2,1)S(1)}, bf16[16,128,512]{2,1,0:T(8,128)(2,1)}, u32[]{:S(2)}) %copy-start.2) | copy-done | bytes 2097176
  33.8 1.3 %absorb.1 = (bf16[640,640]{1,0:T(8,128)(2,1)S(1)}, bf16[128,576]{1,0:T(8,128)(2,1)S(1)}) custom-call(s32[1]{0:T(128)} %bitcast.me_ref, bf16[16,128,512]{2,1,0:T(8,128)(2,1)S(1)} %copy-done.2, bf16[4,4736]{1,0:T(4,128)(2,1)S(1)} %copy-done.4, bf16[4,4736]{1,0:T(4,128)(2,1)S(1)} %collective-permute-done.refs_1_.refs_0_, ...), custom_call_target="tpu_custom_call" | custom-call | tf_op jit(solution)/shard_map/absorb/pallas_call | solution.py:263
  35.5 3.5 %attend.6 = (f32[640,128]{1,0:T(8,128)S(1)}, f32[640,128]{1,0:T(8,128)S(1)}, f32[640,512]{1,0:T(8,128)S(1)}) custom-call(s32[4]{0:T(128)S(1)} %select_reduce_fusion.refs_0_, bf16[640,640]{1,0:T(8,128)(2,1)S(1)} %get-tuple-element.41.refs_1_, bf16[576,1024]{1,0:T(8,128)(2,1)S(1)} %bitcast.7, bf16[128,576]{1,0:T(8,128)(2,1)S(1)} %get-tuple-element.43.refs_3_, ...), custom_call_target="tpu_custom_call" | custom-call | tf_op jit(solution)/shard_map/attend/pallas_call | solution.py:123
  39.0 19.1 %collective-permute-done.9.x_ref.refs_1_ = bf16[576,512]{1,0:T(8,128)(2,1)S(1)} collective-permute-done((bf16[576,512]{1,0:T(8,128)(2,1)S(1)}, bf16[576,512]{1,0:T(8,128)(2,1)S(1)}, u32[]{:S(2)}, u32[]{:S(2)}) %collective-permute-start.9) | collective-permute-done | bytes 589856 | tf_op jit(solution)/shard_map/ppermute | solution.py:358
  58.1 0.8 collective-permute-start.10
  58.9 1.2 %collective-permute-start.8 = (bf16[576,256]{1,0:T(8,128)(2,1)S(1)}, bf16[576,256]{1,0:T(8,128)(2,1)S(1)}, u32[]{:S(2)}, u32[]{:S(2)}) collective-permute-start(bf16[576,256]{1,0:T(8,128)(2,1)S(1)} %collective-permute-done.7.refs_8_.refs_7_.refs_2_), channel_id=1, source_target_pairs={{0,4},{4,0},{8,12},{12,8},{16,20},{20,16},{24,28},{28,24},{1,5},{5... | collective-permute-start | bytes 884744 | tf_op jit(solution)/shard_map/ppermute | solution.py:358
  60.1 3.5 %attend.7 = (f32[640,128]{1,0:T(8,128)S(1)}, f32[640,128]{1,0:T(8,128)S(1)}, f32[640,512]{1,0:T(8,128)S(1)}) custom-call(s32[4]{0:T(128)S(1)} %select_reduce_fusion.refs_0_, bf16[640,640]{1,0:T(8,128)(2,1)S(1)} %get-tuple-element.41.refs_1_, ...), custom_call_target="tpu_custom_call", output_to_operand_aliasing={{0}: (3, {}), {1}: (4, {}), {2}: (5, {})} | custom-call | tf_op jit(solution)/shard_map/attend/pallas_call | solution.py:123
  63.6 4.6 %collective-permute-done.12.x_ref = bf16[640,640]{1,0:T(8,128)(2,1)S(1)} collective-permute-done((bf16[640,640]{1,0:T(8,128)(2,1)S(1)}, bf16[640,640]{1,0:T(8,128)(2,1)S(1)}, u32[]{:S(2)}, u32[]{:S(2)}) %collective-permute-start.12) | collective-permute-done | bytes 819232 | tf_op jit(solution)/shard_map/ppermute | solution.py:358
  68.2 5.0 %attend.8 = (f32[640,128]{1,0:T(8,128)S(1)}, f32[640,128]{1,0:T(8,128)S(1)}, f32[640,512]{1,0:T(8,128)S(1)}) custom-call(s32[4]{0:T(128)S(1)} %select_reduce_fusion.refs_0_, bf16[640,640]{1,0:T(8,128)(2,1)S(1)} %after.6.refs_1_, bf16[576,1024]{1,0:T(8,128)(2,1)S(1)} %bitcast.8, bf16[576,1024]{1,0:T(8,128)(2,1)S(1)} %collective-permute-done.13.refs_2_.refs_3_), custom_call_target="tpu_custom_call" | custom-call | tf_op jit(solution)/shard_map/attend/pallas_call | solution.py:123
  73.2 1.5 %collective-permute-done.11.x_ref = bf16[576,256]{1,0:T(8,128)(2,1)S(1)} collective-permute-done((bf16[576,256]{1,0:T(8,128)(2,1)S(1)}, bf16[576,256]{1,0:T(8,128)(2,1)S(1)}, u32[]{:S(2)}, u32[]{:S(2)}) %collective-permute-start.11) | collective-permute-done | bytes 294944 | tf_op jit(solution)/shard_map/ppermute | solution.py:358
  75.3 5.3 %collective-permute-done.8.refs_3_ = bf16[576,256]{1,0:T(8,128)(2,1)S(1)} collective-permute-done((bf16[576,256]{1,0:T(8,128)(2,1)S(1)}, bf16[576,256]{1,0:T(8,128)(2,1)S(1)}, u32[]{:S(2)}, u32[]{:S(2)}) %collective-permute-start.8) | collective-permute-done | bytes 294944 | tf_op jit(solution)/shard_map/ppermute | solution.py:358
  80.6 4.3 %attend.10 = (f32[640,128]{1,0:T(8,128)S(1)}, f32[640,128]{1,0:T(8,128)S(1)}, f32[640,512]{1,0:T(8,128)S(1)}) custom-call(s32[4]{0:T(128)S(1)} %select_reduce_fusion.refs_0_, bf16[640,640]{1,0:T(8,128)(2,1)S(1)} %after.6.refs_1_, ...), custom_call_target="tpu_custom_call", output_to_operand_aliasing={{0}: (6, {}), {1}: (7, {}), {2}: (8, {})} | custom-call | tf_op jit(solution)/shard_map/attend/pallas_call | solution.py:123
  84.9 0.7 collective-permute-done.14.refs_7_.refs_3_
  85.6 2.5 %attend.11 = bf16[656,512]{1,0:T(8,128)(2,1)S(1)} custom-call(s32[4]{0:T(128)S(1)} %select_reduce_fusion.refs_0_, bf16[640,640]{1,0:T(8,128)(2,1)S(1)} %after.6.refs_1_, bf16[576,256]{1,0:T(8,128)(2,1)S(1)} %after.7.refs_6_.refs_2_, bf16[576,256]{1,0:T(8,128)(2,1)S(1)} %collective-permute-done.14.refs_7_.refs_3_, f32[640,128]{1,0:T(8,128)S(1)} %get-tuple-element.58.refs_4_, ...), custom_call_target="tpu_custom_call" | custom-call | tf_op jit(solution)/shard_map/attend/pallas_call | solution.py:123
  88.3 1.5 %fusion = bf16[1024,576]{0,1:T(8,128)(2,1)} fusion(bf16[1024,576]{0,1:T(8,128)(2,1)S(1)} %copy-done.1, pred[1024]{0:T(1024)(128)(4,1)S(1)} %fusion.1, s32[32]{0:T(128)S(1)} %compare_select_fusion, bf16[128,576]{1,0:T(8,128)(2,1)S(1)} %get-tuple-element.43.refs_3_), kind=kOutput, calls=%fused_computation.1 | convolution fusion | flops 38961152 | bytes 2401792 | tf_op jit(solution)/shard_map/dot_general | solution.py:387
  89.9 5.2 %attend.9 = (f32[640,128]{1,0:T(8,128)S(1)}, f32[640,128]{1,0:T(8,128)S(1)}, f32[640,512]{1,0:T(8,128)S(1)}) custom-call(s32[4]{0:T(128)S(1)} %select_reduce_fusion.refs_0_, bf16[640,640]{1,0:T(8,128)(2,1)S(1)} %get-tuple-element.41.refs_1_, ...), custom_call_target="tpu_custom_call", output_to_operand_aliasing={{0}: (8, {}), {1}: (9, {}), {2}: (10, {})} | custom-call | tf_op jit(solution)/shard_map/attend/pallas_call | solution.py:123
  95.1 8.8 %collective-permute-done.15.far_ref = bf16[656,512]{1,0:T(8,128)(2,1)S(1)} collective-permute-done((bf16[656,512]{1,0:T(8,128)(2,1)S(1)}, bf16[656,512]{1,0:T(8,128)(2,1)S(1)}, u32[]{:S(2)}, u32[]{:S(2)}) %collective-permute-start.15) | collective-permute-done | bytes 671776 | tf_op jit(solution)/shard_map/ppermute | solution.py:358
  104.0 1.2 %finish.1 = (bf16[32,2048]{1,0:T(8,128)(2,1)}, bf16[8,2048]{1,0:T(8,128)(2,1)}) custom-call(f32[640,128]{1,0:T(8,128)S(1)} %get-tuple-element.53.m_ref, f32[640,128]{1,0:T(8,128)S(1)} %get-tuple-element.54.l_ref, f32[640,512]{1,0:T(8,128)S(1)} %get-tuple-element.55.acc_ref, bf16[656,512]{1,0:T(8,128)(2,1)S(1)} %collective-permute-done.15.far_ref, ...), custom_call_target="tpu_custom_call" | custom-call | flops 83886080 | bytes 4063232 | tf_op jit(solution)/shard_map/finish/pallas_call | solution.py:331
  (42 shorter events, 2.3 us)
Async XLA Ops:
  0.6 31.5 %copy-start.7 = (s32[8]{0:T(128)S(1)}, s32[8]{0:T(128)}, u32[]{:S(2)}) copy-start(s32[8]{0:T(128)} %param.19) | copy-start | bytes 100
  1.6 24.1 %collective-permute-start.7 = (bf16[576,256]{1,0:T(8,128)(2,1)S(1)}, bf16[576,256]{1,0:T(8,128)(2,1)S(1)}, u32[]{:S(2)}, u32[]{:S(2)}) collective-permute-start(bf16[576,256]{1,0:T(8,128)(2,1)S(1)} %slice.8), channel_id=1, source_target_pairs={{0,16},{4,20},{8,24},{12,28},{16,0},{20,4},{24,8},{28,12},{1,17},{... | collective-permute-start | bytes 884744 | tf_op jit(solution)/shard_map/ppermute | solution.py:358
  7.5 4.2 %collective-permute-start = (bf16[4,4736]{1,0:T(4,128)(2,1)}, bf16[4,4736]{1,0:T(4,128)(2,1)S(1)}, u32[]{:S(2)}, u32[]{:S(2)}) collective-permute-start(bf16[4,4736]{1,0:T(4,128)(2,1)} %get-tuple-element.34), channel_id=1, source_target_pairs={{0,4},{4,0},{8,12},{12,8},{16,20},{20,16},{24,28},{28,24},{1,5},{5... | collective-permute-start | bytes 113672 | tf_op jit(solution)/shard_map/ppermute | solution.py:358
  9.0 5.9 %collective-permute-start.1 = (bf16[4,4736]{1,0:T(4,128)(2,1)}, bf16[4,4736]{1,0:T(4,128)(2,1)S(1)}, u32[]{:S(2)}, u32[]{:S(2)}) collective-permute-start(bf16[4,4736]{1,0:T(4,128)(2,1)} %get-tuple-element.35), channel_id=1, source_target_pairs={{0,8},{4,12},{8,0},{12,4},{16,24},{20,28},{24,16},{28,20},{1,9},{5... | collective-permute-start | bytes 113672 | tf_op jit(solution)/shard_map/ppermute | solution.py:358
  10.6 6.0 %collective-permute-start.2 = (bf16[4,4736]{1,0:T(4,128)(2,1)}, bf16[4,4736]{1,0:T(4,128)(2,1)S(1)}, u32[]{:S(2)}, u32[]{:S(2)}) collective-permute-start(bf16[4,4736]{1,0:T(4,128)(2,1)} %get-tuple-element.36), channel_id=1, source_target_pairs={{0,12},{4,8},{8,4},{12,0},{16,28},{20,24},{24,20},{28,16},{1,13},{... | collective-permute-start | bytes 113672 | tf_op jit(solution)/shard_map/ppermute | solution.py:358
  11.0 13.0 %collective-permute-start.3 = (bf16[4,4736]{1,0:T(4,128)(2,1)}, bf16[4,4736]{1,0:T(4,128)(2,1)S(1)}, u32[]{:S(2)}, u32[]{:S(2)}) collective-permute-start(bf16[4,4736]{1,0:T(4,128)(2,1)} %get-tuple-element.37), channel_id=1, source_target_pairs={{0,16},{4,20},{8,24},{12,28},{16,0},{20,4},{24,8},{28,12},{1,17},{... | collective-permute-start | bytes 113672 | tf_op jit(solution)/shard_map/ppermute | solution.py:358
  11.7 14.0 %collective-permute-start.4 = (bf16[4,4736]{1,0:T(4,128)(2,1)}, bf16[4,4736]{1,0:T(4,128)(2,1)S(1)}, u32[]{:S(2)}, u32[]{:S(2)}) collective-permute-start(bf16[4,4736]{1,0:T(4,128)(2,1)} %get-tuple-element.38), channel_id=1, source_target_pairs={{0,20},{4,16},{8,28},{12,24},{16,4},{20,0},{24,12},{28,8},{1,21},{... | collective-permute-start | bytes 113672 | tf_op jit(solution)/shard_map/ppermute | solution.py:358
  14.9 10.9 %collective-permute-start.5 = (bf16[4,4736]{1,0:T(4,128)(2,1)}, bf16[4,4736]{1,0:T(4,128)(2,1)S(1)}, u32[]{:S(2)}, u32[]{:S(2)}) collective-permute-start(bf16[4,4736]{1,0:T(4,128)(2,1)} %get-tuple-element.39), channel_id=1, source_target_pairs={{0,24},{4,28},{8,16},{12,20},{16,8},{20,12},{24,0},{28,4},{1,25},{... | collective-permute-start | bytes 113672 | tf_op jit(solution)/shard_map/ppermute | solution.py:358
  16.6 9.2 %collective-permute-start.6 = (bf16[4,4736]{1,0:T(4,128)(2,1)}, bf16[4,4736]{1,0:T(4,128)(2,1)S(1)}, u32[]{:S(2)}, u32[]{:S(2)}) collective-permute-start(bf16[4,4736]{1,0:T(4,128)(2,1)} %get-tuple-element.40), channel_id=1, source_target_pairs={{0,28},{4,24},{8,20},{12,16},{16,12},{20,8},{24,4},{28,0},{1,29},{... | collective-permute-start | bytes 113672 | tf_op jit(solution)/shard_map/ppermute | solution.py:358
  25.7 1.3 %copy-start = (bf16[1024,576]{0,1:T(8,128)(2,1)S(1)}, bf16[1024,576]{0,1:T(8,128)(2,1)}, u32[]{:S(2)}) copy-start(bf16[1024,576]{0,1:T(8,128)(2,1)} %param.13) | copy-start | bytes 3538948
  27.0 5.2 %copy-start.4 = (bf16[4,4736]{1,0:T(4,128)(2,1)S(1)}, bf16[4,4736]{1,0:T(4,128)(2,1)}, u32[]{:S(2)}) copy-start(bf16[4,4736]{1,0:T(4,128)(2,1)} %get-tuple-element.33.refs_0_) | copy-start | bytes 113668
  28.2 31.9 %collective-permute-start.13 = (bf16[576,1024]{1,0:T(8,128)(2,1)}, bf16[576,1024]{1,0:T(8,128)(2,1)S(1)}, u32[]{:S(2)}, u32[]{:S(2)}) collective-permute-start(bf16[576,1024]{1,0:T(8,128)(2,1)} %get-tuple-element.46), channel_id=1, source_target_pairs={{0,4},{4,0},{8,12},{12,8},{16,20},{20,16},{24,28},{28,24},{1,5},{5... | collective-permute-start | bytes 3538952 | tf_op jit(solution)/shard_map/ppermute | solution.py:358
  28.6 29.4 %collective-permute-start.9 = (bf16[576,512]{1,0:T(8,128)(2,1)S(1)}, bf16[576,512]{1,0:T(8,128)(2,1)S(1)}, u32[]{:S(2)}, u32[]{:S(2)}) collective-permute-start(bf16[576,512]{1,0:T(8,128)(2,1)S(1)} %get-tuple-element.42), channel_id=1, source_target_pairs={{0,16},{4,20},{8,24},{12,28},{16,0},{20,4},{24,8},{28,12},{1,17},{... | collective-permute-start | bytes 1769480 | tf_op jit(solution)/shard_map/ppermute | solution.py:358
  32.2 1.6 %copy-start.2 = (bf16[16,128,512]{2,1,0:T(8,128)(2,1)S(1)}, bf16[16,128,512]{2,1,0:T(8,128)(2,1)}, u32[]{:S(2)}) copy-start(bf16[16,128,512]{2,1,0:T(8,128)(2,1)} %w_hbm.1) | copy-start | bytes 6291460
  33.8 1.5 %copy-start.8 = (s32[8]{0:T(128)S(1)}, s32[8]{0:T(128)}, u32[]{:S(2)}) copy-start(s32[8]{0:T(128)} %param.16) | copy-start | bytes 100
  33.8 1.7 %copy-start.1 = (bf16[1024,576]{0,1:T(8,128)(2,1)S(1)}, bf16[1024,576]{0,1:T(8,128)(2,1)}, u32[]{:S(2)}) copy-start(bf16[1024,576]{0,1:T(8,128)(2,1)} %param.13) | copy-start | bytes 3538948
  35.0 33.2 %collective-permute-start.12 = (bf16[640,640]{1,0:T(8,128)(2,1)S(1)}, bf16[640,640]{1,0:T(8,128)(2,1)S(1)}, u32[]{:S(2)}, u32[]{:S(2)}) collective-permute-start(bf16[640,640]{1,0:T(8,128)(2,1)S(1)} %get-tuple-element.41.refs_1_), channel_id=1, source_target_pairs={{0,8},{4,12},{8,0},{12,4},{16,24},{20,28},{24,16},{28,20},{1,9},{5... | collective-permute-start | bytes 2457608 | tf_op jit(solution)/shard_map/ppermute | solution.py:358
  58.1 22.6 %collective-permute-start.10 = (bf16[576,512]{1,0:T(8,128)(2,1)S(1)}, bf16[576,512]{1,0:T(8,128)(2,1)S(1)}, u32[]{:S(2)}, u32[]{:S(2)}) collective-permute-start(bf16[576,512]{1,0:T(8,128)(2,1)S(1)} %after.4.refs_4_), channel_id=1, source_target_pairs={{0,4},{4,0},{8,12},{12,8},{16,20},{20,16},{24,28},{28,24},{1,5},{5... | collective-permute-start | bytes 1769480 | tf_op jit(solution)/shard_map/ppermute | solution.py:358
  58.9 15.8 %collective-permute-start.11 = (bf16[576,256]{1,0:T(8,128)(2,1)S(1)}, bf16[576,256]{1,0:T(8,128)(2,1)S(1)}, u32[]{:S(2)}, u32[]{:S(2)}) collective-permute-start(bf16[576,256]{1,0:T(8,128)(2,1)S(1)} %after.5), channel_id=1, source_target_pairs={{0,16},{4,20},{8,24},{12,28},{16,0},{20,4},{24,8},{28,12},{1,17},{... | collective-permute-start | bytes 884744 | tf_op jit(solution)/shard_map/ppermute | solution.py:358
  58.9 21.7 %collective-permute-start.8 = (bf16[576,256]{1,0:T(8,128)(2,1)S(1)}, bf16[576,256]{1,0:T(8,128)(2,1)S(1)}, u32[]{:S(2)}, u32[]{:S(2)}) collective-permute-start(bf16[576,256]{1,0:T(8,128)(2,1)S(1)} %collective-permute-done.7.refs_8_.refs_7_.refs_2_), channel_id=1, source_target_pairs={{0,4},{4,0},{8,12},{12,8},{16,20},{20,16},{24,28},{28,24},{1,5},{5... | collective-permute-start | bytes 884744 | tf_op jit(solution)/shard_map/ppermute | solution.py:358
  74.7 10.9 %collective-permute-start.14 = (bf16[576,256]{1,0:T(8,128)(2,1)S(1)}, bf16[576,256]{1,0:T(8,128)(2,1)S(1)}, u32[]{:S(2)}, u32[]{:S(2)}) collective-permute-start(bf16[576,256]{1,0:T(8,128)(2,1)S(1)} %after.7.refs_6_.refs_2_), channel_id=1, source_target_pairs={{0,4},{4,0},{8,12},{12,8},{16,20},{20,16},{24,28},{28,24},{1,5},{5... | collective-permute-start | bytes 884744 | tf_op jit(solution)/shard_map/ppermute | solution.py:358
  85.6 2.6 %copy-start.5 = (s32[32]{0:T(128)S(1)}, s32[32]{0:T(128)}, u32[]{:S(2)}) copy-start(s32[32]{0:T(128)} %param.18) | copy-start | bytes 388
  85.6 2.6 %copy-start.6 = (s32[32]{0:T(128)S(1)}, s32[32]{0:T(128)}, u32[]{:S(2)}) copy-start(s32[32]{0:T(128)} %param.17) | copy-start | bytes 388
  88.1 15.8 %collective-permute-start.15 = (bf16[656,512]{1,0:T(8,128)(2,1)S(1)}, bf16[656,512]{1,0:T(8,128)(2,1)S(1)}, u32[]{:S(2)}, u32[]{:S(2)}) collective-permute-start(bf16[656,512]{1,0:T(8,128)(2,1)S(1)} %attend.11), channel_id=1, source_target_pairs={{0,8},{4,12},{8,0},{12,4},{16,24},{20,28},{24,16},{28,20},{1,9},{5... | collective-permute-start | bytes 2015240 | tf_op jit(solution)/shard_map/ppermute | solution.py:358
  89.9 14.1 %copy-start.3 = (bf16[16,512,128]{2,1,0:T(8,128)(2,1)S(1)}, bf16[16,512,128]{2,1,0:T(8,128)(2,1)}, u32[]{:S(2)}) copy-start(bf16[16,512,128]{2,1,0:T(8,128)(2,1)} %w_ref.1) | copy-start | bytes 6291460

commit v6 on v5

--- a/solution.py
+++ b/solution.py
@@ -149,9 +149,10 @@
     )(x, *tokens)
 
 
-def pack_kernel(n, me_ref, query_ref, dec_ref, span_kv_ref, dec_kv_ref, *out_refs):
+def pack_kernel(order, me_ref, query_ref, dec_ref, span_kv_ref, dec_kv_ref, *out_refs):
     per, row = span_kv_ref.shape
     per_dec = dec_ref.shape[0]
+    n = sum(len(x) for x in order)
     part = query_ref.shape[1] // n
     cut = part // per
     pad = -(-row // LANES) * LANES - row
@@ -169,20 +170,22 @@
             strips += [jnp.zeros((1, LANES), jnp.float32)] * (per - len(strips))
             tail.append(jnp.concatenate(strips, axis=0))
     tail = jnp.concatenate(tail, axis=1).astype(jnp.bfloat16)
-    for r, out_ref in enumerate(out_refs):
+    places = [(ref, i, r) for ref, rs in zip(out_refs, order) for i, r in enumerate(rs)]
+    for out_ref, j, r in places:
         begin = (me_ref[0] ^ r) * part
-        out_ref[:, :part] = query_ref[:, pl.ds(pl.multiple_of(begin, LANES), part)]
+        out_ref[j, :, :part] = query_ref[:, pl.ds(pl.multiple_of(begin, LANES), part)]
         for e in range(per_dec):
             strips = []
             for i in range(per):
                 at = pl.multiple_of(begin + i * cut, LANES)
                 strips.append(dec_ref[e : e + 1, pl.ds(at, cut)].astype(jnp.float32))
             at = part + e * cut
-            out_ref[:, at : at + cut] = jnp.concatenate(strips, axis=0).astype(jnp.bfloat16)
-        out_ref[:, part + per_dec * cut :] = tail
-
-
-def pack(n, me, query, dec_query, span_kv, dec_kv):
+            out_ref[j, :, at : at + cut] = jnp.concatenate(strips, axis=0).astype(jnp.bfloat16)
+        out_ref[j, :, part + per_dec * cut :] = tail
+
+
+def pack(order, me, query, dec_query, span_kv, dec_kv):
+    n = sum(len(x) for x in order)
     per, row = span_kv.shape
     per_dec = dec_kv.shape[0]
     part = query.shape[1] // n
@@ -191,22 +194,22 @@
     total = part + per_dec * (part // per) + wide + per_dec * fold
     operands = (query, dec_query, span_kv, dec_kv)
     return pl.pallas_call(
-        functools.partial(pack_kernel, n),
+        functools.partial(pack_kernel, order),
         grid=(1,),
         in_specs=[pl.BlockSpec(memory_space=pltpu.SMEM)]
         + [pl.BlockSpec(x.shape, lambda i: (0, 0)) for x in operands],
-        out_specs=[pl.BlockSpec((per, total), lambda i: (0, 0))] * n,
-        out_shape=[jax.ShapeDtypeStruct((per, total), jnp.bfloat16)] * n,
+        out_specs=[pl.BlockSpec((len(x), per, total), lambda i: (0, 0, 0)) for x in order],
+        out_shape=[jax.ShapeDtypeStruct((len(x), per, total), jnp.bfloat16) for x in order],
         compiler_params=room(60),
         name="pack",
     )(me, *operands)
 
 
-def absorb_kernel(per_dec, n, me_ref, w_hbm, *refs):
-    got_refs, refs = refs[:n], refs[-6:]
+def absorb_kernel(per_dec, order, me_ref, w_hbm, *refs):
+    got_refs, refs = refs[: len(order)], refs[-6:]
     absorbed_ref, extra_ref, w_ref, placed, w_sem, sems = refs
     heads = w_ref.shape[0]
-    _, per, total = placed.shape
+    n, per, total = placed.shape
     row = extra_ref.shape[1]
     count = absorbed_ref.shape[0] // heads
     wide = -(-row // LANES) * LANES
@@ -218,8 +221,9 @@
     weights = pltpu.make_async_copy(w_hbm, w_ref, w_sem)
     weights.start()
     copies = [
-        pltpu.make_async_copy(ref, placed.at[me_ref[0] ^ r], sems.at[r])
-        for r, ref in enumerate(got_refs)
+        pltpu.make_async_copy(ref.at[i], placed.at[me_ref[0] ^ r], sems.at[r])
+        for ref, rs in zip(got_refs, order)
+        for i, r in enumerate(rs)
     ]
     for copy in copies:
         copy.start()
@@ -257,25 +261,25 @@
     extra_ref[...] = jnp.concatenate([new[:, :row], blank], axis=0).astype(jnp.bfloat16)
 
 
-def absorb(count, per_dec, me, got, w_uk, row, tokens):
+def absorb(count, per_dec, me, order, got, w_uk, row):
     heads = w_uk.shape[0]
-    n = len(got)
+    n = sum(len(x) for x in order)
     return pl.pallas_call(
-        functools.partial(absorb_kernel, per_dec, n),
-        in_specs=[pl.BlockSpec(memory_space=pltpu.SMEM)] + [ANY] * (1 + n + len(tokens)),
+        functools.partial(absorb_kernel, per_dec, order),
+        in_specs=[pl.BlockSpec(memory_space=pltpu.SMEM)] + [ANY] * (1 + len(got)),
         out_shape=[
             jax.ShapeDtypeStruct((heads * count, -(-row // LANES) * LANES), jnp.bfloat16),
             jax.ShapeDtypeStruct((LANES, row), jnp.bfloat16),
         ],
         scratch_shapes=[
             pltpu.VMEM(w_uk.shape, w_uk.dtype),
-            pltpu.VMEM((n, *got[0].shape), got[0].dtype),
+            pltpu.VMEM((n, *got[0].shape[1:]), got[0].dtype),
             pltpu.SemaphoreType.DMA(()),
             pltpu.SemaphoreType.DMA((n,)),
         ],
         compiler_params=room(16),
         name="absorb",
-    )(me, w_uk, *got, *tokens)
+    )(me, w_uk, *got)
 
 
 def split_kernel(spans, x_ref, *refs):
@@ -360,21 +364,40 @@
     far, pair = n // 2, n // 4
     near = [1 << b for b in range(pair.bit_length() - 1)]
     keys = cache_kv.T
-    edges = [0, pos_dev // 4, pos_dev // 4 * 3, pos_dev]
+    edges = [0, pos_dev // 8 * 3, pos_dev // 4 * 3, pos_dev]
+
+    lead = keys[:, : edges[1]]
+    pieces = [swap(lead, far)]
 
     place = me[None].astype(jnp.int32)
-    mine = pack(n, place, query, dec_query, span_kv, dec_kv)
-    got = [mine[0]] + [swap(x, r) for r, x in enumerate(mine) if r]
-
-    pieces = [swap(keys[:, : edges[1]], far)]
-    absorbed, extra = absorb(count, rows_dec // n, place, got, w_uk, row, pieces)
+    order = [[r for r in range(n) if not r & 1], [r for r in range(n) if r & 1]]
+    stay, go = pack(order, place, query, dec_query, span_kv, dec_kv)
+    come = swap(go, 1)
+    groups = {r: [(0, stay[i]), (1, come[i])] for i, r in enumerate(order[0])}
+    for stride in near[1:]:
+        away = [r for r in groups if r & stride]
+        moved = swap(jnp.stack([x for r in away for _, x in groups[r]]), stride)
+        held = len(groups[away[0]])
+        for i, r in enumerate(away):
+            kept = groups[r ^ stride]
+            kept += [(o ^ stride, moved[i * held + j]) for j, (o, _) in enumerate(groups.pop(r))]
+    got, order = [], []
+    for r in sorted(groups):
+        got.append(jnp.stack([x for _, x in groups[r]]))
+        order.append([r ^ o for o, _ in groups[r]])
+    got = got[:1] + [swap(x, r) for r, x in zip(sorted(groups)[1:], got[1:])]
+
+    middle = edges[1]
+    *cuts, early, late = split(
+        keys, [*zip(edges[1:], edges[2:]), (0, middle), (middle, pos_dev)], [come]
+    )
+    halves = [(0, early, after(late, *got[1:]))]
+    for stride in near:
+        halves += [(o ^ stride, swap(x, stride), swap(y, stride)) for o, x, y in halves]
+    absorbed, extra = absorb(count, rows_dec // n, place, order, got, w_uk, row)
     new_rows = extra[:span]
     other = swap(absorbed, pair)
-    *cuts, copy = split(keys, [*zip(edges[1:], edges[2:]), (0, pos_dev)], got[1:] + pieces)
-    blocks = [(0, copy)]
-    for stride in near:
-        blocks += [(offset ^ stride, swap(x, stride)) for offset, x in blocks]
-    pieces.append(swap(cuts[0], far))
+    pieces.append(swap(after(cuts[0], pieces[0], halves[-1][1], *got[1:]), far))
 
     def spread(x):
         part = [(far, x)]
@@ -398,25 +421,26 @@
     seen = (index[None, :] < span) & (index[None, :] < limits[:, None])
     seen |= (index[None, :] >= span) & (index[None, :] == queries[:, None])
     bias = jnp.where(seen, 0.0, HIDDEN).astype(jnp.float32)
-    held = [offset for offset, _ in blocks]
+    held = [offset for offset, _, _ in halves]
     offsets = held + [offset ^ far for offset in held]
     which = jnp.stack([me ^ offset for offset in offsets])
     fills = jnp.sum(
         jnp.where(which[:, None] == jnp.arange(n, dtype=jnp.int32)[None, :], cache_fill[None, :], 0),
         axis=1,
     )
-    base = len(blocks)
+    base = len(halves)
     tile = heads // 2 * count
 
     def stage_of(c, part):
         return [(edges[c], base + i, x) for i, (_, x) in enumerate(part)]
 
     home = [(0, 0, keys)]
-    side = [(0, i, x) for i, (_, x) in enumerate(blocks) if i]
+    side = [(a, i, z) for i, (_, x, y) in enumerate(halves) if i for a, z in ((0, x), (middle, y))]
     state = attend(fills, absorbed, home, tile, new=(extra, bias))
-    first = stage_of(0, spread(pieces[0]))
-    pieces.append(swap(after(cuts[1], state[0], pieces[1]), far))
-    first += stage_of(1, spread(after(pieces[1], state[0])))
+    part = spread(pieces[0])
+    side += stage_of(0, part)
+    pieces.append(swap(after(cuts[1], state[0], pieces[1], part[-1][1]), far))
+    first = stage_of(1, spread(after(pieces[1], state[0])))
     state = attend(fills, absorbed, side, tile, state=state)
     other = after(other, state[0])
     guest = attend(fills, other, home + side, tile)

time: 105 us -> 107 us (1.019)
  starting transfers between devices: 21.5 us -> 24.3 us
  local copies, waits for them, and re-layouts: 3.87 us -> 2.03 us
  Pallas kernels: 29.4 us -> 30.7 us
    unnamed x18 -> x14, local copies, waits for them, and re-layouts: 2.88 us -> 0.03 us
    ppermute x16 -> x14, starting transfers between devices: 21.5 us -> 24.3 us  [swap(): return lax.ppermute(x, 'seq', [(i, i ^ stride) for i in range(n)])]
    pallas_call x6, Pallas kernels: 24 us -> 26.2 us  [attend(): pl.pallas_call(functools.partial(attend_kernel, spec, new is not None, st...]
    ppermute x16 -> x14, waiting for transfers between devices: 47.5 us -> 46.9 us  [swap(): return lax.ppermute(x, 'seq', [(i, i ^ stride) for i in range(n)])]
  transfers between devices with their start and end apart: 16 -> 14, of which waited for: 9 -> 5; matrix products, arithmetic and copies ran while one was open for 2% -> 4% of each run, Pallas kernels for 23% -> 24%
where the time goes in v6:
time: 107 us
  waiting for transfers between devices  46.9 us (44%)
  Pallas kernels  30.7 us (29%)
  starting transfers between devices  24.3 us (23%)
  local copies, waits for them, and re-layouts  2.03 us (2%)
  matrix products  1.54 us (1%)
    ppermute x14, waiting for transfers between devices, swap(): return lax.ppermute(x, 'seq', [(i, i ^ stride) for i in range(n)])  46.9 us
    pallas_call x6, Pallas kernels, attend(): pl.pallas_call(functools.partial(attend_kernel, spec, new is not None, st...  26.2 us
    ppermute x14, starting transfers between devices, swap(): return lax.ppermute(x, 'seq', [(i, i ^ stride) for i in range(n)])  24.3 us
  transfers between devices with their start and end apart: 14, of which 5 were waited for; matrix products, arithmetic and copies ran while one was open for 4% of the time, Pallas kernels for 24%

profile of v6, /device:TPU:0, one launch (start us, length us, event | category | flops | bytes accessed | tf_op | source)
XLA Modules:
  0.0 107.0 jit_solution(3717359932011684359)
XLA Ops:
  0.6 1.9 %pack.1 = (bf16[4,4,4736]{2,1,0:T(4,128)(2,1)}, bf16[4,4,4736]{2,1,0:T(4,128)(2,1)}) custom-call(s32[1]{0:T(128)} %bitcast.me_ref, bf16[4,24576]{1,0:T(4,128)(2,1)} %query_ref.1, bf16[1,24576]{1,0:T(2,128)(2,1)} %dec_ref.1, bf16[4,576]{1,0:T(4,128)(2,1)} %span_kv_ref.1, bf16[1,576]{1,0:T(2,128)(2,1)} %dec_kv_ref.1), custom_call_target="tpu_custom_call" | custom-call | tf_op jit(solution)/shard_map/pack/pallas_call | solution.py:196
  2.5 2.9 %collective-permute-start = (bf16[4,4,4736]{2,1,0:T(4,128)(2,1)}, bf16[4,4,4736]{2,1,0:T(4,128)(2,1)S(1)}, u32[]{:S(2)}, u32[]{:S(2)}) collective-permute-start(bf16[4,4,4736]{2,1,0:T(4,128)(2,1)} %get-tuple-element.29), channel_id=1, source_target_pairs={{0,4},{4,0},{8,12},{12,8},{16,20},{20,16},{24,28},{28,24},{1,5},{5... | collective-permute-start | bytes 454664 | tf_op jit(solution)/shard_map/ppermute | solution.py:362
  5.4 1.1 slice.44
  6.5 2.7 %collective-permute-start.4 = (bf16[576,384]{1,0:T(8,128)(2,1)S(1)}, bf16[576,384]{1,0:T(8,128)(2,1)S(1)}, u32[]{:S(2)}, u32[]{:S(2)}) collective-permute-start(bf16[576,384]{1,0:T(8,128)(2,1)S(1)} %slice.44), channel_id=1, source_target_pairs={{0,16},{4,20},{8,24},{12,28},{16,0},{20,4},{24,8},{28,12},{1,17},{... | collective-permute-start | bytes 1327112 | tf_op jit(solution)/shard_map/ppermute | solution.py:362
  9.2 0.9 fusion.8
  10.2 3.4 %collective-permute-start.3 = (bf16[2,4,4736]{2,1,0:T(4,128)(2,1)S(1)}, bf16[2,4,4736]{2,1,0:T(4,128)(2,1)S(1)}, u32[]{:S(2)}, u32[]{:S(2)}) collective-permute-start(bf16[2,4,4736]{2,1,0:T(4,128)(2,1)S(1)} %pad_maximum_fusion.3), channel_id=1, source_target_pairs={{0,24},{4,28},{8,16},{12,20},{16,8},{20,12},{24,0},{28,4},{1,25},{... | collective-permute-start | bytes 227336 | tf_op jit(solution)/shard_map/ppermute | solution.py:362
  13.8 1.1 %collective-permute-start.1 = (bf16[2,4,4736]{2,1,0:T(4,128)(2,1)S(1)}, bf16[2,4,4736]{2,1,0:T(4,128)(2,1)S(1)}, u32[]{:S(2)}, u32[]{:S(2)}) collective-permute-start(bf16[2,4,4736]{2,1,0:T(4,128)(2,1)S(1)} %pad_maximum_fusion.1), channel_id=1, source_target_pairs={{0,8},{4,12},{8,0},{12,4},{16,24},{20,28},{24,16},{28,20},{1,9},{5... | collective-permute-start | bytes 227336 | tf_op jit(solution)/shard_map/ppermute | solution.py:362
  14.9 0.2 split.1
  15.1 1.3 %collective-permute-start.5 = (bf16[576,384]{1,0:T(8,128)(2,1)S(1)}, bf16[576,384]{1,0:T(8,128)(2,1)S(1)}, u32[]{:S(2)}, u32[]{:S(2)}) collective-permute-start(bf16[576,384]{1,0:T(8,128)(2,1)S(1)} %get-tuple-element.32), channel_id=1, source_target_pairs={{0,4},{4,0},{8,12},{12,8},{16,20},{20,16},{24,28},{28,24},{1,5},{5... | collective-permute-start | bytes 1327112 | tf_op jit(solution)/shard_map/ppermute | solution.py:362
  16.4 6.8 %collective-permute-done.3.refs_3_.refs_4_.refs_2_ = bf16[2,4,4736]{2,1,0:T(4,128)(2,1)S(1)} collective-permute-done((bf16[2,4,4736]{2,1,0:T(4,128)(2,1)S(1)}, bf16[2,4,4736]{2,1,0:T(4,128)(2,1)S(1)}, u32[]{:S(2)}, u32[]{:S(2)}) %collective-permute-start.3) | collective-permute-done | bytes 75808 | tf_op jit(solution)/shard_map/ppermute | solution.py:362
  23.2 11.9 %collective-permute-done.2.refs_2_.refs_3_.refs_1_ = bf16[2,4,4736]{2,1,0:T(4,128)(2,1)S(1)} collective-permute-done((bf16[2,4,4736]{2,1,0:T(4,128)(2,1)S(1)}, bf16[2,4,4736]{2,1,0:T(4,128)(2,1)S(1)}, u32[]{:S(2)}, u32[]{:S(2)}) %collective-permute-start.2) | collective-permute-done | bytes 75808 | tf_op jit(solution)/shard_map/ppermute | solution.py:362
  35.1 1.3 %absorb.1 = (bf16[640,640]{1,0:T(8,128)(2,1)S(1)}, bf16[128,576]{1,0:T(8,128)(2,1)S(1)}) custom-call(s32[1]{0:T(128)} %bitcast.me_ref, bf16[16,128,512]{2,1,0:T(8,128)(2,1)S(1)} %copy-done.1, bf16[2,4,4736]{2,1,0:T(4,128)(2,1)S(1)} %pad_maximum_fusion.refs_0_, bf16[2,4,4736]{2,1,0:T(4,128)(2,1)S(1)} %collective-permute-done.1.refs_1_.refs_2_.refs_0_, ...), custom_call_target="tpu_custom_call" | custom-call | tf_op jit(solution)/shard_map/absorb/pallas_call | solution.py:267
  36.4 0.7 collective-permute-start.10
  37.2 0.6 collective-permute-start.11
  37.7 1.5 %collective-permute-start.8 = (bf16[576,384]{1,0:T(8,128)(2,1)S(1)}, bf16[576,384]{1,0:T(8,128)(2,1)S(1)}, u32[]{:S(2)}, u32[]{:S(2)}) collective-permute-start(bf16[576,384]{1,0:T(8,128)(2,1)S(1)} %collective-permute-done.4.refs_0_.refs_4_.refs_5_), channel_id=1, source_target_pairs={{0,4},{4,0},{8,12},{12,8},{16,20},{20,16},{24,28},{28,24},{1,5},{5... | collective-permute-start | bytes 1327112 | tf_op jit(solution)/shard_map/ppermute | solution.py:362
  39.2 3.4 %collective-permute-start.6 = (bf16[576,384]{1,0:T(8,128)(2,1)S(1)}, bf16[576,384]{1,0:T(8,128)(2,1)S(1)}, u32[]{:S(2)}, u32[]{:S(2)}) collective-permute-start(bf16[576,384]{1,0:T(8,128)(2,1)S(1)} %after.6), channel_id=1, source_target_pairs={{0,16},{4,20},{8,24},{12,28},{16,0},{20,4},{24,8},{28,12},{1,17},{... | collective-permute-start | bytes 1327112 | tf_op jit(solution)/shard_map/ppermute | solution.py:362
  42.7 0.2 select_reduce_fusion.refs_0_
  43.0 3.5 %attend.6 = (f32[640,128]{1,0:T(8,128)S(1)}, f32[640,128]{1,0:T(8,128)S(1)}, f32[640,512]{1,0:T(8,128)S(1)}) custom-call(s32[4]{0:T(128)S(1)} %select_reduce_fusion.refs_0_, bf16[640,640]{1,0:T(8,128)(2,1)S(1)} %get-tuple-element.30.refs_1_, bf16[576,1024]{1,0:T(8,128)(2,1)S(1)} %bitcast.7, bf16[128,576]{1,0:T(8,128)(2,1)S(1)} %get-tuple-element.33.refs_3_, ...), custom_call_target="tpu_custom_call" | custom-call | tf_op jit(solution)/shard_map/attend/pallas_call | solution.py:123
  46.4 18.4 %collective-permute-done.8.refs_2_.refs_5_.refs_6_ = bf16[576,384]{1,0:T(8,128)(2,1)S(1)} collective-permute-done((bf16[576,384]{1,0:T(8,128)(2,1)S(1)}, bf16[576,384]{1,0:T(8,128)(2,1)S(1)}, u32[]{:S(2)}, u32[]{:S(2)}) %collective-permute-start.8) | collective-permute-done | bytes 442400 | tf_op jit(solution)/shard_map/ppermute | solution.py:362
  64.8 3.4 %collective-permute-start.9 = (bf16[576,256]{1,0:T(8,128)(2,1)S(1)}, bf16[576,256]{1,0:T(8,128)(2,1)S(1)}, u32[]{:S(2)}, u32[]{:S(2)}) collective-permute-start(bf16[576,256]{1,0:T(8,128)(2,1)S(1)} %after.8), channel_id=1, source_target_pairs={{0,16},{4,20},{8,24},{12,28},{16,0},{20,4},{24,8},{28,12},{1,17},{... | collective-permute-start | bytes 884744 | tf_op jit(solution)/shard_map/ppermute | solution.py:362
  68.2 0.5 collective-permute-start.7
  68.7 5.5 %attend.7 = (f32[640,128]{1,0:T(8,128)S(1)}, f32[640,128]{1,0:T(8,128)S(1)}, f32[640,512]{1,0:T(8,128)S(1)}) custom-call(s32[4]{0:T(128)S(1)} %select_reduce_fusion.refs_0_, bf16[640,640]{1,0:T(8,128)(2,1)S(1)} %get-tuple-element.30.refs_1_, ...), custom_call_target="tpu_custom_call", output_to_operand_aliasing={{0}: (6, {}), {1}: (7, {}), {2}: (8, {})} | custom-call | tf_op jit(solution)/shard_map/attend/pallas_call | solution.py:123
  74.3 7.3 %attend.8 = (f32[640,128]{1,0:T(8,128)S(1)}, f32[640,128]{1,0:T(8,128)S(1)}, f32[640,512]{1,0:T(8,128)S(1)}) custom-call(s32[4]{0:T(128)S(1)} %select_reduce_fusion.refs_0_, bf16[640,640]{1,0:T(8,128)(2,1)S(1)} %after.10.refs_1_, bf16[576,1024]{1,0:T(8,128)(2,1)S(1)} %bitcast.8, bf16[576,384]{1,0:T(8,128)(2,1)S(1)} %collective-permute-done.5.refs_1_.refs_2_.refs_3_, ...), custom_call_target="tpu_custom_call" | custom-call | tf_op jit(solution)/shard_map/attend/pallas_call | solution.py:123
  81.6 1.5 %collective-permute-start.12 = (bf16[576,256]{1,0:T(8,128)(2,1)S(1)}, bf16[576,256]{1,0:T(8,128)(2,1)S(1)}, u32[]{:S(2)}, u32[]{:S(2)}) collective-permute-start(bf16[576,256]{1,0:T(8,128)(2,1)S(1)} %after.11.refs_4_.refs_2_), channel_id=1, source_target_pairs={{0,4},{4,0},{8,12},{12,8},{16,20},{20,16},{24,28},{28,24},{1,5},{5... | collective-permute-start | bytes 884744 | tf_op jit(solution)/shard_map/ppermute | solution.py:362
  83.2 3.3 %attend.10 = (f32[640,128]{1,0:T(8,128)S(1)}, f32[640,128]{1,0:T(8,128)S(1)}, f32[640,512]{1,0:T(8,128)S(1)}) custom-call(s32[4]{0:T(128)S(1)} %select_reduce_fusion.refs_0_, bf16[640,640]{1,0:T(8,128)(2,1)S(1)} %after.10.refs_1_, bf16[576,384]{1,0:T(8,128)(2,1)S(1)} %after.7.refs_2_, ...), custom_call_target="tpu_custom_call", output_to_operand_aliasing={{0}: (4, {}), {1}: (5, {}), {2}: (6, {})} | custom-call | tf_op jit(solution)/shard_map/attend/pallas_call | solution.py:123
  86.5 2.4 %collective-permute-done.12.refs_5_.refs_3_ = bf16[576,256]{1,0:T(8,128)(2,1)S(1)} collective-permute-done((bf16[576,256]{1,0:T(8,128)(2,1)S(1)}, bf16[576,256]{1,0:T(8,128)(2,1)S(1)}, u32[]{:S(2)}, u32[]{:S(2)}) %collective-permute-start.12) | collective-permute-done | bytes 294944 | tf_op jit(solution)/shard_map/ppermute | solution.py:362
  88.9 2.4 %attend.11 = bf16[656,512]{1,0:T(8,128)(2,1)S(1)} custom-call(s32[4]{0:T(128)S(1)} %select_reduce_fusion.refs_0_, bf16[640,640]{1,0:T(8,128)(2,1)S(1)} %after.10.refs_1_, bf16[576,256]{1,0:T(8,128)(2,1)S(1)} %after.11.refs_4_.refs_2_, bf16[576,256]{1,0:T(8,128)(2,1)S(1)} %collective-permute-done.12.refs_5_.refs_3_, ...), custom_call_target="tpu_custom_call" | custom-call | tf_op jit(solution)/shard_map/attend/pallas_call | solution.py:123
  91.2 1.2 %collective-permute-start.13 = (bf16[656,512]{1,0:T(8,128)(2,1)S(1)}, bf16[656,512]{1,0:T(8,128)(2,1)S(1)}, u32[]{:S(2)}, u32[]{:S(2)}) collective-permute-start(bf16[656,512]{1,0:T(8,128)(2,1)S(1)} %attend.11), channel_id=1, source_target_pairs={{0,8},{4,12},{8,0},{12,4},{16,24},{20,28},{24,16},{28,20},{1,9},{5... | collective-permute-start | bytes 2015240 | tf_op jit(solution)/shard_map/ppermute | solution.py:362
  92.5 1.5 %fusion = bf16[1024,576]{0,1:T(8,128)(2,1)} fusion(bf16[1024,576]{0,1:T(8,128)(2,1)S(1)} %copy-done, pred[1024]{0:T(1024)(128)(4,1)S(1)} %fusion.1, s32[32]{0:T(128)S(1)} %compare_select_fusion, bf16[128,576]{1,0:T(8,128)(2,1)S(1)} %get-tuple-element.33.refs_3_), kind=kOutput, calls=%fused_computation.1 | convolution fusion | flops 38961152 | bytes 2401792 | tf_op jit(solution)/shard_map/dot_general | solution.py:410
  94.0 4.2 %attend.9 = (f32[640,128]{1,0:T(8,128)S(1)}, f32[640,128]{1,0:T(8,128)S(1)}, f32[640,512]{1,0:T(8,128)S(1)}) custom-call(s32[4]{0:T(128)S(1)} %select_reduce_fusion.refs_0_, bf16[640,640]{1,0:T(8,128)(2,1)S(1)} %get-tuple-element.30.refs_1_, bf16[576,384]{1,0:T(8,128)(2,1)S(1)} %after.7.refs_2_, ...), custom_call_target="tpu_custom_call", output_to_operand_aliasing={{0}: (6, {}), {1}: (7, {}), {2}: (8, {})} | custom-call | tf_op jit(solution)/shard_map/attend/pallas_call | solution.py:123
  98.3 7.5 %collective-permute-done.13.far_ref = bf16[656,512]{1,0:T(8,128)(2,1)S(1)} collective-permute-done((bf16[656,512]{1,0:T(8,128)(2,1)S(1)}, bf16[656,512]{1,0:T(8,128)(2,1)S(1)}, u32[]{:S(2)}, u32[]{:S(2)}) %collective-permute-start.13) | collective-permute-done | bytes 671776 | tf_op jit(solution)/shard_map/ppermute | solution.py:362
  105.8 1.2 %finish.1 = (bf16[32,2048]{1,0:T(8,128)(2,1)}, bf16[8,2048]{1,0:T(8,128)(2,1)}) custom-call(f32[640,128]{1,0:T(8,128)S(1)} %get-tuple-element.43.m_ref, f32[640,128]{1,0:T(8,128)S(1)} %get-tuple-element.44.l_ref, f32[640,512]{1,0:T(8,128)S(1)} %get-tuple-element.45.acc_ref, bf16[656,512]{1,0:T(8,128)(2,1)S(1)} %collective-permute-done.13.far_ref, ...), custom_call_target="tpu_custom_call" | custom-call | flops 83886080 | bytes 4063232 | tf_op jit(solution)/shard_map/finish/pallas_call | solution.py:335
  (42 shorter events, 0.8 us)
Async XLA Ops:
  0.6 14.3 %copy-start = (bf16[1024,576]{0,1:T(8,128)(2,1)S(1)}, bf16[1024,576]{0,1:T(8,128)(2,1)}, u32[]{:S(2)}) copy-start(bf16[1024,576]{0,1:T(8,128)(2,1)} %param.13) | copy-start | bytes 3538948
  2.5 7.6 %collective-permute-start = (bf16[4,4,4736]{2,1,0:T(4,128)(2,1)}, bf16[4,4,4736]{2,1,0:T(4,128)(2,1)S(1)}, u32[]{:S(2)}, u32[]{:S(2)}) collective-permute-start(bf16[4,4,4736]{2,1,0:T(4,128)(2,1)} %get-tuple-element.29), channel_id=1, source_target_pairs={{0,4},{4,0},{8,12},{12,8},{16,20},{20,16},{24,28},{28,24},{1,5},{5... | collective-permute-start | bytes 454664 | tf_op jit(solution)/shard_map/ppermute | solution.py:362
  6.5 31.2 %collective-permute-start.4 = (bf16[576,384]{1,0:T(8,128)(2,1)S(1)}, bf16[576,384]{1,0:T(8,128)(2,1)S(1)}, u32[]{:S(2)}, u32[]{:S(2)}) collective-permute-start(bf16[576,384]{1,0:T(8,128)(2,1)S(1)} %slice.44), channel_id=1, source_target_pairs={{0,16},{4,20},{8,24},{12,28},{16,0},{20,4},{24,8},{28,12},{1,17},{... | collective-permute-start | bytes 1327112 | tf_op jit(solution)/shard_map/ppermute | solution.py:362
  10.1 25.0 %copy-start.1 = (bf16[16,128,512]{2,1,0:T(8,128)(2,1)S(1)}, bf16[16,128,512]{2,1,0:T(8,128)(2,1)}, u32[]{:S(2)}) copy-start(bf16[16,128,512]{2,1,0:T(8,128)(2,1)} %w_hbm.1) | copy-start | bytes 6291460
  10.2 13.0 %collective-permute-start.3 = (bf16[2,4,4736]{2,1,0:T(4,128)(2,1)S(1)}, bf16[2,4,4736]{2,1,0:T(4,128)(2,1)S(1)}, u32[]{:S(2)}, u32[]{:S(2)}) collective-permute-start(bf16[2,4,4736]{2,1,0:T(4,128)(2,1)S(1)} %pad_maximum_fusion.3), channel_id=1, source_target_pairs={{0,24},{4,28},{8,16},{12,20},{16,8},{20,12},{24,0},{28,4},{1,25},{... | collective-permute-start | bytes 227336 | tf_op jit(solution)/shard_map/ppermute | solution.py:362
  13.7 21.4 %collective-permute-start.2 = (bf16[2,4,4736]{2,1,0:T(4,128)(2,1)S(1)}, bf16[2,4,4736]{2,1,0:T(4,128)(2,1)S(1)}, u32[]{:S(2)}, u32[]{:S(2)}) collective-permute-start(bf16[2,4,4736]{2,1,0:T(4,128)(2,1)S(1)} %pad_maximum_fusion.2), channel_id=1, source_target_pairs={{0,16},{4,20},{8,24},{12,28},{16,0},{20,4},{24,8},{28,12},{1,17},{... | collective-permute-start | bytes 227336 | tf_op jit(solution)/shard_map/ppermute | solution.py:362
  13.8 21.2 %collective-permute-start.1 = (bf16[2,4,4736]{2,1,0:T(4,128)(2,1)S(1)}, bf16[2,4,4736]{2,1,0:T(4,128)(2,1)S(1)}, u32[]{:S(2)}, u32[]{:S(2)}) collective-permute-start(bf16[2,4,4736]{2,1,0:T(4,128)(2,1)S(1)} %pad_maximum_fusion.1), channel_id=1, source_target_pairs={{0,8},{4,12},{8,0},{12,4},{16,24},{20,28},{24,16},{28,20},{1,9},{5... | collective-permute-start | bytes 227336 | tf_op jit(solution)/shard_map/ppermute | solution.py:362
  15.1 22.0 %copy-start.5 = (s32[8]{0:T(128)S(1)}, s32[8]{0:T(128)}, u32[]{:S(2)}) copy-start(s32[8]{0:T(128)} %param.19) | copy-start | bytes 100
  15.1 24.2 %collective-permute-start.5 = (bf16[576,384]{1,0:T(8,128)(2,1)S(1)}, bf16[576,384]{1,0:T(8,128)(2,1)S(1)}, u32[]{:S(2)}, u32[]{:S(2)}) collective-permute-start(bf16[576,384]{1,0:T(8,128)(2,1)S(1)} %get-tuple-element.32), channel_id=1, source_target_pairs={{0,4},{4,0},{8,12},{12,8},{16,20},{20,16},{24,28},{28,24},{1,5},{5... | collective-permute-start | bytes 1327112 | tf_op jit(solution)/shard_map/ppermute | solution.py:362
  36.4 37.9 %collective-permute-start.10 = (bf16[640,640]{1,0:T(8,128)(2,1)S(1)}, bf16[640,640]{1,0:T(8,128)(2,1)S(1)}, u32[]{:S(2)}, u32[]{:S(2)}) collective-permute-start(bf16[640,640]{1,0:T(8,128)(2,1)S(1)} %get-tuple-element.30.refs_1_), channel_id=1, source_target_pairs={{0,8},{4,12},{8,0},{12,4},{16,24},{20,28},{24,16},{28,20},{1,9},{5... | collective-permute-start | bytes 2457608 | tf_op jit(solution)/shard_map/ppermute | solution.py:362
  37.2 5.5 %copy-start.6 = (s32[8]{0:T(128)S(1)}, s32[8]{0:T(128)}, u32[]{:S(2)}) copy-start(s32[8]{0:T(128)} %param.16) | copy-start | bytes 100
  37.2 31.6 %collective-permute-start.11 = (bf16[576,640]{1,0:T(8,128)(2,1)S(1)}, bf16[576,640]{1,0:T(8,128)(2,1)S(1)}, u32[]{:S(2)}, u32[]{:S(2)}) collective-permute-start(bf16[576,640]{1,0:T(8,128)(2,1)S(1)} %after.9), channel_id=1, source_target_pairs={{0,4},{4,0},{8,12},{12,8},{16,20},{20,16},{24,28},{28,24},{1,5},{5... | collective-permute-start | bytes 2211848 | tf_op jit(solution)/shard_map/ppermute | solution.py:362
  37.7 27.1 %collective-permute-start.8 = (bf16[576,384]{1,0:T(8,128)(2,1)S(1)}, bf16[576,384]{1,0:T(8,128)(2,1)S(1)}, u32[]{:S(2)}, u32[]{:S(2)}) collective-permute-start(bf16[576,384]{1,0:T(8,128)(2,1)S(1)} %collective-permute-done.4.refs_0_.refs_4_.refs_5_), channel_id=1, source_target_pairs={{0,4},{4,0},{8,12},{12,8},{16,20},{20,16},{24,28},{28,24},{1,5},{5... | collective-permute-start | bytes 1327112 | tf_op jit(solution)/shard_map/ppermute | solution.py:362
  39.2 25.6 %collective-permute-start.6 = (bf16[576,384]{1,0:T(8,128)(2,1)S(1)}, bf16[576,384]{1,0:T(8,128)(2,1)S(1)}, u32[]{:S(2)}, u32[]{:S(2)}) collective-permute-start(bf16[576,384]{1,0:T(8,128)(2,1)S(1)} %after.6), channel_id=1, source_target_pairs={{0,16},{4,20},{8,24},{12,28},{16,0},{20,4},{24,8},{28,12},{1,17},{... | collective-permute-start | bytes 1327112 | tf_op jit(solution)/shard_map/ppermute | solution.py:362
  64.8 16.8 %collective-permute-start.9 = (bf16[576,256]{1,0:T(8,128)(2,1)S(1)}, bf16[576,256]{1,0:T(8,128)(2,1)S(1)}, u32[]{:S(2)}, u32[]{:S(2)}) collective-permute-start(bf16[576,256]{1,0:T(8,128)(2,1)S(1)} %after.8), channel_id=1, source_target_pairs={{0,16},{4,20},{8,24},{12,28},{16,0},{20,4},{24,8},{28,12},{1,17},{... | collective-permute-start | bytes 884744 | tf_op jit(solution)/shard_map/ppermute | solution.py:362
  68.2 15.0 %collective-permute-start.7 = (bf16[576,384]{1,0:T(8,128)(2,1)S(1)}, bf16[576,384]{1,0:T(8,128)(2,1)S(1)}, u32[]{:S(2)}, u32[]{:S(2)}) collective-permute-start(bf16[576,384]{1,0:T(8,128)(2,1)S(1)} %after.7.refs_2_), channel_id=1, source_target_pairs={{0,4},{4,0},{8,12},{12,8},{16,20},{20,16},{24,28},{28,24},{1,5},{5... | collective-permute-start | bytes 1327112 | tf_op jit(solution)/shard_map/ppermute | solution.py:362
  81.6 7.3 %collective-permute-start.12 = (bf16[576,256]{1,0:T(8,128)(2,1)S(1)}, bf16[576,256]{1,0:T(8,128)(2,1)S(1)}, u32[]{:S(2)}, u32[]{:S(2)}) collective-permute-start(bf16[576,256]{1,0:T(8,128)(2,1)S(1)} %after.11.refs_4_.refs_2_), channel_id=1, source_target_pairs={{0,4},{4,0},{8,12},{12,8},{16,20},{20,16},{24,28},{28,24},{1,5},{5... | collective-permute-start | bytes 884744 | tf_op jit(solution)/shard_map/ppermute | solution.py:362
  88.9 3.5 %copy-start.3 = (s32[32]{0:T(128)S(1)}, s32[32]{0:T(128)}, u32[]{:S(2)}) copy-start(s32[32]{0:T(128)} %param.18) | copy-start | bytes 388
  88.9 3.5 %copy-start.4 = (s32[32]{0:T(128)S(1)}, s32[32]{0:T(128)}, u32[]{:S(2)}) copy-start(s32[32]{0:T(128)} %param.17) | copy-start | bytes 388
  91.2 14.6 %collective-permute-start.13 = (bf16[656,512]{1,0:T(8,128)(2,1)S(1)}, bf16[656,512]{1,0:T(8,128)(2,1)S(1)}, u32[]{:S(2)}, u32[]{:S(2)}) collective-permute-start(bf16[656,512]{1,0:T(8,128)(2,1)S(1)} %attend.11), channel_id=1, source_target_pairs={{0,8},{4,12},{8,0},{12,4},{16,24},{20,28},{24,16},{28,20},{1,9},{5... | collective-permute-start | bytes 2015240 | tf_op jit(solution)/shard_map/ppermute | solution.py:362
  94.0 11.8 %copy-start.2 = (bf16[16,512,128]{2,1,0:T(8,128)(2,1)S(1)}, bf16[16,512,128]{2,1,0:T(8,128)(2,1)}, u32[]{:S(2)}) copy-start(bf16[16,512,128]{2,1,0:T(8,128)(2,1)} %w_ref.1) | copy-start | bytes 6291460

commit v7 on v6

--- a/solution.py
+++ b/solution.py
@@ -261,12 +261,12 @@
     extra_ref[...] = jnp.concatenate([new[:, :row], blank], axis=0).astype(jnp.bfloat16)
 
 
-def absorb(count, per_dec, me, order, got, w_uk, row):
+def absorb(count, per_dec, me, order, got, w_uk, row, tokens):
     heads = w_uk.shape[0]
     n = sum(len(x) for x in order)
     return pl.pallas_call(
         functools.partial(absorb_kernel, per_dec, order),
-        in_specs=[pl.BlockSpec(memory_space=pltpu.SMEM)] + [ANY] * (1 + len(got)),
+        in_specs=[pl.BlockSpec(memory_space=pltpu.SMEM)] + [ANY] * (1 + len(got) + len(tokens)),
         out_shape=[
             jax.ShapeDtypeStruct((heads * count, -(-row // LANES) * LANES), jnp.bfloat16),
             jax.ShapeDtypeStruct((LANES, row), jnp.bfloat16),
@@ -279,7 +279,7 @@
         ],
         compiler_params=room(16),
         name="absorb",
-    )(me, w_uk, *got)
+    )(me, w_uk, *got, *tokens)
 
 
 def split_kernel(spans, x_ref, *refs):
@@ -364,7 +364,7 @@
     far, pair = n // 2, n // 4
     near = [1 << b for b in range(pair.bit_length() - 1)]
     keys = cache_kv.T
-    edges = [0, pos_dev // 8 * 3, pos_dev // 4 * 3, pos_dev]
+    edges = [0, pos_dev // 4, pos_dev // 8 * 5, pos_dev]
 
     lead = keys[:, : edges[1]]
     pieces = [swap(lead, far)]
@@ -387,17 +387,23 @@
         order.append([r ^ o for o, _ in groups[r]])
     got = got[:1] + [swap(x, r) for r, x in zip(sorted(groups)[1:], got[1:])]
 
-    middle = edges[1]
+    middle = pos_dev // 2
     *cuts, early, late = split(
         keys, [*zip(edges[1:], edges[2:]), (0, middle), (middle, pos_dev)], [come]
     )
-    halves = [(0, early, after(late, *got[1:]))]
+    early, late = [(0, early)], [(0, late)]
     for stride in near:
-        halves += [(o ^ stride, swap(x, stride), swap(y, stride)) for o, x, y in halves]
-    absorbed, extra = absorb(count, rows_dec // n, place, order, got, w_uk, row)
+        early += [(o ^ stride, swap(x, stride)) for o, x in early]
+    absorbed, extra = absorb(
+        count, rows_dec // n, place, order, got, w_uk, row, pieces + [x for _, x in early[1:]]
+    )
     new_rows = extra[:span]
     other = swap(absorbed, pair)
-    pieces.append(swap(after(cuts[0], pieces[0], halves[-1][1], *got[1:]), far))
+    late[0] = (0, after(late[0][1], absorbed))
+    for stride in near:
+        late += [(o ^ stride, swap(x, stride)) for o, x in late]
+    halves = [(o, x, y) for (o, x), (_, y) in zip(early, late)]
+    pieces += [swap(after(x, absorbed), far) for x in cuts]
 
     def spread(x):
         part = [(far, x)]
@@ -437,14 +443,14 @@
     home = [(0, 0, keys)]
     side = [(a, i, z) for i, (_, x, y) in enumerate(halves) if i for a, z in ((0, x), (middle, y))]
     state = attend(fills, absorbed, home, tile, new=(extra, bias))
-    part = spread(pieces[0])
-    side += stage_of(0, part)
-    pieces.append(swap(after(cuts[1], state[0], pieces[1], part[-1][1]), far))
+    side += stage_of(0, spread(pieces[0]))
+    state = attend(fills, absorbed, side, tile, state=state)
     first = stage_of(1, spread(after(pieces[1], state[0])))
-    state = attend(fills, absorbed, side, tile, state=state)
-    other = after(other, state[0])
+    other = after(other, state[0], pieces[1])
     guest = attend(fills, other, home + side, tile)
     second = stage_of(2, spread(after(pieces[2], guest[0])))
+    first, second = first + second[:1], second[1:]
+    other = after(other, pieces[2])
     guest = attend(fills, other, first, tile, state=guest)
     sent = attend(fills, other, second, tile, state=guest, last=True)
     back = swap(sent, pair)

time: 107 us -> 105 us (0.981)
  starting transfers between devices: 24.3 us -> 19.2 us
  local copies, waits for them, and re-layouts: 2.03 us -> 5.32 us
  Pallas kernels: 30.7 us -> 29.1 us
    ppermute x14, starting transfers between devices: 24.3 us -> 19.2 us  [swap(): return lax.ppermute(x, 'seq', [(i, i ^ stride) for i in range(n)])]
    unnamed x14 -> x36, local copies, waits for them, and re-layouts: 0.03 us -> 3.4 us
    pallas_call x6, Pallas kernels: 26.2 us -> 24.6 us  [attend(): pl.pallas_call(functools.partial(attend_kernel, spec, new is not None, st...]
  transfers between devices with their start and end apart: 14 -> 14, of which waited for: 5 -> 8; matrix products, arithmetic and copies ran while one was open for 4% -> 4% of each run, Pallas kernels for 24% -> 22%
where the time goes in v7:
time: 105 us
  waiting for transfers between devices  47.9 us (46%)
  Pallas kernels  29.1 us (28%)
  starting transfers between devices  19.2 us (18%)
  local copies, waits for them, and re-layouts  5.32 us (5%)
  matrix products  1.54 us (1%)
    ppermute x14, waiting for transfers between devices, swap(): return lax.ppermute(x, 'seq', [(i, i ^ stride) for i in range(n)])  47.9 us
    pallas_call x6, Pallas kernels, attend(): pl.pallas_call(functools.partial(attend_kernel, spec, new is not None, st...  24.6 us
    ppermute x14, starting transfers between devices, swap(): return lax.ppermute(x, 'seq', [(i, i ^ stride) for i in range(n)])  19.2 us
    unnamed x36, local copies, waits for them, and re-layouts  3.4 us
  transfers between devices with their start and end apart: 14, of which 8 were waited for; matrix products, arithmetic and copies ran while one was open for 4% of the time, Pallas kernels for 22%

profile of v7, /device:TPU:0, one launch (start us, length us, event | category | flops | bytes accessed | tf_op | source)
XLA Modules:
  0.0 104.7 jit_solution(6915367655053296513)
XLA Ops:
  0.6 1.9 %pack.1 = (bf16[4,4,4736]{2,1,0:T(4,128)(2,1)}, bf16[4,4,4736]{2,1,0:T(4,128)(2,1)}) custom-call(s32[1]{0:T(128)} %bitcast.me_ref, bf16[4,24576]{1,0:T(4,128)(2,1)} %query_ref.1, bf16[1,24576]{1,0:T(2,128)(2,1)} %dec_ref.1, bf16[4,576]{1,0:T(4,128)(2,1)} %span_kv_ref.1, bf16[1,576]{1,0:T(2,128)(2,1)} %dec_kv_ref.1), custom_call_target="tpu_custom_call" | custom-call | tf_op jit(solution)/shard_map/pack/pallas_call | solution.py:196
  2.5 2.9 %collective-permute-start = (bf16[4,4,4736]{2,1,0:T(4,128)(2,1)}, bf16[4,4,4736]{2,1,0:T(4,128)(2,1)S(1)}, u32[]{:S(2)}, u32[]{:S(2)}) collective-permute-start(bf16[4,4,4736]{2,1,0:T(4,128)(2,1)} %get-tuple-element.29), channel_id=1, source_target_pairs={{0,4},{4,0},{8,12},{12,8},{16,20},{20,16},{24,28},{28,24},{1,5},{5... | collective-permute-start | bytes 454664 | tf_op jit(solution)/shard_map/ppermute | solution.py:362
  5.4 1.0 slice.44
  6.4 2.7 %collective-permute-start.4 = (bf16[576,256]{1,0:T(8,128)(2,1)S(1)}, bf16[576,256]{1,0:T(8,128)(2,1)S(1)}, u32[]{:S(2)}, u32[]{:S(2)}) collective-permute-start(bf16[576,256]{1,0:T(8,128)(2,1)S(1)} %slice.44), channel_id=1, source_target_pairs={{0,16},{4,20},{8,24},{12,28},{16,0},{20,4},{24,8},{28,12},{1,17},{... | collective-permute-start | bytes 884744 | tf_op jit(solution)/shard_map/ppermute | solution.py:362
  9.1 0.9 fusion.8
  10.1 3.5 %collective-permute-start.3 = (bf16[2,4,4736]{2,1,0:T(4,128)(2,1)S(1)}, bf16[2,4,4736]{2,1,0:T(4,128)(2,1)S(1)}, u32[]{:S(2)}, u32[]{:S(2)}) collective-permute-start(bf16[2,4,4736]{2,1,0:T(4,128)(2,1)S(1)} %pad_maximum_fusion.3), channel_id=1, source_target_pairs={{0,24},{4,28},{8,16},{12,20},{16,8},{20,12},{24,0},{28,4},{1,25},{... | collective-permute-start | bytes 227336 | tf_op jit(solution)/shard_map/ppermute | solution.py:362
  13.9 0.8 copy-done.5
  14.8 1.5 %collective-permute-start.5 = (bf16[576,512]{1,0:T(8,128)(2,1)S(1)}, bf16[576,512]{1,0:T(8,128)(2,1)S(1)}, u32[]{:S(2)}, u32[]{:S(2)}) collective-permute-start(bf16[576,512]{1,0:T(8,128)(2,1)S(1)} %get-tuple-element.30), channel_id=1, source_target_pairs={{0,4},{4,0},{8,12},{12,8},{16,20},{20,16},{24,28},{28,24},{1,5},{5... | collective-permute-start | bytes 1769480 | tf_op jit(solution)/shard_map/ppermute | solution.py:362
  16.3 0.8 collective-permute-start.1
  17.2 2.2 %collective-permute-done.3.refs_3_ = bf16[2,4,4736]{2,1,0:T(4,128)(2,1)S(1)} collective-permute-done((bf16[2,4,4736]{2,1,0:T(4,128)(2,1)S(1)}, bf16[2,4,4736]{2,1,0:T(4,128)(2,1)S(1)}, u32[]{:S(2)}, u32[]{:S(2)}) %collective-permute-start.3) | collective-permute-done | bytes 75808 | tf_op jit(solution)/shard_map/ppermute | solution.py:362
  19.4 9.3 %collective-permute-done.2.refs_2_ = bf16[2,4,4736]{2,1,0:T(4,128)(2,1)S(1)} collective-permute-done((bf16[2,4,4736]{2,1,0:T(4,128)(2,1)S(1)}, bf16[2,4,4736]{2,1,0:T(4,128)(2,1)S(1)}, u32[]{:S(2)}, u32[]{:S(2)}) %collective-permute-start.2) | collective-permute-done | bytes 75808 | tf_op jit(solution)/shard_map/ppermute | solution.py:362
  28.8 1.3 %absorb.1 = (bf16[640,640]{1,0:T(8,128)(2,1)S(1)}, bf16[128,576]{1,0:T(8,128)(2,1)S(1)}) custom-call(s32[1]{0:T(128)} %bitcast.me_ref, bf16[16,128,512]{2,1,0:T(8,128)(2,1)S(1)} %copy-done.3, bf16[2,4,4736]{2,1,0:T(4,128)(2,1)S(1)} %pad_maximum_fusion.refs_0_, bf16[2,4,4736]{2,1,0:T(4,128)(2,1)S(1)} %collective-permute-done.1.refs_1_, ...), custom_call_target="tpu_custom_call" | custom-call | tf_op jit(solution)/shard_map/absorb/pallas_call | solution.py:267
  30.7 0.9 collective-permute-start.11
  31.6 1.1 %copy-done.6 = bf16[576,512]{1,0:T(8,128)(2,1)S(1)} copy-done((bf16[576,512]{1,0:T(8,128)(2,1)S(1)}, bf16[576,512]{1,0:T(8,128)(2,1)}, u32[]{:S(2)}) %copy-start.6) | copy-done | bytes 589848
  32.7 0.8 copy-done.7
  33.5 1.1 %collective-permute-start.7 = (bf16[576,512]{1,0:T(8,128)(2,1)}, bf16[576,512]{1,0:T(8,128)(2,1)S(1)}, u32[]{:S(2)}, u32[]{:S(2)}) collective-permute-start(bf16[576,512]{1,0:T(8,128)(2,1)} %copy-done.7), channel_id=1, source_target_pairs={{0,4},{4,0},{8,12},{12,8},{16,20},{20,16},{24,28},{28,24},{1,5},{5... | collective-permute-start | bytes 1769480 | tf_op jit(solution)/shard_map/ppermute | solution.py:362
  34.9 2.7 %collective-permute-start.6 = (bf16[576,384]{1,0:T(8,128)(2,1)S(1)}, bf16[576,384]{1,0:T(8,128)(2,1)S(1)}, u32[]{:S(2)}, u32[]{:S(2)}) collective-permute-start(bf16[576,384]{1,0:T(8,128)(2,1)S(1)} %after.7), channel_id=1, source_target_pairs={{0,16},{4,20},{8,24},{12,28},{16,0},{20,4},{24,8},{28,12},{1,17},{... | collective-permute-start | bytes 1327112 | tf_op jit(solution)/shard_map/ppermute | solution.py:362
  37.9 1.2 %collective-permute-start.8 = (bf16[576,256]{1,0:T(8,128)(2,1)S(1)}, bf16[576,256]{1,0:T(8,128)(2,1)S(1)}, u32[]{:S(2)}, u32[]{:S(2)}) collective-permute-start(bf16[576,256]{1,0:T(8,128)(2,1)S(1)} %copy-done.2), channel_id=1, source_target_pairs={{0,4},{4,0},{8,12},{12,8},{16,20},{20,16},{24,28},{28,24},{1,5},{5... | collective-permute-start | bytes 884744 | tf_op jit(solution)/shard_map/ppermute | solution.py:362
  39.3 3.4 %attend.6 = (f32[640,128]{1,0:T(8,128)S(1)}, f32[640,128]{1,0:T(8,128)S(1)}, f32[640,512]{1,0:T(8,128)S(1)}) custom-call(s32[4]{0:T(128)S(1)} %select_reduce_fusion.refs_0_, bf16[640,640]{1,0:T(8,128)(2,1)S(1)} %get-tuple-element.31.refs_0_.refs_1_, bf16[576,1024]{1,0:T(8,128)(2,1)S(1)} %bitcast.7, bf16[128,576]{1,0:T(8,128)(2,1)S(1)} %copy-done.13, ...), custom_call_target="tpu_custom_call" | custom-call | tf_op jit(solution)/shard_map/attend/pallas_call | solution.py:123
  42.7 12.1 %collective-permute-done.8.refs_5_.refs_6_ = bf16[576,256]{1,0:T(8,128)(2,1)S(1)} collective-permute-done((bf16[576,256]{1,0:T(8,128)(2,1)S(1)}, bf16[576,256]{1,0:T(8,128)(2,1)S(1)}, u32[]{:S(2)}, u32[]{:S(2)}) %collective-permute-start.8) | collective-permute-done | bytes 294944 | tf_op jit(solution)/shard_map/ppermute | solution.py:362
  54.8 4.2 %attend.7 = (f32[640,128]{1,0:T(8,128)S(1)}, f32[640,128]{1,0:T(8,128)S(1)}, f32[640,512]{1,0:T(8,128)S(1)}) custom-call(s32[4]{0:T(128)S(1)} %select_reduce_fusion.refs_0_, bf16[640,640]{1,0:T(8,128)(2,1)S(1)} %get-tuple-element.31.refs_0_.refs_1_, ...), custom_call_target="tpu_custom_call", output_to_operand_aliasing={{0}: (6, {}), {1}: (7, {}), {2}: (8, {})} | custom-call | tf_op jit(solution)/shard_map/attend/pallas_call | solution.py:123
  59.8 4.8 %collective-permute-done.11.x_ref = bf16[640,640]{1,0:T(8,128)(2,1)S(1)} collective-permute-done((bf16[640,640]{1,0:T(8,128)(2,1)S(1)}, bf16[640,640]{1,0:T(8,128)(2,1)S(1)}, u32[]{:S(2)}, u32[]{:S(2)}) %collective-permute-start.11) | collective-permute-done | bytes 819232 | tf_op jit(solution)/shard_map/ppermute | solution.py:362
  64.6 5.6 %attend.8 = (f32[640,128]{1,0:T(8,128)S(1)}, f32[640,128]{1,0:T(8,128)S(1)}, f32[640,512]{1,0:T(8,128)S(1)}) custom-call(s32[4]{0:T(128)S(1)} %select_reduce_fusion.refs_0_, bf16[640,640]{1,0:T(8,128)(2,1)S(1)} %after.11.refs_1_.x_ref, bf16[576,1024]{1,0:T(8,128)(2,1)S(1)} %bitcast.8, bf16[576,512]{1,0:T(8,128)(2,1)S(1)} %collective-permute-done.5.refs_5_.refs_2_.refs_3_, ...), custom_call_target="tpu_custom_call" | custom-call | tf_op jit(solution)/shard_map/attend/pallas_call | solution.py:123
  70.2 5.6 %collective-permute-done.10.x_ref.refs_0_ = bf16[576,384]{1,0:T(8,128)(2,1)S(1)} collective-permute-done((bf16[576,384]{1,0:T(8,128)(2,1)S(1)}, bf16[576,384]{1,0:T(8,128)(2,1)S(1)}, u32[]{:S(2)}, u32[]{:S(2)}) %collective-permute-start.10) | collective-permute-done | bytes 442400 | tf_op jit(solution)/shard_map/ppermute | solution.py:362
  75.8 1.5 %collective-permute-start.12 = (bf16[576,384]{1,0:T(8,128)(2,1)S(1)}, bf16[576,384]{1,0:T(8,128)(2,1)S(1)}, u32[]{:S(2)}, u32[]{:S(2)}) collective-permute-start(bf16[576,384]{1,0:T(8,128)(2,1)S(1)} %after.12.refs_4_), channel_id=1, source_target_pairs={{0,4},{4,0},{8,12},{12,8},{16,20},{20,16},{24,28},{28,24},{1,5},{5... | collective-permute-start | bytes 1327112 | tf_op jit(solution)/shard_map/ppermute | solution.py:362
  77.3 4.3 %attend.10 = (f32[640,128]{1,0:T(8,128)S(1)}, f32[640,128]{1,0:T(8,128)S(1)}, f32[640,512]{1,0:T(8,128)S(1)}) custom-call(s32[4]{0:T(128)S(1)} %select_reduce_fusion.refs_0_, bf16[640,640]{1,0:T(8,128)(2,1)S(1)} %after.13.refs_1_, bf16[576,384]{1,0:T(8,128)(2,1)S(1)} %after.9.refs_2_, ...), custom_call_target="tpu_custom_call", output_to_operand_aliasing={{0}: (5, {}), {1}: (6, {}), {2}: (7, {})} | custom-call | tf_op jit(solution)/shard_map/attend/pallas_call | solution.py:123
  81.6 4.9 %collective-permute-done.12.refs_5_.refs_2_ = bf16[576,384]{1,0:T(8,128)(2,1)S(1)} collective-permute-done((bf16[576,384]{1,0:T(8,128)(2,1)S(1)}, bf16[576,384]{1,0:T(8,128)(2,1)S(1)}, u32[]{:S(2)}, u32[]{:S(2)}) %collective-permute-start.12) | collective-permute-done | bytes 442400 | tf_op jit(solution)/shard_map/ppermute | solution.py:362
  86.6 2.2 %attend.11 = bf16[656,512]{1,0:T(8,128)(2,1)S(1)} custom-call(s32[4]{0:T(128)S(1)} %select_reduce_fusion.refs_0_, bf16[640,640]{1,0:T(8,128)(2,1)S(1)} %after.13.refs_1_, bf16[576,384]{1,0:T(8,128)(2,1)S(1)} %collective-permute-done.12.refs_5_.refs_2_, f32[640,128]{1,0:T(8,128)S(1)} %get-tuple-element.48.refs_3_, f32[640,128]{1,0:T(8,128)S(1)} %get-tuple-element.49.refs_4_, ...), custom_call_target="tpu_custom_call" | custom-call | tf_op jit(solution)/shard_map/attend/pallas_call | solution.py:123
  89.0 1.5 %fusion = bf16[1024,576]{0,1:T(8,128)(2,1)} fusion(bf16[1024,576]{0,1:T(8,128)(2,1)S(1)} %copy-done, pred[1024]{0:T(1024)(128)(4,1)S(1)} %fusion.1, s32[32]{0:T(128)S(1)} %compare_select_fusion, bf16[128,576]{1,0:T(8,128)(2,1)S(1)} %copy-done.13), kind=kOutput, calls=%fused_computation.1 | convolution fusion | flops 38961152 | bytes 2401792 | tf_op jit(solution)/shard_map/dot_general | solution.py:416
  90.5 4.9 %attend.9 = (f32[640,128]{1,0:T(8,128)S(1)}, f32[640,128]{1,0:T(8,128)S(1)}, f32[640,512]{1,0:T(8,128)S(1)}) custom-call(s32[4]{0:T(128)S(1)} %select_reduce_fusion.refs_0_, bf16[640,640]{1,0:T(8,128)(2,1)S(1)} %get-tuple-element.31.refs_0_.refs_1_, bf16[576,384]{1,0:T(8,128)(2,1)S(1)} %after.9.refs_2_, ...), custom_call_target="tpu_custom_call", output_to_operand_aliasing={{0}: (6, {}), {1}: (7, {}), {2}: (8, {})} | custom-call | tf_op jit(solution)/shard_map/attend/pallas_call | solution.py:123
  95.4 8.1 %collective-permute-done.13.far_ref = bf16[656,512]{1,0:T(8,128)(2,1)S(1)} collective-permute-done((bf16[656,512]{1,0:T(8,128)(2,1)S(1)}, bf16[656,512]{1,0:T(8,128)(2,1)S(1)}, u32[]{:S(2)}, u32[]{:S(2)}) %collective-permute-start.13) | collective-permute-done | bytes 671776 | tf_op jit(solution)/shard_map/ppermute | solution.py:362
  103.5 1.2 %finish.1 = (bf16[32,2048]{1,0:T(8,128)(2,1)}, bf16[8,2048]{1,0:T(8,128)(2,1)}) custom-call(f32[640,128]{1,0:T(8,128)S(1)} %get-tuple-element.43.m_ref, f32[640,128]{1,0:T(8,128)S(1)} %get-tuple-element.44.l_ref, f32[640,512]{1,0:T(8,128)S(1)} %get-tuple-element.45.acc_ref, bf16[656,512]{1,0:T(8,128)(2,1)S(1)} %collective-permute-done.13.far_ref, ...), custom_call_target="tpu_custom_call" | custom-call | flops 83886080 | bytes 4063232 | tf_op jit(solution)/shard_map/finish/pallas_call | solution.py:335
  (65 shorter events, 2.9 us)
Async XLA Ops:
  0.6 13.1 %copy-start = (bf16[1024,576]{0,1:T(8,128)(2,1)S(1)}, bf16[1024,576]{0,1:T(8,128)(2,1)}, u32[]{:S(2)}) copy-start(bf16[1024,576]{0,1:T(8,128)(2,1)} %param.13) | copy-start | bytes 3538948
  2.5 7.5 %collective-permute-start = (bf16[4,4,4736]{2,1,0:T(4,128)(2,1)}, bf16[4,4,4736]{2,1,0:T(4,128)(2,1)S(1)}, u32[]{:S(2)}, u32[]{:S(2)}) collective-permute-start(bf16[4,4,4736]{2,1,0:T(4,128)(2,1)} %get-tuple-element.29), channel_id=1, source_target_pairs={{0,4},{4,0},{8,12},{12,8},{16,20},{20,16},{24,28},{28,24},{1,5},{5... | collective-permute-start | bytes 454664 | tf_op jit(solution)/shard_map/ppermute | solution.py:362
  6.4 22.3 %copy-start.3 = (bf16[16,128,512]{2,1,0:T(8,128)(2,1)S(1)}, bf16[16,128,512]{2,1,0:T(8,128)(2,1)}, u32[]{:S(2)}) copy-start(bf16[16,128,512]{2,1,0:T(8,128)(2,1)} %w_hbm.1) | copy-start | bytes 6291460
  6.4 22.3 %collective-permute-start.4 = (bf16[576,256]{1,0:T(8,128)(2,1)S(1)}, bf16[576,256]{1,0:T(8,128)(2,1)S(1)}, u32[]{:S(2)}, u32[]{:S(2)}) collective-permute-start(bf16[576,256]{1,0:T(8,128)(2,1)S(1)} %slice.44), channel_id=1, source_target_pairs={{0,16},{4,20},{8,24},{12,28},{16,0},{20,4},{24,8},{28,12},{1,17},{... | collective-permute-start | bytes 884744 | tf_op jit(solution)/shard_map/ppermute | solution.py:362
  10.1 9.3 %collective-permute-start.3 = (bf16[2,4,4736]{2,1,0:T(4,128)(2,1)S(1)}, bf16[2,4,4736]{2,1,0:T(4,128)(2,1)S(1)}, u32[]{:S(2)}, u32[]{:S(2)}) collective-permute-start(bf16[2,4,4736]{2,1,0:T(4,128)(2,1)S(1)} %pad_maximum_fusion.3), channel_id=1, source_target_pairs={{0,24},{4,28},{8,16},{12,20},{16,8},{20,12},{24,0},{28,4},{1,25},{... | collective-permute-start | bytes 227336 | tf_op jit(solution)/shard_map/ppermute | solution.py:362
  13.7 15.0 %collective-permute-start.2 = (bf16[2,4,4736]{2,1,0:T(4,128)(2,1)S(1)}, bf16[2,4,4736]{2,1,0:T(4,128)(2,1)S(1)}, u32[]{:S(2)}, u32[]{:S(2)}) collective-permute-start(bf16[2,4,4736]{2,1,0:T(4,128)(2,1)S(1)} %pad_maximum_fusion.2), channel_id=1, source_target_pairs={{0,16},{4,20},{8,24},{12,28},{16,0},{20,4},{24,8},{28,12},{1,17},{... | collective-permute-start | bytes 227336 | tf_op jit(solution)/shard_map/ppermute | solution.py:362
  13.9 0.8 copy-start.5
  14.8 15.3 %copy-start.8 = (bf16[576,384]{1,0:T(8,128)(2,1)}, bf16[576,384]{1,0:T(8,128)(2,1)S(1)}, u32[]{:S(2)}) copy-start(bf16[576,384]{1,0:T(8,128)(2,1)S(1)} %get-tuple-element.39.x_ref) | copy-start | bytes 1327108
  14.8 15.3 %copy-start.10 = (bf16[576,384]{1,0:T(8,128)(2,1)}, bf16[576,384]{1,0:T(8,128)(2,1)S(1)}, u32[]{:S(2)}) copy-start(bf16[576,384]{1,0:T(8,128)(2,1)S(1)} %get-tuple-element.32.x_ref) | copy-start | bytes 1327108
  14.8 14.0 %collective-permute-start.5 = (bf16[576,512]{1,0:T(8,128)(2,1)S(1)}, bf16[576,512]{1,0:T(8,128)(2,1)S(1)}, u32[]{:S(2)}, u32[]{:S(2)}) collective-permute-start(bf16[576,512]{1,0:T(8,128)(2,1)S(1)} %get-tuple-element.30), channel_id=1, source_target_pairs={{0,4},{4,0},{8,12},{12,8},{16,20},{20,16},{24,28},{28,24},{1,5},{5... | collective-permute-start | bytes 1769480 | tf_op jit(solution)/shard_map/ppermute | solution.py:362
  16.3 12.4 %collective-permute-start.1 = (bf16[2,4,4736]{2,1,0:T(4,128)(2,1)S(1)}, bf16[2,4,4736]{2,1,0:T(4,128)(2,1)S(1)}, u32[]{:S(2)}, u32[]{:S(2)}) collective-permute-start(bf16[2,4,4736]{2,1,0:T(4,128)(2,1)S(1)} %pad_maximum_fusion.1), channel_id=1, source_target_pairs={{0,8},{4,12},{8,0},{12,4},{16,24},{20,28},{24,16},{28,20},{1,9},{5... | collective-permute-start | bytes 227336 | tf_op jit(solution)/shard_map/ppermute | solution.py:362
  28.7 1.3 %copy-start.1 = (bf16[576,256]{1,0:T(8,128)(2,1)}, bf16[576,256]{1,0:T(8,128)(2,1)S(1)}, u32[]{:S(2)}) copy-start(bf16[576,256]{1,0:T(8,128)(2,1)S(1)} %collective-permute-done.4.refs_4_.refs_5_) | copy-start | bytes 884740
  30.1 0.7 copy-start.12
  30.7 3.9 %copy-start.16 = (s32[8]{0:T(128)S(1)}, s32[8]{0:T(128)}, u32[]{:S(2)}) copy-start(s32[8]{0:T(128)} %param.16) | copy-start | bytes 100
  30.7 33.9 %collective-permute-start.11 = (bf16[640,640]{1,0:T(8,128)(2,1)S(1)}, bf16[640,640]{1,0:T(8,128)(2,1)S(1)}, u32[]{:S(2)}, u32[]{:S(2)}) collective-permute-start(bf16[640,640]{1,0:T(8,128)(2,1)S(1)} %get-tuple-element.31.refs_0_.refs_1_), channel_id=1, source_target_pairs={{0,8},{4,12},{8,0},{12,4},{16,24},{20,28},{24,16},{28,20},{1,9},{5... | collective-permute-start | bytes 2457608 | tf_op jit(solution)/shard_map/ppermute | solution.py:362
  31.6 1.1 %copy-start.6 = (bf16[576,512]{1,0:T(8,128)(2,1)S(1)}, bf16[576,512]{1,0:T(8,128)(2,1)}, u32[]{:S(2)}) copy-start(bf16[576,512]{1,0:T(8,128)(2,1)} %copy-done.5) | copy-start | bytes 1769476
  32.7 2.2 %copy-start.11 = (bf16[576,384]{1,0:T(8,128)(2,1)S(1)}, bf16[576,384]{1,0:T(8,128)(2,1)}, u32[]{:S(2)}) copy-start(bf16[576,384]{1,0:T(8,128)(2,1)} %copy-done.10) | copy-start | bytes 1327108
  32.7 0.8 copy-start.7
  33.5 4.1 %copy-start.9 = (bf16[576,384]{1,0:T(8,128)(2,1)S(1)}, bf16[576,384]{1,0:T(8,128)(2,1)}, u32[]{:S(2)}) copy-start(bf16[576,384]{1,0:T(8,128)(2,1)} %copy-done.8) | copy-start | bytes 1327108
  33.5 21.3 %collective-permute-start.7 = (bf16[576,512]{1,0:T(8,128)(2,1)}, bf16[576,512]{1,0:T(8,128)(2,1)S(1)}, u32[]{:S(2)}, u32[]{:S(2)}) collective-permute-start(bf16[576,512]{1,0:T(8,128)(2,1)} %copy-done.7), channel_id=1, source_target_pairs={{0,4},{4,0},{8,12},{12,8},{16,20},{20,16},{24,28},{28,24},{1,5},{5... | collective-permute-start | bytes 1769480 | tf_op jit(solution)/shard_map/ppermute | solution.py:362
  34.9 3.0 %copy-start.2 = (bf16[576,256]{1,0:T(8,128)(2,1)S(1)}, bf16[576,256]{1,0:T(8,128)(2,1)}, u32[]{:S(2)}) copy-start(bf16[576,256]{1,0:T(8,128)(2,1)} %copy-done.1) | copy-start | bytes 884740
  34.9 4.3 %copy-start.17 = (s32[8]{0:T(128)S(1)}, s32[8]{0:T(128)}, u32[]{:S(2)}) copy-start(s32[8]{0:T(128)} %param.19) | copy-start | bytes 100
  34.9 4.4 %copy-start.13 = (bf16[128,576]{1,0:T(8,128)(2,1)S(1)}, bf16[128,576]{1,0:T(8,128)(2,1)}, u32[]{:S(2)}) copy-start(bf16[128,576]{1,0:T(8,128)(2,1)} %copy-done.12) | copy-start | bytes 442372
  34.9 24.9 %collective-permute-start.6 = (bf16[576,384]{1,0:T(8,128)(2,1)S(1)}, bf16[576,384]{1,0:T(8,128)(2,1)S(1)}, u32[]{:S(2)}, u32[]{:S(2)}) collective-permute-start(bf16[576,384]{1,0:T(8,128)(2,1)S(1)} %after.7), channel_id=1, source_target_pairs={{0,16},{4,20},{8,24},{12,28},{16,0},{20,4},{24,8},{28,12},{1,17},{... | collective-permute-start | bytes 1327112 | tf_op jit(solution)/shard_map/ppermute | solution.py:362
  37.6 38.3 %collective-permute-start.10 = (bf16[576,384]{1,0:T(8,128)(2,1)S(1)}, bf16[576,384]{1,0:T(8,128)(2,1)S(1)}, u32[]{:S(2)}, u32[]{:S(2)}) collective-permute-start(bf16[576,384]{1,0:T(8,128)(2,1)S(1)} %after.10), channel_id=1, source_target_pairs={{0,16},{4,20},{8,24},{12,28},{16,0},{20,4},{24,8},{28,12},{1,17},{... | collective-permute-start | bytes 1327112 | tf_op jit(solution)/shard_map/ppermute | solution.py:362
  37.9 16.9 %collective-permute-start.8 = (bf16[576,256]{1,0:T(8,128)(2,1)S(1)}, bf16[576,256]{1,0:T(8,128)(2,1)S(1)}, u32[]{:S(2)}, u32[]{:S(2)}) collective-permute-start(bf16[576,256]{1,0:T(8,128)(2,1)S(1)} %copy-done.2), channel_id=1, source_target_pairs={{0,4},{4,0},{8,12},{12,8},{16,20},{20,16},{24,28},{28,24},{1,5},{5... | collective-permute-start | bytes 884744 | tf_op jit(solution)/shard_map/ppermute | solution.py:362
  64.6 12.7 %collective-permute-start.9 = (bf16[576,384]{1,0:T(8,128)(2,1)S(1)}, bf16[576,384]{1,0:T(8,128)(2,1)S(1)}, u32[]{:S(2)}, u32[]{:S(2)}) collective-permute-start(bf16[576,384]{1,0:T(8,128)(2,1)S(1)} %after.9.refs_2_), channel_id=1, source_target_pairs={{0,4},{4,0},{8,12},{12,8},{16,20},{20,16},{24,28},{28,24},{1,5},{5... | collective-permute-start | bytes 1327112 | tf_op jit(solution)/shard_map/ppermute | solution.py:362
  75.8 10.7 %collective-permute-start.12 = (bf16[576,384]{1,0:T(8,128)(2,1)S(1)}, bf16[576,384]{1,0:T(8,128)(2,1)S(1)}, u32[]{:S(2)}, u32[]{:S(2)}) collective-permute-start(bf16[576,384]{1,0:T(8,128)(2,1)S(1)} %after.12.refs_4_), channel_id=1, source_target_pairs={{0,4},{4,0},{8,12},{12,8},{16,20},{20,16},{24,28},{28,24},{1,5},{5... | collective-permute-start | bytes 1327112 | tf_op jit(solution)/shard_map/ppermute | solution.py:362
  86.6 2.3 %copy-start.14 = (s32[32]{0:T(128)S(1)}, s32[32]{0:T(128)}, u32[]{:S(2)}) copy-start(s32[32]{0:T(128)} %param.18) | copy-start | bytes 388
  86.6 2.3 %copy-start.15 = (s32[32]{0:T(128)S(1)}, s32[32]{0:T(128)}, u32[]{:S(2)}) copy-start(s32[32]{0:T(128)} %param.17) | copy-start | bytes 388
  88.8 14.8 %collective-permute-start.13 = (bf16[656,512]{1,0:T(8,128)(2,1)S(1)}, bf16[656,512]{1,0:T(8,128)(2,1)S(1)}, u32[]{:S(2)}, u32[]{:S(2)}) collective-permute-start(bf16[656,512]{1,0:T(8,128)(2,1)S(1)} %attend.11), channel_id=1, source_target_pairs={{0,8},{4,12},{8,0},{12,4},{16,24},{20,28},{24,16},{28,20},{1,9},{5... | collective-permute-start | bytes 2015240 | tf_op jit(solution)/shard_map/ppermute | solution.py:362
  90.5 13.0 %copy-start.4 = (bf16[16,512,128]{2,1,0:T(8,128)(2,1)S(1)}, bf16[16,512,128]{2,1,0:T(8,128)(2,1)}, u32[]{:S(2)}) copy-start(bf16[16,512,128]{2,1,0:T(8,128)(2,1)} %w_ref.1) | copy-start | bytes 6291460

commit v8 on v6

--- a/solution.py
+++ b/solution.py
@@ -282,20 +282,19 @@
     )(me, w_uk, *got)
 
 
-def split_kernel(spans, x_ref, *refs):
+def cut_kernel(spans, x_ref, *refs):
     for (a, b), ref in zip(spans, refs[-len(spans) :]):
         ref[...] = x_ref[:, a:b]
 
 
-def split(x, spans, tokens):
+def cut(x, spans, tokens):
     return pl.pallas_call(
-        functools.partial(split_kernel, spans),
-        grid=(1,),
-        in_specs=[pl.BlockSpec(x.shape, lambda i: (0, 0))] + [ANY] * len(tokens),
-        out_specs=[pl.BlockSpec((x.shape[0], b - a), lambda i: (0, 0)) for a, b in spans],
+        functools.partial(cut_kernel, spans),
+        in_specs=[WHOLE] + [ANY] * len(tokens),
+        out_specs=[WHOLE] * len(spans),
         out_shape=[jax.ShapeDtypeStruct((x.shape[0], b - a), x.dtype) for a, b in spans],
-        compiler_params=room(16),
-        name="split",
+        compiler_params=room(4),
+        name="cut",
     )(x, *tokens)
 
 
@@ -364,10 +363,7 @@
     far, pair = n // 2, n // 4
     near = [1 << b for b in range(pair.bit_length() - 1)]
     keys = cache_kv.T
-    edges = [0, pos_dev // 8 * 3, pos_dev // 4 * 3, pos_dev]
-
-    lead = keys[:, : edges[1]]
-    pieces = [swap(lead, far)]
+    edges = [i * (pos_dev // 8) for i in (0, 3, 6, 8)]
 
     place = me[None].astype(jnp.int32)
     order = [[r for r in range(n) if not r & 1], [r for r in range(n) if r & 1]]
@@ -387,17 +383,16 @@
         order.append([r ^ o for o, _ in groups[r]])
     got = got[:1] + [swap(x, r) for r, x in zip(sorted(groups)[1:], got[1:])]
 
-    middle = edges[1]
-    *cuts, early, late = split(
-        keys, [*zip(edges[1:], edges[2:]), (0, middle), (middle, pos_dev)], [come]
-    )
-    halves = [(0, early, after(late, *got[1:]))]
+    absorbed, extra = absorb(count, rows_dec // n, place, order, got, w_uk, row)
+    other = swap(absorbed, pair)
+    spans = [*zip(edges, edges[1:])]
+    cuts = cut(keys, spans[:1], got[1:]) + cut(keys, spans[1:], [absorbed])
+    pieces = [swap(x, far) for x in cuts]
+    extra = after(extra, pieces[0])
+    new_rows = extra[:span]
+    blocks = [(0, cut(keys, [(0, pos_dev)], got[1:])[0])]
     for stride in near:
-        halves += [(o ^ stride, swap(x, stride), swap(y, stride)) for o, x, y in halves]
-    absorbed, extra = absorb(count, rows_dec // n, place, order, got, w_uk, row)
-    new_rows = extra[:span]
-    other = swap(absorbed, pair)
-    pieces.append(swap(after(cuts[0], pieces[0], halves[-1][1], *got[1:]), far))
+        blocks += [(offset ^ stride, swap(x, stride)) for offset, x in blocks]
 
     def spread(x):
         part = [(far, x)]
@@ -421,30 +416,30 @@
     seen = (index[None, :] < span) & (index[None, :] < limits[:, None])
     seen |= (index[None, :] >= span) & (index[None, :] == queries[:, None])
     bias = jnp.where(seen, 0.0, HIDDEN).astype(jnp.float32)
-    held = [offset for offset, _, _ in halves]
+    held = [offset for offset, _ in blocks]
     offsets = held + [offset ^ far for offset in held]
     which = jnp.stack([me ^ offset for offset in offsets])
     fills = jnp.sum(
         jnp.where(which[:, None] == jnp.arange(n, dtype=jnp.int32)[None, :], cache_fill[None, :], 0),
         axis=1,
     )
-    base = len(halves)
+    base = len(blocks)
     tile = heads // 2 * count
 
     def stage_of(c, part):
         return [(edges[c], base + i, x) for i, (_, x) in enumerate(part)]
 
     home = [(0, 0, keys)]
-    side = [(a, i, z) for i, (_, x, y) in enumerate(halves) if i for a, z in ((0, x), (middle, y))]
+    side = [(0, i, x) for i, (_, x) in enumerate(blocks) if i]
+    side += stage_of(0, spread(pieces[0]))
     state = attend(fills, absorbed, home, tile, new=(extra, bias))
-    part = spread(pieces[0])
-    side += stage_of(0, part)
-    pieces.append(swap(after(cuts[1], state[0], pieces[1], part[-1][1]), far))
     first = stage_of(1, spread(after(pieces[1], state[0])))
     state = attend(fills, absorbed, side, tile, state=state)
-    other = after(other, state[0])
+    other = after(other, state[0], pieces[1])
     guest = attend(fills, other, home + side, tile)
     second = stage_of(2, spread(after(pieces[2], guest[0])))
+    first, second = first + second[:1], second[1:]
+    other = after(other, pieces[2])
     guest = attend(fills, other, first, tile, state=guest)
     sent = attend(fills, other, second, tile, state=guest, last=True)
     back = swap(sent, pair)

time: 107 us -> 105 us (0.981)
  starting transfers between devices: 24.3 us -> 16.3 us
  Pallas kernels: 30.7 us -> 34.1 us
  waiting for transfers between devices: 46.9 us -> 50 us
    ppermute x14 -> x13, starting transfers between devices: 24.3 us -> 16.3 us  [swap(): return lax.ppermute(x, 'seq', [(i, i ^ stride) for i in range(n)])]
    ppermute x14 -> x13, waiting for transfers between devices: 46.9 us -> 50 us  [swap(): return lax.ppermute(x, 'seq', [(i, i ^ stride) for i in range(n)])]
    pallas_call x1 -> x3, Pallas kernels: 0.16 us -> 1.99 us  [cut(): pl.pallas_call(functools.partial(cut_kernel, spans), in_specs=[WHOLE] + [...]
    pallas_call x6, Pallas kernels: 26.2 us -> 27.7 us  [attend(): pl.pallas_call(functools.partial(attend_kernel, spec, new is not None, st...]
  transfers between devices with their start and end apart: 14 -> 13, of which waited for: 5 -> 9; matrix products, arithmetic and copies ran while one was open for 4% -> 3% of each run, Pallas kernels for 24% -> 27%
where the time goes in v8:
time: 105 us
  waiting for transfers between devices  50 us (48%)
  Pallas kernels  34.1 us (32%)
  starting transfers between devices  16.3 us (16%)
  matrix products  1.54 us (1%)
    ppermute x13, waiting for transfers between devices, swap(): return lax.ppermute(x, 'seq', [(i, i ^ stride) for i in range(n)])  50 us
    pallas_call x6, Pallas kernels, attend(): pl.pallas_call(functools.partial(attend_kernel, spec, new is not None, st...  27.7 us
    ppermute x13, starting transfers between devices, swap(): return lax.ppermute(x, 'seq', [(i, i ^ stride) for i in range(n)])  16.3 us
  transfers between devices with their start and end apart: 13, of which 9 were waited for; matrix products, arithmetic and copies ran while one was open for 3% of the time, Pallas kernels for 27%

profile of v8, /device:TPU:0, one launch (start us, length us, event | category | flops | bytes accessed | tf_op | source)
XLA Modules:
  0.0 104.5 jit_solution(15669744974026745396)
XLA Ops:
  0.6 1.9 %pack.1 = (bf16[4,4,4736]{2,1,0:T(4,128)(2,1)}, bf16[4,4,4736]{2,1,0:T(4,128)(2,1)}) custom-call(s32[1]{0:T(128)} %bitcast.me_ref, bf16[4,24576]{1,0:T(4,128)(2,1)} %query_ref.1, bf16[1,24576]{1,0:T(2,128)(2,1)} %dec_ref.1, bf16[4,576]{1,0:T(4,128)(2,1)} %span_kv_ref.1, bf16[1,576]{1,0:T(2,128)(2,1)} %dec_kv_ref.1), custom_call_target="tpu_custom_call" | custom-call | tf_op jit(solution)/shard_map/pack/pallas_call | solution.py:196
  2.5 2.9 %collective-permute-start = (bf16[4,4,4736]{2,1,0:T(4,128)(2,1)}, bf16[4,4,4736]{2,1,0:T(4,128)(2,1)S(1)}, u32[]{:S(2)}, u32[]{:S(2)}) collective-permute-start(bf16[4,4,4736]{2,1,0:T(4,128)(2,1)} %get-tuple-element.27), channel_id=1, source_target_pairs={{0,4},{4,0},{8,12},{12,8},{16,20},{20,16},{24,28},{28,24},{1,5},{5... | collective-permute-start | bytes 454664 | tf_op jit(solution)/shard_map/ppermute | solution.py:361
  5.4 0.9 fusion.8
  6.3 3.3 %collective-permute-done = bf16[4,4,4736]{2,1,0:T(4,128)(2,1)S(1)} collective-permute-done((bf16[4,4,4736]{2,1,0:T(4,128)(2,1)}, bf16[4,4,4736]{2,1,0:T(4,128)(2,1)S(1)}, u32[]{:S(2)}, u32[]{:S(2)}) %collective-permute-start) | collective-permute-done | bytes 151584 | tf_op jit(solution)/shard_map/ppermute | solution.py:361
  9.7 3.9 %collective-permute-start.3 = (bf16[2,4,4736]{2,1,0:T(4,128)(2,1)S(1)}, bf16[2,4,4736]{2,1,0:T(4,128)(2,1)S(1)}, u32[]{:S(2)}, u32[]{:S(2)}) collective-permute-start(bf16[2,4,4736]{2,1,0:T(4,128)(2,1)S(1)} %pad_maximum_fusion.3), channel_id=1, source_target_pairs={{0,24},{4,28},{8,16},{12,20},{16,8},{20,12},{24,0},{28,4},{1,25},{... | collective-permute-start | bytes 227336 | tf_op jit(solution)/shard_map/ppermute | solution.py:361
  13.8 0.6 collective-permute-start.1
  14.5 2.3 %collective-permute-done.3.refs_3_.refs_2_ = bf16[2,4,4736]{2,1,0:T(4,128)(2,1)S(1)} collective-permute-done((bf16[2,4,4736]{2,1,0:T(4,128)(2,1)S(1)}, bf16[2,4,4736]{2,1,0:T(4,128)(2,1)S(1)}, u32[]{:S(2)}, u32[]{:S(2)}) %collective-permute-start.3) | collective-permute-done | bytes 75808 | tf_op jit(solution)/shard_map/ppermute | solution.py:361
  16.7 2.8 %collective-permute-done.2.refs_2_.refs_1_ = bf16[2,4,4736]{2,1,0:T(4,128)(2,1)S(1)} collective-permute-done((bf16[2,4,4736]{2,1,0:T(4,128)(2,1)S(1)}, bf16[2,4,4736]{2,1,0:T(4,128)(2,1)S(1)}, u32[]{:S(2)}, u32[]{:S(2)}) %collective-permute-start.2) | collective-permute-done | bytes 75808 | tf_op jit(solution)/shard_map/ppermute | solution.py:361
  19.6 0.8 cut.4
  20.4 1.6 %collective-permute-start.5 = (bf16[576,384]{1,0:T(8,128)(2,1)}, bf16[576,384]{1,0:T(8,128)(2,1)S(1)}, u32[]{:S(2)}, u32[]{:S(2)}) collective-permute-start(bf16[576,384]{1,0:T(8,128)(2,1)} %cut.4), channel_id=1, source_target_pairs={{0,16},{4,20},{8,24},{12,28},{16,0},{20,4},{24,8},{28,12},{1,17},{... | collective-permute-start | bytes 1327112 | tf_op jit(solution)/shard_map/ppermute | solution.py:361
  22.0 1.1 %cut.5 = bf16[576,1024]{1,0:T(8,128)(2,1)} custom-call(bf16[576,1024]{1,0:T(8,128)(2,1)S(1)} %bitcast.6, bf16[2,4,4736]{2,1,0:T(4,128)(2,1)S(1)} %collective-permute-done.1.refs_1_.refs_0_, bf16[2,4,4736]{2,1,0:T(4,128)(2,1)S(1)} %collective-permute-done.2.refs_2_.refs_1_, bf16[2,4,4736]{2,1,0:T(4,128)(2,1)S(1)} %collective-permute-done.3.refs_3_.refs_2_), custom_call_target="tpu_custom_call" | custom-call | tf_op jit(solution)/shard_map/cut/pallas_call | solution.py:291
  23.1 1.5 %collective-permute-start.9 = (bf16[576,1024]{1,0:T(8,128)(2,1)}, bf16[576,1024]{1,0:T(8,128)(2,1)}, u32[]{:S(2)}, u32[]{:S(2)}) collective-permute-start(bf16[576,1024]{1,0:T(8,128)(2,1)} %cut.5), channel_id=1, source_target_pairs={{0,4},{4,0},{8,12},{12,8},{16,20},{20,16},{24,28},{28,24},{1,5},{5... | collective-permute-start | bytes 3538952 | tf_op jit(solution)/shard_map/ppermute | solution.py:361
  24.6 1.3 %absorb.1 = (bf16[640,640]{1,0:T(8,128)(2,1)S(1)}, bf16[128,576]{1,0:T(8,128)(2,1)S(1)}) custom-call(s32[1]{0:T(128)} %bitcast.me_ref, bf16[16,128,512]{2,1,0:T(8,128)(2,1)S(1)} %copy-done.1, bf16[2,4,4736]{2,1,0:T(4,128)(2,1)S(1)} %pad_maximum_fusion.refs_0_, bf16[2,4,4736]{2,1,0:T(4,128)(2,1)S(1)} %collective-permute-done.1.refs_1_.refs_0_, ...), custom_call_target="tpu_custom_call" | custom-call | tf_op jit(solution)/shard_map/absorb/pallas_call | solution.py:267
  26.0 1.4 %collective-permute-start.8 = (bf16[640,640]{1,0:T(8,128)(2,1)S(1)}, bf16[640,640]{1,0:T(8,128)(2,1)S(1)}, u32[]{:S(2)}, u32[]{:S(2)}) collective-permute-start(bf16[640,640]{1,0:T(8,128)(2,1)S(1)} %get-tuple-element.28.refs_0_.refs_1_), channel_id=1, source_target_pairs={{0,8},{4,12},{8,0},{12,4},{16,24},{20,28},{24,16},{28,20},{1,9},{5... | collective-permute-start | bytes 2457608 | tf_op jit(solution)/shard_map/ppermute | solution.py:361
  27.5 0.6 collective-permute-start.4
  28.1 13.2 %collective-permute-done.5.refs_0_.refs_3_.refs_4_ = bf16[576,384]{1,0:T(8,128)(2,1)S(1)} collective-permute-done((bf16[576,384]{1,0:T(8,128)(2,1)}, bf16[576,384]{1,0:T(8,128)(2,1)S(1)}, u32[]{:S(2)}, u32[]{:S(2)}) %collective-permute-start.5) | collective-permute-done | bytes 442400 | tf_op jit(solution)/shard_map/ppermute | solution.py:361
  41.3 1.5 %collective-permute-start.10 = (bf16[576,384]{1,0:T(8,128)(2,1)S(1)}, bf16[576,384]{1,0:T(8,128)(2,1)S(1)}, u32[]{:S(2)}, u32[]{:S(2)}) collective-permute-start(bf16[576,384]{1,0:T(8,128)(2,1)S(1)} %collective-permute-done.5.refs_0_.refs_3_.refs_4_), channel_id=1, source_target_pairs={{0,4},{4,0},{8,12},{12,8},{16,20},{20,16},{24,28},{28,24},{1,5},{5... | collective-permute-start | bytes 1327112 | tf_op jit(solution)/shard_map/ppermute | solution.py:361
  43.2 3.4 %attend.6 = (f32[640,128]{1,0:T(8,128)S(1)}, f32[640,128]{1,0:T(8,128)S(1)}, f32[640,512]{1,0:T(8,128)S(1)}) custom-call(s32[4]{0:T(128)S(1)} %select_reduce_fusion.refs_0_, bf16[640,640]{1,0:T(8,128)(2,1)S(1)} %get-tuple-element.28.refs_0_.refs_1_, bf16[576,1024]{1,0:T(8,128)(2,1)S(1)} %bitcast.8, bf16[128,576]{1,0:T(8,128)(2,1)S(1)} %after.5.refs_3_, ...), custom_call_target="tpu_custom_call" | custom-call | tf_op jit(solution)/shard_map/attend/pallas_call | solution.py:123
  46.7 12.0 %collective-permute-done.10.refs_4_.refs_5_ = bf16[576,384]{1,0:T(8,128)(2,1)S(1)} collective-permute-done((bf16[576,384]{1,0:T(8,128)(2,1)S(1)}, bf16[576,384]{1,0:T(8,128)(2,1)S(1)}, u32[]{:S(2)}, u32[]{:S(2)}) %collective-permute-start.10) | collective-permute-done | bytes 442400 | tf_op jit(solution)/shard_map/ppermute | solution.py:361
  58.7 5.9 %attend.7 = (f32[640,128]{1,0:T(8,128)S(1)}, f32[640,128]{1,0:T(8,128)S(1)}, f32[640,512]{1,0:T(8,128)S(1)}) custom-call(s32[4]{0:T(128)S(1)} %select_reduce_fusion.refs_0_, bf16[640,640]{1,0:T(8,128)(2,1)S(1)} %get-tuple-element.28.refs_0_.refs_1_, ...), custom_call_target="tpu_custom_call", output_to_operand_aliasing={{0}: (5, {}), {1}: (6, {}), {2}: (7, {})} | custom-call | tf_op jit(solution)/shard_map/attend/pallas_call | solution.py:123
  64.6 1.9 %collective-permute-done.4.x_ref.refs_1_ = bf16[576,384]{1,0:T(8,128)(2,1)S(1)} collective-permute-done((bf16[576,384]{1,0:T(8,128)(2,1)S(1)}, bf16[576,384]{1,0:T(8,128)(2,1)S(1)}, u32[]{:S(2)}, u32[]{:S(2)}) %collective-permute-start.4) | collective-permute-done | bytes 442400 | tf_op jit(solution)/shard_map/ppermute | solution.py:361
  66.5 1.5 %collective-permute-start.6 = (bf16[576,384]{1,0:T(8,128)(2,1)S(1)}, bf16[576,384]{1,0:T(8,128)(2,1)S(1)}, u32[]{:S(2)}, u32[]{:S(2)}) collective-permute-start(bf16[576,384]{1,0:T(8,128)(2,1)S(1)} %after.6.refs_2_), channel_id=1, source_target_pairs={{0,4},{4,0},{8,12},{12,8},{16,20},{20,16},{24,28},{28,24},{1,5},{5... | collective-permute-start | bytes 1327112 | tf_op jit(solution)/shard_map/ppermute | solution.py:361
  68.0 7.7 %attend.8 = (f32[640,128]{1,0:T(8,128)S(1)}, f32[640,128]{1,0:T(8,128)S(1)}, f32[640,512]{1,0:T(8,128)S(1)}) custom-call(s32[4]{0:T(128)S(1)} %select_reduce_fusion.refs_0_, bf16[640,640]{1,0:T(8,128)(2,1)S(1)} %after.7.refs_1_.x_ref, bf16[576,1024]{1,0:T(8,128)(2,1)S(1)} %bitcast.9, bf16[576,1024]{1,0:T(8,128)(2,1)} %collective-permute-done.9.refs_2_.refs_3_, ...), custom_call_target="tpu_custom_call" | custom-call | tf_op jit(solution)/shard_map/attend/pallas_call | solution.py:123
  75.7 0.6 collective-permute-start.11
  76.3 2.6 %collective-permute-done.6.refs_3_ = bf16[576,384]{1,0:T(8,128)(2,1)S(1)} collective-permute-done((bf16[576,384]{1,0:T(8,128)(2,1)S(1)}, bf16[576,384]{1,0:T(8,128)(2,1)S(1)}, u32[]{:S(2)}, u32[]{:S(2)}) %collective-permute-start.6) | collective-permute-done | bytes 442400 | tf_op jit(solution)/shard_map/ppermute | solution.py:361
  79.0 4.4 %attend.10 = (f32[640,128]{1,0:T(8,128)S(1)}, f32[640,128]{1,0:T(8,128)S(1)}, f32[640,512]{1,0:T(8,128)S(1)}) custom-call(s32[4]{0:T(128)S(1)} %select_reduce_fusion.refs_0_, bf16[640,640]{1,0:T(8,128)(2,1)S(1)} %after.9.refs_1_, bf16[576,384]{1,0:T(8,128)(2,1)S(1)} %after.6.refs_2_, ...), custom_call_target="tpu_custom_call", output_to_operand_aliasing={{0}: (5, {}), {1}: (6, {}), {2}: (7, {})} | custom-call | tf_op jit(solution)/shard_map/attend/pallas_call | solution.py:123
  83.4 1.5 %collective-permute-done.11.refs_5_.refs_2_ = bf16[576,256]{1,0:T(8,128)(2,1)S(1)} collective-permute-done((bf16[576,256]{1,0:T(8,128)(2,1)S(1)}, bf16[576,256]{1,0:T(8,128)(2,1)S(1)}, u32[]{:S(2)}, u32[]{:S(2)}) %collective-permute-start.11) | collective-permute-done | bytes 294944 | tf_op jit(solution)/shard_map/ppermute | solution.py:361
  84.9 2.2 %attend.11 = bf16[656,512]{1,0:T(8,128)(2,1)S(1)} custom-call(s32[4]{0:T(128)S(1)} %select_reduce_fusion.refs_0_, bf16[640,640]{1,0:T(8,128)(2,1)S(1)} %after.9.refs_1_, bf16[576,256]{1,0:T(8,128)(2,1)S(1)} %collective-permute-done.11.refs_5_.refs_2_, f32[640,128]{1,0:T(8,128)S(1)} %get-tuple-element.44.refs_3_, f32[640,128]{1,0:T(8,128)S(1)} %get-tuple-element.45.refs_4_, ...), custom_call_target="tpu_custom_call" | custom-call | tf_op jit(solution)/shard_map/attend/pallas_call | solution.py:123
  87.2 1.5 %fusion = bf16[1024,576]{0,1:T(8,128)(2,1)} fusion(bf16[1024,576]{0,1:T(8,128)(2,1)S(1)} %copy-done, pred[1024]{0:T(1024)(128)(4,1)S(1)} %fusion.1, s32[32]{0:T(128)S(1)} %compare_select_fusion, bf16[128,576]{1,0:T(8,128)(2,1)S(1)} %after.5.refs_3_), kind=kOutput, calls=%fused_computation.1 | convolution fusion | flops 38961152 | bytes 2401792 | tf_op jit(solution)/shard_map/dot_general | solution.py:405
  88.8 4.2 %attend.9 = (f32[640,128]{1,0:T(8,128)S(1)}, f32[640,128]{1,0:T(8,128)S(1)}, f32[640,512]{1,0:T(8,128)S(1)}) custom-call(s32[4]{0:T(128)S(1)} %select_reduce_fusion.refs_0_, bf16[640,640]{1,0:T(8,128)(2,1)S(1)} %get-tuple-element.28.refs_0_.refs_1_, bf16[576,384]{1,0:T(8,128)(2,1)S(1)} %after.6.refs_2_, ...), custom_call_target="tpu_custom_call", output_to_operand_aliasing={{0}: (6, {}), {1}: (7, {}), {2}: (8, {})} | custom-call | tf_op jit(solution)/shard_map/attend/pallas_call | solution.py:123
  93.0 10.3 %collective-permute-done.12.far_ref = bf16[656,512]{1,0:T(8,128)(2,1)S(1)} collective-permute-done((bf16[656,512]{1,0:T(8,128)(2,1)S(1)}, bf16[656,512]{1,0:T(8,128)(2,1)S(1)}, u32[]{:S(2)}, u32[]{:S(2)}) %collective-permute-start.12) | collective-permute-done | bytes 671776 | tf_op jit(solution)/shard_map/ppermute | solution.py:361
  103.3 1.2 %finish.1 = (bf16[32,2048]{1,0:T(8,128)(2,1)}, bf16[8,2048]{1,0:T(8,128)(2,1)}) custom-call(f32[640,128]{1,0:T(8,128)S(1)} %get-tuple-element.39.m_ref, f32[640,128]{1,0:T(8,128)S(1)} %get-tuple-element.40.l_ref, f32[640,512]{1,0:T(8,128)S(1)} %get-tuple-element.41.acc_ref, bf16[656,512]{1,0:T(8,128)(2,1)S(1)} %collective-permute-done.12.far_ref, ...), custom_call_target="tpu_custom_call" | custom-call | flops 83886080 | bytes 4063232 | tf_op jit(solution)/shard_map/finish/pallas_call | solution.py:334
  (41 shorter events, 1.2 us)
Async XLA Ops:
  0.6 18.9 %copy-start = (bf16[1024,576]{0,1:T(8,128)(2,1)S(1)}, bf16[1024,576]{0,1:T(8,128)(2,1)}, u32[]{:S(2)}) copy-start(bf16[1024,576]{0,1:T(8,128)(2,1)} %param.13) | copy-start | bytes 3538948
  2.5 7.1 %collective-permute-start = (bf16[4,4,4736]{2,1,0:T(4,128)(2,1)}, bf16[4,4,4736]{2,1,0:T(4,128)(2,1)S(1)}, u32[]{:S(2)}, u32[]{:S(2)}) collective-permute-start(bf16[4,4,4736]{2,1,0:T(4,128)(2,1)} %get-tuple-element.27), channel_id=1, source_target_pairs={{0,4},{4,0},{8,12},{12,8},{16,20},{20,16},{24,28},{28,24},{1,5},{5... | collective-permute-start | bytes 454664 | tf_op jit(solution)/shard_map/ppermute | solution.py:361
  9.7 7.0 %collective-permute-start.3 = (bf16[2,4,4736]{2,1,0:T(4,128)(2,1)S(1)}, bf16[2,4,4736]{2,1,0:T(4,128)(2,1)S(1)}, u32[]{:S(2)}, u32[]{:S(2)}) collective-permute-start(bf16[2,4,4736]{2,1,0:T(4,128)(2,1)S(1)} %pad_maximum_fusion.3), channel_id=1, source_target_pairs={{0,24},{4,28},{8,16},{12,20},{16,8},{20,12},{24,0},{28,4},{1,25},{... | collective-permute-start | bytes 227336 | tf_op jit(solution)/shard_map/ppermute | solution.py:361
  13.7 5.8 %collective-permute-start.2 = (bf16[2,4,4736]{2,1,0:T(4,128)(2,1)S(1)}, bf16[2,4,4736]{2,1,0:T(4,128)(2,1)S(1)}, u32[]{:S(2)}, u32[]{:S(2)}) collective-permute-start(bf16[2,4,4736]{2,1,0:T(4,128)(2,1)S(1)} %pad_maximum_fusion.2), channel_id=1, source_target_pairs={{0,16},{4,20},{8,24},{12,28},{16,0},{20,4},{24,8},{28,12},{1,17},{... | collective-permute-start | bytes 227336 | tf_op jit(solution)/shard_map/ppermute | solution.py:361
  13.8 5.7 %collective-permute-start.1 = (bf16[2,4,4736]{2,1,0:T(4,128)(2,1)S(1)}, bf16[2,4,4736]{2,1,0:T(4,128)(2,1)S(1)}, u32[]{:S(2)}, u32[]{:S(2)}) collective-permute-start(bf16[2,4,4736]{2,1,0:T(4,128)(2,1)S(1)} %pad_maximum_fusion.1), channel_id=1, source_target_pairs={{0,8},{4,12},{8,0},{12,4},{16,24},{20,28},{24,16},{28,20},{1,9},{5... | collective-permute-start | bytes 227336 | tf_op jit(solution)/shard_map/ppermute | solution.py:361
  20.4 4.2 %copy-start.1 = (bf16[16,128,512]{2,1,0:T(8,128)(2,1)S(1)}, bf16[16,128,512]{2,1,0:T(8,128)(2,1)}, u32[]{:S(2)}) copy-start(bf16[16,128,512]{2,1,0:T(8,128)(2,1)} %w_hbm.1) | copy-start | bytes 6291460
  20.4 20.9 %collective-permute-start.5 = (bf16[576,384]{1,0:T(8,128)(2,1)}, bf16[576,384]{1,0:T(8,128)(2,1)S(1)}, u32[]{:S(2)}, u32[]{:S(2)}) collective-permute-start(bf16[576,384]{1,0:T(8,128)(2,1)} %cut.4), channel_id=1, source_target_pairs={{0,16},{4,20},{8,24},{12,28},{16,0},{20,4},{24,8},{28,12},{1,17},{... | collective-permute-start | bytes 1327112 | tf_op jit(solution)/shard_map/ppermute | solution.py:361
  23.1 4.2 %copy-start.5 = (s32[8]{0:T(128)S(1)}, s32[8]{0:T(128)}, u32[]{:S(2)}) copy-start(s32[8]{0:T(128)} %param.19) | copy-start | bytes 100
  23.1 35.6 %collective-permute-start.9 = (bf16[576,1024]{1,0:T(8,128)(2,1)}, bf16[576,1024]{1,0:T(8,128)(2,1)}, u32[]{:S(2)}, u32[]{:S(2)}) collective-permute-start(bf16[576,1024]{1,0:T(8,128)(2,1)} %cut.5), channel_id=1, source_target_pairs={{0,4},{4,0},{8,12},{12,8},{16,20},{20,16},{24,28},{28,24},{1,5},{5... | collective-permute-start | bytes 3538952 | tf_op jit(solution)/shard_map/ppermute | solution.py:361
  25.9 17.1 %copy-start.6 = (s32[8]{0:T(128)S(1)}, s32[8]{0:T(128)}, u32[]{:S(2)}) copy-start(s32[8]{0:T(128)} %param.16) | copy-start | bytes 100
  26.0 40.6 %collective-permute-start.8 = (bf16[640,640]{1,0:T(8,128)(2,1)S(1)}, bf16[640,640]{1,0:T(8,128)(2,1)S(1)}, u32[]{:S(2)}, u32[]{:S(2)}) collective-permute-start(bf16[640,640]{1,0:T(8,128)(2,1)S(1)} %get-tuple-element.28.refs_0_.refs_1_), channel_id=1, source_target_pairs={{0,8},{4,12},{8,0},{12,4},{16,24},{20,28},{24,16},{28,20},{1,9},{5... | collective-permute-start | bytes 2457608 | tf_op jit(solution)/shard_map/ppermute | solution.py:361
  27.5 39.0 %collective-permute-start.4 = (bf16[576,384]{1,0:T(8,128)(2,1)S(1)}, bf16[576,384]{1,0:T(8,128)(2,1)S(1)}, u32[]{:S(2)}, u32[]{:S(2)}) collective-permute-start(bf16[576,384]{1,0:T(8,128)(2,1)S(1)} %get-tuple-element.29), channel_id=1, source_target_pairs={{0,16},{4,20},{8,24},{12,28},{16,0},{20,4},{24,8},{28,12},{1,17},{... | collective-permute-start | bytes 1327112 | tf_op jit(solution)/shard_map/ppermute | solution.py:361
  41.3 17.4 %collective-permute-start.10 = (bf16[576,384]{1,0:T(8,128)(2,1)S(1)}, bf16[576,384]{1,0:T(8,128)(2,1)S(1)}, u32[]{:S(2)}, u32[]{:S(2)}) collective-permute-start(bf16[576,384]{1,0:T(8,128)(2,1)S(1)} %collective-permute-done.5.refs_0_.refs_3_.refs_4_), channel_id=1, source_target_pairs={{0,4},{4,0},{8,12},{12,8},{16,20},{20,16},{24,28},{28,24},{1,5},{5... | collective-permute-start | bytes 1327112 | tf_op jit(solution)/shard_map/ppermute | solution.py:361
  42.9 32.8 %collective-permute-start.7 = (bf16[576,256]{1,0:T(8,128)(2,1)S(1)}, bf16[576,256]{1,0:T(8,128)(2,1)S(1)}, u32[]{:S(2)}, u32[]{:S(2)}) collective-permute-start(bf16[576,256]{1,0:T(8,128)(2,1)S(1)} %get-tuple-element.32), channel_id=1, source_target_pairs={{0,16},{4,20},{8,24},{12,28},{16,0},{20,4},{24,8},{28,12},{1,17},{... | collective-permute-start | bytes 884744 | tf_op jit(solution)/shard_map/ppermute | solution.py:361
  66.5 12.4 %collective-permute-start.6 = (bf16[576,384]{1,0:T(8,128)(2,1)S(1)}, bf16[576,384]{1,0:T(8,128)(2,1)S(1)}, u32[]{:S(2)}, u32[]{:S(2)}) collective-permute-start(bf16[576,384]{1,0:T(8,128)(2,1)S(1)} %after.6.refs_2_), channel_id=1, source_target_pairs={{0,4},{4,0},{8,12},{12,8},{16,20},{20,16},{24,28},{28,24},{1,5},{5... | collective-permute-start | bytes 1327112 | tf_op jit(solution)/shard_map/ppermute | solution.py:361
  75.7 9.1 %collective-permute-start.11 = (bf16[576,256]{1,0:T(8,128)(2,1)S(1)}, bf16[576,256]{1,0:T(8,128)(2,1)S(1)}, u32[]{:S(2)}, u32[]{:S(2)}) collective-permute-start(bf16[576,256]{1,0:T(8,128)(2,1)S(1)} %after.8.refs_4_), channel_id=1, source_target_pairs={{0,4},{4,0},{8,12},{12,8},{16,20},{20,16},{24,28},{28,24},{1,5},{5... | collective-permute-start | bytes 884744 | tf_op jit(solution)/shard_map/ppermute | solution.py:361
  84.9 2.2 %copy-start.3 = (s32[32]{0:T(128)S(1)}, s32[32]{0:T(128)}, u32[]{:S(2)}) copy-start(s32[32]{0:T(128)} %param.18) | copy-start | bytes 388
  84.9 2.2 %copy-start.4 = (s32[32]{0:T(128)S(1)}, s32[32]{0:T(128)}, u32[]{:S(2)}) copy-start(s32[32]{0:T(128)} %param.17) | copy-start | bytes 388
  87.0 16.3 %collective-permute-start.12 = (bf16[656,512]{1,0:T(8,128)(2,1)S(1)}, bf16[656,512]{1,0:T(8,128)(2,1)S(1)}, u32[]{:S(2)}, u32[]{:S(2)}) collective-permute-start(bf16[656,512]{1,0:T(8,128)(2,1)S(1)} %attend.11), channel_id=1, source_target_pairs={{0,8},{4,12},{8,0},{12,4},{16,24},{20,28},{24,16},{28,20},{1,9},{5... | collective-permute-start | bytes 2015240 | tf_op jit(solution)/shard_map/ppermute | solution.py:361
  88.8 14.5 %copy-start.2 = (bf16[16,512,128]{2,1,0:T(8,128)(2,1)S(1)}, bf16[16,512,128]{2,1,0:T(8,128)(2,1)}, u32[]{:S(2)}) copy-start(bf16[16,512,128]{2,1,0:T(8,128)(2,1)} %w_ref.1) | copy-start | bytes 6291460

commit v9 on v8

--- a/solution.py
+++ b/solution.py
@@ -363,7 +363,7 @@
     far, pair = n // 2, n // 4
     near = [1 << b for b in range(pair.bit_length() - 1)]
     keys = cache_kv.T
-    edges = [i * (pos_dev // 8) for i in (0, 3, 6, 8)]
+    edges = [i * (pos_dev // 8) for i in (0, 3, 5, 7, 8)]
 
     place = me[None].astype(jnp.int32)
     order = [[r for r in range(n) if not r & 1], [r for r in range(n) if r & 1]]
@@ -431,19 +431,21 @@
 
     home = [(0, 0, keys)]
     side = [(0, i, x) for i, (_, x) in enumerate(blocks) if i]
-    side += stage_of(0, spread(pieces[0]))
     state = attend(fills, absorbed, home, tile, new=(extra, bias))
-    first = stage_of(1, spread(after(pieces[1], state[0])))
+    first = stage_of(0, spread(pieces[0]))
     state = attend(fills, absorbed, side, tile, state=state)
+    first += stage_of(1, spread(after(pieces[1], state[0])))
     other = after(other, state[0], pieces[1])
     guest = attend(fills, other, home + side, tile)
     second = stage_of(2, spread(after(pieces[2], guest[0])))
-    first, second = first + second[:1], second[1:]
     other = after(other, pieces[2])
     guest = attend(fills, other, first, tile, state=guest)
-    sent = attend(fills, other, second, tile, state=guest, last=True)
+    third = stage_of(3, spread(after(pieces[3], guest[0])))
+    second, third = second + third[:1], third[1:]
+    guest = attend(fills, other, second, tile, state=guest)
+    sent = attend(fills, other, third, tile, state=guest, last=True)
     back = swap(sent, pair)
-    state = attend(fills, absorbed, first + second, tile, state=state)
+    state = attend(fills, absorbed, first + second + third, tile, state=state)
     span_out, dec_out = finish(count, span, state, back, w_uv)
     return (span_out, dec_out, new_cache)
 

time: 105 us -> 103 us (0.981)
  waiting for transfers between devices: 50 us -> 36.4 us
  local copies, waits for them, and re-layouts: 0.98 us -> 6.19 us
  starting transfers between devices: 16.3 us -> 19.6 us
  Pallas kernels: 34.1 us -> 35.4 us
  other arithmetic: 0.75 us -> 2.01 us
    ppermute x13 -> x15, waiting for transfers between devices: 50 us -> 36.4 us  [swap(): return lax.ppermute(x, 'seq', [(i, i ^ stride) for i in range(n)])]
    unnamed x15 -> x28, local copies, waits for them, and re-layouts: 0.05 us -> 5.26 us
    ppermute x13 -> x15, starting transfers between devices: 16.3 us -> 19.6 us  [swap(): return lax.ppermute(x, 'seq', [(i, i ^ stride) for i in range(n)])]
    pallas_call x6 -> x7, Pallas kernels: 27.7 us -> 28.3 us  [attend(): pl.pallas_call(functools.partial(attend_kernel, spec, new is not None, st...]
  transfers between devices with their start and end apart: 13 -> 15, of which waited for: 9 -> 9; matrix products, arithmetic and copies ran while one was open for 3% -> 5% of each run, Pallas kernels for 27% -> 29%
where the time goes in v9:
time: 103 us
  waiting for transfers between devices  36.4 us (35%)
  Pallas kernels  35.4 us (34%)
  starting transfers between devices  19.6 us (19%)
  local copies, waits for them, and re-layouts  6.19 us (6%)
  matrix products  2.32 us (2%)
  other arithmetic  2.01 us (2%)
    ppermute x15, waiting for transfers between devices, swap(): return lax.ppermute(x, 'seq', [(i, i ^ stride) for i in range(n)])  36.4 us
    pallas_call x7, Pallas kernels, attend(): pl.pallas_call(functools.partial(attend_kernel, spec, new is not None, st...  28.3 us
    ppermute x15, starting transfers between devices, swap(): return lax.ppermute(x, 'seq', [(i, i ^ stride) for i in range(n)])  19.6 us
    unnamed x28, local copies, waits for them, and re-layouts  5.26 us
    pallas_call x3, Pallas kernels, cut(): pl.pallas_call(functools.partial(cut_kernel, spans), in_specs=[WHOLE] + [...  2.69 us
    dot_general x1, matrix products, body(): lax.dot_general(new_rows, onehot.astype(jnp.bfloat16), (((0,), (0,)), (()...  2.32 us
  transfers between devices with their start and end apart: 15, of which 9 were waited for; matrix products, arithmetic and copies ran while one was open for 5% of the time, Pallas kernels for 29%

profile of v9, /device:TPU:0, one launch (start us, length us, event | category | flops | bytes accessed | tf_op | source)
XLA Modules:
  0.0 102.8 jit_solution(353272112037360704)
XLA Ops:
  0.6 1.8 %pack.1 = (bf16[4,4,4736]{2,1,0:T(4,128)(2,1)}, bf16[4,4,4736]{2,1,0:T(4,128)(2,1)}) custom-call(s32[1]{0:T(128)} %bitcast.me_ref, bf16[4,24576]{1,0:T(4,128)(2,1)} %query_ref.1, bf16[1,24576]{1,0:T(2,128)(2,1)} %dec_ref.1, bf16[4,576]{1,0:T(4,128)(2,1)} %span_kv_ref.1, bf16[1,576]{1,0:T(2,128)(2,1)} %dec_kv_ref.1), custom_call_target="tpu_custom_call" | custom-call | tf_op jit(solution)/shard_map/pack/pallas_call | solution.py:196
  2.5 2.9 %collective-permute-start = (bf16[4,4,4736]{2,1,0:T(4,128)(2,1)}, bf16[4,4,4736]{2,1,0:T(4,128)(2,1)S(1)}, u32[]{:S(2)}, u32[]{:S(2)}) collective-permute-start(bf16[4,4,4736]{2,1,0:T(4,128)(2,1)} %get-tuple-element.31), channel_id=1, source_target_pairs={{0,4},{4,0},{8,12},{12,8},{16,20},{20,16},{24,28},{28,24},{1,5},{5... | collective-permute-start | bytes 454664 | tf_op jit(solution)/shard_map/ppermute | solution.py:361
  5.4 0.9 fusion.8
  6.3 3.3 %collective-permute-done = bf16[4,4,4736]{2,1,0:T(4,128)(2,1)S(1)} collective-permute-done((bf16[4,4,4736]{2,1,0:T(4,128)(2,1)}, bf16[4,4,4736]{2,1,0:T(4,128)(2,1)S(1)}, u32[]{:S(2)}, u32[]{:S(2)}) %collective-permute-start) | collective-permute-done | bytes 151584 | tf_op jit(solution)/shard_map/ppermute | solution.py:361
  9.7 3.9 %collective-permute-start.3 = (bf16[2,4,4736]{2,1,0:T(4,128)(2,1)S(1)}, bf16[2,4,4736]{2,1,0:T(4,128)(2,1)S(1)}, u32[]{:S(2)}, u32[]{:S(2)}) collective-permute-start(bf16[2,4,4736]{2,1,0:T(4,128)(2,1)S(1)} %pad_maximum_fusion.3), channel_id=1, source_target_pairs={{0,24},{4,28},{8,16},{12,20},{16,8},{20,12},{24,0},{28,4},{1,25},{... | collective-permute-start | bytes 227336 | tf_op jit(solution)/shard_map/ppermute | solution.py:361
  14.4 2.3 %collective-permute-done.3.refs_3_.refs_2_ = bf16[2,4,4736]{2,1,0:T(4,128)(2,1)S(1)} collective-permute-done((bf16[2,4,4736]{2,1,0:T(4,128)(2,1)S(1)}, bf16[2,4,4736]{2,1,0:T(4,128)(2,1)S(1)}, u32[]{:S(2)}, u32[]{:S(2)}) %collective-permute-start.3) | collective-permute-done | bytes 75808 | tf_op jit(solution)/shard_map/ppermute | solution.py:361
  16.7 2.8 %collective-permute-done.2.refs_2_.refs_1_ = bf16[2,4,4736]{2,1,0:T(4,128)(2,1)S(1)} collective-permute-done((bf16[2,4,4736]{2,1,0:T(4,128)(2,1)S(1)}, bf16[2,4,4736]{2,1,0:T(4,128)(2,1)S(1)}, u32[]{:S(2)}, u32[]{:S(2)}) %collective-permute-start.2) | collective-permute-done | bytes 75808 | tf_op jit(solution)/shard_map/ppermute | solution.py:361
  19.6 1.1 %cut.5 = bf16[576,1024]{1,0:T(8,128)(2,1)} custom-call(bf16[576,1024]{1,0:T(8,128)(2,1)S(1)} %bitcast.5, bf16[2,4,4736]{2,1,0:T(4,128)(2,1)S(1)} %collective-permute-done.1.refs_1_.refs_0_, bf16[2,4,4736]{2,1,0:T(4,128)(2,1)S(1)} %collective-permute-done.2.refs_2_.refs_1_, bf16[2,4,4736]{2,1,0:T(4,128)(2,1)S(1)} %collective-permute-done.3.refs_3_.refs_2_), custom_call_target="tpu_custom_call" | custom-call | tf_op jit(solution)/shard_map/cut/pallas_call | solution.py:291
  20.7 1.5 %collective-permute-start.7 = (bf16[576,1024]{1,0:T(8,128)(2,1)}, bf16[576,1024]{1,0:T(8,128)(2,1)}, u32[]{:S(2)}, u32[]{:S(2)}) collective-permute-start(bf16[576,1024]{1,0:T(8,128)(2,1)} %cut.5), channel_id=1, source_target_pairs={{0,4},{4,0},{8,12},{12,8},{16,20},{20,16},{24,28},{28,24},{1,5},{5... | collective-permute-start | bytes 3538952 | tf_op jit(solution)/shard_map/ppermute | solution.py:361
  22.2 1.3 %absorb.1 = (bf16[640,640]{1,0:T(8,128)(2,1)S(1)}, bf16[128,576]{1,0:T(8,128)(2,1)S(1)}) custom-call(s32[1]{0:T(128)} %bitcast.me_ref, bf16[16,128,512]{2,1,0:T(8,128)(2,1)S(1)} %copy-done.1, bf16[2,4,4736]{2,1,0:T(4,128)(2,1)S(1)} %pad_maximum_fusion.refs_0_, bf16[2,4,4736]{2,1,0:T(4,128)(2,1)S(1)} %collective-permute-done.1.refs_1_.refs_0_, ...), custom_call_target="tpu_custom_call" | custom-call | tf_op jit(solution)/shard_map/absorb/pallas_call | solution.py:267
  25.5 2.4 %collective-permute-start.4 = (bf16[576,384]{1,0:T(8,128)(2,1)}, bf16[576,384]{1,0:T(8,128)(2,1)S(1)}, u32[]{:S(2)}, u32[]{:S(2)}) collective-permute-start(bf16[576,384]{1,0:T(8,128)(2,1)} %cut.3), channel_id=1, source_target_pairs={{0,16},{4,20},{8,24},{12,28},{16,0},{20,4},{24,8},{28,12},{1,17},{... | collective-permute-start | bytes 1327112 | tf_op jit(solution)/shard_map/ppermute | solution.py:361
  31.4 2.4 %collective-permute-start.9 = (bf16[576,256]{1,0:T(8,128)(2,1)}, bf16[576,256]{1,0:T(8,128)(2,1)S(1)}, u32[]{:S(2)}, u32[]{:S(2)}) collective-permute-start(bf16[576,256]{1,0:T(8,128)(2,1)} %copy-done.8), channel_id=1, source_target_pairs={{0,16},{4,20},{8,24},{12,28},{16,0},{20,4},{24,8},{28,12},{1,17},{... | collective-permute-start | bytes 884744 | tf_op jit(solution)/shard_map/ppermute | solution.py:361
  33.7 19.3 %collective-permute-done.4.refs_0_.refs_2_ = bf16[576,384]{1,0:T(8,128)(2,1)S(1)} collective-permute-done((bf16[576,384]{1,0:T(8,128)(2,1)}, bf16[576,384]{1,0:T(8,128)(2,1)S(1)}, u32[]{:S(2)}, u32[]{:S(2)}) %collective-permute-start.4) | collective-permute-done | bytes 442400 | tf_op jit(solution)/shard_map/ppermute | solution.py:361
  54.8 0.9 copy-done.4
  56.4 0.9 copy-done.6
  58.0 3.4 %attend.7 = (f32[640,128]{1,0:T(8,128)S(1)}, f32[640,128]{1,0:T(8,128)S(1)}, f32[640,512]{1,0:T(8,128)S(1)}) custom-call(s32[4]{0:T(128)S(1)} %select_reduce_fusion.refs_0_, bf16[640,640]{1,0:T(8,128)(2,1)S(1)} %get-tuple-element.32.refs_0_.refs_1_, bf16[576,1024]{1,0:T(8,128)(2,1)S(1)} %bitcast.8, bf16[128,576]{1,0:T(8,128)(2,1)S(1)} %copy-done.6, ...), custom_call_target="tpu_custom_call" | custom-call | tf_op jit(solution)/shard_map/attend/pallas_call | solution.py:123
  61.4 4.2 %attend.8 = (f32[640,128]{1,0:T(8,128)S(1)}, f32[640,128]{1,0:T(8,128)S(1)}, f32[640,512]{1,0:T(8,128)S(1)}) custom-call(s32[4]{0:T(128)S(1)} %select_reduce_fusion.refs_0_, bf16[640,640]{1,0:T(8,128)(2,1)S(1)} %get-tuple-element.32.refs_0_.refs_1_, ...), custom_call_target="tpu_custom_call", output_to_operand_aliasing={{0}: (3, {}), {1}: (4, {}), {2}: (5, {})} | custom-call | tf_op jit(solution)/shard_map/attend/pallas_call | solution.py:123
  65.6 2.5 %collective-permute-done.6.x_ref.refs_1_ = bf16[576,256]{1,0:T(8,128)(2,1)S(1)} collective-permute-done((bf16[576,256]{1,0:T(8,128)(2,1)}, bf16[576,256]{1,0:T(8,128)(2,1)S(1)}, u32[]{:S(2)}, u32[]{:S(2)}) %collective-permute-start.6) | collective-permute-done | bytes 294944 | tf_op jit(solution)/shard_map/ppermute | solution.py:361
  69.0 5.7 %attend.9 = (f32[640,128]{1,0:T(8,128)S(1)}, f32[640,128]{1,0:T(8,128)S(1)}, f32[640,512]{1,0:T(8,128)S(1)}) custom-call(s32[4]{0:T(128)S(1)} %select_reduce_fusion.refs_0_, bf16[640,640]{1,0:T(8,128)(2,1)S(1)} %after.8.refs_1_.x_ref, bf16[576,1024]{1,0:T(8,128)(2,1)S(1)} %bitcast.9, bf16[576,1024]{1,0:T(8,128)(2,1)} %collective-permute-done.7.refs_2_.refs_3_), custom_call_target="tpu_custom_call" | custom-call | tf_op jit(solution)/shard_map/attend/pallas_call | solution.py:123
  74.7 1.2 %collective-permute-start.11 = (bf16[576,256]{1,0:T(8,128)(2,1)S(1)}, bf16[576,256]{1,0:T(8,128)(2,1)S(1)}, u32[]{:S(2)}, u32[]{:S(2)}) collective-permute-start(bf16[576,256]{1,0:T(8,128)(2,1)S(1)} %after.9.refs_6_.refs_2_), channel_id=1, source_target_pairs={{0,4},{4,0},{8,12},{12,8},{16,20},{20,16},{24,28},{28,24},{1,5},{5... | collective-permute-start | bytes 884744 | tf_op jit(solution)/shard_map/ppermute | solution.py:361
  76.0 0.9 collective-permute-start.12
  76.9 0.9 collective-permute-done.8.refs_5_
  77.8 4.4 %attend.10 = (f32[640,128]{1,0:T(8,128)S(1)}, f32[640,128]{1,0:T(8,128)S(1)}, f32[640,512]{1,0:T(8,128)S(1)}) custom-call(s32[4]{0:T(128)S(1)} %select_reduce_fusion.refs_0_, bf16[640,640]{1,0:T(8,128)(2,1)S(1)} %after.10.refs_1_, ...), custom_call_target="tpu_custom_call", output_to_operand_aliasing={{0}: (6, {}), {1}: (7, {}), {2}: (8, {})} | custom-call | tf_op jit(solution)/shard_map/attend/pallas_call | solution.py:123
  82.2 1.4 %collective-permute-done.12.x_ref = bf16[576,128]{1,0:T(8,128)(2,1)S(1)} collective-permute-done((bf16[576,128]{1,0:T(8,128)(2,1)S(1)}, bf16[576,128]{1,0:T(8,128)(2,1)S(1)}, u32[]{:S(2)}, u32[]{:S(2)}) %collective-permute-start.12) | collective-permute-done | bytes 147488 | tf_op jit(solution)/shard_map/ppermute | solution.py:361
  83.6 0.8 collective-permute-start.13
  84.5 3.1 %attend.12 = (f32[640,128]{1,0:T(8,128)S(1)}, f32[640,128]{1,0:T(8,128)S(1)}, f32[640,512]{1,0:T(8,128)S(1)}) custom-call(s32[4]{0:T(128)S(1)} %select_reduce_fusion.refs_0_, bf16[640,640]{1,0:T(8,128)(2,1)S(1)} %after.10.refs_1_, bf16[576,256]{1,0:T(8,128)(2,1)S(1)} %after.9.refs_6_.refs_2_, ...), custom_call_target="tpu_custom_call", output_to_operand_aliasing={{0}: (5, {}), {1}: (6, {}), {2}: (7, {})} | custom-call | tf_op jit(solution)/shard_map/attend/pallas_call | solution.py:123
  87.5 1.2 %collective-permute-done.13.refs_9_.refs_2_ = bf16[576,128]{1,0:T(8,128)(2,1)S(1)} collective-permute-done((bf16[576,128]{1,0:T(8,128)(2,1)S(1)}, bf16[576,128]{1,0:T(8,128)(2,1)S(1)}, u32[]{:S(2)}, u32[]{:S(2)}) %collective-permute-start.13) | collective-permute-done | bytes 147488 | tf_op jit(solution)/shard_map/ppermute | solution.py:361
  88.8 1.8 %attend.13 = bf16[656,512]{1,0:T(8,128)(2,1)S(1)} custom-call(s32[4]{0:T(128)S(1)} %select_reduce_fusion.refs_0_, bf16[640,640]{1,0:T(8,128)(2,1)S(1)} %after.10.refs_1_, bf16[576,128]{1,0:T(8,128)(2,1)S(1)} %collective-permute-done.13.refs_9_.refs_2_, f32[640,128]{1,0:T(8,128)S(1)} %get-tuple-element.52.refs_3_, f32[640,128]{1,0:T(8,128)S(1)} %get-tuple-element.53.refs_4_, ...), custom_call_target="tpu_custom_call" | custom-call | tf_op jit(solution)/shard_map/attend/pallas_call | solution.py:123
  90.8 2.3 %fusion = bf16[1024,576]{0,1:T(8,128)(2,1)} fusion(bf16[1024,576]{0,1:T(8,128)(2,1)S(1)} %copy-done, pred[1024]{0:T(1024)(128)(4,1)S(1)} %fusion.1, s32[32]{0:T(128)S(1)} %compare_select_fusion, bf16[128,576]{1,0:T(8,128)(2,1)} %copy-done.5), kind=kOutput, calls=%fused_computation.1 | convolution fusion | flops 38961152 | bytes 2401408 | tf_op jit(solution)/shard_map/dot_general | solution.py:405
  93.1 5.8 %attend.11 = (f32[640,128]{1,0:T(8,128)S(1)}, f32[640,128]{1,0:T(8,128)S(1)}, f32[640,512]{1,0:T(8,128)S(1)}) custom-call(s32[4]{0:T(128)S(1)} %select_reduce_fusion.refs_0_, bf16[640,640]{1,0:T(8,128)(2,1)S(1)} %get-tuple-element.32.refs_0_.refs_1_, ...), custom_call_target="tpu_custom_call", output_to_operand_aliasing={{0}: (10, {}), {1}: (11, {}), {2}: (12, {})} | custom-call | tf_op jit(solution)/shard_map/attend/pallas_call | solution.py:123
  98.9 2.6 %collective-permute-done.14.far_ref = bf16[656,512]{1,0:T(8,128)(2,1)S(1)} collective-permute-done((bf16[656,512]{1,0:T(8,128)(2,1)S(1)}, bf16[656,512]{1,0:T(8,128)(2,1)S(1)}, u32[]{:S(2)}, u32[]{:S(2)}) %collective-permute-start.14) | collective-permute-done | bytes 671776 | tf_op jit(solution)/shard_map/ppermute | solution.py:361
  101.5 1.3 %finish.1 = (bf16[32,2048]{1,0:T(8,128)(2,1)}, bf16[8,2048]{1,0:T(8,128)(2,1)}) custom-call(f32[640,128]{1,0:T(8,128)S(1)} %get-tuple-element.47.m_ref, f32[640,128]{1,0:T(8,128)S(1)} %get-tuple-element.48.l_ref, f32[640,512]{1,0:T(8,128)S(1)} %get-tuple-element.49.acc_ref, bf16[656,512]{1,0:T(8,128)(2,1)S(1)} %collective-permute-done.14.far_ref, ...), custom_call_target="tpu_custom_call" | custom-call | flops 83886080 | bytes 4063232 | tf_op jit(solution)/shard_map/finish/pallas_call | solution.py:334
  (60 shorter events, 10.7 us)
Async XLA Ops:
  0.6 18.9 %copy-start = (bf16[1024,576]{0,1:T(8,128)(2,1)S(1)}, bf16[1024,576]{0,1:T(8,128)(2,1)}, u32[]{:S(2)}) copy-start(bf16[1024,576]{0,1:T(8,128)(2,1)} %param.13) | copy-start | bytes 3538948
  2.5 7.1 %collective-permute-start = (bf16[4,4,4736]{2,1,0:T(4,128)(2,1)}, bf16[4,4,4736]{2,1,0:T(4,128)(2,1)S(1)}, u32[]{:S(2)}, u32[]{:S(2)}) collective-permute-start(bf16[4,4,4736]{2,1,0:T(4,128)(2,1)} %get-tuple-element.31), channel_id=1, source_target_pairs={{0,4},{4,0},{8,12},{12,8},{16,20},{20,16},{24,28},{28,24},{1,5},{5... | collective-permute-start | bytes 454664 | tf_op jit(solution)/shard_map/ppermute | solution.py:361
  9.7 7.0 %collective-permute-start.3 = (bf16[2,4,4736]{2,1,0:T(4,128)(2,1)S(1)}, bf16[2,4,4736]{2,1,0:T(4,128)(2,1)S(1)}, u32[]{:S(2)}, u32[]{:S(2)}) collective-permute-start(bf16[2,4,4736]{2,1,0:T(4,128)(2,1)S(1)} %pad_maximum_fusion.3), channel_id=1, source_target_pairs={{0,24},{4,28},{8,16},{12,20},{16,8},{20,12},{24,0},{28,4},{1,25},{... | collective-permute-start | bytes 227336 | tf_op jit(solution)/shard_map/ppermute | solution.py:361
  13.7 5.8 %collective-permute-start.2 = (bf16[2,4,4736]{2,1,0:T(4,128)(2,1)S(1)}, bf16[2,4,4736]{2,1,0:T(4,128)(2,1)S(1)}, u32[]{:S(2)}, u32[]{:S(2)}) collective-permute-start(bf16[2,4,4736]{2,1,0:T(4,128)(2,1)S(1)} %pad_maximum_fusion.2), channel_id=1, source_target_pairs={{0,16},{4,20},{8,24},{12,28},{16,0},{20,4},{24,8},{28,12},{1,17},{... | collective-permute-start | bytes 227336 | tf_op jit(solution)/shard_map/ppermute | solution.py:361
  13.8 5.7 %collective-permute-start.1 = (bf16[2,4,4736]{2,1,0:T(4,128)(2,1)S(1)}, bf16[2,4,4736]{2,1,0:T(4,128)(2,1)S(1)}, u32[]{:S(2)}, u32[]{:S(2)}) collective-permute-start(bf16[2,4,4736]{2,1,0:T(4,128)(2,1)S(1)} %pad_maximum_fusion.1), channel_id=1, source_target_pairs={{0,8},{4,12},{8,0},{12,4},{16,24},{20,28},{24,16},{28,20},{1,9},{5... | collective-permute-start | bytes 227336 | tf_op jit(solution)/shard_map/ppermute | solution.py:361
  19.6 2.6 %copy-start.1 = (bf16[16,128,512]{2,1,0:T(8,128)(2,1)S(1)}, bf16[16,128,512]{2,1,0:T(8,128)(2,1)}, u32[]{:S(2)}) copy-start(bf16[16,128,512]{2,1,0:T(8,128)(2,1)} %w_hbm.1) | copy-start | bytes 6291460
  20.7 40.8 %collective-permute-start.7 = (bf16[576,1024]{1,0:T(8,128)(2,1)}, bf16[576,1024]{1,0:T(8,128)(2,1)}, u32[]{:S(2)}, u32[]{:S(2)}) collective-permute-start(bf16[576,1024]{1,0:T(8,128)(2,1)} %cut.5), channel_id=1, source_target_pairs={{0,4},{4,0},{8,12},{12,8},{16,20},{20,16},{24,28},{28,24},{1,5},{5... | collective-permute-start | bytes 3538952 | tf_op jit(solution)/shard_map/ppermute | solution.py:361
  23.5 0.7 copy-start.3
  24.2 3.7 %copy-start.13 = (s32[8]{0:T(128)S(1)}, s32[8]{0:T(128)}, u32[]{:S(2)}) copy-start(s32[8]{0:T(128)} %param.19) | copy-start | bytes 100
  24.2 44.0 %collective-permute-start.10 = (bf16[640,640]{1,0:T(8,128)(2,1)S(1)}, bf16[640,640]{1,0:T(8,128)(2,1)S(1)}, u32[]{:S(2)}, u32[]{:S(2)}) collective-permute-start(bf16[640,640]{1,0:T(8,128)(2,1)S(1)} %get-tuple-element.32.refs_0_.refs_1_), channel_id=1, source_target_pairs={{0,8},{4,12},{8,0},{12,4},{16,24},{20,28},{24,16},{28,20},{1,9},{5... | collective-permute-start | bytes 2457608 | tf_op jit(solution)/shard_map/ppermute | solution.py:361
  25.5 27.5 %collective-permute-start.4 = (bf16[576,384]{1,0:T(8,128)(2,1)}, bf16[576,384]{1,0:T(8,128)(2,1)S(1)}, u32[]{:S(2)}, u32[]{:S(2)}) collective-permute-start(bf16[576,384]{1,0:T(8,128)(2,1)} %cut.3), channel_id=1, source_target_pairs={{0,16},{4,20},{8,24},{12,28},{16,0},{20,4},{24,8},{28,12},{1,17},{... | collective-permute-start | bytes 1327112 | tf_op jit(solution)/shard_map/ppermute | solution.py:361
  28.8 0.7 copy-start.8
  29.5 0.7 copy-start.9
  30.1 38.0 %collective-permute-start.6 = (bf16[576,256]{1,0:T(8,128)(2,1)}, bf16[576,256]{1,0:T(8,128)(2,1)S(1)}, u32[]{:S(2)}, u32[]{:S(2)}) collective-permute-start(bf16[576,256]{1,0:T(8,128)(2,1)} %get-tuple-element.33), channel_id=1, source_target_pairs={{0,16},{4,20},{8,24},{12,28},{16,0},{20,4},{24,8},{28,12},{1,17},{... | collective-permute-start | bytes 884744 | tf_op jit(solution)/shard_map/ppermute | solution.py:361
  31.4 43.3 %collective-permute-start.9 = (bf16[576,256]{1,0:T(8,128)(2,1)}, bf16[576,256]{1,0:T(8,128)(2,1)S(1)}, u32[]{:S(2)}, u32[]{:S(2)}) collective-permute-start(bf16[576,256]{1,0:T(8,128)(2,1)} %copy-done.8), channel_id=1, source_target_pairs={{0,16},{4,20},{8,24},{12,28},{16,0},{20,4},{24,8},{28,12},{1,17},{... | collective-permute-start | bytes 884744 | tf_op jit(solution)/shard_map/ppermute | solution.py:361
  53.0 23.8 %collective-permute-start.5 = (bf16[576,384]{1,0:T(8,128)(2,1)S(1)}, bf16[576,384]{1,0:T(8,128)(2,1)S(1)}, u32[]{:S(2)}, u32[]{:S(2)}) collective-permute-start(bf16[576,384]{1,0:T(8,128)(2,1)S(1)} %collective-permute-done.4.refs_0_.refs_2_), channel_id=1, source_target_pairs={{0,4},{4,0},{8,12},{12,8},{16,20},{20,16},{24,28},{28,24},{1,5},{5... | collective-permute-start | bytes 1327112 | tf_op jit(solution)/shard_map/ppermute | solution.py:361
  54.8 0.9 copy-start.4
  55.7 0.7 copy-start.5
  56.4 0.9 copy-start.6
  57.3 0.7 copy-start.7
  68.2 9.6 %collective-permute-start.8 = (bf16[576,256]{1,0:T(8,128)(2,1)S(1)}, bf16[576,256]{1,0:T(8,128)(2,1)S(1)}, u32[]{:S(2)}, u32[]{:S(2)}) collective-permute-start(bf16[576,256]{1,0:T(8,128)(2,1)S(1)} %after.7.refs_4_), channel_id=1, source_target_pairs={{0,4},{4,0},{8,12},{12,8},{16,20},{20,16},{24,28},{28,24},{1,5},{5... | collective-permute-start | bytes 884744 | tf_op jit(solution)/shard_map/ppermute | solution.py:361
  74.7 1.3 %copy-start.10 = (bf16[576,128]{1,0:T(8,128)(2,1)S(1)}, bf16[576,128]{1,0:T(8,128)(2,1)}, u32[]{:S(2)}) copy-start(bf16[576,128]{1,0:T(8,128)(2,1)} %copy-done.9) | copy-start | bytes 442372
  74.7 9.7 %collective-permute-start.11 = (bf16[576,256]{1,0:T(8,128)(2,1)S(1)}, bf16[576,256]{1,0:T(8,128)(2,1)S(1)}, u32[]{:S(2)}, u32[]{:S(2)}) collective-permute-start(bf16[576,256]{1,0:T(8,128)(2,1)S(1)} %after.9.refs_6_.refs_2_), channel_id=1, source_target_pairs={{0,4},{4,0},{8,12},{12,8},{16,20},{20,16},{24,28},{28,24},{1,5},{5... | collective-permute-start | bytes 884744 | tf_op jit(solution)/shard_map/ppermute | solution.py:361
  76.0 7.6 %collective-permute-start.12 = (bf16[576,128]{1,0:T(8,128)(2,1)S(1)}, bf16[576,128]{1,0:T(8,128)(2,1)S(1)}, u32[]{:S(2)}, u32[]{:S(2)}) collective-permute-start(bf16[576,128]{1,0:T(8,128)(2,1)S(1)} %copy-done.10), channel_id=1, source_target_pairs={{0,16},{4,20},{8,24},{12,28},{16,0},{20,4},{24,8},{28,12},{1,17},{... | collective-permute-start | bytes 442376 | tf_op jit(solution)/shard_map/ppermute | solution.py:361
  83.6 5.1 %collective-permute-start.13 = (bf16[576,128]{1,0:T(8,128)(2,1)S(1)}, bf16[576,128]{1,0:T(8,128)(2,1)S(1)}, u32[]{:S(2)}, u32[]{:S(2)}) collective-permute-start(bf16[576,128]{1,0:T(8,128)(2,1)S(1)} %after.11.refs_8_.refs_4_), channel_id=1, source_target_pairs={{0,4},{4,0},{8,12},{12,8},{16,20},{20,16},{24,28},{28,24},{1,5},{5... | collective-permute-start | bytes 442376 | tf_op jit(solution)/shard_map/ppermute | solution.py:361
  88.7 1.9 %copy-start.11 = (s32[32]{0:T(128)S(1)}, s32[32]{0:T(128)}, u32[]{:S(2)}) copy-start(s32[32]{0:T(128)} %param.18) | copy-start | bytes 388
  88.7 1.9 %copy-start.12 = (s32[32]{0:T(128)S(1)}, s32[32]{0:T(128)}, u32[]{:S(2)}) copy-start(s32[32]{0:T(128)} %param.17) | copy-start | bytes 388
  90.6 10.9 %collective-permute-start.14 = (bf16[656,512]{1,0:T(8,128)(2,1)S(1)}, bf16[656,512]{1,0:T(8,128)(2,1)S(1)}, u32[]{:S(2)}, u32[]{:S(2)}) collective-permute-start(bf16[656,512]{1,0:T(8,128)(2,1)S(1)} %attend.13), channel_id=1, source_target_pairs={{0,8},{4,12},{8,0},{12,4},{16,24},{20,28},{24,16},{28,20},{1,9},{5... | collective-permute-start | bytes 2015240 | tf_op jit(solution)/shard_map/ppermute | solution.py:361
  93.1 8.4 %copy-start.2 = (bf16[16,512,128]{2,1,0:T(8,128)(2,1)S(1)}, bf16[16,512,128]{2,1,0:T(8,128)(2,1)}, u32[]{:S(2)}) copy-start(bf16[16,512,128]{2,1,0:T(8,128)(2,1)} %w_ref.1) | copy-start | bytes 6291460

commit v10 on v8

--- a/solution.py
+++ b/solution.py
@@ -261,12 +261,12 @@
     extra_ref[...] = jnp.concatenate([new[:, :row], blank], axis=0).astype(jnp.bfloat16)
 
 
-def absorb(count, per_dec, me, order, got, w_uk, row):
+def absorb(count, per_dec, me, order, got, w_uk, row, tokens):
     heads = w_uk.shape[0]
     n = sum(len(x) for x in order)
     return pl.pallas_call(
         functools.partial(absorb_kernel, per_dec, order),
-        in_specs=[pl.BlockSpec(memory_space=pltpu.SMEM)] + [ANY] * (1 + len(got)),
+        in_specs=[pl.BlockSpec(memory_space=pltpu.SMEM)] + [ANY] * (1 + len(got) + len(tokens)),
         out_shape=[
             jax.ShapeDtypeStruct((heads * count, -(-row // LANES) * LANES), jnp.bfloat16),
             jax.ShapeDtypeStruct((LANES, row), jnp.bfloat16),
@@ -279,7 +279,7 @@
         ],
         compiler_params=room(16),
         name="absorb",
-    )(me, w_uk, *got)
+    )(me, w_uk, *got, *tokens)
 
 
 def cut_kernel(spans, x_ref, *refs):
@@ -363,7 +363,9 @@
     far, pair = n // 2, n // 4
     near = [1 << b for b in range(pair.bit_length() - 1)]
     keys = cache_kv.T
-    edges = [i * (pos_dev // 8) for i in (0, 3, 6, 8)]
+    edges = [i * (pos_dev // 8) for i in (0, 1, 5, 7, 8)]
+
+    pieces = [swap(keys[:, : edges[1]], far)]
 
     place = me[None].astype(jnp.int32)
     order = [[r for r in range(n) if not r & 1], [r for r in range(n) if r & 1]]
@@ -383,13 +385,12 @@
         order.append([r ^ o for o, _ in groups[r]])
     got = got[:1] + [swap(x, r) for r, x in zip(sorted(groups)[1:], got[1:])]
 
-    absorbed, extra = absorb(count, rows_dec // n, place, order, got, w_uk, row)
+    absorbed, extra = absorb(count, rows_dec // n, place, order, got, w_uk, row, pieces)
+    new_rows = extra[:span]
     other = swap(absorbed, pair)
     spans = [*zip(edges, edges[1:])]
-    cuts = cut(keys, spans[:1], got[1:]) + cut(keys, spans[1:], [absorbed])
-    pieces = [swap(x, far) for x in cuts]
-    extra = after(extra, pieces[0])
-    new_rows = extra[:span]
+    cuts = cut(keys, spans[1:2], got[1:]) + cut(keys, spans[2:], [absorbed])
+    pieces += [swap(x, far) for x in cuts]
     blocks = [(0, cut(keys, [(0, pos_dev)], got[1:])[0])]
     for stride in near:
         blocks += [(offset ^ stride, swap(x, stride)) for offset, x in blocks]
@@ -431,19 +432,19 @@
 
     home = [(0, 0, keys)]
     side = [(0, i, x) for i, (_, x) in enumerate(blocks) if i]
-    side += stage_of(0, spread(pieces[0]))
     state = attend(fills, absorbed, home, tile, new=(extra, bias))
-    first = stage_of(1, spread(after(pieces[1], state[0])))
+    lead = stage_of(0, spread(pieces[0]))
+    lead += stage_of(1, spread(after(pieces[1], state[0])))
     state = attend(fills, absorbed, side, tile, state=state)
-    other = after(other, state[0], pieces[1])
-    guest = attend(fills, other, home + side, tile)
-    second = stage_of(2, spread(after(pieces[2], guest[0])))
+    first = stage_of(2, spread(after(pieces[2], state[0])))
+    other = after(other, state[0], pieces[2])
+    guest = attend(fills, other, home + side + lead, tile)
+    second = stage_of(3, spread(after(pieces[3], guest[0])))
     first, second = first + second[:1], second[1:]
-    other = after(other, pieces[2])
     guest = attend(fills, other, first, tile, state=guest)
     sent = attend(fills, other, second, tile, state=guest, last=True)
     back = swap(sent, pair)
-    state = attend(fills, absorbed, first + second, tile, state=state)
+    state = attend(fills, absorbed, lead + first + second, tile, state=state)
     span_out, dec_out = finish(count, span, state, back, w_uv)
     return (span_out, dec_out, new_cache)
 

time: 105 us -> 102 us (0.971)
  starting transfers between devices: 16.3 us -> 24.3 us
  waiting for transfers between devices: 50 us -> 42.4 us
  Pallas kernels: 34.1 us -> 30 us
    ppermute x13 -> x15, starting transfers between devices: 16.3 us -> 24.3 us  [swap(): return lax.ppermute(x, 'seq', [(i, i ^ stride) for i in range(n)])]
    ppermute x13 -> x15, waiting for transfers between devices: 50 us -> 42.4 us  [swap(): return lax.ppermute(x, 'seq', [(i, i ^ stride) for i in range(n)])]
    pallas_call x6, Pallas kernels: 27.7 us -> 25.5 us  [attend(): pl.pallas_call(functools.partial(attend_kernel, spec, new is not None, st...]
    pallas_call x3, Pallas kernels: 1.99 us -> 0.16 us  [cut(): pl.pallas_call(functools.partial(cut_kernel, spans), in_specs=[WHOLE] + [...]
  transfers between devices with their start and end apart: 13 -> 15, of which waited for: 9 -> 7; matrix products, arithmetic and copies ran while one was open for 3% -> 4% of each run, Pallas kernels for 27% -> 25%
where the time goes in v10:
time: 102 us
  waiting for transfers between devices  42.4 us (42%)
  Pallas kernels  30 us (29%)
  starting transfers between devices  24.3 us (24%)
  local copies, waits for them, and re-layouts  1.89 us (2%)
  matrix products  1.54 us (2%)
    ppermute x15, waiting for transfers between devices, swap(): return lax.ppermute(x, 'seq', [(i, i ^ stride) for i in range(n)])  42.4 us
    pallas_call x6, Pallas kernels, attend(): pl.pallas_call(functools.partial(attend_kernel, spec, new is not None, st...  25.5 us
    ppermute x15, starting transfers between devices, swap(): return lax.ppermute(x, 'seq', [(i, i ^ stride) for i in range(n)])  24.3 us
  transfers between devices with their start and end apart: 15, of which 7 were waited for; matrix products, arithmetic and copies ran while one was open for 4% of the time, Pallas kernels for 25%

profile of v10, /device:TPU:0, one launch (start us, length us, event | category | flops | bytes accessed | tf_op | source)
XLA Modules:
  0.0 101.7 jit_solution(10363987344355954552)
XLA Ops:
  0.7 1.9 %pack.1 = (bf16[4,4,4736]{2,1,0:T(4,128)(2,1)}, bf16[4,4,4736]{2,1,0:T(4,128)(2,1)}) custom-call(s32[1]{0:T(128)} %bitcast.me_ref, bf16[4,24576]{1,0:T(4,128)(2,1)} %query_ref.1, bf16[1,24576]{1,0:T(2,128)(2,1)} %dec_ref.1, bf16[4,576]{1,0:T(4,128)(2,1)} %span_kv_ref.1, bf16[1,576]{1,0:T(2,128)(2,1)} %dec_kv_ref.1), custom_call_target="tpu_custom_call" | custom-call | tf_op jit(solution)/shard_map/pack/pallas_call | solution.py:196
  2.5 2.9 %collective-permute-start = (bf16[4,4,4736]{2,1,0:T(4,128)(2,1)}, bf16[4,4,4736]{2,1,0:T(4,128)(2,1)S(1)}, u32[]{:S(2)}, u32[]{:S(2)}) collective-permute-start(bf16[4,4,4736]{2,1,0:T(4,128)(2,1)} %get-tuple-element.27), channel_id=1, source_target_pairs={{0,4},{4,0},{8,12},{12,8},{16,20},{20,16},{24,28},{28,24},{1,5},{5... | collective-permute-start | bytes 454664 | tf_op jit(solution)/shard_map/ppermute | solution.py:361
  5.5 0.9 slice.44
  6.4 2.7 %collective-permute-start.4 = (bf16[576,128]{1,0:T(8,128)(2,1)S(1)}, bf16[576,128]{1,0:T(8,128)(2,1)S(1)}, u32[]{:S(2)}, u32[]{:S(2)}) collective-permute-start(bf16[576,128]{1,0:T(8,128)(2,1)S(1)} %slice.44), channel_id=1, source_target_pairs={{0,16},{4,20},{8,24},{12,28},{16,0},{20,4},{24,8},{28,12},{1,17},{... | collective-permute-start | bytes 442376 | tf_op jit(solution)/shard_map/ppermute | solution.py:361
  9.0 0.9 fusion.8
  10.1 3.6 %collective-permute-start.3 = (bf16[2,4,4736]{2,1,0:T(4,128)(2,1)S(1)}, bf16[2,4,4736]{2,1,0:T(4,128)(2,1)S(1)}, u32[]{:S(2)}, u32[]{:S(2)}) collective-permute-start(bf16[2,4,4736]{2,1,0:T(4,128)(2,1)S(1)} %pad_maximum_fusion.3), channel_id=1, source_target_pairs={{0,24},{4,28},{8,16},{12,20},{16,8},{20,12},{24,0},{28,4},{1,25},{... | collective-permute-start | bytes 227336 | tf_op jit(solution)/shard_map/ppermute | solution.py:361
  13.8 0.9 collective-permute-start.1
  14.9 1.8 %collective-permute-done.3.refs_3_.refs_2_ = bf16[2,4,4736]{2,1,0:T(4,128)(2,1)S(1)} collective-permute-done((bf16[2,4,4736]{2,1,0:T(4,128)(2,1)S(1)}, bf16[2,4,4736]{2,1,0:T(4,128)(2,1)S(1)}, u32[]{:S(2)}, u32[]{:S(2)}) %collective-permute-start.3) | collective-permute-done | bytes 75808 | tf_op jit(solution)/shard_map/ppermute | solution.py:361
  16.6 5.7 %collective-permute-done.2.refs_2_.refs_1_ = bf16[2,4,4736]{2,1,0:T(4,128)(2,1)S(1)} collective-permute-done((bf16[2,4,4736]{2,1,0:T(4,128)(2,1)S(1)}, bf16[2,4,4736]{2,1,0:T(4,128)(2,1)S(1)}, u32[]{:S(2)}, u32[]{:S(2)}) %collective-permute-start.2) | collective-permute-done | bytes 75808 | tf_op jit(solution)/shard_map/ppermute | solution.py:361
  22.4 1.1 %collective-permute-start.6 = (bf16[576,512]{1,0:T(8,128)(2,1)S(1)}, bf16[576,512]{1,0:T(8,128)(2,1)S(1)}, u32[]{:S(2)}, u32[]{:S(2)}) collective-permute-start(bf16[576,512]{1,0:T(8,128)(2,1)S(1)} %cut.3), channel_id=1, source_target_pairs={{0,16},{4,20},{8,24},{12,28},{16,0},{20,4},{24,8},{28,12},{1,17},{... | collective-permute-start | bytes 1769480 | tf_op jit(solution)/shard_map/ppermute | solution.py:361
  23.6 0.6 collective-permute-start.9
  24.3 1.3 %absorb.1 = (bf16[640,640]{1,0:T(8,128)(2,1)S(1)}, bf16[128,576]{1,0:T(8,128)(2,1)S(1)}) custom-call(s32[1]{0:T(128)} %bitcast.me_ref, bf16[16,128,512]{2,1,0:T(8,128)(2,1)S(1)} %copy-done.1, bf16[2,4,4736]{2,1,0:T(4,128)(2,1)S(1)} %pad_maximum_fusion.refs_0_, bf16[2,4,4736]{2,1,0:T(4,128)(2,1)S(1)} %collective-permute-done.1.refs_1_.refs_0_, ...), custom_call_target="tpu_custom_call" | custom-call | tf_op jit(solution)/shard_map/absorb/pallas_call | solution.py:267
  25.6 3.0 %collective-permute-start.12 = (bf16[640,640]{1,0:T(8,128)(2,1)S(1)}, bf16[640,640]{1,0:T(8,128)(2,1)S(1)}, u32[]{:S(2)}, u32[]{:S(2)}) collective-permute-start(bf16[640,640]{1,0:T(8,128)(2,1)S(1)} %get-tuple-element.28.refs_1_.refs_0_), channel_id=1, source_target_pairs={{0,8},{4,12},{8,0},{12,4},{16,24},{20,28},{24,16},{28,20},{1,9},{5... | collective-permute-start | bytes 2457608 | tf_op jit(solution)/shard_map/ppermute | solution.py:361
  28.7 0.2 select_reduce_fusion.refs_0_
  29.0 3.5 %attend.6 = (f32[640,128]{1,0:T(8,128)S(1)}, f32[640,128]{1,0:T(8,128)S(1)}, f32[640,512]{1,0:T(8,128)S(1)}) custom-call(s32[4]{0:T(128)S(1)} %select_reduce_fusion.refs_0_, bf16[640,640]{1,0:T(8,128)(2,1)S(1)} %get-tuple-element.28.refs_1_.refs_0_, bf16[576,1024]{1,0:T(8,128)(2,1)S(1)} %bitcast.8, bf16[128,576]{1,0:T(8,128)(2,1)S(1)} %get-tuple-element.29.refs_3_, ...), custom_call_target="tpu_custom_call" | custom-call | tf_op jit(solution)/shard_map/attend/pallas_call | solution.py:123
  32.4 17.5 %collective-permute-done.6.x_ref = bf16[576,512]{1,0:T(8,128)(2,1)S(1)} collective-permute-done((bf16[576,512]{1,0:T(8,128)(2,1)S(1)}, bf16[576,512]{1,0:T(8,128)(2,1)S(1)}, u32[]{:S(2)}, u32[]{:S(2)}) %collective-permute-start.6) | collective-permute-done | bytes 589856 | tf_op jit(solution)/shard_map/ppermute | solution.py:361
  50.0 0.5 collective-permute-start.7
  50.6 1.6 %collective-permute-start.5 = (bf16[576,128]{1,0:T(8,128)(2,1)S(1)}, bf16[576,128]{1,0:T(8,128)(2,1)S(1)}, u32[]{:S(2)}, u32[]{:S(2)}) collective-permute-start(bf16[576,128]{1,0:T(8,128)(2,1)S(1)} %collective-permute-done.4.refs_4_.refs_2_), channel_id=1, source_target_pairs={{0,4},{4,0},{8,12},{12,8},{16,20},{20,16},{24,28},{28,24},{1,5},{5... | collective-permute-start | bytes 442376 | tf_op jit(solution)/shard_map/ppermute | solution.py:361
  52.2 3.5 %attend.7 = (f32[640,128]{1,0:T(8,128)S(1)}, f32[640,128]{1,0:T(8,128)S(1)}, f32[640,512]{1,0:T(8,128)S(1)}) custom-call(s32[4]{0:T(128)S(1)} %select_reduce_fusion.refs_0_, bf16[640,640]{1,0:T(8,128)(2,1)S(1)} %get-tuple-element.28.refs_1_.refs_0_, ...), custom_call_target="tpu_custom_call", output_to_operand_aliasing={{0}: (3, {}), {1}: (4, {}), {2}: (5, {})} | custom-call | tf_op jit(solution)/shard_map/attend/pallas_call | solution.py:123
  55.7 8.8 %collective-permute-done.8.x_ref.refs_1_ = bf16[576,256]{1,0:T(8,128)(2,1)S(1)} collective-permute-done((bf16[576,256]{1,0:T(8,128)(2,1)S(1)}, bf16[576,256]{1,0:T(8,128)(2,1)S(1)}, u32[]{:S(2)}, u32[]{:S(2)}) %collective-permute-start.8) | collective-permute-done | bytes 294944 | tf_op jit(solution)/shard_map/ppermute | solution.py:361
  64.5 1.5 %collective-permute-start.10 = (bf16[576,256]{1,0:T(8,128)(2,1)S(1)}, bf16[576,256]{1,0:T(8,128)(2,1)S(1)}, u32[]{:S(2)}, u32[]{:S(2)}) collective-permute-start(bf16[576,256]{1,0:T(8,128)(2,1)S(1)} %after.5.refs_6_.refs_2_), channel_id=1, source_target_pairs={{0,4},{4,0},{8,12},{12,8},{16,20},{20,16},{24,28},{28,24},{1,5},{5... | collective-permute-start | bytes 884744 | tf_op jit(solution)/shard_map/ppermute | solution.py:361
  66.1 3.3 %collective-permute-done.5.refs_5_.refs_3_ = bf16[576,128]{1,0:T(8,128)(2,1)S(1)} collective-permute-done((bf16[576,128]{1,0:T(8,128)(2,1)S(1)}, bf16[576,128]{1,0:T(8,128)(2,1)S(1)}, u32[]{:S(2)}, u32[]{:S(2)}) %collective-permute-start.5) | collective-permute-done | bytes 147488 | tf_op jit(solution)/shard_map/ppermute | solution.py:361
  69.4 7.6 %attend.8 = (f32[640,128]{1,0:T(8,128)S(1)}, f32[640,128]{1,0:T(8,128)S(1)}, f32[640,512]{1,0:T(8,128)S(1)}) custom-call(s32[4]{0:T(128)S(1)} %select_reduce_fusion.refs_0_, bf16[640,640]{1,0:T(8,128)(2,1)S(1)} %after.6.refs_1_, bf16[576,1024]{1,0:T(8,128)(2,1)S(1)} %bitcast.10, bf16[576,1024]{1,0:T(8,128)(2,1)S(1)} %collective-permute-done.9.refs_2_.refs_3_, ...), custom_call_target="tpu_custom_call" | custom-call | tf_op jit(solution)/shard_map/attend/pallas_call | solution.py:123
  77.0 0.6 collective-permute-start.13
  77.6 3.3 %attend.10 = (f32[640,128]{1,0:T(8,128)S(1)}, f32[640,128]{1,0:T(8,128)S(1)}, f32[640,512]{1,0:T(8,128)S(1)}) custom-call(s32[4]{0:T(128)S(1)} %select_reduce_fusion.refs_0_, bf16[640,640]{1,0:T(8,128)(2,1)S(1)} %after.6.refs_1_, bf16[576,256]{1,0:T(8,128)(2,1)S(1)} %after.5.refs_6_.refs_2_, ...), custom_call_target="tpu_custom_call", output_to_operand_aliasing={{0}: (5, {}), {1}: (6, {}), {2}: (7, {})} | custom-call | tf_op jit(solution)/shard_map/attend/pallas_call | solution.py:123
  80.8 1.4 %collective-permute-done.13.refs_9_.refs_2_ = bf16[576,128]{1,0:T(8,128)(2,1)S(1)} collective-permute-done((bf16[576,128]{1,0:T(8,128)(2,1)S(1)}, bf16[576,128]{1,0:T(8,128)(2,1)S(1)}, u32[]{:S(2)}, u32[]{:S(2)}) %collective-permute-start.13) | collective-permute-done | bytes 147488 | tf_op jit(solution)/shard_map/ppermute | solution.py:361
  82.2 1.8 %attend.11 = bf16[656,512]{1,0:T(8,128)(2,1)S(1)} custom-call(s32[4]{0:T(128)S(1)} %select_reduce_fusion.refs_0_, bf16[640,640]{1,0:T(8,128)(2,1)S(1)} %after.6.refs_1_, bf16[576,128]{1,0:T(8,128)(2,1)S(1)} %collective-permute-done.13.refs_9_.refs_2_, f32[640,128]{1,0:T(8,128)S(1)} %get-tuple-element.44.refs_3_, f32[640,128]{1,0:T(8,128)S(1)} %get-tuple-element.45.refs_4_, ...), custom_call_target="tpu_custom_call" | custom-call | tf_op jit(solution)/shard_map/attend/pallas_call | solution.py:123
  84.0 5.1 %collective-permute-start.14 = (bf16[656,512]{1,0:T(8,128)(2,1)S(1)}, bf16[656,512]{1,0:T(8,128)(2,1)S(1)}, u32[]{:S(2)}, u32[]{:S(2)}) collective-permute-start(bf16[656,512]{1,0:T(8,128)(2,1)S(1)} %attend.11), channel_id=1, source_target_pairs={{0,8},{4,12},{8,0},{12,4},{16,24},{20,28},{24,16},{28,20},{1,9},{5... | collective-permute-start | bytes 2015240 | tf_op jit(solution)/shard_map/ppermute | solution.py:361
  89.2 1.5 %fusion = bf16[1024,576]{0,1:T(8,128)(2,1)} fusion(bf16[1024,576]{0,1:T(8,128)(2,1)S(1)} %copy-done, pred[1024]{0:T(1024)(128)(4,1)S(1)} %fusion.1, s32[32]{0:T(128)S(1)} %compare_select_fusion, bf16[128,576]{1,0:T(8,128)(2,1)S(1)} %get-tuple-element.29.refs_3_), kind=kOutput, calls=%fused_computation.1 | convolution fusion | flops 38961152 | bytes 2401792 | tf_op jit(solution)/shard_map/dot_general | solution.py:406
  90.7 5.8 %attend.9 = (f32[640,128]{1,0:T(8,128)S(1)}, f32[640,128]{1,0:T(8,128)S(1)}, f32[640,512]{1,0:T(8,128)S(1)}) custom-call(s32[4]{0:T(128)S(1)} %select_reduce_fusion.refs_0_, bf16[640,640]{1,0:T(8,128)(2,1)S(1)} %get-tuple-element.28.refs_1_.refs_0_, ...), custom_call_target="tpu_custom_call", output_to_operand_aliasing={{0}: (10, {}), {1}: (11, {}), {2}: (12, {})} | custom-call | tf_op jit(solution)/shard_map/attend/pallas_call | solution.py:123
  96.6 3.9 %collective-permute-done.14.far_ref = bf16[656,512]{1,0:T(8,128)(2,1)S(1)} collective-permute-done((bf16[656,512]{1,0:T(8,128)(2,1)S(1)}, bf16[656,512]{1,0:T(8,128)(2,1)S(1)}, u32[]{:S(2)}, u32[]{:S(2)}) %collective-permute-start.14) | collective-permute-done | bytes 671776 | tf_op jit(solution)/shard_map/ppermute | solution.py:361
  100.5 1.2 %finish.1 = (bf16[32,2048]{1,0:T(8,128)(2,1)}, bf16[8,2048]{1,0:T(8,128)(2,1)}) custom-call(f32[640,128]{1,0:T(8,128)S(1)} %get-tuple-element.39.m_ref, f32[640,128]{1,0:T(8,128)S(1)} %get-tuple-element.40.l_ref, f32[640,512]{1,0:T(8,128)S(1)} %get-tuple-element.41.acc_ref, bf16[656,512]{1,0:T(8,128)(2,1)S(1)} %collective-permute-done.14.far_ref, ...), custom_call_target="tpu_custom_call" | custom-call | flops 83886080 | bytes 4063232 | tf_op jit(solution)/shard_map/finish/pallas_call | solution.py:334
  (44 shorter events, 1.0 us)
Async XLA Ops:
  0.6 21.7 %copy-start = (bf16[1024,576]{0,1:T(8,128)(2,1)S(1)}, bf16[1024,576]{0,1:T(8,128)(2,1)}, u32[]{:S(2)}) copy-start(bf16[1024,576]{0,1:T(8,128)(2,1)} %param.13) | copy-start | bytes 3538948
  0.6 14.1 %copy-start.5 = (s32[8]{0:T(128)S(1)}, s32[8]{0:T(128)}, u32[]{:S(2)}) copy-start(s32[8]{0:T(128)} %param.19) | copy-start | bytes 100
  2.5 7.4 %collective-permute-start = (bf16[4,4,4736]{2,1,0:T(4,128)(2,1)}, bf16[4,4,4736]{2,1,0:T(4,128)(2,1)S(1)}, u32[]{:S(2)}, u32[]{:S(2)}) collective-permute-start(bf16[4,4,4736]{2,1,0:T(4,128)(2,1)} %get-tuple-element.27), channel_id=1, source_target_pairs={{0,4},{4,0},{8,12},{12,8},{16,20},{20,16},{24,28},{28,24},{1,5},{5... | collective-permute-start | bytes 454664 | tf_op jit(solution)/shard_map/ppermute | solution.py:361
  6.4 17.9 %collective-permute-start.4 = (bf16[576,128]{1,0:T(8,128)(2,1)S(1)}, bf16[576,128]{1,0:T(8,128)(2,1)S(1)}, u32[]{:S(2)}, u32[]{:S(2)}) collective-permute-start(bf16[576,128]{1,0:T(8,128)(2,1)S(1)} %slice.44), channel_id=1, source_target_pairs={{0,16},{4,20},{8,24},{12,28},{16,0},{20,4},{24,8},{28,12},{1,17},{... | collective-permute-start | bytes 442376 | tf_op jit(solution)/shard_map/ppermute | solution.py:361
  10.1 6.5 %collective-permute-start.3 = (bf16[2,4,4736]{2,1,0:T(4,128)(2,1)S(1)}, bf16[2,4,4736]{2,1,0:T(4,128)(2,1)S(1)}, u32[]{:S(2)}, u32[]{:S(2)}) collective-permute-start(bf16[2,4,4736]{2,1,0:T(4,128)(2,1)S(1)} %pad_maximum_fusion.3), channel_id=1, source_target_pairs={{0,24},{4,28},{8,16},{12,20},{16,8},{20,12},{24,0},{28,4},{1,25},{... | collective-permute-start | bytes 227336 | tf_op jit(solution)/shard_map/ppermute | solution.py:361
  13.7 8.6 %collective-permute-start.2 = (bf16[2,4,4736]{2,1,0:T(4,128)(2,1)S(1)}, bf16[2,4,4736]{2,1,0:T(4,128)(2,1)S(1)}, u32[]{:S(2)}, u32[]{:S(2)}) collective-permute-start(bf16[2,4,4736]{2,1,0:T(4,128)(2,1)S(1)} %pad_maximum_fusion.2), channel_id=1, source_target_pairs={{0,16},{4,20},{8,24},{12,28},{16,0},{20,4},{24,8},{28,12},{1,17},{... | collective-permute-start | bytes 227336 | tf_op jit(solution)/shard_map/ppermute | solution.py:361
  13.8 8.5 %collective-permute-start.1 = (bf16[2,4,4736]{2,1,0:T(4,128)(2,1)S(1)}, bf16[2,4,4736]{2,1,0:T(4,128)(2,1)S(1)}, u32[]{:S(2)}, u32[]{:S(2)}) collective-permute-start(bf16[2,4,4736]{2,1,0:T(4,128)(2,1)S(1)} %pad_maximum_fusion.1), channel_id=1, source_target_pairs={{0,8},{4,12},{8,0},{12,4},{16,24},{20,28},{24,16},{28,20},{1,9},{5... | collective-permute-start | bytes 227336 | tf_op jit(solution)/shard_map/ppermute | solution.py:361
  22.4 1.9 %copy-start.1 = (bf16[16,128,512]{2,1,0:T(8,128)(2,1)S(1)}, bf16[16,128,512]{2,1,0:T(8,128)(2,1)}, u32[]{:S(2)}) copy-start(bf16[16,128,512]{2,1,0:T(8,128)(2,1)} %w_hbm.1) | copy-start | bytes 6291460
  22.4 27.6 %collective-permute-start.6 = (bf16[576,512]{1,0:T(8,128)(2,1)S(1)}, bf16[576,512]{1,0:T(8,128)(2,1)S(1)}, u32[]{:S(2)}, u32[]{:S(2)}) collective-permute-start(bf16[576,512]{1,0:T(8,128)(2,1)S(1)} %cut.3), channel_id=1, source_target_pairs={{0,16},{4,20},{8,24},{12,28},{16,0},{20,4},{24,8},{28,12},{1,17},{... | collective-permute-start | bytes 1769480 | tf_op jit(solution)/shard_map/ppermute | solution.py:361
  23.6 28.6 %collective-permute-start.9 = (bf16[576,1024]{1,0:T(8,128)(2,1)S(1)}, bf16[576,1024]{1,0:T(8,128)(2,1)S(1)}, u32[]{:S(2)}, u32[]{:S(2)}) collective-permute-start(bf16[576,1024]{1,0:T(8,128)(2,1)S(1)} %cut.5), channel_id=1, source_target_pairs={{0,4},{4,0},{8,12},{12,8},{16,20},{20,16},{24,28},{28,24},{1,5},{5... | collective-permute-start | bytes 3538952 | tf_op jit(solution)/shard_map/ppermute | solution.py:361
  24.2 4.5 %copy-start.6 = (s32[8]{0:T(128)S(1)}, s32[8]{0:T(128)}, u32[]{:S(2)}) copy-start(s32[8]{0:T(128)} %param.16) | copy-start | bytes 100
  25.6 39.0 %collective-permute-start.12 = (bf16[640,640]{1,0:T(8,128)(2,1)S(1)}, bf16[640,640]{1,0:T(8,128)(2,1)S(1)}, u32[]{:S(2)}, u32[]{:S(2)}) collective-permute-start(bf16[640,640]{1,0:T(8,128)(2,1)S(1)} %get-tuple-element.28.refs_1_.refs_0_), channel_id=1, source_target_pairs={{0,8},{4,12},{8,0},{12,4},{16,24},{20,28},{24,16},{28,20},{1,9},{5... | collective-permute-start | bytes 2457608 | tf_op jit(solution)/shard_map/ppermute | solution.py:361
  50.0 19.4 %collective-permute-start.7 = (bf16[576,512]{1,0:T(8,128)(2,1)S(1)}, bf16[576,512]{1,0:T(8,128)(2,1)S(1)}, u32[]{:S(2)}, u32[]{:S(2)}) collective-permute-start(bf16[576,512]{1,0:T(8,128)(2,1)S(1)} %after.4.refs_6_.refs_4_), channel_id=1, source_target_pairs={{0,4},{4,0},{8,12},{12,8},{16,20},{20,16},{24,28},{28,24},{1,5},{5... | collective-permute-start | bytes 1769480 | tf_op jit(solution)/shard_map/ppermute | solution.py:361
  50.5 14.0 %collective-permute-start.8 = (bf16[576,256]{1,0:T(8,128)(2,1)S(1)}, bf16[576,256]{1,0:T(8,128)(2,1)S(1)}, u32[]{:S(2)}, u32[]{:S(2)}) collective-permute-start(bf16[576,256]{1,0:T(8,128)(2,1)S(1)} %get-tuple-element.31), channel_id=1, source_target_pairs={{0,16},{4,20},{8,24},{12,28},{16,0},{20,4},{24,8},{28,12},{1,17},{... | collective-permute-start | bytes 884744 | tf_op jit(solution)/shard_map/ppermute | solution.py:361
  50.6 18.8 %collective-permute-start.5 = (bf16[576,128]{1,0:T(8,128)(2,1)S(1)}, bf16[576,128]{1,0:T(8,128)(2,1)S(1)}, u32[]{:S(2)}, u32[]{:S(2)}) collective-permute-start(bf16[576,128]{1,0:T(8,128)(2,1)S(1)} %collective-permute-done.4.refs_4_.refs_2_), channel_id=1, source_target_pairs={{0,4},{4,0},{8,12},{12,8},{16,20},{20,16},{24,28},{28,24},{1,5},{5... | collective-permute-start | bytes 442376 | tf_op jit(solution)/shard_map/ppermute | solution.py:361
  64.5 13.0 %collective-permute-start.10 = (bf16[576,256]{1,0:T(8,128)(2,1)S(1)}, bf16[576,256]{1,0:T(8,128)(2,1)S(1)}, u32[]{:S(2)}, u32[]{:S(2)}) collective-permute-start(bf16[576,256]{1,0:T(8,128)(2,1)S(1)} %after.5.refs_6_.refs_2_), channel_id=1, source_target_pairs={{0,4},{4,0},{8,12},{12,8},{16,20},{20,16},{24,28},{28,24},{1,5},{5... | collective-permute-start | bytes 884744 | tf_op jit(solution)/shard_map/ppermute | solution.py:361
  66.1 10.9 %collective-permute-start.11 = (bf16[576,128]{1,0:T(8,128)(2,1)S(1)}, bf16[576,128]{1,0:T(8,128)(2,1)S(1)}, u32[]{:S(2)}, u32[]{:S(2)}) collective-permute-start(bf16[576,128]{1,0:T(8,128)(2,1)S(1)} %get-tuple-element.35), channel_id=1, source_target_pairs={{0,16},{4,20},{8,24},{12,28},{16,0},{20,4},{24,8},{28,12},{1,17},{... | collective-permute-start | bytes 442376 | tf_op jit(solution)/shard_map/ppermute | solution.py:361
  77.0 5.2 %collective-permute-start.13 = (bf16[576,128]{1,0:T(8,128)(2,1)S(1)}, bf16[576,128]{1,0:T(8,128)(2,1)S(1)}, u32[]{:S(2)}, u32[]{:S(2)}) collective-permute-start(bf16[576,128]{1,0:T(8,128)(2,1)S(1)} %after.7.refs_8_.refs_4_), channel_id=1, source_target_pairs={{0,4},{4,0},{8,12},{12,8},{16,20},{20,16},{24,28},{28,24},{1,5},{5... | collective-permute-start | bytes 442376 | tf_op jit(solution)/shard_map/ppermute | solution.py:361
  82.2 6.9 %copy-start.3 = (s32[32]{0:T(128)S(1)}, s32[32]{0:T(128)}, u32[]{:S(2)}) copy-start(s32[32]{0:T(128)} %param.18) | copy-start | bytes 388
  82.2 6.9 %copy-start.4 = (s32[32]{0:T(128)S(1)}, s32[32]{0:T(128)}, u32[]{:S(2)}) copy-start(s32[32]{0:T(128)} %param.17) | copy-start | bytes 388
  84.0 16.5 %collective-permute-start.14 = (bf16[656,512]{1,0:T(8,128)(2,1)S(1)}, bf16[656,512]{1,0:T(8,128)(2,1)S(1)}, u32[]{:S(2)}, u32[]{:S(2)}) collective-permute-start(bf16[656,512]{1,0:T(8,128)(2,1)S(1)} %attend.11), channel_id=1, source_target_pairs={{0,8},{4,12},{8,0},{12,4},{16,24},{20,28},{24,16},{28,20},{1,9},{5... | collective-permute-start | bytes 2015240 | tf_op jit(solution)/shard_map/ppermute | solution.py:361
  90.7 9.8 %copy-start.2 = (bf16[16,512,128]{2,1,0:T(8,128)(2,1)S(1)}, bf16[16,512,128]{2,1,0:T(8,128)(2,1)}, u32[]{:S(2)}) copy-start(bf16[16,512,128]{2,1,0:T(8,128)(2,1)} %w_ref.1) | copy-start | bytes 6291460

commit v11 on v8

--- a/solution.py
+++ b/solution.py
@@ -431,19 +431,18 @@
 
     home = [(0, 0, keys)]
     side = [(0, i, x) for i, (_, x) in enumerate(blocks) if i]
-    side += stage_of(0, spread(pieces[0]))
     state = attend(fills, absorbed, home, tile, new=(extra, bias))
+    lead = stage_of(0, spread(pieces[0]))
+    state = attend(fills, absorbed, side, tile, state=state)
     first = stage_of(1, spread(after(pieces[1], state[0])))
-    state = attend(fills, absorbed, side, tile, state=state)
     other = after(other, state[0], pieces[1])
-    guest = attend(fills, other, home + side, tile)
+    guest = attend(fills, other, home + side + lead, tile)
     second = stage_of(2, spread(after(pieces[2], guest[0])))
     first, second = first + second[:1], second[1:]
-    other = after(other, pieces[2])
     guest = attend(fills, other, first, tile, state=guest)
     sent = attend(fills, other, second, tile, state=guest, last=True)
     back = swap(sent, pair)
-    state = attend(fills, absorbed, first + second, tile, state=state)
+    state = attend(fills, absorbed, lead + first + second, tile, state=state)
     span_out, dec_out = finish(count, span, state, back, w_uv)
     return (span_out, dec_out, new_cache)
 

time: 105 us -> 104 us (level)
  waiting for transfers between devices: 50 us -> 47.5 us
    ppermute x13, waiting for transfers between devices: 50 us -> 47.5 us  [swap(): return lax.ppermute(x, 'seq', [(i, i ^ stride) for i in range(n)])]
  transfers between devices with their start and end apart: 13 -> 13, of which waited for: 9 -> 9; matrix products, arithmetic and copies ran while one was open for 3% -> 3% of each run, Pallas kernels for 27% -> 29%
where the time goes in v11:
time: 104 us
  waiting for transfers between devices  47.5 us (46%)
  Pallas kernels  35 us (34%)
  starting transfers between devices  16.3 us (16%)
  local copies, waits for them, and re-layouts  1.69 us (2%)
  matrix products  1.55 us (1%)
    ppermute x13, waiting for transfers between devices, swap(): return lax.ppermute(x, 'seq', [(i, i ^ stride) for i in range(n)])  47.5 us
    pallas_call x6, Pallas kernels, attend(): pl.pallas_call(functools.partial(attend_kernel, spec, new is not None, st...  28.6 us
    ppermute x13, starting transfers between devices, swap(): return lax.ppermute(x, 'seq', [(i, i ^ stride) for i in range(n)])  16.3 us
  transfers between devices with their start and end apart: 13, of which 9 were waited for; matrix products, arithmetic and copies ran while one was open for 3% of the time, Pallas kernels for 29%

profile of v11, /device:TPU:0, one launch (start us, length us, event | category | flops | bytes accessed | tf_op | source)
XLA Modules:
  0.0 103.6 jit_solution(7710209650100089439)
XLA Ops:
  0.6 1.9 %pack.1 = (bf16[4,4,4736]{2,1,0:T(4,128)(2,1)}, bf16[4,4,4736]{2,1,0:T(4,128)(2,1)}) custom-call(s32[1]{0:T(128)} %bitcast.me_ref, bf16[4,24576]{1,0:T(4,128)(2,1)} %query_ref.1, bf16[1,24576]{1,0:T(2,128)(2,1)} %dec_ref.1, bf16[4,576]{1,0:T(4,128)(2,1)} %span_kv_ref.1, bf16[1,576]{1,0:T(2,128)(2,1)} %dec_kv_ref.1), custom_call_target="tpu_custom_call" | custom-call | tf_op jit(solution)/shard_map/pack/pallas_call | solution.py:196
  2.5 2.9 %collective-permute-start = (bf16[4,4,4736]{2,1,0:T(4,128)(2,1)}, bf16[4,4,4736]{2,1,0:T(4,128)(2,1)S(1)}, u32[]{:S(2)}, u32[]{:S(2)}) collective-permute-start(bf16[4,4,4736]{2,1,0:T(4,128)(2,1)} %get-tuple-element.27), channel_id=1, source_target_pairs={{0,4},{4,0},{8,12},{12,8},{16,20},{20,16},{24,28},{28,24},{1,5},{5... | collective-permute-start | bytes 454664 | tf_op jit(solution)/shard_map/ppermute | solution.py:361
  5.4 0.9 fusion.8
  6.3 3.3 %collective-permute-done = bf16[4,4,4736]{2,1,0:T(4,128)(2,1)S(1)} collective-permute-done((bf16[4,4,4736]{2,1,0:T(4,128)(2,1)}, bf16[4,4,4736]{2,1,0:T(4,128)(2,1)S(1)}, u32[]{:S(2)}, u32[]{:S(2)}) %collective-permute-start) | collective-permute-done | bytes 151584 | tf_op jit(solution)/shard_map/ppermute | solution.py:361
  9.7 3.9 %collective-permute-start.3 = (bf16[2,4,4736]{2,1,0:T(4,128)(2,1)S(1)}, bf16[2,4,4736]{2,1,0:T(4,128)(2,1)S(1)}, u32[]{:S(2)}, u32[]{:S(2)}) collective-permute-start(bf16[2,4,4736]{2,1,0:T(4,128)(2,1)S(1)} %pad_maximum_fusion.3), channel_id=1, source_target_pairs={{0,24},{4,28},{8,16},{12,20},{16,8},{20,12},{24,0},{28,4},{1,25},{... | collective-permute-start | bytes 227336 | tf_op jit(solution)/shard_map/ppermute | solution.py:361
  13.8 0.6 collective-permute-start.1
  14.5 2.3 %collective-permute-done.3.refs_3_.refs_2_ = bf16[2,4,4736]{2,1,0:T(4,128)(2,1)S(1)} collective-permute-done((bf16[2,4,4736]{2,1,0:T(4,128)(2,1)S(1)}, bf16[2,4,4736]{2,1,0:T(4,128)(2,1)S(1)}, u32[]{:S(2)}, u32[]{:S(2)}) %collective-permute-start.3) | collective-permute-done | bytes 75808 | tf_op jit(solution)/shard_map/ppermute | solution.py:361
  16.7 2.8 %collective-permute-done.2.refs_2_.refs_1_ = bf16[2,4,4736]{2,1,0:T(4,128)(2,1)S(1)} collective-permute-done((bf16[2,4,4736]{2,1,0:T(4,128)(2,1)S(1)}, bf16[2,4,4736]{2,1,0:T(4,128)(2,1)S(1)}, u32[]{:S(2)}, u32[]{:S(2)}) %collective-permute-start.2) | collective-permute-done | bytes 75808 | tf_op jit(solution)/shard_map/ppermute | solution.py:361
  19.6 1.7 %collective-permute-start.4 = (bf16[576,384]{1,0:T(8,128)(2,1)S(1)}, bf16[576,384]{1,0:T(8,128)(2,1)}, u32[]{:S(2)}, u32[]{:S(2)}) collective-permute-start(bf16[576,384]{1,0:T(8,128)(2,1)S(1)} %cut.3), channel_id=1, source_target_pairs={{0,16},{4,20},{8,24},{12,28},{16,0},{20,4},{24,8},{28,12},{1,17},{... | collective-permute-start | bytes 1327112 | tf_op jit(solution)/shard_map/ppermute | solution.py:361
  21.3 1.1 %cut.5 = bf16[576,1024]{1,0:T(8,128)(2,1)} custom-call(bf16[576,1024]{1,0:T(8,128)(2,1)S(1)} %bitcast.6, bf16[2,4,4736]{2,1,0:T(4,128)(2,1)S(1)} %collective-permute-done.1.refs_1_.refs_0_, bf16[2,4,4736]{2,1,0:T(4,128)(2,1)S(1)} %collective-permute-done.2.refs_2_.refs_1_, bf16[2,4,4736]{2,1,0:T(4,128)(2,1)S(1)} %collective-permute-done.3.refs_3_.refs_2_), custom_call_target="tpu_custom_call" | custom-call | tf_op jit(solution)/shard_map/cut/pallas_call | solution.py:291
  22.4 1.5 %collective-permute-start.7 = (bf16[576,1024]{1,0:T(8,128)(2,1)}, bf16[576,1024]{1,0:T(8,128)(2,1)}, u32[]{:S(2)}, u32[]{:S(2)}) collective-permute-start(bf16[576,1024]{1,0:T(8,128)(2,1)} %cut.5), channel_id=1, source_target_pairs={{0,4},{4,0},{8,12},{12,8},{16,20},{20,16},{24,28},{28,24},{1,5},{5... | collective-permute-start | bytes 3538952 | tf_op jit(solution)/shard_map/ppermute | solution.py:361
  23.9 1.3 %absorb.1 = (bf16[640,640]{1,0:T(8,128)(2,1)S(1)}, bf16[128,576]{1,0:T(8,128)(2,1)S(1)}) custom-call(s32[1]{0:T(128)} %bitcast.me_ref, bf16[16,128,512]{2,1,0:T(8,128)(2,1)S(1)} %copy-done.1, bf16[2,4,4736]{2,1,0:T(4,128)(2,1)S(1)} %pad_maximum_fusion.refs_0_, bf16[2,4,4736]{2,1,0:T(4,128)(2,1)S(1)} %collective-permute-done.1.refs_1_.refs_0_, ...), custom_call_target="tpu_custom_call" | custom-call | tf_op jit(solution)/shard_map/absorb/pallas_call | solution.py:267
  25.3 1.4 %collective-permute-start.10 = (bf16[640,640]{1,0:T(8,128)(2,1)S(1)}, bf16[640,640]{1,0:T(8,128)(2,1)S(1)}, u32[]{:S(2)}, u32[]{:S(2)}) collective-permute-start(bf16[640,640]{1,0:T(8,128)(2,1)S(1)} %get-tuple-element.28.refs_0_.refs_1_), channel_id=1, source_target_pairs={{0,8},{4,12},{8,0},{12,4},{16,24},{20,28},{24,16},{28,20},{1,9},{5... | collective-permute-start | bytes 2457608 | tf_op jit(solution)/shard_map/ppermute | solution.py:361
  26.7 0.8 cut.4
  27.5 0.7 copy-done.3
  28.8 11.7 %collective-permute-done.4.refs_0_.refs_4_.refs_2_ = bf16[576,384]{1,0:T(8,128)(2,1)} collective-permute-done((bf16[576,384]{1,0:T(8,128)(2,1)S(1)}, bf16[576,384]{1,0:T(8,128)(2,1)}, u32[]{:S(2)}, u32[]{:S(2)}) %collective-permute-start.4) | collective-permute-done | bytes 442400 | tf_op jit(solution)/shard_map/ppermute | solution.py:361
  40.5 1.5 %collective-permute-start.5 = (bf16[576,384]{1,0:T(8,128)(2,1)}, bf16[576,384]{1,0:T(8,128)(2,1)}, u32[]{:S(2)}, u32[]{:S(2)}) collective-permute-start(bf16[576,384]{1,0:T(8,128)(2,1)} %collective-permute-done.4.refs_0_.refs_4_.refs_2_), channel_id=1, source_target_pairs={{0,4},{4,0},{8,12},{12,8},{16,20},{20,16},{24,28},{28,24},{1,5},{5... | collective-permute-start | bytes 1327112 | tf_op jit(solution)/shard_map/ppermute | solution.py:361
  42.4 3.4 %attend.6 = (f32[640,128]{1,0:T(8,128)S(1)}, f32[640,128]{1,0:T(8,128)S(1)}, f32[640,512]{1,0:T(8,128)S(1)}) custom-call(s32[4]{0:T(128)S(1)} %select_reduce_fusion.refs_0_, bf16[640,640]{1,0:T(8,128)(2,1)S(1)} %get-tuple-element.28.refs_0_.refs_1_, bf16[576,1024]{1,0:T(8,128)(2,1)S(1)} %bitcast.8, bf16[128,576]{1,0:T(8,128)(2,1)S(1)} %after.4.refs_3_, ...), custom_call_target="tpu_custom_call" | custom-call | tf_op jit(solution)/shard_map/attend/pallas_call | solution.py:123
  45.8 5.8 %collective-permute-done.7.refs_2_.refs_3_ = bf16[576,1024]{1,0:T(8,128)(2,1)} collective-permute-done((bf16[576,1024]{1,0:T(8,128)(2,1)}, bf16[576,1024]{1,0:T(8,128)(2,1)}, u32[]{:S(2)}, u32[]{:S(2)}) %collective-permute-start.7) | collective-permute-done | bytes 1179680 | tf_op jit(solution)/shard_map/ppermute | solution.py:361
  51.6 4.2 %attend.7 = (f32[640,128]{1,0:T(8,128)S(1)}, f32[640,128]{1,0:T(8,128)S(1)}, f32[640,512]{1,0:T(8,128)S(1)}) custom-call(s32[4]{0:T(128)S(1)} %select_reduce_fusion.refs_0_, bf16[640,640]{1,0:T(8,128)(2,1)S(1)} %get-tuple-element.28.refs_0_.refs_1_, ...), custom_call_target="tpu_custom_call", output_to_operand_aliasing={{0}: (3, {}), {1}: (4, {}), {2}: (5, {})} | custom-call | tf_op jit(solution)/shard_map/attend/pallas_call | solution.py:123
  55.8 9.8 %collective-permute-done.6.x_ref.refs_1_ = bf16[576,384]{1,0:T(8,128)(2,1)S(1)} collective-permute-done((bf16[576,384]{1,0:T(8,128)(2,1)}, bf16[576,384]{1,0:T(8,128)(2,1)S(1)}, u32[]{:S(2)}, u32[]{:S(2)}) %collective-permute-start.6) | collective-permute-done | bytes 442400 | tf_op jit(solution)/shard_map/ppermute | solution.py:361
  65.6 1.5 %collective-permute-start.8 = (bf16[576,384]{1,0:T(8,128)(2,1)S(1)}, bf16[576,384]{1,0:T(8,128)(2,1)S(1)}, u32[]{:S(2)}, u32[]{:S(2)}) collective-permute-start(bf16[576,384]{1,0:T(8,128)(2,1)S(1)} %after.5.refs_4_.refs_2_), channel_id=1, source_target_pairs={{0,4},{4,0},{8,12},{12,8},{16,20},{20,16},{24,28},{28,24},{1,5},{5... | collective-permute-start | bytes 1327112 | tf_op jit(solution)/shard_map/ppermute | solution.py:361
  67.1 7.7 %attend.8 = (f32[640,128]{1,0:T(8,128)S(1)}, f32[640,128]{1,0:T(8,128)S(1)}, f32[640,512]{1,0:T(8,128)S(1)}) custom-call(s32[4]{0:T(128)S(1)} %select_reduce_fusion.refs_0_, bf16[640,640]{1,0:T(8,128)(2,1)S(1)} %after.6.refs_1_, bf16[576,1024]{1,0:T(8,128)(2,1)S(1)} %bitcast.9, bf16[576,1024]{1,0:T(8,128)(2,1)} %collective-permute-done.7.refs_2_.refs_3_, ...), custom_call_target="tpu_custom_call" | custom-call | tf_op jit(solution)/shard_map/attend/pallas_call | solution.py:123
  74.9 0.6 collective-permute-start.11
  75.4 2.6 %collective-permute-done.8.refs_5_.refs_3_ = bf16[576,384]{1,0:T(8,128)(2,1)S(1)} collective-permute-done((bf16[576,384]{1,0:T(8,128)(2,1)S(1)}, bf16[576,384]{1,0:T(8,128)(2,1)S(1)}, u32[]{:S(2)}, u32[]{:S(2)}) %collective-permute-start.8) | collective-permute-done | bytes 442400 | tf_op jit(solution)/shard_map/ppermute | solution.py:361
  78.0 4.6 %attend.10 = (f32[640,128]{1,0:T(8,128)S(1)}, f32[640,128]{1,0:T(8,128)S(1)}, f32[640,512]{1,0:T(8,128)S(1)}) custom-call(s32[4]{0:T(128)S(1)} %select_reduce_fusion.refs_0_, bf16[640,640]{1,0:T(8,128)(2,1)S(1)} %after.6.refs_1_, bf16[576,384]{1,0:T(8,128)(2,1)S(1)} %after.5.refs_4_.refs_2_, ...), custom_call_target="tpu_custom_call", output_to_operand_aliasing={{0}: (5, {}), {1}: (6, {}), {2}: (7, {})} | custom-call | tf_op jit(solution)/shard_map/attend/pallas_call | solution.py:123
  82.6 1.4 %collective-permute-done.11.refs_7_.refs_2_ = bf16[576,256]{1,0:T(8,128)(2,1)S(1)} collective-permute-done((bf16[576,256]{1,0:T(8,128)(2,1)S(1)}, bf16[576,256]{1,0:T(8,128)(2,1)S(1)}, u32[]{:S(2)}, u32[]{:S(2)}) %collective-permute-start.11) | collective-permute-done | bytes 294944 | tf_op jit(solution)/shard_map/ppermute | solution.py:361
  83.9 2.2 %attend.11 = bf16[656,512]{1,0:T(8,128)(2,1)S(1)} custom-call(s32[4]{0:T(128)S(1)} %select_reduce_fusion.refs_0_, bf16[640,640]{1,0:T(8,128)(2,1)S(1)} %after.6.refs_1_, bf16[576,256]{1,0:T(8,128)(2,1)S(1)} %collective-permute-done.11.refs_7_.refs_2_, f32[640,128]{1,0:T(8,128)S(1)} %get-tuple-element.44.refs_3_, f32[640,128]{1,0:T(8,128)S(1)} %get-tuple-element.45.refs_4_, ...), custom_call_target="tpu_custom_call" | custom-call | tf_op jit(solution)/shard_map/attend/pallas_call | solution.py:123
  86.3 1.5 %fusion = bf16[1024,576]{0,1:T(8,128)(2,1)} fusion(bf16[1024,576]{0,1:T(8,128)(2,1)S(1)} %copy-done, pred[1024]{0:T(1024)(128)(4,1)S(1)} %fusion.1, s32[32]{0:T(128)S(1)} %compare_select_fusion, bf16[128,576]{1,0:T(8,128)(2,1)S(1)} %after.4.refs_3_), kind=kOutput, calls=%fused_computation.1 | convolution fusion | flops 38961152 | bytes 2401792 | tf_op jit(solution)/shard_map/dot_general | solution.py:405
  87.9 6.6 %attend.9 = (f32[640,128]{1,0:T(8,128)S(1)}, f32[640,128]{1,0:T(8,128)S(1)}, f32[640,512]{1,0:T(8,128)S(1)}) custom-call(s32[4]{0:T(128)S(1)} %select_reduce_fusion.refs_0_, bf16[640,640]{1,0:T(8,128)(2,1)S(1)} %get-tuple-element.28.refs_0_.refs_1_, ...), custom_call_target="tpu_custom_call", output_to_operand_aliasing={{0}: (8, {}), {1}: (9, {}), {2}: (10, {})} | custom-call | tf_op jit(solution)/shard_map/attend/pallas_call | solution.py:123
  94.4 7.9 %collective-permute-done.12.far_ref = bf16[656,512]{1,0:T(8,128)(2,1)S(1)} collective-permute-done((bf16[656,512]{1,0:T(8,128)(2,1)S(1)}, bf16[656,512]{1,0:T(8,128)(2,1)S(1)}, u32[]{:S(2)}, u32[]{:S(2)}) %collective-permute-start.12) | collective-permute-done | bytes 671776 | tf_op jit(solution)/shard_map/ppermute | solution.py:361
  102.4 1.3 %finish.1 = (bf16[32,2048]{1,0:T(8,128)(2,1)}, bf16[8,2048]{1,0:T(8,128)(2,1)}) custom-call(f32[640,128]{1,0:T(8,128)S(1)} %get-tuple-element.39.m_ref, f32[640,128]{1,0:T(8,128)S(1)} %get-tuple-element.40.l_ref, f32[640,512]{1,0:T(8,128)S(1)} %get-tuple-element.41.acc_ref, bf16[656,512]{1,0:T(8,128)(2,1)S(1)} %collective-permute-done.12.far_ref, ...), custom_call_target="tpu_custom_call" | custom-call | flops 83886080 | bytes 4063232 | tf_op jit(solution)/shard_map/finish/pallas_call | solution.py:334
  (41 shorter events, 1.7 us)
Async XLA Ops:
  0.6 18.9 %copy-start = (bf16[1024,576]{0,1:T(8,128)(2,1)S(1)}, bf16[1024,576]{0,1:T(8,128)(2,1)}, u32[]{:S(2)}) copy-start(bf16[1024,576]{0,1:T(8,128)(2,1)} %param.13) | copy-start | bytes 3538948
  2.5 7.1 %collective-permute-start = (bf16[4,4,4736]{2,1,0:T(4,128)(2,1)}, bf16[4,4,4736]{2,1,0:T(4,128)(2,1)S(1)}, u32[]{:S(2)}, u32[]{:S(2)}) collective-permute-start(bf16[4,4,4736]{2,1,0:T(4,128)(2,1)} %get-tuple-element.27), channel_id=1, source_target_pairs={{0,4},{4,0},{8,12},{12,8},{16,20},{20,16},{24,28},{28,24},{1,5},{5... | collective-permute-start | bytes 454664 | tf_op jit(solution)/shard_map/ppermute | solution.py:361
  9.7 7.0 %collective-permute-start.3 = (bf16[2,4,4736]{2,1,0:T(4,128)(2,1)S(1)}, bf16[2,4,4736]{2,1,0:T(4,128)(2,1)S(1)}, u32[]{:S(2)}, u32[]{:S(2)}) collective-permute-start(bf16[2,4,4736]{2,1,0:T(4,128)(2,1)S(1)} %pad_maximum_fusion.3), channel_id=1, source_target_pairs={{0,24},{4,28},{8,16},{12,20},{16,8},{20,12},{24,0},{28,4},{1,25},{... | collective-permute-start | bytes 227336 | tf_op jit(solution)/shard_map/ppermute | solution.py:361
  13.7 5.8 %collective-permute-start.2 = (bf16[2,4,4736]{2,1,0:T(4,128)(2,1)S(1)}, bf16[2,4,4736]{2,1,0:T(4,128)(2,1)S(1)}, u32[]{:S(2)}, u32[]{:S(2)}) collective-permute-start(bf16[2,4,4736]{2,1,0:T(4,128)(2,1)S(1)} %pad_maximum_fusion.2), channel_id=1, source_target_pairs={{0,16},{4,20},{8,24},{12,28},{16,0},{20,4},{24,8},{28,12},{1,17},{... | collective-permute-start | bytes 227336 | tf_op jit(solution)/shard_map/ppermute | solution.py:361
  13.8 5.7 %collective-permute-start.1 = (bf16[2,4,4736]{2,1,0:T(4,128)(2,1)S(1)}, bf16[2,4,4736]{2,1,0:T(4,128)(2,1)S(1)}, u32[]{:S(2)}, u32[]{:S(2)}) collective-permute-start(bf16[2,4,4736]{2,1,0:T(4,128)(2,1)S(1)} %pad_maximum_fusion.1), channel_id=1, source_target_pairs={{0,8},{4,12},{8,0},{12,4},{16,24},{20,28},{24,16},{28,20},{1,9},{5... | collective-permute-start | bytes 227336 | tf_op jit(solution)/shard_map/ppermute | solution.py:361
  19.6 4.3 %copy-start.1 = (bf16[16,128,512]{2,1,0:T(8,128)(2,1)S(1)}, bf16[16,128,512]{2,1,0:T(8,128)(2,1)}, u32[]{:S(2)}) copy-start(bf16[16,128,512]{2,1,0:T(8,128)(2,1)} %w_hbm.1) | copy-start | bytes 6291460
  19.6 20.9 %collective-permute-start.4 = (bf16[576,384]{1,0:T(8,128)(2,1)S(1)}, bf16[576,384]{1,0:T(8,128)(2,1)}, u32[]{:S(2)}, u32[]{:S(2)}) collective-permute-start(bf16[576,384]{1,0:T(8,128)(2,1)S(1)} %cut.3), channel_id=1, source_target_pairs={{0,16},{4,20},{8,24},{12,28},{16,0},{20,4},{24,8},{28,12},{1,17},{... | collective-permute-start | bytes 1327112 | tf_op jit(solution)/shard_map/ppermute | solution.py:361
  22.4 4.2 %copy-start.6 = (s32[8]{0:T(128)S(1)}, s32[8]{0:T(128)}, u32[]{:S(2)}) copy-start(s32[8]{0:T(128)} %param.19) | copy-start | bytes 100
  22.4 29.2 %collective-permute-start.7 = (bf16[576,1024]{1,0:T(8,128)(2,1)}, bf16[576,1024]{1,0:T(8,128)(2,1)}, u32[]{:S(2)}, u32[]{:S(2)}) collective-permute-start(bf16[576,1024]{1,0:T(8,128)(2,1)} %cut.5), channel_id=1, source_target_pairs={{0,4},{4,0},{8,12},{12,8},{16,20},{20,16},{24,28},{28,24},{1,5},{5... | collective-permute-start | bytes 3538952 | tf_op jit(solution)/shard_map/ppermute | solution.py:361
  25.2 17.0 %copy-start.7 = (s32[8]{0:T(128)S(1)}, s32[8]{0:T(128)}, u32[]{:S(2)}) copy-start(s32[8]{0:T(128)} %param.16) | copy-start | bytes 100
  25.3 40.4 %collective-permute-start.10 = (bf16[640,640]{1,0:T(8,128)(2,1)S(1)}, bf16[640,640]{1,0:T(8,128)(2,1)S(1)}, u32[]{:S(2)}, u32[]{:S(2)}) collective-permute-start(bf16[640,640]{1,0:T(8,128)(2,1)S(1)} %get-tuple-element.28.refs_0_.refs_1_), channel_id=1, source_target_pairs={{0,8},{4,12},{8,0},{12,4},{16,24},{20,28},{24,16},{28,20},{1,9},{5... | collective-permute-start | bytes 2457608 | tf_op jit(solution)/shard_map/ppermute | solution.py:361
  27.5 0.7 copy-start.3
  28.3 37.3 %collective-permute-start.6 = (bf16[576,384]{1,0:T(8,128)(2,1)}, bf16[576,384]{1,0:T(8,128)(2,1)S(1)}, u32[]{:S(2)}, u32[]{:S(2)}) collective-permute-start(bf16[576,384]{1,0:T(8,128)(2,1)} %get-tuple-element.29), channel_id=1, source_target_pairs={{0,16},{4,20},{8,24},{12,28},{16,0},{20,4},{24,8},{28,12},{1,17},{... | collective-permute-start | bytes 1327112 | tf_op jit(solution)/shard_map/ppermute | solution.py:361
  40.5 26.6 %collective-permute-start.5 = (bf16[576,384]{1,0:T(8,128)(2,1)}, bf16[576,384]{1,0:T(8,128)(2,1)}, u32[]{:S(2)}, u32[]{:S(2)}) collective-permute-start(bf16[576,384]{1,0:T(8,128)(2,1)} %collective-permute-done.4.refs_0_.refs_4_.refs_2_), channel_id=1, source_target_pairs={{0,4},{4,0},{8,12},{12,8},{16,20},{20,16},{24,28},{28,24},{1,5},{5... | collective-permute-start | bytes 1327112 | tf_op jit(solution)/shard_map/ppermute | solution.py:361
  42.1 32.8 %collective-permute-start.9 = (bf16[576,256]{1,0:T(8,128)(2,1)}, bf16[576,256]{1,0:T(8,128)(2,1)S(1)}, u32[]{:S(2)}, u32[]{:S(2)}) collective-permute-start(bf16[576,256]{1,0:T(8,128)(2,1)} %copy-done.3), channel_id=1, source_target_pairs={{0,16},{4,20},{8,24},{12,28},{16,0},{20,4},{24,8},{28,12},{1,17},{... | collective-permute-start | bytes 884744 | tf_op jit(solution)/shard_map/ppermute | solution.py:361
  65.6 12.4 %collective-permute-start.8 = (bf16[576,384]{1,0:T(8,128)(2,1)S(1)}, bf16[576,384]{1,0:T(8,128)(2,1)S(1)}, u32[]{:S(2)}, u32[]{:S(2)}) collective-permute-start(bf16[576,384]{1,0:T(8,128)(2,1)S(1)} %after.5.refs_4_.refs_2_), channel_id=1, source_target_pairs={{0,4},{4,0},{8,12},{12,8},{16,20},{20,16},{24,28},{28,24},{1,5},{5... | collective-permute-start | bytes 1327112 | tf_op jit(solution)/shard_map/ppermute | solution.py:361
  74.9 9.1 %collective-permute-start.11 = (bf16[576,256]{1,0:T(8,128)(2,1)S(1)}, bf16[576,256]{1,0:T(8,128)(2,1)S(1)}, u32[]{:S(2)}, u32[]{:S(2)}) collective-permute-start(bf16[576,256]{1,0:T(8,128)(2,1)S(1)} %after.7.refs_6_.refs_4_), channel_id=1, source_target_pairs={{0,4},{4,0},{8,12},{12,8},{16,20},{20,16},{24,28},{28,24},{1,5},{5... | collective-permute-start | bytes 884744 | tf_op jit(solution)/shard_map/ppermute | solution.py:361
  83.9 2.2 %copy-start.4 = (s32[32]{0:T(128)S(1)}, s32[32]{0:T(128)}, u32[]{:S(2)}) copy-start(s32[32]{0:T(128)} %param.18) | copy-start | bytes 388
  83.9 2.2 %copy-start.5 = (s32[32]{0:T(128)S(1)}, s32[32]{0:T(128)}, u32[]{:S(2)}) copy-start(s32[32]{0:T(128)} %param.17) | copy-start | bytes 388
  86.1 16.2 %collective-permute-start.12 = (bf16[656,512]{1,0:T(8,128)(2,1)S(1)}, bf16[656,512]{1,0:T(8,128)(2,1)S(1)}, u32[]{:S(2)}, u32[]{:S(2)}) collective-permute-start(bf16[656,512]{1,0:T(8,128)(2,1)S(1)} %attend.11), channel_id=1, source_target_pairs={{0,8},{4,12},{8,0},{12,4},{16,24},{20,28},{24,16},{28,20},{1,9},{5... | collective-permute-start | bytes 2015240 | tf_op jit(solution)/shard_map/ppermute | solution.py:361
  87.9 14.5 %copy-start.2 = (bf16[16,512,128]{2,1,0:T(8,128)(2,1)S(1)}, bf16[16,512,128]{2,1,0:T(8,128)(2,1)}, u32[]{:S(2)}) copy-start(bf16[16,512,128]{2,1,0:T(8,128)(2,1)} %w_ref.1) | copy-start | bytes 6291460

commit v12 on v10

--- a/solution.py
+++ b/solution.py
@@ -433,12 +433,14 @@
     home = [(0, 0, keys)]
     side = [(0, i, x) for i, (_, x) in enumerate(blocks) if i]
     state = attend(fills, absorbed, home, tile, new=(extra, bias))
-    lead = stage_of(0, spread(pieces[0]))
-    lead += stage_of(1, spread(after(pieces[1], state[0])))
+    lead = stage_of(1, spread(after(pieces[1], state[0])))
+    lead += stage_of(0, spread(pieces[0]))
     state = attend(fills, absorbed, side, tile, state=state)
-    first = stage_of(2, spread(after(pieces[2], state[0])))
-    other = after(other, state[0], pieces[2])
-    guest = attend(fills, other, home + side + lead, tile)
+    other = after(other, state[0])
+    guest = attend(fills, other, home + side, tile)
+    first = stage_of(2, spread(after(pieces[2], guest[0])))
+    other = after(other, pieces[2])
+    guest = attend(fills, other, lead, tile, state=guest)
     second = stage_of(3, spread(after(pieces[3], guest[0])))
     first, second = first + second[:1], second[1:]
     guest = attend(fills, other, first, tile, state=guest)

time: 102 us -> 100 us (0.980)
  starting transfers between devices: 24.3 us -> 19.3 us
  Pallas kernels: 30 us -> 31.6 us
  waiting for transfers between devices: 42.4 us -> 43.9 us
    ppermute x15, starting transfers between devices: 24.3 us -> 19.3 us  [swap(): return lax.ppermute(x, 'seq', [(i, i ^ stride) for i in range(n)])]
    pallas_call x6 -> x7, Pallas kernels: 25.5 us -> 27.1 us  [attend(): pl.pallas_call(functools.partial(attend_kernel, spec, new is not None, st...]
    ppermute x15, waiting for transfers between devices: 42.4 us -> 43.9 us  [swap(): return lax.ppermute(x, 'seq', [(i, i ^ stride) for i in range(n)])]
  transfers between devices with their start and end apart: 15 -> 15, of which waited for: 7 -> 7; matrix products, arithmetic and copies ran while one was open for 4% -> 4% of each run, Pallas kernels for 25% -> 27%
where the time goes in v12:
time: 100 us; the launch traced here: 99.9 us
  waiting for transfers between devices  43.9 us (44%)
  Pallas kernels  31.6 us (32%)
  starting transfers between devices  19.3 us (19%)
  local copies, waits for them, and re-layouts  1.89 us (2%)
  matrix products  1.54 us (2%)
    ppermute x15, waiting for transfers between devices, swap(): return lax.ppermute(x, 'seq', [(i, i ^ stride) for i in range(n)])  43.9 us
    pallas_call x7, Pallas kernels, attend(): pl.pallas_call(functools.partial(attend_kernel, spec, new is not None, st...  27.1 us
    ppermute x15, starting transfers between devices, swap(): return lax.ppermute(x, 'seq', [(i, i ^ stride) for i in range(n)])  19.3 us
  transfers between devices with their start and end apart: 15, of which 7 were waited for; matrix products, arithmetic and copies ran while one was open for 4% of the time, Pallas kernels for 27%

profile of v12, /device:TPU:0, one launch (start us, length us, event | category | flops | bytes accessed | tf_op | source)
XLA Modules:
  0.0 99.9 jit_solution(350642745001782908)
XLA Ops:
  0.7 1.9 %pack.1 = (bf16[4,4,4736]{2,1,0:T(4,128)(2,1)}, bf16[4,4,4736]{2,1,0:T(4,128)(2,1)}) custom-call(s32[1]{0:T(128)} %bitcast.me_ref, bf16[4,24576]{1,0:T(4,128)(2,1)} %query_ref.1, bf16[1,24576]{1,0:T(2,128)(2,1)} %dec_ref.1, bf16[4,576]{1,0:T(4,128)(2,1)} %span_kv_ref.1, bf16[1,576]{1,0:T(2,128)(2,1)} %dec_kv_ref.1), custom_call_target="tpu_custom_call" | custom-call | tf_op jit(solution)/shard_map/pack/pallas_call | solution.py:196
  2.5 2.9 %collective-permute-start = (bf16[4,4,4736]{2,1,0:T(4,128)(2,1)}, bf16[4,4,4736]{2,1,0:T(4,128)(2,1)S(1)}, u32[]{:S(2)}, u32[]{:S(2)}) collective-permute-start(bf16[4,4,4736]{2,1,0:T(4,128)(2,1)} %get-tuple-element.30), channel_id=1, source_target_pairs={{0,4},{4,0},{8,12},{12,8},{16,20},{20,16},{24,28},{28,24},{1,5},{5... | collective-permute-start | bytes 454664 | tf_op jit(solution)/shard_map/ppermute | solution.py:361
  5.5 0.9 slice.44
  6.4 2.7 %collective-permute-start.4 = (bf16[576,128]{1,0:T(8,128)(2,1)S(1)}, bf16[576,128]{1,0:T(8,128)(2,1)S(1)}, u32[]{:S(2)}, u32[]{:S(2)}) collective-permute-start(bf16[576,128]{1,0:T(8,128)(2,1)S(1)} %slice.44), channel_id=1, source_target_pairs={{0,16},{4,20},{8,24},{12,28},{16,0},{20,4},{24,8},{28,12},{1,17},{... | collective-permute-start | bytes 442376 | tf_op jit(solution)/shard_map/ppermute | solution.py:361
  9.0 0.9 fusion.8
  10.1 3.6 %collective-permute-start.3 = (bf16[2,4,4736]{2,1,0:T(4,128)(2,1)S(1)}, bf16[2,4,4736]{2,1,0:T(4,128)(2,1)S(1)}, u32[]{:S(2)}, u32[]{:S(2)}) collective-permute-start(bf16[2,4,4736]{2,1,0:T(4,128)(2,1)S(1)} %pad_maximum_fusion.3), channel_id=1, source_target_pairs={{0,24},{4,28},{8,16},{12,20},{16,8},{20,12},{24,0},{28,4},{1,25},{... | collective-permute-start | bytes 227336 | tf_op jit(solution)/shard_map/ppermute | solution.py:361
  13.8 0.9 collective-permute-start.1
  14.8 1.8 %collective-permute-done.3.refs_3_.refs_2_ = bf16[2,4,4736]{2,1,0:T(4,128)(2,1)S(1)} collective-permute-done((bf16[2,4,4736]{2,1,0:T(4,128)(2,1)S(1)}, bf16[2,4,4736]{2,1,0:T(4,128)(2,1)S(1)}, u32[]{:S(2)}, u32[]{:S(2)}) %collective-permute-start.3) | collective-permute-done | bytes 75808 | tf_op jit(solution)/shard_map/ppermute | solution.py:361
  16.6 5.7 %collective-permute-done.2.refs_2_.refs_1_ = bf16[2,4,4736]{2,1,0:T(4,128)(2,1)S(1)} collective-permute-done((bf16[2,4,4736]{2,1,0:T(4,128)(2,1)S(1)}, bf16[2,4,4736]{2,1,0:T(4,128)(2,1)S(1)}, u32[]{:S(2)}, u32[]{:S(2)}) %collective-permute-start.2) | collective-permute-done | bytes 75808 | tf_op jit(solution)/shard_map/ppermute | solution.py:361
  22.4 1.1 %collective-permute-start.5 = (bf16[576,512]{1,0:T(8,128)(2,1)S(1)}, bf16[576,512]{1,0:T(8,128)(2,1)S(1)}, u32[]{:S(2)}, u32[]{:S(2)}) collective-permute-start(bf16[576,512]{1,0:T(8,128)(2,1)S(1)} %cut.3), channel_id=1, source_target_pairs={{0,16},{4,20},{8,24},{12,28},{16,0},{20,4},{24,8},{28,12},{1,17},{... | collective-permute-start | bytes 1769480 | tf_op jit(solution)/shard_map/ppermute | solution.py:361
  23.6 0.6 collective-permute-start.10
  24.3 1.3 %absorb.1 = (bf16[640,640]{1,0:T(8,128)(2,1)S(1)}, bf16[128,576]{1,0:T(8,128)(2,1)S(1)}) custom-call(s32[1]{0:T(128)} %bitcast.me_ref, bf16[16,128,512]{2,1,0:T(8,128)(2,1)S(1)} %copy-done.1, bf16[2,4,4736]{2,1,0:T(4,128)(2,1)S(1)} %pad_maximum_fusion.refs_0_, bf16[2,4,4736]{2,1,0:T(4,128)(2,1)S(1)} %collective-permute-done.1.refs_1_.refs_0_, ...), custom_call_target="tpu_custom_call" | custom-call | tf_op jit(solution)/shard_map/absorb/pallas_call | solution.py:267
  25.6 3.0 %collective-permute-start.9 = (bf16[640,640]{1,0:T(8,128)(2,1)S(1)}, bf16[640,640]{1,0:T(8,128)(2,1)S(1)}, u32[]{:S(2)}, u32[]{:S(2)}) collective-permute-start(bf16[640,640]{1,0:T(8,128)(2,1)S(1)} %get-tuple-element.31.refs_1_.refs_0_), channel_id=1, source_target_pairs={{0,8},{4,12},{8,0},{12,4},{16,24},{20,28},{24,16},{28,20},{1,9},{5... | collective-permute-start | bytes 2457608 | tf_op jit(solution)/shard_map/ppermute | solution.py:361
  28.7 0.2 select_reduce_fusion.refs_0_
  29.0 3.5 %attend.7 = (f32[640,128]{1,0:T(8,128)S(1)}, f32[640,128]{1,0:T(8,128)S(1)}, f32[640,512]{1,0:T(8,128)S(1)}) custom-call(s32[4]{0:T(128)S(1)} %select_reduce_fusion.refs_0_, bf16[640,640]{1,0:T(8,128)(2,1)S(1)} %get-tuple-element.31.refs_1_.refs_0_, bf16[576,1024]{1,0:T(8,128)(2,1)S(1)} %bitcast.8, bf16[128,576]{1,0:T(8,128)(2,1)S(1)} %get-tuple-element.32.refs_3_, ...), custom_call_target="tpu_custom_call" | custom-call | tf_op jit(solution)/shard_map/attend/pallas_call | solution.py:123
  32.4 17.5 %collective-permute-done.5.x_ref = bf16[576,512]{1,0:T(8,128)(2,1)S(1)} collective-permute-done((bf16[576,512]{1,0:T(8,128)(2,1)S(1)}, bf16[576,512]{1,0:T(8,128)(2,1)S(1)}, u32[]{:S(2)}, u32[]{:S(2)}) %collective-permute-start.5) | collective-permute-done | bytes 589856 | tf_op jit(solution)/shard_map/ppermute | solution.py:361
  50.0 0.5 collective-permute-start.6
  50.6 1.6 %collective-permute-start.7 = (bf16[576,128]{1,0:T(8,128)(2,1)S(1)}, bf16[576,128]{1,0:T(8,128)(2,1)S(1)}, u32[]{:S(2)}, u32[]{:S(2)}) collective-permute-start(bf16[576,128]{1,0:T(8,128)(2,1)S(1)} %collective-permute-done.4.refs_4_), channel_id=1, source_target_pairs={{0,4},{4,0},{8,12},{12,8},{16,20},{20,16},{24,28},{28,24},{1,5},{5... | collective-permute-start | bytes 442376 | tf_op jit(solution)/shard_map/ppermute | solution.py:361
  52.2 3.5 %attend.8 = (f32[640,128]{1,0:T(8,128)S(1)}, f32[640,128]{1,0:T(8,128)S(1)}, f32[640,512]{1,0:T(8,128)S(1)}) custom-call(s32[4]{0:T(128)S(1)} %select_reduce_fusion.refs_0_, bf16[640,640]{1,0:T(8,128)(2,1)S(1)} %get-tuple-element.31.refs_1_.refs_0_, ...), custom_call_target="tpu_custom_call", output_to_operand_aliasing={{0}: (3, {}), {1}: (4, {}), {2}: (5, {})} | custom-call | tf_op jit(solution)/shard_map/attend/pallas_call | solution.py:123
  55.7 6.4 %collective-permute-done.9.x_ref = bf16[640,640]{1,0:T(8,128)(2,1)S(1)} collective-permute-done((bf16[640,640]{1,0:T(8,128)(2,1)S(1)}, bf16[640,640]{1,0:T(8,128)(2,1)S(1)}, u32[]{:S(2)}, u32[]{:S(2)}) %collective-permute-start.9) | collective-permute-done | bytes 819232 | tf_op jit(solution)/shard_map/ppermute | solution.py:361
  62.0 4.9 %attend.9 = (f32[640,128]{1,0:T(8,128)S(1)}, f32[640,128]{1,0:T(8,128)S(1)}, f32[640,512]{1,0:T(8,128)S(1)}) custom-call(s32[4]{0:T(128)S(1)} %select_reduce_fusion.refs_0_, bf16[640,640]{1,0:T(8,128)(2,1)S(1)} %after.6.refs_1_.x_ref, bf16[576,1024]{1,0:T(8,128)(2,1)S(1)} %bitcast.10, bf16[576,1024]{1,0:T(8,128)(2,1)S(1)} %collective-permute-done.10.refs_2_.refs_3_), custom_call_target="tpu_custom_call" | custom-call | tf_op jit(solution)/shard_map/attend/pallas_call | solution.py:123
  67.0 0.6 collective-permute-start.11
  67.6 4.4 %attend.10 = (f32[640,128]{1,0:T(8,128)S(1)}, f32[640,128]{1,0:T(8,128)S(1)}, f32[640,512]{1,0:T(8,128)S(1)}) custom-call(s32[4]{0:T(128)S(1)} %select_reduce_fusion.refs_0_, bf16[640,640]{1,0:T(8,128)(2,1)S(1)} %after.8.refs_1_, bf16[576,512]{1,0:T(8,128)(2,1)S(1)} %after.5.refs_2_, ...), custom_call_target="tpu_custom_call", output_to_operand_aliasing={{0}: (6, {}), {1}: (7, {}), {2}: (8, {})} | custom-call | tf_op jit(solution)/shard_map/attend/pallas_call | solution.py:123
  72.0 4.0 %collective-permute-done.12.x_ref = bf16[576,128]{1,0:T(8,128)(2,1)S(1)} collective-permute-done((bf16[576,128]{1,0:T(8,128)(2,1)S(1)}, bf16[576,128]{1,0:T(8,128)(2,1)S(1)}, u32[]{:S(2)}, u32[]{:S(2)}) %collective-permute-start.12) | collective-permute-done | bytes 147488 | tf_op jit(solution)/shard_map/ppermute | solution.py:361
  76.0 1.5 %collective-permute-start.13 = (bf16[576,128]{1,0:T(8,128)(2,1)S(1)}, bf16[576,128]{1,0:T(8,128)(2,1)S(1)}, u32[]{:S(2)}, u32[]{:S(2)}) collective-permute-start(bf16[576,128]{1,0:T(8,128)(2,1)S(1)} %after.9.refs_8_.refs_4_), channel_id=1, source_target_pairs={{0,4},{4,0},{8,12},{12,8},{16,20},{20,16},{24,28},{28,24},{1,5},{5... | collective-permute-start | bytes 442376 | tf_op jit(solution)/shard_map/ppermute | solution.py:361
  77.5 3.1 %attend.12 = (f32[640,128]{1,0:T(8,128)S(1)}, f32[640,128]{1,0:T(8,128)S(1)}, f32[640,512]{1,0:T(8,128)S(1)}) custom-call(s32[4]{0:T(128)S(1)} %select_reduce_fusion.refs_0_, bf16[640,640]{1,0:T(8,128)(2,1)S(1)} %after.8.refs_1_, bf16[576,256]{1,0:T(8,128)(2,1)S(1)} %after.7.refs_6_.refs_2_, ...), custom_call_target="tpu_custom_call", output_to_operand_aliasing={{0}: (5, {}), {1}: (6, {}), {2}: (7, {})} | custom-call | tf_op jit(solution)/shard_map/attend/pallas_call | solution.py:123
  80.6 0.5 collective-permute-done.13.refs_9_.refs_2_
  81.1 1.8 %attend.13 = bf16[656,512]{1,0:T(8,128)(2,1)S(1)} custom-call(s32[4]{0:T(128)S(1)} %select_reduce_fusion.refs_0_, bf16[640,640]{1,0:T(8,128)(2,1)S(1)} %after.8.refs_1_, bf16[576,128]{1,0:T(8,128)(2,1)S(1)} %collective-permute-done.13.refs_9_.refs_2_, f32[640,128]{1,0:T(8,128)S(1)} %get-tuple-element.50.refs_3_, f32[640,128]{1,0:T(8,128)S(1)} %get-tuple-element.51.refs_4_, ...), custom_call_target="tpu_custom_call" | custom-call | tf_op jit(solution)/shard_map/attend/pallas_call | solution.py:123
  83.1 1.5 %fusion = bf16[1024,576]{0,1:T(8,128)(2,1)} fusion(bf16[1024,576]{0,1:T(8,128)(2,1)S(1)} %copy-done, pred[1024]{0:T(1024)(128)(4,1)S(1)} %fusion.1, s32[32]{0:T(128)S(1)} %compare_select_fusion, bf16[128,576]{1,0:T(8,128)(2,1)S(1)} %get-tuple-element.32.refs_3_), kind=kOutput, calls=%fused_computation.1 | convolution fusion | flops 38961152 | bytes 2401792 | tf_op jit(solution)/shard_map/dot_general | solution.py:406
  84.7 5.9 %attend.11 = (f32[640,128]{1,0:T(8,128)S(1)}, f32[640,128]{1,0:T(8,128)S(1)}, f32[640,512]{1,0:T(8,128)S(1)}) custom-call(s32[4]{0:T(128)S(1)} %select_reduce_fusion.refs_0_, bf16[640,640]{1,0:T(8,128)(2,1)S(1)} %get-tuple-element.31.refs_1_.refs_0_, ...), custom_call_target="tpu_custom_call", output_to_operand_aliasing={{0}: (10, {}), {1}: (11, {}), {2}: (12, {})} | custom-call | tf_op jit(solution)/shard_map/attend/pallas_call | solution.py:123
  90.6 8.1 %collective-permute-done.14.far_ref = bf16[656,512]{1,0:T(8,128)(2,1)S(1)} collective-permute-done((bf16[656,512]{1,0:T(8,128)(2,1)S(1)}, bf16[656,512]{1,0:T(8,128)(2,1)S(1)}, u32[]{:S(2)}, u32[]{:S(2)}) %collective-permute-start.14) | collective-permute-done | bytes 671776 | tf_op jit(solution)/shard_map/ppermute | solution.py:361
  98.6 1.2 %finish.1 = (bf16[32,2048]{1,0:T(8,128)(2,1)}, bf16[8,2048]{1,0:T(8,128)(2,1)}) custom-call(f32[640,128]{1,0:T(8,128)S(1)} %get-tuple-element.45.m_ref, f32[640,128]{1,0:T(8,128)S(1)} %get-tuple-element.46.l_ref, f32[640,512]{1,0:T(8,128)S(1)} %get-tuple-element.47.acc_ref, bf16[656,512]{1,0:T(8,128)(2,1)S(1)} %collective-permute-done.14.far_ref, ...), custom_call_target="tpu_custom_call" | custom-call | flops 83886080 | bytes 4063232 | tf_op jit(solution)/shard_map/finish/pallas_call | solution.py:334
  (46 shorter events, 1.0 us)
Async XLA Ops:
  0.6 21.7 %copy-start = (bf16[1024,576]{0,1:T(8,128)(2,1)S(1)}, bf16[1024,576]{0,1:T(8,128)(2,1)}, u32[]{:S(2)}) copy-start(bf16[1024,576]{0,1:T(8,128)(2,1)} %param.13) | copy-start | bytes 3538948
  0.6 14.1 %copy-start.5 = (s32[8]{0:T(128)S(1)}, s32[8]{0:T(128)}, u32[]{:S(2)}) copy-start(s32[8]{0:T(128)} %param.19) | copy-start | bytes 100
  2.5 7.4 %collective-permute-start = (bf16[4,4,4736]{2,1,0:T(4,128)(2,1)}, bf16[4,4,4736]{2,1,0:T(4,128)(2,1)S(1)}, u32[]{:S(2)}, u32[]{:S(2)}) collective-permute-start(bf16[4,4,4736]{2,1,0:T(4,128)(2,1)} %get-tuple-element.30), channel_id=1, source_target_pairs={{0,4},{4,0},{8,12},{12,8},{16,20},{20,16},{24,28},{28,24},{1,5},{5... | collective-permute-start | bytes 454664 | tf_op jit(solution)/shard_map/ppermute | solution.py:361
  6.4 17.9 %collective-permute-start.4 = (bf16[576,128]{1,0:T(8,128)(2,1)S(1)}, bf16[576,128]{1,0:T(8,128)(2,1)S(1)}, u32[]{:S(2)}, u32[]{:S(2)}) collective-permute-start(bf16[576,128]{1,0:T(8,128)(2,1)S(1)} %slice.44), channel_id=1, source_target_pairs={{0,16},{4,20},{8,24},{12,28},{16,0},{20,4},{24,8},{28,12},{1,17},{... | collective-permute-start | bytes 442376 | tf_op jit(solution)/shard_map/ppermute | solution.py:361
  10.1 6.5 %collective-permute-start.3 = (bf16[2,4,4736]{2,1,0:T(4,128)(2,1)S(1)}, bf16[2,4,4736]{2,1,0:T(4,128)(2,1)S(1)}, u32[]{:S(2)}, u32[]{:S(2)}) collective-permute-start(bf16[2,4,4736]{2,1,0:T(4,128)(2,1)S(1)} %pad_maximum_fusion.3), channel_id=1, source_target_pairs={{0,24},{4,28},{8,16},{12,20},{16,8},{20,12},{24,0},{28,4},{1,25},{... | collective-permute-start | bytes 227336 | tf_op jit(solution)/shard_map/ppermute | solution.py:361
  13.7 8.6 %collective-permute-start.2 = (bf16[2,4,4736]{2,1,0:T(4,128)(2,1)S(1)}, bf16[2,4,4736]{2,1,0:T(4,128)(2,1)S(1)}, u32[]{:S(2)}, u32[]{:S(2)}) collective-permute-start(bf16[2,4,4736]{2,1,0:T(4,128)(2,1)S(1)} %pad_maximum_fusion.2), channel_id=1, source_target_pairs={{0,16},{4,20},{8,24},{12,28},{16,0},{20,4},{24,8},{28,12},{1,17},{... | collective-permute-start | bytes 227336 | tf_op jit(solution)/shard_map/ppermute | solution.py:361
  13.8 8.5 %collective-permute-start.1 = (bf16[2,4,4736]{2,1,0:T(4,128)(2,1)S(1)}, bf16[2,4,4736]{2,1,0:T(4,128)(2,1)S(1)}, u32[]{:S(2)}, u32[]{:S(2)}) collective-permute-start(bf16[2,4,4736]{2,1,0:T(4,128)(2,1)S(1)} %pad_maximum_fusion.1), channel_id=1, source_target_pairs={{0,8},{4,12},{8,0},{12,4},{16,24},{20,28},{24,16},{28,20},{1,9},{5... | collective-permute-start | bytes 227336 | tf_op jit(solution)/shard_map/ppermute | solution.py:361
  22.4 1.9 %copy-start.1 = (bf16[16,128,512]{2,1,0:T(8,128)(2,1)S(1)}, bf16[16,128,512]{2,1,0:T(8,128)(2,1)}, u32[]{:S(2)}) copy-start(bf16[16,128,512]{2,1,0:T(8,128)(2,1)} %w_hbm.1) | copy-start | bytes 6291460
  22.4 27.6 %collective-permute-start.5 = (bf16[576,512]{1,0:T(8,128)(2,1)S(1)}, bf16[576,512]{1,0:T(8,128)(2,1)S(1)}, u32[]{:S(2)}, u32[]{:S(2)}) collective-permute-start(bf16[576,512]{1,0:T(8,128)(2,1)S(1)} %cut.3), channel_id=1, source_target_pairs={{0,16},{4,20},{8,24},{12,28},{16,0},{20,4},{24,8},{28,12},{1,17},{... | collective-permute-start | bytes 1769480 | tf_op jit(solution)/shard_map/ppermute | solution.py:361
  23.6 28.6 %collective-permute-start.10 = (bf16[576,1024]{1,0:T(8,128)(2,1)S(1)}, bf16[576,1024]{1,0:T(8,128)(2,1)S(1)}, u32[]{:S(2)}, u32[]{:S(2)}) collective-permute-start(bf16[576,1024]{1,0:T(8,128)(2,1)S(1)} %cut.5), channel_id=1, source_target_pairs={{0,4},{4,0},{8,12},{12,8},{16,20},{20,16},{24,28},{28,24},{1,5},{5... | collective-permute-start | bytes 3538952 | tf_op jit(solution)/shard_map/ppermute | solution.py:361
  24.2 4.5 %copy-start.6 = (s32[8]{0:T(128)S(1)}, s32[8]{0:T(128)}, u32[]{:S(2)}) copy-start(s32[8]{0:T(128)} %param.16) | copy-start | bytes 100
  25.6 36.5 %collective-permute-start.9 = (bf16[640,640]{1,0:T(8,128)(2,1)S(1)}, bf16[640,640]{1,0:T(8,128)(2,1)S(1)}, u32[]{:S(2)}, u32[]{:S(2)}) collective-permute-start(bf16[640,640]{1,0:T(8,128)(2,1)S(1)} %get-tuple-element.31.refs_1_.refs_0_), channel_id=1, source_target_pairs={{0,8},{4,12},{8,0},{12,4},{16,24},{20,28},{24,16},{28,20},{1,9},{5... | collective-permute-start | bytes 2457608 | tf_op jit(solution)/shard_map/ppermute | solution.py:361
  50.0 17.6 %collective-permute-start.6 = (bf16[576,512]{1,0:T(8,128)(2,1)S(1)}, bf16[576,512]{1,0:T(8,128)(2,1)S(1)}, u32[]{:S(2)}, u32[]{:S(2)}) collective-permute-start(bf16[576,512]{1,0:T(8,128)(2,1)S(1)} %after.5.refs_2_), channel_id=1, source_target_pairs={{0,4},{4,0},{8,12},{12,8},{16,20},{20,16},{24,28},{28,24},{1,5},{5... | collective-permute-start | bytes 1769480 | tf_op jit(solution)/shard_map/ppermute | solution.py:361
  50.5 16.5 %collective-permute-start.8 = (bf16[576,256]{1,0:T(8,128)(2,1)S(1)}, bf16[576,256]{1,0:T(8,128)(2,1)S(1)}, u32[]{:S(2)}, u32[]{:S(2)}) collective-permute-start(bf16[576,256]{1,0:T(8,128)(2,1)S(1)} %get-tuple-element.34), channel_id=1, source_target_pairs={{0,16},{4,20},{8,24},{12,28},{16,0},{20,4},{24,8},{28,12},{1,17},{... | collective-permute-start | bytes 884744 | tf_op jit(solution)/shard_map/ppermute | solution.py:361
  50.6 17.0 %collective-permute-start.7 = (bf16[576,128]{1,0:T(8,128)(2,1)S(1)}, bf16[576,128]{1,0:T(8,128)(2,1)S(1)}, u32[]{:S(2)}, u32[]{:S(2)}) collective-permute-start(bf16[576,128]{1,0:T(8,128)(2,1)S(1)} %collective-permute-done.4.refs_4_), channel_id=1, source_target_pairs={{0,4},{4,0},{8,12},{12,8},{16,20},{20,16},{24,28},{28,24},{1,5},{5... | collective-permute-start | bytes 442376 | tf_op jit(solution)/shard_map/ppermute | solution.py:361
  67.0 10.5 %collective-permute-start.11 = (bf16[576,256]{1,0:T(8,128)(2,1)S(1)}, bf16[576,256]{1,0:T(8,128)(2,1)S(1)}, u32[]{:S(2)}, u32[]{:S(2)}) collective-permute-start(bf16[576,256]{1,0:T(8,128)(2,1)S(1)} %after.7.refs_6_.refs_2_), channel_id=1, source_target_pairs={{0,4},{4,0},{8,12},{12,8},{16,20},{20,16},{24,28},{28,24},{1,5},{5... | collective-permute-start | bytes 884744 | tf_op jit(solution)/shard_map/ppermute | solution.py:361
  67.6 8.4 %collective-permute-start.12 = (bf16[576,128]{1,0:T(8,128)(2,1)S(1)}, bf16[576,128]{1,0:T(8,128)(2,1)S(1)}, u32[]{:S(2)}, u32[]{:S(2)}) collective-permute-start(bf16[576,128]{1,0:T(8,128)(2,1)S(1)} %get-tuple-element.39), channel_id=1, source_target_pairs={{0,16},{4,20},{8,24},{12,28},{16,0},{20,4},{24,8},{28,12},{1,17},{... | collective-permute-start | bytes 442376 | tf_op jit(solution)/shard_map/ppermute | solution.py:361
  76.0 5.1 %collective-permute-start.13 = (bf16[576,128]{1,0:T(8,128)(2,1)S(1)}, bf16[576,128]{1,0:T(8,128)(2,1)S(1)}, u32[]{:S(2)}, u32[]{:S(2)}) collective-permute-start(bf16[576,128]{1,0:T(8,128)(2,1)S(1)} %after.9.refs_8_.refs_4_), channel_id=1, source_target_pairs={{0,4},{4,0},{8,12},{12,8},{16,20},{20,16},{24,28},{28,24},{1,5},{5... | collective-permute-start | bytes 442376 | tf_op jit(solution)/shard_map/ppermute | solution.py:361
  81.1 1.9 %copy-start.3 = (s32[32]{0:T(128)S(1)}, s32[32]{0:T(128)}, u32[]{:S(2)}) copy-start(s32[32]{0:T(128)} %param.18) | copy-start | bytes 388
  81.1 1.9 %copy-start.4 = (s32[32]{0:T(128)S(1)}, s32[32]{0:T(128)}, u32[]{:S(2)}) copy-start(s32[32]{0:T(128)} %param.17) | copy-start | bytes 388
  83.0 15.7 %collective-permute-start.14 = (bf16[656,512]{1,0:T(8,128)(2,1)S(1)}, bf16[656,512]{1,0:T(8,128)(2,1)S(1)}, u32[]{:S(2)}, u32[]{:S(2)}) collective-permute-start(bf16[656,512]{1,0:T(8,128)(2,1)S(1)} %attend.13), channel_id=1, source_target_pairs={{0,8},{4,12},{8,0},{12,4},{16,24},{20,28},{24,16},{28,20},{1,9},{5... | collective-permute-start | bytes 2015240 | tf_op jit(solution)/shard_map/ppermute | solution.py:361
  84.7 14.0 %copy-start.2 = (bf16[16,512,128]{2,1,0:T(8,128)(2,1)S(1)}, bf16[16,512,128]{2,1,0:T(8,128)(2,1)}, u32[]{:S(2)}) copy-start(bf16[16,512,128]{2,1,0:T(8,128)(2,1)} %w_ref.1) | copy-start | bytes 6291460

commit v13 on v12

--- a/solution.py
+++ b/solution.py
@@ -39,18 +39,27 @@
         m_in, l_in, acc_in = refs.pop(0), refs.pop(0), refs.pop(0)
     scale = score_scale * LOG2E
     weights = []
-    for at in range(0, q_ref.shape[0], tile):
+    sides = DC // (keys[0].shape[0] - DC)
+    count = q_ref.shape[0] * sides // (sides + 1)
+    fold = count // sides
+    folded = q_ref[count:, :].astype(jnp.float32)
+    ropes = jnp.split(folded, sides, axis=1)
+    for at in range(0, count, tile):
         rows = slice(at, at + tile)
-        q = q_ref[rows, : keys[0].shape[0]]
+        q = q_ref[rows, :]
+        rope = jnp.concatenate(ropes[at // fold : (at + tile) // fold], axis=0)
+        rope = rope.astype(jnp.bfloat16)
         scores = []
         for (start, width, which), ref in zip(pieces, keys):
-            s = jnp.dot(q, ref[...], preferred_element_type=jnp.float32)
+            s = jnp.dot(q, ref[:DC, :], preferred_element_type=jnp.float32)
+            s = s + jnp.dot(rope, ref[DC:, :], preferred_element_type=jnp.float32)
             slot = start + lax.broadcasted_iota(jnp.int32, (1, width), 1)
             scores.append(jnp.where(slot < fills[which], s, HIDDEN))
         if extra:
+            across = (((1,), (1,)), ((), ()))
             s = lax.dot_general(
-                q, new_ref[...], (((1,), (1,)), ((), ())), preferred_element_type=jnp.float32
-            )
+                q, new_ref[:, :DC], across, preferred_element_type=jnp.float32
+            ) + lax.dot_general(rope, new_ref[:, DC:], across, preferred_element_type=jnp.float32)
             bias = bias_ref[...]
             scores.append(s + jnp.concatenate([bias] * (tile // bias.shape[0]), axis=0))
         peak = functools.reduce(jnp.maximum, [jnp.max(s, axis=1, keepdims=True) for s in scores])
@@ -85,7 +94,6 @@
     if not last:
         return
     out = refs[0]
-    count = q_ref.shape[0]
     weight = jnp.concatenate(weights, axis=0)
     tail = out.shape[0] - count
     place = lax.broadcasted_iota(jnp.int32, (tail, LANES), 0)
@@ -101,7 +109,8 @@
 
 
 def attend(fills, q, pieces, tile, new=None, state=None, last=False):
-    rows = q.shape[0]
+    row = pieces[0][2].shape[0]
+    rows = q.shape[0] * DC // row
     spec = tuple((start, keys.shape[1], which) for start, which, keys in pieces)
     operands = [fills, q] + [keys for _, _, keys in pieces]
     if new is not None:
@@ -211,7 +220,7 @@
     heads = w_ref.shape[0]
     n, per, total = placed.shape
     row = extra_ref.shape[1]
-    count = absorbed_ref.shape[0] // heads
+    count = absorbed_ref.shape[0] * DC // row // heads
     wide = -(-row // LANES) * LANES
     fold = -(-wide // (per * LANES)) * LANES
     part = (total - wide - per_dec * fold) * per // (per + per_dec)
@@ -246,17 +255,18 @@
             fresh.append(unfold(x[:, begin : begin + fold], LANES)[:, :wide])
     q = jnp.concatenate(queries, axis=0).astype(jnp.bfloat16)
     new = jnp.concatenate(fresh, axis=0)
-    blank = jnp.zeros((count, absorbed_ref.shape[1] - row), jnp.float32)
     weights.wait()
+    ropes = []
     for h in range(0, heads, 2):
         parts = []
         for g in (h, h + 1):
             mine = q[:, g * width : (g + 1) * width]
-            latent = jnp.dot(mine[:, :DN], w_ref[g], preferred_element_type=jnp.float32)
-            rope = mine[:, DN:].astype(jnp.float32)
-            parts.append(jnp.concatenate([latent, rope, blank], axis=1))
+            parts.append(jnp.dot(mine[:, :DN], w_ref[g], preferred_element_type=jnp.float32))
+            ropes.append(mine[:, DN:].astype(jnp.float32))
         pair = jnp.concatenate(parts, axis=0).astype(jnp.bfloat16)
         absorbed_ref[h * count : (h + 2) * count, :] = pair
+    ropes = jnp.split(jnp.concatenate(ropes, axis=0), DC // (row - DC), axis=0)
+    absorbed_ref[heads * count :, :] = jnp.concatenate(ropes, axis=1).astype(jnp.bfloat16)
     blank = jnp.zeros((extra_ref.shape[0] - count, row), jnp.float32)
     extra_ref[...] = jnp.concatenate([new[:, :row], blank], axis=0).astype(jnp.bfloat16)
 
@@ -268,7 +278,7 @@
         functools.partial(absorb_kernel, per_dec, order),
         in_specs=[pl.BlockSpec(memory_space=pltpu.SMEM)] + [ANY] * (1 + len(got) + len(tokens)),
         out_shape=[
-            jax.ShapeDtypeStruct((heads * count, -(-row // LANES) * LANES), jnp.bfloat16),
+            jax.ShapeDtypeStruct((heads * count * row // DC, DC), jnp.bfloat16),
             jax.ShapeDtypeStruct((LANES, row), jnp.bfloat16),
         ],
         scratch_shapes=[

time: 100 us -> 98.5 us (0.985)
  waiting for transfers between devices: 43.9 us -> 39.1 us
  starting transfers between devices: 19.3 us -> 22 us
    ppermute x15, waiting for transfers between devices: 43.9 us -> 39.1 us  [swap(): return lax.ppermute(x, 'seq', [(i, i ^ stride) for i in range(n)])]
    ppermute x15, starting transfers between devices: 19.3 us -> 22 us  [swap(): return lax.ppermute(x, 'seq', [(i, i ^ stride) for i in range(n)])]
  transfers between devices with their start and end apart: 15 -> 15, of which waited for: 7 -> 9; matrix products, arithmetic and copies ran while one was open for 4% -> 5% of each run, Pallas kernels for 27% -> 27%
where the time goes in v13:
time: 98.5 us; the launch traced here: 98.2 us
  waiting for transfers between devices  39.1 us (40%)
  Pallas kernels  31.5 us (32%)
  starting transfers between devices  22 us (22%)
  local copies, waits for them, and re-layouts  1.88 us (2%)
  matrix products  1.55 us (2%)
  other arithmetic  1.4 us (1%)
    ppermute x15, waiting for transfers between devices, swap(): return lax.ppermute(x, 'seq', [(i, i ^ stride) for i in range(n)])  39.1 us
    pallas_call x7, Pallas kernels, attend(): pl.pallas_call(functools.partial(attend_kernel, spec, new is not None, st...  27 us
    ppermute x15, starting transfers between devices, swap(): return lax.ppermute(x, 'seq', [(i, i ^ stride) for i in range(n)])  22 us
  transfers between devices with their start and end apart: 15, of which 9 were waited for; matrix products, arithmetic and copies ran while one was open for 5% of the time, Pallas kernels for 27%

profile of v13, /device:TPU:0, one launch (start us, length us, event | category | flops | bytes accessed | tf_op | source)
XLA Modules:
  0.0 98.2 jit_solution(13692974602720781397)
XLA Ops:
  0.6 1.9 %pack.1 = (bf16[4,4,4736]{2,1,0:T(4,128)(2,1)}, bf16[4,4,4736]{2,1,0:T(4,128)(2,1)}) custom-call(s32[1]{0:T(128)} %bitcast.me_ref, bf16[4,24576]{1,0:T(4,128)(2,1)} %query_ref.1, bf16[1,24576]{1,0:T(2,128)(2,1)} %dec_ref.1, bf16[4,576]{1,0:T(4,128)(2,1)} %span_kv_ref.1, bf16[1,576]{1,0:T(2,128)(2,1)} %dec_kv_ref.1), custom_call_target="tpu_custom_call" | custom-call | tf_op jit(solution)/shard_map/pack/pallas_call | solution.py:205
  2.5 2.9 %collective-permute-start = (bf16[4,4,4736]{2,1,0:T(4,128)(2,1)}, bf16[4,4,4736]{2,1,0:T(4,128)(2,1)S(1)}, u32[]{:S(2)}, u32[]{:S(2)}) collective-permute-start(bf16[4,4,4736]{2,1,0:T(4,128)(2,1)} %get-tuple-element.30), channel_id=1, source_target_pairs={{0,4},{4,0},{8,12},{12,8},{16,20},{20,16},{24,28},{28,24},{1,5},{5... | collective-permute-start | bytes 454664 | tf_op jit(solution)/shard_map/ppermute | solution.py:371
  5.4 0.9 slice.44
  6.4 2.7 %collective-permute-start.4 = (bf16[576,128]{1,0:T(8,128)(2,1)S(1)}, bf16[576,128]{1,0:T(8,128)(2,1)S(1)}, u32[]{:S(2)}, u32[]{:S(2)}) collective-permute-start(bf16[576,128]{1,0:T(8,128)(2,1)S(1)} %slice.44), channel_id=1, source_target_pairs={{0,16},{4,20},{8,24},{12,28},{16,0},{20,4},{24,8},{28,12},{1,17},{... | collective-permute-start | bytes 442376 | tf_op jit(solution)/shard_map/ppermute | solution.py:371
  9.0 0.9 fusion.8
  10.0 0.8 select_reduce_fusion.refs_0_
  11.0 2.7 %collective-permute-start.3 = (bf16[2,4,4736]{2,1,0:T(4,128)(2,1)S(1)}, bf16[2,4,4736]{2,1,0:T(4,128)(2,1)S(1)}, u32[]{:S(2)}, u32[]{:S(2)}) collective-permute-start(bf16[2,4,4736]{2,1,0:T(4,128)(2,1)S(1)} %pad_maximum_fusion.3), channel_id=1, source_target_pairs={{0,24},{4,28},{8,16},{12,20},{16,8},{20,12},{24,0},{28,4},{1,25},{... | collective-permute-start | bytes 227336 | tf_op jit(solution)/shard_map/ppermute | solution.py:371
  14.2 1.4 %collective-permute-start.1 = (bf16[2,4,4736]{2,1,0:T(4,128)(2,1)S(1)}, bf16[2,4,4736]{2,1,0:T(4,128)(2,1)S(1)}, u32[]{:S(2)}, u32[]{:S(2)}) collective-permute-start(bf16[2,4,4736]{2,1,0:T(4,128)(2,1)S(1)} %pad_maximum_fusion.1), channel_id=1, source_target_pairs={{0,8},{4,12},{8,0},{12,4},{16,24},{20,28},{24,16},{28,20},{1,9},{5... | collective-permute-start | bytes 227336 | tf_op jit(solution)/shard_map/ppermute | solution.py:371
  15.7 1.6 %collective-permute-done.3.refs_3_.refs_2_ = bf16[2,4,4736]{2,1,0:T(4,128)(2,1)S(1)} collective-permute-done((bf16[2,4,4736]{2,1,0:T(4,128)(2,1)S(1)}, bf16[2,4,4736]{2,1,0:T(4,128)(2,1)S(1)}, u32[]{:S(2)}, u32[]{:S(2)}) %collective-permute-start.3) | collective-permute-done | bytes 75808 | tf_op jit(solution)/shard_map/ppermute | solution.py:371
  17.2 5.1 %collective-permute-done.2.refs_2_.refs_1_ = bf16[2,4,4736]{2,1,0:T(4,128)(2,1)S(1)} collective-permute-done((bf16[2,4,4736]{2,1,0:T(4,128)(2,1)S(1)}, bf16[2,4,4736]{2,1,0:T(4,128)(2,1)S(1)}, u32[]{:S(2)}, u32[]{:S(2)}) %collective-permute-start.2) | collective-permute-done | bytes 75808 | tf_op jit(solution)/shard_map/ppermute | solution.py:371
  22.4 1.1 %collective-permute-start.5 = (bf16[576,512]{1,0:T(8,128)(2,1)S(1)}, bf16[576,512]{1,0:T(8,128)(2,1)S(1)}, u32[]{:S(2)}, u32[]{:S(2)}) collective-permute-start(bf16[576,512]{1,0:T(8,128)(2,1)S(1)} %cut.3), channel_id=1, source_target_pairs={{0,16},{4,20},{8,24},{12,28},{16,0},{20,4},{24,8},{28,12},{1,17},{... | collective-permute-start | bytes 1769480 | tf_op jit(solution)/shard_map/ppermute | solution.py:371
  23.6 0.6 collective-permute-start.10
  24.3 1.3 %absorb.1 = (bf16[720,512]{1,0:T(8,128)(2,1)S(1)}, bf16[128,576]{1,0:T(8,128)(2,1)S(1)}) custom-call(s32[1]{0:T(128)} %bitcast.me_ref, bf16[16,128,512]{2,1,0:T(8,128)(2,1)S(1)} %copy-done.1, bf16[2,4,4736]{2,1,0:T(4,128)(2,1)S(1)} %pad_maximum_fusion.refs_0_, bf16[2,4,4736]{2,1,0:T(4,128)(2,1)S(1)} %collective-permute-done.1.refs_1_.refs_0_, ...), custom_call_target="tpu_custom_call" | custom-call | tf_op jit(solution)/shard_map/absorb/pallas_call | solution.py:277
  25.6 3.0 %collective-permute-start.9 = (bf16[720,512]{1,0:T(8,128)(2,1)S(1)}, bf16[720,512]{1,0:T(8,128)(2,1)S(1)}, u32[]{:S(2)}, u32[]{:S(2)}) collective-permute-start(bf16[720,512]{1,0:T(8,128)(2,1)S(1)} %get-tuple-element.31.refs_1_.refs_0_), channel_id=1, source_target_pairs={{0,8},{4,12},{8,0},{12,4},{16,24},{20,28},{24,16},{28,20},{1,9},{5... | collective-permute-start | bytes 2211848 | tf_op jit(solution)/shard_map/ppermute | solution.py:371
  28.8 3.3 %attend.7 = (f32[640,128]{1,0:T(8,128)S(1)}, f32[640,128]{1,0:T(8,128)S(1)}, f32[640,512]{1,0:T(8,128)S(1)}) custom-call(s32[4]{0:T(128)S(1)} %select_reduce_fusion.refs_0_, bf16[720,512]{1,0:T(8,128)(2,1)S(1)} %get-tuple-element.31.refs_1_.refs_0_, bf16[576,1024]{1,0:T(8,128)(2,1)S(1)} %bitcast.8, bf16[128,576]{1,0:T(8,128)(2,1)S(1)} %get-tuple-element.32.refs_3_, ...), custom_call_target="tpu_custom_call" | custom-call | tf_op jit(solution)/shard_map/attend/pallas_call | solution.py:132
  32.1 17.8 %collective-permute-done.5.x_ref = bf16[576,512]{1,0:T(8,128)(2,1)S(1)} collective-permute-done((bf16[576,512]{1,0:T(8,128)(2,1)S(1)}, bf16[576,512]{1,0:T(8,128)(2,1)S(1)}, u32[]{:S(2)}, u32[]{:S(2)}) %collective-permute-start.5) | collective-permute-done | bytes 589856 | tf_op jit(solution)/shard_map/ppermute | solution.py:371
  50.6 1.6 %collective-permute-start.7 = (bf16[576,128]{1,0:T(8,128)(2,1)S(1)}, bf16[576,128]{1,0:T(8,128)(2,1)S(1)}, u32[]{:S(2)}, u32[]{:S(2)}) collective-permute-start(bf16[576,128]{1,0:T(8,128)(2,1)S(1)} %collective-permute-done.4.refs_4_), channel_id=1, source_target_pairs={{0,4},{4,0},{8,12},{12,8},{16,20},{20,16},{24,28},{28,24},{1,5},{5... | collective-permute-start | bytes 442376 | tf_op jit(solution)/shard_map/ppermute | solution.py:371
  52.2 3.4 %attend.8 = (f32[640,128]{1,0:T(8,128)S(1)}, f32[640,128]{1,0:T(8,128)S(1)}, f32[640,512]{1,0:T(8,128)S(1)}) custom-call(s32[4]{0:T(128)S(1)} %select_reduce_fusion.refs_0_, bf16[720,512]{1,0:T(8,128)(2,1)S(1)} %get-tuple-element.31.refs_1_.refs_0_, ...), custom_call_target="tpu_custom_call", output_to_operand_aliasing={{0}: (3, {}), {1}: (4, {}), {2}: (5, {})} | custom-call | tf_op jit(solution)/shard_map/attend/pallas_call | solution.py:132
  55.6 3.1 %collective-permute-done.9.x_ref = bf16[720,512]{1,0:T(8,128)(2,1)S(1)} collective-permute-done((bf16[720,512]{1,0:T(8,128)(2,1)S(1)}, bf16[720,512]{1,0:T(8,128)(2,1)S(1)}, u32[]{:S(2)}, u32[]{:S(2)}) %collective-permute-start.9) | collective-permute-done | bytes 737312 | tf_op jit(solution)/shard_map/ppermute | solution.py:371
  58.7 5.0 %attend.9 = (f32[640,128]{1,0:T(8,128)S(1)}, f32[640,128]{1,0:T(8,128)S(1)}, f32[640,512]{1,0:T(8,128)S(1)}) custom-call(s32[4]{0:T(128)S(1)} %select_reduce_fusion.refs_0_, bf16[720,512]{1,0:T(8,128)(2,1)S(1)} %after.6.refs_1_.x_ref, bf16[576,1024]{1,0:T(8,128)(2,1)S(1)} %bitcast.10, bf16[576,1024]{1,0:T(8,128)(2,1)S(1)} %collective-permute-done.10.refs_2_.refs_3_), custom_call_target="tpu_custom_call" | custom-call | tf_op jit(solution)/shard_map/attend/pallas_call | solution.py:132
  63.7 0.6 collective-permute-done.8.x_ref.refs_0_
  64.3 1.3 %collective-permute-start.11 = (bf16[576,256]{1,0:T(8,128)(2,1)S(1)}, bf16[576,256]{1,0:T(8,128)(2,1)S(1)}, u32[]{:S(2)}, u32[]{:S(2)}) collective-permute-start(bf16[576,256]{1,0:T(8,128)(2,1)S(1)} %after.7.refs_6_.refs_2_), channel_id=1, source_target_pairs={{0,4},{4,0},{8,12},{12,8},{16,20},{20,16},{24,28},{28,24},{1,5},{5... | collective-permute-start | bytes 884744 | tf_op jit(solution)/shard_map/ppermute | solution.py:371
  65.7 2.9 %collective-permute-done.7.refs_5_ = bf16[576,128]{1,0:T(8,128)(2,1)S(1)} collective-permute-done((bf16[576,128]{1,0:T(8,128)(2,1)S(1)}, bf16[576,128]{1,0:T(8,128)(2,1)S(1)}, u32[]{:S(2)}, u32[]{:S(2)}) %collective-permute-start.7) | collective-permute-done | bytes 147488 | tf_op jit(solution)/shard_map/ppermute | solution.py:371
  68.6 4.3 %attend.10 = (f32[640,128]{1,0:T(8,128)S(1)}, f32[640,128]{1,0:T(8,128)S(1)}, f32[640,512]{1,0:T(8,128)S(1)}) custom-call(s32[4]{0:T(128)S(1)} %select_reduce_fusion.refs_0_, bf16[720,512]{1,0:T(8,128)(2,1)S(1)} %after.8.refs_1_, bf16[576,512]{1,0:T(8,128)(2,1)S(1)} %after.5.refs_2_, ...), custom_call_target="tpu_custom_call", output_to_operand_aliasing={{0}: (6, {}), {1}: (7, {}), {2}: (8, {})} | custom-call | tf_op jit(solution)/shard_map/attend/pallas_call | solution.py:132
  73.3 1.5 %collective-permute-done.11.refs_7_.refs_3_ = bf16[576,256]{1,0:T(8,128)(2,1)S(1)} collective-permute-done((bf16[576,256]{1,0:T(8,128)(2,1)S(1)}, bf16[576,256]{1,0:T(8,128)(2,1)S(1)}, u32[]{:S(2)}, u32[]{:S(2)}) %collective-permute-start.11) | collective-permute-done | bytes 294944 | tf_op jit(solution)/shard_map/ppermute | solution.py:371
  74.9 3.1 %attend.12 = (f32[640,128]{1,0:T(8,128)S(1)}, f32[640,128]{1,0:T(8,128)S(1)}, f32[640,512]{1,0:T(8,128)S(1)}) custom-call(s32[4]{0:T(128)S(1)} %select_reduce_fusion.refs_0_, bf16[720,512]{1,0:T(8,128)(2,1)S(1)} %after.8.refs_1_, bf16[576,256]{1,0:T(8,128)(2,1)S(1)} %after.7.refs_6_.refs_2_, ...), custom_call_target="tpu_custom_call", output_to_operand_aliasing={{0}: (5, {}), {1}: (6, {}), {2}: (7, {})} | custom-call | tf_op jit(solution)/shard_map/attend/pallas_call | solution.py:132
  78.1 2.0 %attend.13 = bf16[656,512]{1,0:T(8,128)(2,1)S(1)} custom-call(s32[4]{0:T(128)S(1)} %select_reduce_fusion.refs_0_, bf16[720,512]{1,0:T(8,128)(2,1)S(1)} %after.8.refs_1_, bf16[576,128]{1,0:T(8,128)(2,1)S(1)} %collective-permute-done.13.refs_9_.refs_2_, f32[640,128]{1,0:T(8,128)S(1)} %get-tuple-element.50.refs_3_, f32[640,128]{1,0:T(8,128)S(1)} %get-tuple-element.51.refs_4_, ...), custom_call_target="tpu_custom_call" | custom-call | tf_op jit(solution)/shard_map/attend/pallas_call | solution.py:132
  80.1 3.1 %collective-permute-start.14 = (bf16[656,512]{1,0:T(8,128)(2,1)S(1)}, bf16[656,512]{1,0:T(8,128)(2,1)S(1)}, u32[]{:S(2)}, u32[]{:S(2)}) collective-permute-start(bf16[656,512]{1,0:T(8,128)(2,1)S(1)} %attend.13), channel_id=1, source_target_pairs={{0,8},{4,12},{8,0},{12,4},{16,24},{20,28},{24,16},{28,20},{1,9},{5... | collective-permute-start | bytes 2015240 | tf_op jit(solution)/shard_map/ppermute | solution.py:371
  83.3 1.5 %fusion = bf16[1024,576]{0,1:T(8,128)(2,1)} fusion(bf16[1024,576]{0,1:T(8,128)(2,1)S(1)} %copy-done, pred[1024]{0:T(1024)(128)(4,1)S(1)} %fusion.1, s32[32]{0:T(128)S(1)} %compare_select_fusion, bf16[128,576]{1,0:T(8,128)(2,1)S(1)} %get-tuple-element.32.refs_3_), kind=kOutput, calls=%fused_computation.1 | convolution fusion | flops 38961152 | bytes 2401792 | tf_op jit(solution)/shard_map/dot_general | solution.py:416
  84.9 5.9 %attend.11 = (f32[640,128]{1,0:T(8,128)S(1)}, f32[640,128]{1,0:T(8,128)S(1)}, f32[640,512]{1,0:T(8,128)S(1)}) custom-call(s32[4]{0:T(128)S(1)} %select_reduce_fusion.refs_0_, bf16[720,512]{1,0:T(8,128)(2,1)S(1)} %get-tuple-element.31.refs_1_.refs_0_, ...), custom_call_target="tpu_custom_call", output_to_operand_aliasing={{0}: (10, {}), {1}: (11, {}), {2}: (12, {})} | custom-call | tf_op jit(solution)/shard_map/attend/pallas_call | solution.py:132
  90.8 6.2 %collective-permute-done.14.far_ref = bf16[656,512]{1,0:T(8,128)(2,1)S(1)} collective-permute-done((bf16[656,512]{1,0:T(8,128)(2,1)S(1)}, bf16[656,512]{1,0:T(8,128)(2,1)S(1)}, u32[]{:S(2)}, u32[]{:S(2)}) %collective-permute-start.14) | collective-permute-done | bytes 671776 | tf_op jit(solution)/shard_map/ppermute | solution.py:371
  97.0 1.2 %finish.1 = (bf16[32,2048]{1,0:T(8,128)(2,1)}, bf16[8,2048]{1,0:T(8,128)(2,1)}) custom-call(f32[640,128]{1,0:T(8,128)S(1)} %get-tuple-element.45.m_ref, f32[640,128]{1,0:T(8,128)S(1)} %get-tuple-element.46.l_ref, f32[640,512]{1,0:T(8,128)S(1)} %get-tuple-element.47.acc_ref, bf16[656,512]{1,0:T(8,128)(2,1)S(1)} %collective-permute-done.14.far_ref, ...), custom_call_target="tpu_custom_call" | custom-call | flops 83886080 | bytes 4063232 | tf_op jit(solution)/shard_map/finish/pallas_call | solution.py:344
  (44 shorter events, 2.5 us)
Async XLA Ops:
  0.6 21.7 %copy-start = (bf16[1024,576]{0,1:T(8,128)(2,1)S(1)}, bf16[1024,576]{0,1:T(8,128)(2,1)}, u32[]{:S(2)}) copy-start(bf16[1024,576]{0,1:T(8,128)(2,1)} %param.13) | copy-start | bytes 3538948
  2.5 8.3 %collective-permute-start = (bf16[4,4,4736]{2,1,0:T(4,128)(2,1)}, bf16[4,4,4736]{2,1,0:T(4,128)(2,1)S(1)}, u32[]{:S(2)}, u32[]{:S(2)}) collective-permute-start(bf16[4,4,4736]{2,1,0:T(4,128)(2,1)} %get-tuple-element.30), channel_id=1, source_target_pairs={{0,4},{4,0},{8,12},{12,8},{16,20},{20,16},{24,28},{28,24},{1,5},{5... | collective-permute-start | bytes 454664 | tf_op jit(solution)/shard_map/ppermute | solution.py:371
  6.4 17.9 %collective-permute-start.4 = (bf16[576,128]{1,0:T(8,128)(2,1)S(1)}, bf16[576,128]{1,0:T(8,128)(2,1)S(1)}, u32[]{:S(2)}, u32[]{:S(2)}) collective-permute-start(bf16[576,128]{1,0:T(8,128)(2,1)S(1)} %slice.44), channel_id=1, source_target_pairs={{0,16},{4,20},{8,24},{12,28},{16,0},{20,4},{24,8},{28,12},{1,17},{... | collective-permute-start | bytes 442376 | tf_op jit(solution)/shard_map/ppermute | solution.py:371
  11.0 6.3 %collective-permute-start.3 = (bf16[2,4,4736]{2,1,0:T(4,128)(2,1)S(1)}, bf16[2,4,4736]{2,1,0:T(4,128)(2,1)S(1)}, u32[]{:S(2)}, u32[]{:S(2)}) collective-permute-start(bf16[2,4,4736]{2,1,0:T(4,128)(2,1)S(1)} %pad_maximum_fusion.3), channel_id=1, source_target_pairs={{0,24},{4,28},{8,16},{12,20},{16,8},{20,12},{24,0},{28,4},{1,25},{... | collective-permute-start | bytes 227336 | tf_op jit(solution)/shard_map/ppermute | solution.py:371
  13.7 8.6 %collective-permute-start.2 = (bf16[2,4,4736]{2,1,0:T(4,128)(2,1)S(1)}, bf16[2,4,4736]{2,1,0:T(4,128)(2,1)S(1)}, u32[]{:S(2)}, u32[]{:S(2)}) collective-permute-start(bf16[2,4,4736]{2,1,0:T(4,128)(2,1)S(1)} %pad_maximum_fusion.2), channel_id=1, source_target_pairs={{0,16},{4,20},{8,24},{12,28},{16,0},{20,4},{24,8},{28,12},{1,17},{... | collective-permute-start | bytes 227336 | tf_op jit(solution)/shard_map/ppermute | solution.py:371
  14.2 8.1 %collective-permute-start.1 = (bf16[2,4,4736]{2,1,0:T(4,128)(2,1)S(1)}, bf16[2,4,4736]{2,1,0:T(4,128)(2,1)S(1)}, u32[]{:S(2)}, u32[]{:S(2)}) collective-permute-start(bf16[2,4,4736]{2,1,0:T(4,128)(2,1)S(1)} %pad_maximum_fusion.1), channel_id=1, source_target_pairs={{0,8},{4,12},{8,0},{12,4},{16,24},{20,28},{24,16},{28,20},{1,9},{5... | collective-permute-start | bytes 227336 | tf_op jit(solution)/shard_map/ppermute | solution.py:371
  22.3 1.9 %copy-start.1 = (bf16[16,128,512]{2,1,0:T(8,128)(2,1)S(1)}, bf16[16,128,512]{2,1,0:T(8,128)(2,1)}, u32[]{:S(2)}) copy-start(bf16[16,128,512]{2,1,0:T(8,128)(2,1)} %w_hbm.1) | copy-start | bytes 6291460
  22.4 27.6 %collective-permute-start.5 = (bf16[576,512]{1,0:T(8,128)(2,1)S(1)}, bf16[576,512]{1,0:T(8,128)(2,1)S(1)}, u32[]{:S(2)}, u32[]{:S(2)}) collective-permute-start(bf16[576,512]{1,0:T(8,128)(2,1)S(1)} %cut.3), channel_id=1, source_target_pairs={{0,16},{4,20},{8,24},{12,28},{16,0},{20,4},{24,8},{28,12},{1,17},{... | collective-permute-start | bytes 1769480 | tf_op jit(solution)/shard_map/ppermute | solution.py:371
  23.6 28.6 %collective-permute-start.10 = (bf16[576,1024]{1,0:T(8,128)(2,1)S(1)}, bf16[576,1024]{1,0:T(8,128)(2,1)S(1)}, u32[]{:S(2)}, u32[]{:S(2)}) collective-permute-start(bf16[576,1024]{1,0:T(8,128)(2,1)S(1)} %cut.5), channel_id=1, source_target_pairs={{0,4},{4,0},{8,12},{12,8},{16,20},{20,16},{24,28},{28,24},{1,5},{5... | collective-permute-start | bytes 3538952 | tf_op jit(solution)/shard_map/ppermute | solution.py:371
  24.2 4.4 %copy-start.5 = (s32[8]{0:T(128)S(1)}, s32[8]{0:T(128)}, u32[]{:S(2)}) copy-start(s32[8]{0:T(128)} %param.19) | copy-start | bytes 100
  25.6 33.2 %collective-permute-start.9 = (bf16[720,512]{1,0:T(8,128)(2,1)S(1)}, bf16[720,512]{1,0:T(8,128)(2,1)S(1)}, u32[]{:S(2)}, u32[]{:S(2)}) collective-permute-start(bf16[720,512]{1,0:T(8,128)(2,1)S(1)} %get-tuple-element.31.refs_1_.refs_0_), channel_id=1, source_target_pairs={{0,8},{4,12},{8,0},{12,4},{16,24},{20,28},{24,16},{28,20},{1,9},{5... | collective-permute-start | bytes 2211848 | tf_op jit(solution)/shard_map/ppermute | solution.py:371
  50.0 18.7 %collective-permute-start.6 = (bf16[576,512]{1,0:T(8,128)(2,1)S(1)}, bf16[576,512]{1,0:T(8,128)(2,1)S(1)}, u32[]{:S(2)}, u32[]{:S(2)}) collective-permute-start(bf16[576,512]{1,0:T(8,128)(2,1)S(1)} %after.5.refs_2_), channel_id=1, source_target_pairs={{0,4},{4,0},{8,12},{12,8},{16,20},{20,16},{24,28},{28,24},{1,5},{5... | collective-permute-start | bytes 1769480 | tf_op jit(solution)/shard_map/ppermute | solution.py:371
  50.5 13.8 %collective-permute-start.8 = (bf16[576,256]{1,0:T(8,128)(2,1)S(1)}, bf16[576,256]{1,0:T(8,128)(2,1)S(1)}, u32[]{:S(2)}, u32[]{:S(2)}) collective-permute-start(bf16[576,256]{1,0:T(8,128)(2,1)S(1)} %get-tuple-element.34), channel_id=1, source_target_pairs={{0,16},{4,20},{8,24},{12,28},{16,0},{20,4},{24,8},{28,12},{1,17},{... | collective-permute-start | bytes 884744 | tf_op jit(solution)/shard_map/ppermute | solution.py:371
  50.6 18.0 %collective-permute-start.7 = (bf16[576,128]{1,0:T(8,128)(2,1)S(1)}, bf16[576,128]{1,0:T(8,128)(2,1)S(1)}, u32[]{:S(2)}, u32[]{:S(2)}) collective-permute-start(bf16[576,128]{1,0:T(8,128)(2,1)S(1)} %collective-permute-done.4.refs_4_), channel_id=1, source_target_pairs={{0,4},{4,0},{8,12},{12,8},{16,20},{20,16},{24,28},{28,24},{1,5},{5... | collective-permute-start | bytes 442376 | tf_op jit(solution)/shard_map/ppermute | solution.py:371
  64.3 10.5 %collective-permute-start.11 = (bf16[576,256]{1,0:T(8,128)(2,1)S(1)}, bf16[576,256]{1,0:T(8,128)(2,1)S(1)}, u32[]{:S(2)}, u32[]{:S(2)}) collective-permute-start(bf16[576,256]{1,0:T(8,128)(2,1)S(1)} %after.7.refs_6_.refs_2_), channel_id=1, source_target_pairs={{0,4},{4,0},{8,12},{12,8},{16,20},{20,16},{24,28},{28,24},{1,5},{5... | collective-permute-start | bytes 884744 | tf_op jit(solution)/shard_map/ppermute | solution.py:371
  65.7 7.2 %collective-permute-start.12 = (bf16[576,128]{1,0:T(8,128)(2,1)S(1)}, bf16[576,128]{1,0:T(8,128)(2,1)S(1)}, u32[]{:S(2)}, u32[]{:S(2)}) collective-permute-start(bf16[576,128]{1,0:T(8,128)(2,1)S(1)} %get-tuple-element.39), channel_id=1, source_target_pairs={{0,16},{4,20},{8,24},{12,28},{16,0},{20,4},{24,8},{28,12},{1,17},{... | collective-permute-start | bytes 442376 | tf_op jit(solution)/shard_map/ppermute | solution.py:371
  72.9 5.2 %collective-permute-start.13 = (bf16[576,128]{1,0:T(8,128)(2,1)S(1)}, bf16[576,128]{1,0:T(8,128)(2,1)S(1)}, u32[]{:S(2)}, u32[]{:S(2)}) collective-permute-start(bf16[576,128]{1,0:T(8,128)(2,1)S(1)} %after.9.refs_8_.refs_4_), channel_id=1, source_target_pairs={{0,4},{4,0},{8,12},{12,8},{16,20},{20,16},{24,28},{28,24},{1,5},{5... | collective-permute-start | bytes 442376 | tf_op jit(solution)/shard_map/ppermute | solution.py:371
  78.1 5.1 %copy-start.3 = (s32[32]{0:T(128)S(1)}, s32[32]{0:T(128)}, u32[]{:S(2)}) copy-start(s32[32]{0:T(128)} %param.18) | copy-start | bytes 388
  78.1 5.1 %copy-start.4 = (s32[32]{0:T(128)S(1)}, s32[32]{0:T(128)}, u32[]{:S(2)}) copy-start(s32[32]{0:T(128)} %param.17) | copy-start | bytes 388
  80.1 16.9 %collective-permute-start.14 = (bf16[656,512]{1,0:T(8,128)(2,1)S(1)}, bf16[656,512]{1,0:T(8,128)(2,1)S(1)}, u32[]{:S(2)}, u32[]{:S(2)}) collective-permute-start(bf16[656,512]{1,0:T(8,128)(2,1)S(1)} %attend.13), channel_id=1, source_target_pairs={{0,8},{4,12},{8,0},{12,4},{16,24},{20,28},{24,16},{28,20},{1,9},{5... | collective-permute-start | bytes 2015240 | tf_op jit(solution)/shard_map/ppermute | solution.py:371
  84.9 12.1 %copy-start.2 = (bf16[16,512,128]{2,1,0:T(8,128)(2,1)S(1)}, bf16[16,512,128]{2,1,0:T(8,128)(2,1)}, u32[]{:S(2)}) copy-start(bf16[16,512,128]{2,1,0:T(8,128)(2,1)} %w_ref.1) | copy-start | bytes 6291460

commit v14 on v13

--- a/solution.py
+++ b/solution.py
@@ -373,7 +373,7 @@
     far, pair = n // 2, n // 4
     near = [1 << b for b in range(pair.bit_length() - 1)]
     keys = cache_kv.T
-    edges = [i * (pos_dev // 8) for i in (0, 1, 5, 7, 8)]
+    edges = [i * (pos_dev // 8) for i in (0, 1, 4, 6, 8)]
 
     pieces = [swap(keys[:, : edges[1]], far)]
 

time: 98.5 us -> 98 us (level)
  waiting for transfers between devices: 39.1 us -> 37.9 us
    ppermute x15, waiting for transfers between devices: 39.1 us -> 37.9 us  [swap(): return lax.ppermute(x, 'seq', [(i, i ^ stride) for i in range(n)])]
where the time goes in v14:
time: 98 us; the launch traced here: 97.8 us
  waiting for transfers between devices  37.9 us (39%)
  Pallas kernels  31.7 us (32%)
  starting transfers between devices  22.6 us (23%)
  local copies, waits for them, and re-layouts  1.88 us (2%)
  matrix products  1.55 us (2%)
  other arithmetic  1.4 us (1%)
    ppermute x15, waiting for transfers between devices, swap(): return lax.ppermute(x, 'seq', [(i, i ^ stride) for i in range(n)])  37.9 us
    pallas_call x7, Pallas kernels, attend(): pl.pallas_call(functools.partial(attend_kernel, spec, new is not None, st...  27.1 us
    ppermute x15, starting transfers between devices, swap(): return lax.ppermute(x, 'seq', [(i, i ^ stride) for i in range(n)])  22.6 us
  transfers between devices with their start and end apart: 15, of which 9 were waited for; matrix products, arithmetic and copies ran while one was open for 5% of the time, Pallas kernels for 27%

profile of v14, /device:TPU:0, one launch (start us, length us, event | category | flops | bytes accessed | tf_op | source)
XLA Modules:
  0.0 97.8 jit_solution(10332351782695820326)
XLA Ops:
  0.6 1.9 %pack.1 = (bf16[4,4,4736]{2,1,0:T(4,128)(2,1)}, bf16[4,4,4736]{2,1,0:T(4,128)(2,1)}) custom-call(s32[1]{0:T(128)} %bitcast.me_ref, bf16[4,24576]{1,0:T(4,128)(2,1)} %query_ref.1, bf16[1,24576]{1,0:T(2,128)(2,1)} %dec_ref.1, bf16[4,576]{1,0:T(4,128)(2,1)} %span_kv_ref.1, bf16[1,576]{1,0:T(2,128)(2,1)} %dec_kv_ref.1), custom_call_target="tpu_custom_call" | custom-call | tf_op jit(solution)/shard_map/pack/pallas_call | solution.py:205
  2.5 2.9 %collective-permute-start = (bf16[4,4,4736]{2,1,0:T(4,128)(2,1)}, bf16[4,4,4736]{2,1,0:T(4,128)(2,1)S(1)}, u32[]{:S(2)}, u32[]{:S(2)}) collective-permute-start(bf16[4,4,4736]{2,1,0:T(4,128)(2,1)} %get-tuple-element.30), channel_id=1, source_target_pairs={{0,4},{4,0},{8,12},{12,8},{16,20},{20,16},{24,28},{28,24},{1,5},{5... | collective-permute-start | bytes 454664 | tf_op jit(solution)/shard_map/ppermute | solution.py:371
  5.4 0.9 slice.44
  6.4 2.7 %collective-permute-start.4 = (bf16[576,128]{1,0:T(8,128)(2,1)S(1)}, bf16[576,128]{1,0:T(8,128)(2,1)S(1)}, u32[]{:S(2)}, u32[]{:S(2)}) collective-permute-start(bf16[576,128]{1,0:T(8,128)(2,1)S(1)} %slice.44), channel_id=1, source_target_pairs={{0,16},{4,20},{8,24},{12,28},{16,0},{20,4},{24,8},{28,12},{1,17},{... | collective-permute-start | bytes 442376 | tf_op jit(solution)/shard_map/ppermute | solution.py:371
  9.0 0.9 fusion.8
  10.0 0.8 select_reduce_fusion.refs_0_
  11.0 2.7 %collective-permute-start.3 = (bf16[2,4,4736]{2,1,0:T(4,128)(2,1)S(1)}, bf16[2,4,4736]{2,1,0:T(4,128)(2,1)S(1)}, u32[]{:S(2)}, u32[]{:S(2)}) collective-permute-start(bf16[2,4,4736]{2,1,0:T(4,128)(2,1)S(1)} %pad_maximum_fusion.3), channel_id=1, source_target_pairs={{0,24},{4,28},{8,16},{12,20},{16,8},{20,12},{24,0},{28,4},{1,25},{... | collective-permute-start | bytes 227336 | tf_op jit(solution)/shard_map/ppermute | solution.py:371
  14.2 1.4 %collective-permute-start.1 = (bf16[2,4,4736]{2,1,0:T(4,128)(2,1)S(1)}, bf16[2,4,4736]{2,1,0:T(4,128)(2,1)S(1)}, u32[]{:S(2)}, u32[]{:S(2)}) collective-permute-start(bf16[2,4,4736]{2,1,0:T(4,128)(2,1)S(1)} %pad_maximum_fusion.1), channel_id=1, source_target_pairs={{0,8},{4,12},{8,0},{12,4},{16,24},{20,28},{24,16},{28,20},{1,9},{5... | collective-permute-start | bytes 227336 | tf_op jit(solution)/shard_map/ppermute | solution.py:371
  15.7 1.6 %collective-permute-done.3.refs_3_.refs_2_ = bf16[2,4,4736]{2,1,0:T(4,128)(2,1)S(1)} collective-permute-done((bf16[2,4,4736]{2,1,0:T(4,128)(2,1)S(1)}, bf16[2,4,4736]{2,1,0:T(4,128)(2,1)S(1)}, u32[]{:S(2)}, u32[]{:S(2)}) %collective-permute-start.3) | collective-permute-done | bytes 75808 | tf_op jit(solution)/shard_map/ppermute | solution.py:371
  17.2 5.1 %collective-permute-done.2.refs_2_.refs_1_ = bf16[2,4,4736]{2,1,0:T(4,128)(2,1)S(1)} collective-permute-done((bf16[2,4,4736]{2,1,0:T(4,128)(2,1)S(1)}, bf16[2,4,4736]{2,1,0:T(4,128)(2,1)S(1)}, u32[]{:S(2)}, u32[]{:S(2)}) %collective-permute-start.2) | collective-permute-done | bytes 75808 | tf_op jit(solution)/shard_map/ppermute | solution.py:371
  22.4 1.1 %collective-permute-start.5 = (bf16[576,384]{1,0:T(8,128)(2,1)S(1)}, bf16[576,384]{1,0:T(8,128)(2,1)S(1)}, u32[]{:S(2)}, u32[]{:S(2)}) collective-permute-start(bf16[576,384]{1,0:T(8,128)(2,1)S(1)} %cut.3), channel_id=1, source_target_pairs={{0,16},{4,20},{8,24},{12,28},{16,0},{20,4},{24,8},{28,12},{1,17},{... | collective-permute-start | bytes 1327112 | tf_op jit(solution)/shard_map/ppermute | solution.py:371
  24.3 1.3 %absorb.1 = (bf16[720,512]{1,0:T(8,128)(2,1)S(1)}, bf16[128,576]{1,0:T(8,128)(2,1)S(1)}) custom-call(s32[1]{0:T(128)} %bitcast.me_ref, bf16[16,128,512]{2,1,0:T(8,128)(2,1)S(1)} %copy-done.1, bf16[2,4,4736]{2,1,0:T(4,128)(2,1)S(1)} %pad_maximum_fusion.refs_0_, bf16[2,4,4736]{2,1,0:T(4,128)(2,1)S(1)} %collective-permute-done.1.refs_1_.refs_0_, ...), custom_call_target="tpu_custom_call" | custom-call | tf_op jit(solution)/shard_map/absorb/pallas_call | solution.py:277
  25.6 3.0 %collective-permute-start.9 = (bf16[720,512]{1,0:T(8,128)(2,1)S(1)}, bf16[720,512]{1,0:T(8,128)(2,1)S(1)}, u32[]{:S(2)}, u32[]{:S(2)}) collective-permute-start(bf16[720,512]{1,0:T(8,128)(2,1)S(1)} %get-tuple-element.31.refs_1_.refs_0_), channel_id=1, source_target_pairs={{0,8},{4,12},{8,0},{12,4},{16,24},{20,28},{24,16},{28,20},{1,9},{5... | collective-permute-start | bytes 2211848 | tf_op jit(solution)/shard_map/ppermute | solution.py:371
  28.8 3.3 %attend.7 = (f32[640,128]{1,0:T(8,128)S(1)}, f32[640,128]{1,0:T(8,128)S(1)}, f32[640,512]{1,0:T(8,128)S(1)}) custom-call(s32[4]{0:T(128)S(1)} %select_reduce_fusion.refs_0_, bf16[720,512]{1,0:T(8,128)(2,1)S(1)} %get-tuple-element.31.refs_1_.refs_0_, bf16[576,1024]{1,0:T(8,128)(2,1)S(1)} %bitcast.8, bf16[128,576]{1,0:T(8,128)(2,1)S(1)} %get-tuple-element.32.refs_3_, ...), custom_call_target="tpu_custom_call" | custom-call | tf_op jit(solution)/shard_map/attend/pallas_call | solution.py:132
  32.1 11.5 %collective-permute-done.5.x_ref = bf16[576,384]{1,0:T(8,128)(2,1)S(1)} collective-permute-done((bf16[576,384]{1,0:T(8,128)(2,1)S(1)}, bf16[576,384]{1,0:T(8,128)(2,1)S(1)}, u32[]{:S(2)}, u32[]{:S(2)}) %collective-permute-start.5) | collective-permute-done | bytes 442400 | tf_op jit(solution)/shard_map/ppermute | solution.py:371
  44.3 2.9 %collective-permute-start.12 = (bf16[576,256]{1,0:T(8,128)(2,1)S(1)}, bf16[576,256]{1,0:T(8,128)(2,1)S(1)}, u32[]{:S(2)}, u32[]{:S(2)}) collective-permute-start(bf16[576,256]{1,0:T(8,128)(2,1)S(1)} %get-tuple-element.39), channel_id=1, source_target_pairs={{0,16},{4,20},{8,24},{12,28},{16,0},{20,4},{24,8},{28,12},{1,17},{... | collective-permute-start | bytes 884744 | tf_op jit(solution)/shard_map/ppermute | solution.py:371
  47.2 5.3 %collective-permute-done.10.refs_2_.refs_3_ = bf16[576,1024]{1,0:T(8,128)(2,1)S(1)} collective-permute-done((bf16[576,1024]{1,0:T(8,128)(2,1)S(1)}, bf16[576,1024]{1,0:T(8,128)(2,1)S(1)}, u32[]{:S(2)}, u32[]{:S(2)}) %collective-permute-start.10) | collective-permute-done | bytes 1179680 | tf_op jit(solution)/shard_map/ppermute | solution.py:371
  53.1 3.4 %attend.8 = (f32[640,128]{1,0:T(8,128)S(1)}, f32[640,128]{1,0:T(8,128)S(1)}, f32[640,512]{1,0:T(8,128)S(1)}) custom-call(s32[4]{0:T(128)S(1)} %select_reduce_fusion.refs_0_, bf16[720,512]{1,0:T(8,128)(2,1)S(1)} %get-tuple-element.31.refs_1_.refs_0_, ...), custom_call_target="tpu_custom_call", output_to_operand_aliasing={{0}: (3, {}), {1}: (4, {}), {2}: (5, {})} | custom-call | tf_op jit(solution)/shard_map/attend/pallas_call | solution.py:132
  56.4 2.4 %collective-permute-done.9.x_ref = bf16[720,512]{1,0:T(8,128)(2,1)S(1)} collective-permute-done((bf16[720,512]{1,0:T(8,128)(2,1)S(1)}, bf16[720,512]{1,0:T(8,128)(2,1)S(1)}, u32[]{:S(2)}, u32[]{:S(2)}) %collective-permute-start.9) | collective-permute-done | bytes 737312 | tf_op jit(solution)/shard_map/ppermute | solution.py:371
  58.9 5.0 %attend.9 = (f32[640,128]{1,0:T(8,128)S(1)}, f32[640,128]{1,0:T(8,128)S(1)}, f32[640,512]{1,0:T(8,128)S(1)}) custom-call(s32[4]{0:T(128)S(1)} %select_reduce_fusion.refs_0_, bf16[720,512]{1,0:T(8,128)(2,1)S(1)} %after.6.refs_1_.x_ref, bf16[576,1024]{1,0:T(8,128)(2,1)S(1)} %bitcast.10, bf16[576,1024]{1,0:T(8,128)(2,1)S(1)} %collective-permute-done.10.refs_2_.refs_3_), custom_call_target="tpu_custom_call" | custom-call | tf_op jit(solution)/shard_map/attend/pallas_call | solution.py:132
  63.8 3.5 %collective-permute-done.8.x_ref.refs_0_ = bf16[576,256]{1,0:T(8,128)(2,1)S(1)} collective-permute-done((bf16[576,256]{1,0:T(8,128)(2,1)S(1)}, bf16[576,256]{1,0:T(8,128)(2,1)S(1)}, u32[]{:S(2)}, u32[]{:S(2)}) %collective-permute-start.8) | collective-permute-done | bytes 294944 | tf_op jit(solution)/shard_map/ppermute | solution.py:371
  67.3 1.5 %collective-permute-start.11 = (bf16[576,256]{1,0:T(8,128)(2,1)S(1)}, bf16[576,256]{1,0:T(8,128)(2,1)S(1)}, u32[]{:S(2)}, u32[]{:S(2)}) collective-permute-start(bf16[576,256]{1,0:T(8,128)(2,1)S(1)} %after.7.refs_6_.refs_2_), channel_id=1, source_target_pairs={{0,4},{4,0},{8,12},{12,8},{16,20},{20,16},{24,28},{28,24},{1,5},{5... | collective-permute-start | bytes 884744 | tf_op jit(solution)/shard_map/ppermute | solution.py:371
  68.8 4.1 %attend.10 = (f32[640,128]{1,0:T(8,128)S(1)}, f32[640,128]{1,0:T(8,128)S(1)}, f32[640,512]{1,0:T(8,128)S(1)}) custom-call(s32[4]{0:T(128)S(1)} %select_reduce_fusion.refs_0_, bf16[720,512]{1,0:T(8,128)(2,1)S(1)} %after.8.refs_1_, bf16[576,384]{1,0:T(8,128)(2,1)S(1)} %after.5.refs_2_, ...), custom_call_target="tpu_custom_call", output_to_operand_aliasing={{0}: (6, {}), {1}: (7, {}), {2}: (8, {})} | custom-call | tf_op jit(solution)/shard_map/attend/pallas_call | solution.py:132
  73.0 0.6 collective-permute-start.13
  73.6 2.5 %collective-permute-done.11.refs_7_.refs_3_ = bf16[576,256]{1,0:T(8,128)(2,1)S(1)} collective-permute-done((bf16[576,256]{1,0:T(8,128)(2,1)S(1)}, bf16[576,256]{1,0:T(8,128)(2,1)S(1)}, u32[]{:S(2)}, u32[]{:S(2)}) %collective-permute-start.11) | collective-permute-done | bytes 294944 | tf_op jit(solution)/shard_map/ppermute | solution.py:371
  76.1 3.3 %attend.12 = (f32[640,128]{1,0:T(8,128)S(1)}, f32[640,128]{1,0:T(8,128)S(1)}, f32[640,512]{1,0:T(8,128)S(1)}) custom-call(s32[4]{0:T(128)S(1)} %select_reduce_fusion.refs_0_, bf16[720,512]{1,0:T(8,128)(2,1)S(1)} %after.8.refs_1_, bf16[576,256]{1,0:T(8,128)(2,1)S(1)} %after.7.refs_6_.refs_2_, ...), custom_call_target="tpu_custom_call", output_to_operand_aliasing={{0}: (5, {}), {1}: (6, {}), {2}: (7, {})} | custom-call | tf_op jit(solution)/shard_map/attend/pallas_call | solution.py:132
  79.8 2.1 %attend.13 = bf16[656,512]{1,0:T(8,128)(2,1)S(1)} custom-call(s32[4]{0:T(128)S(1)} %select_reduce_fusion.refs_0_, bf16[720,512]{1,0:T(8,128)(2,1)S(1)} %after.8.refs_1_, bf16[576,256]{1,0:T(8,128)(2,1)S(1)} %collective-permute-done.13.refs_9_.refs_2_, f32[640,128]{1,0:T(8,128)S(1)} %get-tuple-element.50.refs_3_, f32[640,128]{1,0:T(8,128)S(1)} %get-tuple-element.51.refs_4_, ...), custom_call_target="tpu_custom_call" | custom-call | tf_op jit(solution)/shard_map/attend/pallas_call | solution.py:132
  81.9 1.5 %collective-permute-start.14 = (bf16[656,512]{1,0:T(8,128)(2,1)S(1)}, bf16[656,512]{1,0:T(8,128)(2,1)S(1)}, u32[]{:S(2)}, u32[]{:S(2)}) collective-permute-start(bf16[656,512]{1,0:T(8,128)(2,1)S(1)} %attend.13), channel_id=1, source_target_pairs={{0,8},{4,12},{8,0},{12,4},{16,24},{20,28},{24,16},{28,20},{1,9},{5... | collective-permute-start | bytes 2015240 | tf_op jit(solution)/shard_map/ppermute | solution.py:371
  83.5 1.5 %fusion = bf16[1024,576]{0,1:T(8,128)(2,1)} fusion(bf16[1024,576]{0,1:T(8,128)(2,1)S(1)} %copy-done, pred[1024]{0:T(1024)(128)(4,1)S(1)} %fusion.1, s32[32]{0:T(128)S(1)} %compare_select_fusion, bf16[128,576]{1,0:T(8,128)(2,1)S(1)} %get-tuple-element.32.refs_3_), kind=kOutput, calls=%fused_computation.1 | convolution fusion | flops 38961152 | bytes 2401792 | tf_op jit(solution)/shard_map/dot_general | solution.py:416
  85.0 5.9 %attend.11 = (f32[640,128]{1,0:T(8,128)S(1)}, f32[640,128]{1,0:T(8,128)S(1)}, f32[640,512]{1,0:T(8,128)S(1)}) custom-call(s32[4]{0:T(128)S(1)} %select_reduce_fusion.refs_0_, bf16[720,512]{1,0:T(8,128)(2,1)S(1)} %get-tuple-element.31.refs_1_.refs_0_, ...), custom_call_target="tpu_custom_call", output_to_operand_aliasing={{0}: (10, {}), {1}: (11, {}), {2}: (12, {})} | custom-call | tf_op jit(solution)/shard_map/attend/pallas_call | solution.py:132
  91.0 5.6 %collective-permute-done.14.far_ref = bf16[656,512]{1,0:T(8,128)(2,1)S(1)} collective-permute-done((bf16[656,512]{1,0:T(8,128)(2,1)S(1)}, bf16[656,512]{1,0:T(8,128)(2,1)S(1)}, u32[]{:S(2)}, u32[]{:S(2)}) %collective-permute-start.14) | collective-permute-done | bytes 671776 | tf_op jit(solution)/shard_map/ppermute | solution.py:371
  96.5 1.2 %finish.1 = (bf16[32,2048]{1,0:T(8,128)(2,1)}, bf16[8,2048]{1,0:T(8,128)(2,1)}) custom-call(f32[640,128]{1,0:T(8,128)S(1)} %get-tuple-element.45.m_ref, f32[640,128]{1,0:T(8,128)S(1)} %get-tuple-element.46.l_ref, f32[640,512]{1,0:T(8,128)S(1)} %get-tuple-element.47.acc_ref, bf16[656,512]{1,0:T(8,128)(2,1)S(1)} %collective-permute-done.14.far_ref, ...), custom_call_target="tpu_custom_call" | custom-call | flops 83886080 | bytes 4063232 | tf_op jit(solution)/shard_map/finish/pallas_call | solution.py:344
  (44 shorter events, 3.4 us)
Async XLA Ops:
  0.6 21.7 %copy-start = (bf16[1024,576]{0,1:T(8,128)(2,1)S(1)}, bf16[1024,576]{0,1:T(8,128)(2,1)}, u32[]{:S(2)}) copy-start(bf16[1024,576]{0,1:T(8,128)(2,1)} %param.13) | copy-start | bytes 3538948
  2.5 8.3 %collective-permute-start = (bf16[4,4,4736]{2,1,0:T(4,128)(2,1)}, bf16[4,4,4736]{2,1,0:T(4,128)(2,1)S(1)}, u32[]{:S(2)}, u32[]{:S(2)}) collective-permute-start(bf16[4,4,4736]{2,1,0:T(4,128)(2,1)} %get-tuple-element.30), channel_id=1, source_target_pairs={{0,4},{4,0},{8,12},{12,8},{16,20},{20,16},{24,28},{28,24},{1,5},{5... | collective-permute-start | bytes 454664 | tf_op jit(solution)/shard_map/ppermute | solution.py:371
  6.4 17.9 %collective-permute-start.4 = (bf16[576,128]{1,0:T(8,128)(2,1)S(1)}, bf16[576,128]{1,0:T(8,128)(2,1)S(1)}, u32[]{:S(2)}, u32[]{:S(2)}) collective-permute-start(bf16[576,128]{1,0:T(8,128)(2,1)S(1)} %slice.44), channel_id=1, source_target_pairs={{0,16},{4,20},{8,24},{12,28},{16,0},{20,4},{24,8},{28,12},{1,17},{... | collective-permute-start | bytes 442376 | tf_op jit(solution)/shard_map/ppermute | solution.py:371
  11.0 6.3 %collective-permute-start.3 = (bf16[2,4,4736]{2,1,0:T(4,128)(2,1)S(1)}, bf16[2,4,4736]{2,1,0:T(4,128)(2,1)S(1)}, u32[]{:S(2)}, u32[]{:S(2)}) collective-permute-start(bf16[2,4,4736]{2,1,0:T(4,128)(2,1)S(1)} %pad_maximum_fusion.3), channel_id=1, source_target_pairs={{0,24},{4,28},{8,16},{12,20},{16,8},{20,12},{24,0},{28,4},{1,25},{... | collective-permute-start | bytes 227336 | tf_op jit(solution)/shard_map/ppermute | solution.py:371
  13.7 8.6 %collective-permute-start.2 = (bf16[2,4,4736]{2,1,0:T(4,128)(2,1)S(1)}, bf16[2,4,4736]{2,1,0:T(4,128)(2,1)S(1)}, u32[]{:S(2)}, u32[]{:S(2)}) collective-permute-start(bf16[2,4,4736]{2,1,0:T(4,128)(2,1)S(1)} %pad_maximum_fusion.2), channel_id=1, source_target_pairs={{0,16},{4,20},{8,24},{12,28},{16,0},{20,4},{24,8},{28,12},{1,17},{... | collective-permute-start | bytes 227336 | tf_op jit(solution)/shard_map/ppermute | solution.py:371
  14.2 8.1 %collective-permute-start.1 = (bf16[2,4,4736]{2,1,0:T(4,128)(2,1)S(1)}, bf16[2,4,4736]{2,1,0:T(4,128)(2,1)S(1)}, u32[]{:S(2)}, u32[]{:S(2)}) collective-permute-start(bf16[2,4,4736]{2,1,0:T(4,128)(2,1)S(1)} %pad_maximum_fusion.1), channel_id=1, source_target_pairs={{0,8},{4,12},{8,0},{12,4},{16,24},{20,28},{24,16},{28,20},{1,9},{5... | collective-permute-start | bytes 227336 | tf_op jit(solution)/shard_map/ppermute | solution.py:371
  22.3 1.9 %copy-start.1 = (bf16[16,128,512]{2,1,0:T(8,128)(2,1)S(1)}, bf16[16,128,512]{2,1,0:T(8,128)(2,1)}, u32[]{:S(2)}) copy-start(bf16[16,128,512]{2,1,0:T(8,128)(2,1)} %w_hbm.1) | copy-start | bytes 6291460
  22.4 21.3 %collective-permute-start.5 = (bf16[576,384]{1,0:T(8,128)(2,1)S(1)}, bf16[576,384]{1,0:T(8,128)(2,1)S(1)}, u32[]{:S(2)}, u32[]{:S(2)}) collective-permute-start(bf16[576,384]{1,0:T(8,128)(2,1)S(1)} %cut.3), channel_id=1, source_target_pairs={{0,16},{4,20},{8,24},{12,28},{16,0},{20,4},{24,8},{28,12},{1,17},{... | collective-permute-start | bytes 1327112 | tf_op jit(solution)/shard_map/ppermute | solution.py:371
  23.6 28.9 %collective-permute-start.10 = (bf16[576,1024]{1,0:T(8,128)(2,1)S(1)}, bf16[576,1024]{1,0:T(8,128)(2,1)S(1)}, u32[]{:S(2)}, u32[]{:S(2)}) collective-permute-start(bf16[576,1024]{1,0:T(8,128)(2,1)S(1)} %cut.5), channel_id=1, source_target_pairs={{0,4},{4,0},{8,12},{12,8},{16,20},{20,16},{24,28},{28,24},{1,5},{5... | collective-permute-start | bytes 3538952 | tf_op jit(solution)/shard_map/ppermute | solution.py:371
  24.2 4.4 %copy-start.5 = (s32[8]{0:T(128)S(1)}, s32[8]{0:T(128)}, u32[]{:S(2)}) copy-start(s32[8]{0:T(128)} %param.19) | copy-start | bytes 100
  25.6 33.3 %collective-permute-start.9 = (bf16[720,512]{1,0:T(8,128)(2,1)S(1)}, bf16[720,512]{1,0:T(8,128)(2,1)S(1)}, u32[]{:S(2)}, u32[]{:S(2)}) collective-permute-start(bf16[720,512]{1,0:T(8,128)(2,1)S(1)} %get-tuple-element.31.refs_1_.refs_0_), channel_id=1, source_target_pairs={{0,8},{4,12},{8,0},{12,4},{16,24},{20,28},{24,16},{28,20},{1,9},{5... | collective-permute-start | bytes 2211848 | tf_op jit(solution)/shard_map/ppermute | solution.py:371
  43.6 25.2 %collective-permute-start.6 = (bf16[576,384]{1,0:T(8,128)(2,1)S(1)}, bf16[576,384]{1,0:T(8,128)(2,1)S(1)}, u32[]{:S(2)}, u32[]{:S(2)}) collective-permute-start(bf16[576,384]{1,0:T(8,128)(2,1)S(1)} %after.5.refs_2_), channel_id=1, source_target_pairs={{0,4},{4,0},{8,12},{12,8},{16,20},{20,16},{24,28},{28,24},{1,5},{5... | collective-permute-start | bytes 1327112 | tf_op jit(solution)/shard_map/ppermute | solution.py:371
  44.2 23.1 %collective-permute-start.8 = (bf16[576,256]{1,0:T(8,128)(2,1)S(1)}, bf16[576,256]{1,0:T(8,128)(2,1)S(1)}, u32[]{:S(2)}, u32[]{:S(2)}) collective-permute-start(bf16[576,256]{1,0:T(8,128)(2,1)S(1)} %get-tuple-element.34), channel_id=1, source_target_pairs={{0,16},{4,20},{8,24},{12,28},{16,0},{20,4},{24,8},{28,12},{1,17},{... | collective-permute-start | bytes 884744 | tf_op jit(solution)/shard_map/ppermute | solution.py:371
  44.3 28.7 %collective-permute-start.12 = (bf16[576,256]{1,0:T(8,128)(2,1)S(1)}, bf16[576,256]{1,0:T(8,128)(2,1)S(1)}, u32[]{:S(2)}, u32[]{:S(2)}) collective-permute-start(bf16[576,256]{1,0:T(8,128)(2,1)S(1)} %get-tuple-element.39), channel_id=1, source_target_pairs={{0,16},{4,20},{8,24},{12,28},{16,0},{20,4},{24,8},{28,12},{1,17},{... | collective-permute-start | bytes 884744 | tf_op jit(solution)/shard_map/ppermute | solution.py:371
  52.5 16.3 %collective-permute-start.7 = (bf16[576,128]{1,0:T(8,128)(2,1)S(1)}, bf16[576,128]{1,0:T(8,128)(2,1)S(1)}, u32[]{:S(2)}, u32[]{:S(2)}) collective-permute-start(bf16[576,128]{1,0:T(8,128)(2,1)S(1)} %collective-permute-done.4.refs_4_), channel_id=1, source_target_pairs={{0,4},{4,0},{8,12},{12,8},{16,20},{20,16},{24,28},{28,24},{1,5},{5... | collective-permute-start | bytes 442376 | tf_op jit(solution)/shard_map/ppermute | solution.py:371
  67.3 8.8 %collective-permute-start.11 = (bf16[576,256]{1,0:T(8,128)(2,1)S(1)}, bf16[576,256]{1,0:T(8,128)(2,1)S(1)}, u32[]{:S(2)}, u32[]{:S(2)}) collective-permute-start(bf16[576,256]{1,0:T(8,128)(2,1)S(1)} %after.7.refs_6_.refs_2_), channel_id=1, source_target_pairs={{0,4},{4,0},{8,12},{12,8},{16,20},{20,16},{24,28},{28,24},{1,5},{5... | collective-permute-start | bytes 884744 | tf_op jit(solution)/shard_map/ppermute | solution.py:371
  73.0 6.8 %collective-permute-start.13 = (bf16[576,256]{1,0:T(8,128)(2,1)S(1)}, bf16[576,256]{1,0:T(8,128)(2,1)S(1)}, u32[]{:S(2)}, u32[]{:S(2)}) collective-permute-start(bf16[576,256]{1,0:T(8,128)(2,1)S(1)} %after.9.refs_8_.refs_4_), channel_id=1, source_target_pairs={{0,4},{4,0},{8,12},{12,8},{16,20},{20,16},{24,28},{28,24},{1,5},{5... | collective-permute-start | bytes 884744 | tf_op jit(solution)/shard_map/ppermute | solution.py:371
  79.8 3.6 %copy-start.3 = (s32[32]{0:T(128)S(1)}, s32[32]{0:T(128)}, u32[]{:S(2)}) copy-start(s32[32]{0:T(128)} %param.18) | copy-start | bytes 388
  79.8 3.6 %copy-start.4 = (s32[32]{0:T(128)S(1)}, s32[32]{0:T(128)}, u32[]{:S(2)}) copy-start(s32[32]{0:T(128)} %param.17) | copy-start | bytes 388
  81.9 14.6 %collective-permute-start.14 = (bf16[656,512]{1,0:T(8,128)(2,1)S(1)}, bf16[656,512]{1,0:T(8,128)(2,1)S(1)}, u32[]{:S(2)}, u32[]{:S(2)}) collective-permute-start(bf16[656,512]{1,0:T(8,128)(2,1)S(1)} %attend.13), channel_id=1, source_target_pairs={{0,8},{4,12},{8,0},{12,4},{16,24},{20,28},{24,16},{28,20},{1,9},{5... | collective-permute-start | bytes 2015240 | tf_op jit(solution)/shard_map/ppermute | solution.py:371
  85.0 11.5 %copy-start.2 = (bf16[16,512,128]{2,1,0:T(8,128)(2,1)S(1)}, bf16[16,512,128]{2,1,0:T(8,128)(2,1)}, u32[]{:S(2)}) copy-start(bf16[16,512,128]{2,1,0:T(8,128)(2,1)} %w_ref.1) | copy-start | bytes 6291460

commit v15 on v14

--- a/solution.py
+++ b/solution.py
@@ -373,7 +373,7 @@
     far, pair = n // 2, n // 4
     near = [1 << b for b in range(pair.bit_length() - 1)]
     keys = cache_kv.T
-    edges = [i * (pos_dev // 8) for i in (0, 1, 4, 6, 8)]
+    edges = [i * (pos_dev // 8) for i in (0, 1, 4, 7, 8)]
 
     pieces = [swap(keys[:, : edges[1]], far)]
 

time: 98 us -> 109 us (1.11)
  waiting for transfers between devices: 37.9 us -> 50.8 us
  starting transfers between devices: 22.6 us -> 20.1 us
  Pallas kernels: 31.7 us -> 32.8 us
    ppermute x15, waiting for transfers between devices: 37.9 us -> 50.8 us  [swap(): return lax.ppermute(x, 'seq', [(i, i ^ stride) for i in range(n)])]
    ppermute x15, starting transfers between devices: 22.6 us -> 20.1 us  [swap(): return lax.ppermute(x, 'seq', [(i, i ^ stride) for i in range(n)])]
    pallas_call x7, Pallas kernels: 27.1 us -> 28.3 us  [attend(): pl.pallas_call(functools.partial(attend_kernel, spec, new is not None, st...]
  transfers between devices with their start and end apart: 15 -> 15, of which waited for: 9 -> 7; matrix products, arithmetic and copies ran while one was open for 5% -> 4% of each run, Pallas kernels for 27% -> 25%
where the time goes in v15:
time: 109 us
  waiting for transfers between devices  50.8 us (47%)
  Pallas kernels  32.8 us (30%)
  starting transfers between devices  20.1 us (18%)
  local copies, waits for them, and re-layouts  1.89 us (2%)
  matrix products  1.55 us (1%)
    ppermute x15, waiting for transfers between devices, swap(): return lax.ppermute(x, 'seq', [(i, i ^ stride) for i in range(n)])  50.8 us
    pallas_call x7, Pallas kernels, attend(): pl.pallas_call(functools.partial(attend_kernel, spec, new is not None, st...  28.3 us
    ppermute x15, starting transfers between devices, swap(): return lax.ppermute(x, 'seq', [(i, i ^ stride) for i in range(n)])  20.1 us
  transfers between devices with their start and end apart: 15, of which 7 were waited for; matrix products, arithmetic and copies ran while one was open for 4% of the time, Pallas kernels for 25%

profile of v15, /device:TPU:0, one launch (start us, length us, event | category | flops | bytes accessed | tf_op | source)
XLA Modules:
  0.0 108.9 jit_solution(15218456556357689145)
XLA Ops:
  0.6 1.9 %pack.1 = (bf16[4,4,4736]{2,1,0:T(4,128)(2,1)}, bf16[4,4,4736]{2,1,0:T(4,128)(2,1)}) custom-call(s32[1]{0:T(128)} %bitcast.me_ref, bf16[4,24576]{1,0:T(4,128)(2,1)} %query_ref.1, bf16[1,24576]{1,0:T(2,128)(2,1)} %dec_ref.1, bf16[4,576]{1,0:T(4,128)(2,1)} %span_kv_ref.1, bf16[1,576]{1,0:T(2,128)(2,1)} %dec_kv_ref.1), custom_call_target="tpu_custom_call" | custom-call | tf_op jit(solution)/shard_map/pack/pallas_call | solution.py:205
  2.5 2.9 %collective-permute-start = (bf16[4,4,4736]{2,1,0:T(4,128)(2,1)}, bf16[4,4,4736]{2,1,0:T(4,128)(2,1)S(1)}, u32[]{:S(2)}, u32[]{:S(2)}) collective-permute-start(bf16[4,4,4736]{2,1,0:T(4,128)(2,1)} %get-tuple-element.30), channel_id=1, source_target_pairs={{0,4},{4,0},{8,12},{12,8},{16,20},{20,16},{24,28},{28,24},{1,5},{5... | collective-permute-start | bytes 454664 | tf_op jit(solution)/shard_map/ppermute | solution.py:371
  5.4 0.9 slice.44
  6.4 2.7 %collective-permute-start.4 = (bf16[576,128]{1,0:T(8,128)(2,1)S(1)}, bf16[576,128]{1,0:T(8,128)(2,1)S(1)}, u32[]{:S(2)}, u32[]{:S(2)}) collective-permute-start(bf16[576,128]{1,0:T(8,128)(2,1)S(1)} %slice.44), channel_id=1, source_target_pairs={{0,16},{4,20},{8,24},{12,28},{16,0},{20,4},{24,8},{28,12},{1,17},{... | collective-permute-start | bytes 442376 | tf_op jit(solution)/shard_map/ppermute | solution.py:371
  9.0 0.9 fusion.8
  10.0 3.6 %collective-permute-start.3 = (bf16[2,4,4736]{2,1,0:T(4,128)(2,1)S(1)}, bf16[2,4,4736]{2,1,0:T(4,128)(2,1)S(1)}, u32[]{:S(2)}, u32[]{:S(2)}) collective-permute-start(bf16[2,4,4736]{2,1,0:T(4,128)(2,1)S(1)} %pad_maximum_fusion.3), channel_id=1, source_target_pairs={{0,24},{4,28},{8,16},{12,20},{16,8},{20,12},{24,0},{28,4},{1,25},{... | collective-permute-start | bytes 227336 | tf_op jit(solution)/shard_map/ppermute | solution.py:371
  13.8 0.9 collective-permute-start.1
  14.7 1.8 %collective-permute-done.3.refs_3_.refs_2_ = bf16[2,4,4736]{2,1,0:T(4,128)(2,1)S(1)} collective-permute-done((bf16[2,4,4736]{2,1,0:T(4,128)(2,1)S(1)}, bf16[2,4,4736]{2,1,0:T(4,128)(2,1)S(1)}, u32[]{:S(2)}, u32[]{:S(2)}) %collective-permute-start.3) | collective-permute-done | bytes 75808 | tf_op jit(solution)/shard_map/ppermute | solution.py:371
  16.6 5.7 %collective-permute-done.2.refs_2_.refs_1_ = bf16[2,4,4736]{2,1,0:T(4,128)(2,1)S(1)} collective-permute-done((bf16[2,4,4736]{2,1,0:T(4,128)(2,1)S(1)}, bf16[2,4,4736]{2,1,0:T(4,128)(2,1)S(1)}, u32[]{:S(2)}, u32[]{:S(2)}) %collective-permute-start.2) | collective-permute-done | bytes 75808 | tf_op jit(solution)/shard_map/ppermute | solution.py:371
  22.4 0.6 collective-permute-start.10
  23.0 1.3 %absorb.1 = (bf16[720,512]{1,0:T(8,128)(2,1)S(1)}, bf16[128,576]{1,0:T(8,128)(2,1)S(1)}) custom-call(s32[1]{0:T(128)} %bitcast.me_ref, bf16[16,128,512]{2,1,0:T(8,128)(2,1)S(1)} %copy-done.1, bf16[2,4,4736]{2,1,0:T(4,128)(2,1)S(1)} %pad_maximum_fusion.refs_0_, bf16[2,4,4736]{2,1,0:T(4,128)(2,1)S(1)} %collective-permute-done.1.refs_1_.refs_0_, ...), custom_call_target="tpu_custom_call" | custom-call | tf_op jit(solution)/shard_map/absorb/pallas_call | solution.py:277
  24.3 0.8 collective-permute-start.9
  25.2 0.2 select_reduce_fusion.refs_0_
  25.4 3.4 %collective-permute-start.5 = (bf16[576,384]{1,0:T(8,128)(2,1)S(1)}, bf16[576,384]{1,0:T(8,128)(2,1)S(1)}, u32[]{:S(2)}, u32[]{:S(2)}) collective-permute-start(bf16[576,384]{1,0:T(8,128)(2,1)S(1)} %cut.3), channel_id=1, source_target_pairs={{0,16},{4,20},{8,24},{12,28},{16,0},{20,4},{24,8},{28,12},{1,17},{... | collective-permute-start | bytes 1327112 | tf_op jit(solution)/shard_map/ppermute | solution.py:371
  29.2 3.3 %attend.7 = (f32[640,128]{1,0:T(8,128)S(1)}, f32[640,128]{1,0:T(8,128)S(1)}, f32[640,512]{1,0:T(8,128)S(1)}) custom-call(s32[4]{0:T(128)S(1)} %select_reduce_fusion.refs_0_, bf16[720,512]{1,0:T(8,128)(2,1)S(1)} %get-tuple-element.31.refs_1_.refs_0_, bf16[576,1024]{1,0:T(8,128)(2,1)S(1)} %bitcast.9, bf16[128,576]{1,0:T(8,128)(2,1)S(1)} %get-tuple-element.32.refs_3_, ...), custom_call_target="tpu_custom_call" | custom-call | tf_op jit(solution)/shard_map/attend/pallas_call | solution.py:132
  32.6 19.0 %collective-permute-done.5.x_ref = bf16[576,384]{1,0:T(8,128)(2,1)S(1)} collective-permute-done((bf16[576,384]{1,0:T(8,128)(2,1)S(1)}, bf16[576,384]{1,0:T(8,128)(2,1)S(1)}, u32[]{:S(2)}, u32[]{:S(2)}) %collective-permute-start.5) | collective-permute-done | bytes 442400 | tf_op jit(solution)/shard_map/ppermute | solution.py:371
  51.5 1.5 %collective-permute-start.6 = (bf16[576,384]{1,0:T(8,128)(2,1)S(1)}, bf16[576,384]{1,0:T(8,128)(2,1)S(1)}, u32[]{:S(2)}, u32[]{:S(2)}) collective-permute-start(bf16[576,384]{1,0:T(8,128)(2,1)S(1)} %after.5.refs_2_), channel_id=1, source_target_pairs={{0,4},{4,0},{8,12},{12,8},{16,20},{20,16},{24,28},{28,24},{1,5},{5... | collective-permute-start | bytes 1327112 | tf_op jit(solution)/shard_map/ppermute | solution.py:371
  53.0 3.4 %attend.8 = (f32[640,128]{1,0:T(8,128)S(1)}, f32[640,128]{1,0:T(8,128)S(1)}, f32[640,512]{1,0:T(8,128)S(1)}) custom-call(s32[4]{0:T(128)S(1)} %select_reduce_fusion.refs_0_, bf16[720,512]{1,0:T(8,128)(2,1)S(1)} %get-tuple-element.31.refs_1_.refs_0_, ...), custom_call_target="tpu_custom_call", output_to_operand_aliasing={{0}: (3, {}), {1}: (4, {}), {2}: (5, {})} | custom-call | tf_op jit(solution)/shard_map/attend/pallas_call | solution.py:132
  56.4 0.3 collective-permute-done.9.x_ref
  56.7 5.0 %attend.9 = (f32[640,128]{1,0:T(8,128)S(1)}, f32[640,128]{1,0:T(8,128)S(1)}, f32[640,512]{1,0:T(8,128)S(1)}) custom-call(s32[4]{0:T(128)S(1)} %select_reduce_fusion.refs_0_, bf16[720,512]{1,0:T(8,128)(2,1)S(1)} %after.6.refs_1_.x_ref, bf16[576,1024]{1,0:T(8,128)(2,1)S(1)} %bitcast.10, bf16[576,1024]{1,0:T(8,128)(2,1)S(1)} %collective-permute-done.10.refs_2_.refs_3_), custom_call_target="tpu_custom_call" | custom-call | tf_op jit(solution)/shard_map/attend/pallas_call | solution.py:132
  61.6 5.5 %collective-permute-done.8.x_ref.refs_0_ = bf16[576,384]{1,0:T(8,128)(2,1)S(1)} collective-permute-done((bf16[576,384]{1,0:T(8,128)(2,1)S(1)}, bf16[576,384]{1,0:T(8,128)(2,1)S(1)}, u32[]{:S(2)}, u32[]{:S(2)}) %collective-permute-start.8) | collective-permute-done | bytes 442400 | tf_op jit(solution)/shard_map/ppermute | solution.py:371
  67.1 1.5 %collective-permute-start.11 = (bf16[576,384]{1,0:T(8,128)(2,1)S(1)}, bf16[576,384]{1,0:T(8,128)(2,1)S(1)}, u32[]{:S(2)}, u32[]{:S(2)}) collective-permute-start(bf16[576,384]{1,0:T(8,128)(2,1)S(1)} %after.7.refs_6_.refs_2_), channel_id=1, source_target_pairs={{0,4},{4,0},{8,12},{12,8},{16,20},{20,16},{24,28},{28,24},{1,5},{5... | collective-permute-start | bytes 1327112 | tf_op jit(solution)/shard_map/ppermute | solution.py:371
  68.6 0.5 collective-permute-start.7
  69.2 12.1 %collective-permute-done.7.refs_5_ = bf16[576,128]{1,0:T(8,128)(2,1)S(1)} collective-permute-done((bf16[576,128]{1,0:T(8,128)(2,1)S(1)}, bf16[576,128]{1,0:T(8,128)(2,1)S(1)}, u32[]{:S(2)}, u32[]{:S(2)}) %collective-permute-start.7) | collective-permute-done | bytes 147488 | tf_op jit(solution)/shard_map/ppermute | solution.py:371
  81.3 4.3 %attend.10 = (f32[640,128]{1,0:T(8,128)S(1)}, f32[640,128]{1,0:T(8,128)S(1)}, f32[640,512]{1,0:T(8,128)S(1)}) custom-call(s32[4]{0:T(128)S(1)} %select_reduce_fusion.refs_0_, bf16[720,512]{1,0:T(8,128)(2,1)S(1)} %after.8.refs_1_, bf16[576,384]{1,0:T(8,128)(2,1)S(1)} %after.5.refs_2_, ...), custom_call_target="tpu_custom_call", output_to_operand_aliasing={{0}: (6, {}), {1}: (7, {}), {2}: (8, {})} | custom-call | tf_op jit(solution)/shard_map/attend/pallas_call | solution.py:132
  85.6 1.6 %collective-permute-start.13 = (bf16[576,128]{1,0:T(8,128)(2,1)S(1)}, bf16[576,128]{1,0:T(8,128)(2,1)S(1)}, u32[]{:S(2)}, u32[]{:S(2)}) collective-permute-start(bf16[576,128]{1,0:T(8,128)(2,1)S(1)} %after.9.refs_8_.refs_4_), channel_id=1, source_target_pairs={{0,4},{4,0},{8,12},{12,8},{16,20},{20,16},{24,28},{28,24},{1,5},{5... | collective-permute-start | bytes 442376 | tf_op jit(solution)/shard_map/ppermute | solution.py:371
  87.2 3.8 %attend.12 = (f32[640,128]{1,0:T(8,128)S(1)}, f32[640,128]{1,0:T(8,128)S(1)}, f32[640,512]{1,0:T(8,128)S(1)}) custom-call(s32[4]{0:T(128)S(1)} %select_reduce_fusion.refs_0_, bf16[720,512]{1,0:T(8,128)(2,1)S(1)} %after.8.refs_1_, bf16[576,384]{1,0:T(8,128)(2,1)S(1)} %after.7.refs_6_.refs_2_, ...), custom_call_target="tpu_custom_call", output_to_operand_aliasing={{0}: (5, {}), {1}: (6, {}), {2}: (7, {})} | custom-call | tf_op jit(solution)/shard_map/attend/pallas_call | solution.py:132
  90.9 2.0 %attend.13 = bf16[656,512]{1,0:T(8,128)(2,1)S(1)} custom-call(s32[4]{0:T(128)S(1)} %select_reduce_fusion.refs_0_, bf16[720,512]{1,0:T(8,128)(2,1)S(1)} %after.8.refs_1_, bf16[576,128]{1,0:T(8,128)(2,1)S(1)} %collective-permute-done.13.refs_9_.refs_2_, f32[640,128]{1,0:T(8,128)S(1)} %get-tuple-element.50.refs_3_, f32[640,128]{1,0:T(8,128)S(1)} %get-tuple-element.51.refs_4_, ...), custom_call_target="tpu_custom_call" | custom-call | tf_op jit(solution)/shard_map/attend/pallas_call | solution.py:132
  93.1 1.5 %fusion = bf16[1024,576]{0,1:T(8,128)(2,1)} fusion(bf16[1024,576]{0,1:T(8,128)(2,1)S(1)} %copy-done, pred[1024]{0:T(1024)(128)(4,1)S(1)} %fusion.1, s32[32]{0:T(128)S(1)} %compare_select_fusion, bf16[128,576]{1,0:T(8,128)(2,1)S(1)} %get-tuple-element.32.refs_3_), kind=kOutput, calls=%fused_computation.1 | convolution fusion | flops 38961152 | bytes 2401792 | tf_op jit(solution)/shard_map/dot_general | solution.py:416
  94.7 6.5 %attend.11 = (f32[640,128]{1,0:T(8,128)S(1)}, f32[640,128]{1,0:T(8,128)S(1)}, f32[640,512]{1,0:T(8,128)S(1)}) custom-call(s32[4]{0:T(128)S(1)} %select_reduce_fusion.refs_0_, bf16[720,512]{1,0:T(8,128)(2,1)S(1)} %get-tuple-element.31.refs_1_.refs_0_, ...), custom_call_target="tpu_custom_call", output_to_operand_aliasing={{0}: (10, {}), {1}: (11, {}), {2}: (12, {})} | custom-call | tf_op jit(solution)/shard_map/attend/pallas_call | solution.py:132
  101.2 6.4 %collective-permute-done.14.far_ref = bf16[656,512]{1,0:T(8,128)(2,1)S(1)} collective-permute-done((bf16[656,512]{1,0:T(8,128)(2,1)S(1)}, bf16[656,512]{1,0:T(8,128)(2,1)S(1)}, u32[]{:S(2)}, u32[]{:S(2)}) %collective-permute-start.14) | collective-permute-done | bytes 671776 | tf_op jit(solution)/shard_map/ppermute | solution.py:371
  107.7 1.2 %finish.1 = (bf16[32,2048]{1,0:T(8,128)(2,1)}, bf16[8,2048]{1,0:T(8,128)(2,1)}) custom-call(f32[640,128]{1,0:T(8,128)S(1)} %get-tuple-element.45.m_ref, f32[640,128]{1,0:T(8,128)S(1)} %get-tuple-element.46.l_ref, f32[640,512]{1,0:T(8,128)S(1)} %get-tuple-element.47.acc_ref, bf16[656,512]{1,0:T(8,128)(2,1)S(1)} %collective-permute-done.14.far_ref, ...), custom_call_target="tpu_custom_call" | custom-call | flops 83886080 | bytes 4063232 | tf_op jit(solution)/shard_map/finish/pallas_call | solution.py:344
  (46 shorter events, 1.1 us)
Async XLA Ops:
  0.6 21.7 %copy-start = (bf16[1024,576]{0,1:T(8,128)(2,1)S(1)}, bf16[1024,576]{0,1:T(8,128)(2,1)}, u32[]{:S(2)}) copy-start(bf16[1024,576]{0,1:T(8,128)(2,1)} %param.13) | copy-start | bytes 3538948
  2.5 7.4 %collective-permute-start = (bf16[4,4,4736]{2,1,0:T(4,128)(2,1)}, bf16[4,4,4736]{2,1,0:T(4,128)(2,1)S(1)}, u32[]{:S(2)}, u32[]{:S(2)}) collective-permute-start(bf16[4,4,4736]{2,1,0:T(4,128)(2,1)} %get-tuple-element.30), channel_id=1, source_target_pairs={{0,4},{4,0},{8,12},{12,8},{16,20},{20,16},{24,28},{28,24},{1,5},{5... | collective-permute-start | bytes 454664 | tf_op jit(solution)/shard_map/ppermute | solution.py:371
  6.4 16.6 %collective-permute-start.4 = (bf16[576,128]{1,0:T(8,128)(2,1)S(1)}, bf16[576,128]{1,0:T(8,128)(2,1)S(1)}, u32[]{:S(2)}, u32[]{:S(2)}) collective-permute-start(bf16[576,128]{1,0:T(8,128)(2,1)S(1)} %slice.44), channel_id=1, source_target_pairs={{0,16},{4,20},{8,24},{12,28},{16,0},{20,4},{24,8},{28,12},{1,17},{... | collective-permute-start | bytes 442376 | tf_op jit(solution)/shard_map/ppermute | solution.py:371
  10.0 6.6 %collective-permute-start.3 = (bf16[2,4,4736]{2,1,0:T(4,128)(2,1)S(1)}, bf16[2,4,4736]{2,1,0:T(4,128)(2,1)S(1)}, u32[]{:S(2)}, u32[]{:S(2)}) collective-permute-start(bf16[2,4,4736]{2,1,0:T(4,128)(2,1)S(1)} %pad_maximum_fusion.3), channel_id=1, source_target_pairs={{0,24},{4,28},{8,16},{12,20},{16,8},{20,12},{24,0},{28,4},{1,25},{... | collective-permute-start | bytes 227336 | tf_op jit(solution)/shard_map/ppermute | solution.py:371
  13.7 8.6 %collective-permute-start.2 = (bf16[2,4,4736]{2,1,0:T(4,128)(2,1)S(1)}, bf16[2,4,4736]{2,1,0:T(4,128)(2,1)S(1)}, u32[]{:S(2)}, u32[]{:S(2)}) collective-permute-start(bf16[2,4,4736]{2,1,0:T(4,128)(2,1)S(1)} %pad_maximum_fusion.2), channel_id=1, source_target_pairs={{0,16},{4,20},{8,24},{12,28},{16,0},{20,4},{24,8},{28,12},{1,17},{... | collective-permute-start | bytes 227336 | tf_op jit(solution)/shard_map/ppermute | solution.py:371
  13.8 8.5 %collective-permute-start.1 = (bf16[2,4,4736]{2,1,0:T(4,128)(2,1)S(1)}, bf16[2,4,4736]{2,1,0:T(4,128)(2,1)S(1)}, u32[]{:S(2)}, u32[]{:S(2)}) collective-permute-start(bf16[2,4,4736]{2,1,0:T(4,128)(2,1)S(1)} %pad_maximum_fusion.1), channel_id=1, source_target_pairs={{0,8},{4,12},{8,0},{12,4},{16,24},{20,28},{24,16},{28,20},{1,9},{5... | collective-permute-start | bytes 227336 | tf_op jit(solution)/shard_map/ppermute | solution.py:371
  14.7 8.3 %copy-start.1 = (bf16[16,128,512]{2,1,0:T(8,128)(2,1)S(1)}, bf16[16,128,512]{2,1,0:T(8,128)(2,1)}, u32[]{:S(2)}) copy-start(bf16[16,128,512]{2,1,0:T(8,128)(2,1)} %w_hbm.1) | copy-start | bytes 6291460
  22.4 30.6 %collective-permute-start.10 = (bf16[576,1024]{1,0:T(8,128)(2,1)S(1)}, bf16[576,1024]{1,0:T(8,128)(2,1)S(1)}, u32[]{:S(2)}, u32[]{:S(2)}) collective-permute-start(bf16[576,1024]{1,0:T(8,128)(2,1)S(1)} %cut.5), channel_id=1, source_target_pairs={{0,4},{4,0},{8,12},{12,8},{16,20},{20,16},{24,28},{28,24},{1,5},{5... | collective-permute-start | bytes 3538952 | tf_op jit(solution)/shard_map/ppermute | solution.py:371
  23.0 2.2 %copy-start.5 = (s32[8]{0:T(128)S(1)}, s32[8]{0:T(128)}, u32[]{:S(2)}) copy-start(s32[8]{0:T(128)} %param.16) | copy-start | bytes 100
  24.3 32.4 %collective-permute-start.9 = (bf16[720,512]{1,0:T(8,128)(2,1)S(1)}, bf16[720,512]{1,0:T(8,128)(2,1)S(1)}, u32[]{:S(2)}, u32[]{:S(2)}) collective-permute-start(bf16[720,512]{1,0:T(8,128)(2,1)S(1)} %get-tuple-element.31.refs_1_.refs_0_), channel_id=1, source_target_pairs={{0,8},{4,12},{8,0},{12,4},{16,24},{20,28},{24,16},{28,20},{1,9},{5... | collective-permute-start | bytes 2211848 | tf_op jit(solution)/shard_map/ppermute | solution.py:371
  25.4 3.6 %copy-start.6 = (s32[8]{0:T(128)S(1)}, s32[8]{0:T(128)}, u32[]{:S(2)}) copy-start(s32[8]{0:T(128)} %param.19) | copy-start | bytes 100
  25.4 26.1 %collective-permute-start.5 = (bf16[576,384]{1,0:T(8,128)(2,1)S(1)}, bf16[576,384]{1,0:T(8,128)(2,1)S(1)}, u32[]{:S(2)}, u32[]{:S(2)}) collective-permute-start(bf16[576,384]{1,0:T(8,128)(2,1)S(1)} %cut.3), channel_id=1, source_target_pairs={{0,16},{4,20},{8,24},{12,28},{16,0},{20,4},{24,8},{28,12},{1,17},{... | collective-permute-start | bytes 1327112 | tf_op jit(solution)/shard_map/ppermute | solution.py:371
  28.9 38.2 %collective-permute-start.8 = (bf16[576,384]{1,0:T(8,128)(2,1)S(1)}, bf16[576,384]{1,0:T(8,128)(2,1)S(1)}, u32[]{:S(2)}, u32[]{:S(2)}) collective-permute-start(bf16[576,384]{1,0:T(8,128)(2,1)S(1)} %get-tuple-element.34), channel_id=1, source_target_pairs={{0,16},{4,20},{8,24},{12,28},{16,0},{20,4},{24,8},{28,12},{1,17},{... | collective-permute-start | bytes 1327112 | tf_op jit(solution)/shard_map/ppermute | solution.py:371
  51.5 29.7 %collective-permute-start.6 = (bf16[576,384]{1,0:T(8,128)(2,1)S(1)}, bf16[576,384]{1,0:T(8,128)(2,1)S(1)}, u32[]{:S(2)}, u32[]{:S(2)}) collective-permute-start(bf16[576,384]{1,0:T(8,128)(2,1)S(1)} %after.5.refs_2_), channel_id=1, source_target_pairs={{0,4},{4,0},{8,12},{12,8},{16,20},{20,16},{24,28},{28,24},{1,5},{5... | collective-permute-start | bytes 1327112 | tf_op jit(solution)/shard_map/ppermute | solution.py:371
  67.1 20.0 %collective-permute-start.11 = (bf16[576,384]{1,0:T(8,128)(2,1)S(1)}, bf16[576,384]{1,0:T(8,128)(2,1)S(1)}, u32[]{:S(2)}, u32[]{:S(2)}) collective-permute-start(bf16[576,384]{1,0:T(8,128)(2,1)S(1)} %after.7.refs_6_.refs_2_), channel_id=1, source_target_pairs={{0,4},{4,0},{8,12},{12,8},{16,20},{20,16},{24,28},{28,24},{1,5},{5... | collective-permute-start | bytes 1327112 | tf_op jit(solution)/shard_map/ppermute | solution.py:371
  68.6 12.6 %collective-permute-start.7 = (bf16[576,128]{1,0:T(8,128)(2,1)S(1)}, bf16[576,128]{1,0:T(8,128)(2,1)S(1)}, u32[]{:S(2)}, u32[]{:S(2)}) collective-permute-start(bf16[576,128]{1,0:T(8,128)(2,1)S(1)} %collective-permute-done.4.refs_4_), channel_id=1, source_target_pairs={{0,4},{4,0},{8,12},{12,8},{16,20},{20,16},{24,28},{28,24},{1,5},{5... | collective-permute-start | bytes 442376 | tf_op jit(solution)/shard_map/ppermute | solution.py:371
  69.2 16.4 %collective-permute-start.12 = (bf16[576,128]{1,0:T(8,128)(2,1)S(1)}, bf16[576,128]{1,0:T(8,128)(2,1)S(1)}, u32[]{:S(2)}, u32[]{:S(2)}) collective-permute-start(bf16[576,128]{1,0:T(8,128)(2,1)S(1)} %get-tuple-element.39), channel_id=1, source_target_pairs={{0,16},{4,20},{8,24},{12,28},{16,0},{20,4},{24,8},{28,12},{1,17},{... | collective-permute-start | bytes 442376 | tf_op jit(solution)/shard_map/ppermute | solution.py:371
  85.6 5.3 %collective-permute-start.13 = (bf16[576,128]{1,0:T(8,128)(2,1)S(1)}, bf16[576,128]{1,0:T(8,128)(2,1)S(1)}, u32[]{:S(2)}, u32[]{:S(2)}) collective-permute-start(bf16[576,128]{1,0:T(8,128)(2,1)S(1)} %after.9.refs_8_.refs_4_), channel_id=1, source_target_pairs={{0,4},{4,0},{8,12},{12,8},{16,20},{20,16},{24,28},{28,24},{1,5},{5... | collective-permute-start | bytes 442376 | tf_op jit(solution)/shard_map/ppermute | solution.py:371
  90.9 2.1 %copy-start.3 = (s32[32]{0:T(128)S(1)}, s32[32]{0:T(128)}, u32[]{:S(2)}) copy-start(s32[32]{0:T(128)} %param.18) | copy-start | bytes 388
  90.9 2.1 %copy-start.4 = (s32[32]{0:T(128)S(1)}, s32[32]{0:T(128)}, u32[]{:S(2)}) copy-start(s32[32]{0:T(128)} %param.17) | copy-start | bytes 388
  92.9 14.7 %collective-permute-start.14 = (bf16[656,512]{1,0:T(8,128)(2,1)S(1)}, bf16[656,512]{1,0:T(8,128)(2,1)S(1)}, u32[]{:S(2)}, u32[]{:S(2)}) collective-permute-start(bf16[656,512]{1,0:T(8,128)(2,1)S(1)} %attend.13), channel_id=1, source_target_pairs={{0,8},{4,12},{8,0},{12,4},{16,24},{20,28},{24,16},{28,20},{1,9},{5... | collective-permute-start | bytes 2015240 | tf_op jit(solution)/shard_map/ppermute | solution.py:371
  94.7 13.0 %copy-start.2 = (bf16[16,512,128]{2,1,0:T(8,128)(2,1)S(1)}, bf16[16,512,128]{2,1,0:T(8,128)(2,1)}, u32[]{:S(2)}) copy-start(bf16[16,512,128]{2,1,0:T(8,128)(2,1)} %w_ref.1) | copy-start | bytes 6291460
